TPU v7x, 32 devices: a whole 2x2x4 slice. The times are simulated.
32 devices in a mesh: rx: 4 (over x, core), ry: 4 (over z), tp: 2 (over y).
Axes of the slice: x: 2, y: 2, z: 4, core: 2. Of those that a mesh axis runs over, the one named last changes fastest.
Arguments:
- weights: float32 [4, 4, 2, 8192, 1024], P('rx', 'ry', None, 'tp'), may hold values from -6 to 6
- factors_rx: float32 [4, 4, 2, 8, 1024], P('rx', 'ry'), may hold values from -6 to 6
- factors_ry: float32 [4, 4, 2, 8, 1024], P('rx', 'ry'), may hold values from -6 to 6
Outputs:
- mixed_weights: float32 [4, 4, 2, 8192, 1024], P('rx', 'ry', None, 'tp')
- next_rx: float32 [4, 4, 2, 8, 1024], P('rx', 'ry')
- next_ry: float32 [4, 4, 2, 8, 1024], P('rx', 'ry')
All inputs are finite; a program needn't handle non-finite values.
Results may differ from a plain program's by a relative error of at most 0.00007.
Values sent between devices are 32-bit elements; how exact they have to be, the bound alone decides.
No kernel may reach another device: no remote copies, remote signals or barrier semaphores. Data moves between devices by JAX's collectives and lax.ppermute only.
A program may use at most 128 MiB of HBM per device.

v0:
```python
import jax
import jax.numpy as jnp
from jax import lax
from jax.sharding import PartitionSpec as P

highest = lax.Precision.HIGHEST
mixing = 0.2


def shifted(value, axis, steps):
    count = lax.axis_size(axis)
    pairs = [(source, (source + steps) % count) for source in range(count)]
    return lax.ppermute(value, axis, pairs)


def with_halo(block, sides, width):
    for axis, dim in sides:
        count = lax.axis_size(axis)
        forward = [(i, i + 1) for i in range(count - 1)]
        forward.append((count - 1, 0))
        backward = [(target, source) for source, target in forward]
        low = lax.ppermute(
            lax.slice_in_dim(block, block.shape[dim] - width, None, axis=dim), axis, forward
        )
        high = lax.ppermute(lax.slice_in_dim(block, 0, width, axis=dim), axis, backward)
        block = jnp.concatenate([low, block, high], axis=dim)
    return block


def select_edges(grid):
    return jnp.stack([grid[2, 1, 1], grid[0, 1, 0], grid[1, 2, 3], grid[1, 0, 2]], 0)


def per_device(weights, factors_rx, factors_ry):
    lower_rx = shifted(factors_rx, "rx", 1)
    lower_ry = shifted(factors_ry, "ry", 1)
    factor_set = jnp.stack([factors_rx[0, 0], lower_rx[0, 0], factors_ry[0, 0], lower_ry[0, 0]], 0)
    local_rows = weights[0, 0]
    projected = jnp.einsum("emrk,mdk->emrd", factor_set, local_rows, precision=highest)
    near_grid = with_halo(projected[None, None], (("rx", 0), ("ry", 1)), 1)
    differ = projected - select_edges(near_grid)
    gram_local = jnp.einsum("emrd,emsd->emrs", differ, differ, precision=highest)
    gram_total = lax.psum(gram_local, "tp")
    lower_factor = jnp.linalg.cholesky(gram_total)
    normalised = lax.linalg.triangular_solve(lower_factor, differ, left_side=True, lower=True)
    back_terms = jnp.einsum("emrd,mdk->emrk", normalised, local_rows, precision=highest)
    shares = lax.psum_scatter(back_terms, "tp", scatter_dimension=3, tiled=True)
    share_grid = with_halo(shares[None, None], (("rx", 0), ("ry", 1)), 1)
    updated = lax.all_gather(shares + select_edges(share_grid), "tp", axis=3, tiled=True)
    correction = jnp.einsum("emrd,emrk->mdk", normalised, updated, precision=highest)
    mixed_weights = weights - mixing * correction[None, None]
    return (mixed_weights, updated[0][None, None], updated[2][None, None])


def solution(mesh):
    return jax.shard_map(
        per_device,
        mesh=mesh,
        in_specs=(
            P("rx", "ry", None, "tp", None),
            P("rx", "ry", None, None, None),
            P("rx", "ry", None, None, None),
        ),
        out_specs=(
            P("rx", "ry", None, "tp", None),
            P("rx", "ry", None, None, None),
            P("rx", "ry", None, None, None),
        ),
        check_vma=False,
    )
```

profile of v0, /device:TPU:0, one launch (start us, length us, event | category | flops | bytes accessed | tf_op | source)
XLA Modules:
  0.0 344.4 jit_solution(4049643030944067987)
XLA Ops:
  7.2 0.0 reduce-scatter.2.cloned.1.call-start
  7.2 0.5 collective-permute-start
  7.7 2.6 collective-permute-start.1
  10.4 1.4 collective-permute-done
  11.8 3.0 collective-permute-done.1
  14.8 33.8 %fusion.4 = f32[4,2,8,4096]{3,2,0,1:T(8,128)S(1)} fusion(f32[1,1,2,4096,1024]{4,3,2,1,0:T(8,128)} %param.3, f32[1,2,8,1024]{3,2,0,1:T(8,128)S(1)} %bitcast.84, f32[1,2,8,1024]{3,2,0,1:T(8,128)} %bitcast.81, f32[1,2,8,1024]{3,2,0,1:T(8,128)S(1)} %bitcast.83, f32[1,2,8,1024]{3,2,0,1:T(8,128)} %bitcast.82), kind=kOutput, calls=%fused_computation.6 | convolution fusion | flops 3221422080 | bytes 34865152 | tf_op jit(solution)/shard_map/emrk,mdk->emrd/dot_general | solution.py:39
  48.7 0.1 copy.85
  48.7 1.5 collective-permute-start.2
  50.3 0.0 collective-permute-start.3
  50.3 23.3 %collective-permute-done.2 = f32[1,1,4,2,8,4096]{5,4,3,2,1,0:T(8,128)S(1)} collective-permute-done((f32[1,1,4,2,8,4096]{5,4,3,2,1,0:T(8,128)S(1)}, f32[1,1,4,2,8,4096]{5,4,3,2,1,0:T(8,128)S(1)}, u32[]{:S(2)}, u32[]{:S(2)}) %collective-permute-start.2) | collective-permute-done | bytes 1048608 | tf_op jit(solution)/shard_map/ppermute | solution.py:25
  73.6 1.5 collective-permute-done.3
  75.1 0.3 pad_maximum_fusion
  75.4 0.1 collective-permute-start.5
  75.5 3.8 %collective-permute-start.4 = (f32[3,1,4,2,8,4096]{5,4,3,2,1,0:T(8,128)S(1)}, f32[3,1,4,2,8,4096]{5,4,3,2,1,0:T(8,128)S(1)}, u32[]{:S(2)}, u32[]{:S(2)}) collective-permute-start(f32[3,1,4,2,8,4096]{5,4,3,2,1,0:T(8,128)S(1)} %pad_maximum_fusion), channel_id=1, source_target_pairs={{2,0},{4,2},{6,4},{0,6},{3,1},{5,3},{7,5},{1,7},{10,8},{12,10},{14... | collective-permute-start | bytes 9437192 | tf_op jit(solution)/shard_map/ppermute | solution.py:25
  79.4 68.9 %collective-permute-done.5 = f32[3,1,4,2,8,4096]{5,4,3,2,1,0:T(8,128)S(1)} collective-permute-done((f32[3,1,4,2,8,4096]{5,4,3,2,1,0:T(8,128)S(1)}, f32[3,1,4,2,8,4096]{5,4,3,2,1,0:T(8,128)S(1)}, u32[]{:S(2)}, u32[]{:S(2)}) %collective-permute-start.5) | collective-permute-done | bytes 3145760 | tf_op jit(solution)/shard_map/ppermute | solution.py:22
  148.3 64.2 %collective-permute-done.4 = f32[3,1,4,2,8,4096]{5,4,3,2,1,0:T(8,128)S(1)} collective-permute-done((f32[3,1,4,2,8,4096]{5,4,3,2,1,0:T(8,128)S(1)}, f32[3,1,4,2,8,4096]{5,4,3,2,1,0:T(8,128)S(1)}, u32[]{:S(2)}, u32[]{:S(2)}) %collective-permute-start.4) | collective-permute-done | bytes 3145760 | tf_op jit(solution)/shard_map/ppermute | solution.py:25
  212.5 2.3 fusion.13
  214.8 8.7 %psum.7 = f32[4,2,8,8]{2,3,1,0:T(8,128)S(1)} all-reduce(f32[4,2,8,8]{2,3,1,0:T(8,128)S(1)} %fusion.13), channel_id=1, replica_groups=mesh['rx'=4,'ry'=4,'tp'=2] {'tp'}, use_global_device_ids=true, to_apply=%region_0.0 | all-reduce | flops 512 | bytes 4096 | tf_op jit(solution)/shard_map/psum | solution.py:43
  223.5 0.1 copy.60
  223.6 5.8 %custom-call.7 = f32[4,2,8,8]{3,2,1,0:T(8,128)S(1)} custom-call(f32[4,2,8,8]{3,2,1,0:T(8,128)S(1)} %fusion.24), custom_call_target="Cholesky" | custom-call | tf_op jit(solution)/shard_map/jit(cholesky)/cholesky | solution.py:44
  229.4 0.1 select_reduce_fusion
  229.5 0.1 compare_reduce_fusion
  229.7 0.1 select_bitcast_fusion
  229.8 5.0 %custom-call.8 = f32[4,2,1,8,8]{3,4,2,1,0:T(8,128)S(1)} custom-call(f32[4,2,1,8,8]{4,3,2,1,0:T(8,128)S(1)} %select_bitcast_fusion), custom_call_target="InvertDiagBlocksLowerTriangular" | custom-call | tf_op jit(solution)/shard_map/triangular_solve | solution.py:45
  234.8 1.1 fusion.11
  235.9 23.5 %fusion.7 = f32[4,2,8,1024]{3,2,0,1:T(8,128)} fusion(f32[1,1,2,4096,1024]{4,3,2,1,0:T(8,128)} %param.3, f32[4,2,8,4096]{3,2,1,0:T(8,128)S(1)} %fusion.11), kind=kOutput, calls=%fused_computation.8 | convolution fusion | flops 3221225472 | bytes 34865152 | tf_op jit(solution)/shard_map/emrd,mdk->emrk/dot_general | solution.py:46
  259.4 0.0 reduce-scatter.2.cloned.1.call-update
  259.4 10.7 %reduce-scatter.2.cloned.1.call-done = f32[4,2,8,512]{3,2,0,1:T(8,128)} async-done(((f32[4,2,8,1024]{3,2,0,1:T(8,128)}), f32[4,2,8,512]{3,2,0,1:T(8,128)}) %reduce-scatter.2.cloned.1.call-update) | async-done | bytes 131088 | tf_op jit(solution)/shard_map/reduce_scatter | solution.py:47
  270.1 0.9 copy.86
  271.0 0.9 collective-permute-start.6
  272.0 0.0 collective-permute-start.7
  272.0 3.8 %collective-permute-done.6 = f32[1,1,4,2,8,512]{5,4,3,2,1,0:T(8,128)S(1)} collective-permute-done((f32[1,1,4,2,8,512]{5,4,3,2,1,0:T(8,128)S(1)}, f32[1,1,4,2,8,512]{5,4,3,2,1,0:T(8,128)S(1)}, u32[]{:S(2)}, u32[]{:S(2)}) %collective-permute-start.6) | collective-permute-done | bytes 131104 | tf_op jit(solution)/shard_map/ppermute | solution.py:25
  275.8 1.1 collective-permute-done.7
  276.9 1.5 collective-permute-start.9
  278.5 2.3 collective-permute-start.8
  280.8 10.1 %collective-permute-done.9 = f32[3,1,4,2,8,512]{5,4,3,2,1,0:T(8,128)S(1)} collective-permute-done((f32[3,1,4,2,8,512]{5,4,3,2,1,0:T(8,128)S(1)}, f32[3,1,4,2,8,512]{5,4,3,2,1,0:T(8,128)S(1)}, u32[]{:S(2)}, u32[]{:S(2)}) %collective-permute-start.9) | collective-permute-done | bytes 393248 | tf_op jit(solution)/shard_map/ppermute | solution.py:22
  290.9 6.0 %collective-permute-done.8 = f32[3,1,4,2,8,512]{5,4,3,2,1,0:T(8,128)S(1)} collective-permute-done((f32[3,1,4,2,8,512]{5,4,3,2,1,0:T(8,128)S(1)}, f32[3,1,4,2,8,512]{5,4,3,2,1,0:T(8,128)S(1)}, u32[]{:S(2)}, u32[]{:S(2)}) %collective-permute-start.8) | collective-permute-done | bytes 393248 | tf_op jit(solution)/shard_map/ppermute | solution.py:25
  296.9 0.9 maximum_add_fusion
  297.8 5.6 %all_gather.3 = f32[4,2,8,1024]{3,2,0,1:T(8,128)S(1)} all-gather(f32[4,2,8,512]{3,2,0,1:T(8,128)S(1)} %maximum_add_fusion), channel_id=1, replica_groups=mesh['rx'=4,'ry'=4,'tp'=2] {'tp'}, dimensions={3}, use_global_device_ids=true | all-gather | bytes 393216 | tf_op jit(solution)/shard_map/all_gather | solution.py:49
  303.5 33.5 %bitcast_subtract_fusion = f32[1,1,2,4096,1024]{4,3,2,1,0:T(8,128)} fusion(f32[1,1,2,4096,1024]{4,3,2,1,0:T(8,128)} %param.3, f32[4,2,8,4096]{3,2,1,0:T(8,128)S(1)} %fusion.11, f32[4,2,8,1024]{3,2,0,1:T(8,128)S(1)} %all_gather.3), kind=kOutput, calls=%fused_computation | convolution fusion | flops 3238002688 | bytes 68419584 | tf_op jit(solution)/shard_map/emrd,emrk->mdk/dot_general | solution.py:50
  336.9 0.7 slice_bitcast_fusion.4
  (12 shorter events, 0.1 us)
Async XLA Ops:
  7.2 263.0 %reduce-scatter.2.cloned.1.call-start = ((), (), s32[]{:S(2)}) async-start(), calls=%async_computation.1 | async-start | bytes 393216 | tf_op jit(solution)/shard_map/reduce_scatter | solution.py:47
  7.2 4.6 %collective-permute-start = (f32[1,1,2,8,1024]{4,3,2,1,0:T(8,128)}, f32[1,1,2,8,1024]{4,3,2,1,0:T(8,128)S(1)}, u32[]{:S(2)}, u32[]{:S(2)}) collective-permute-start(f32[1,1,2,8,1024]{4,3,2,1,0:T(8,128)} %param.4), channel_id=1, source_target_pairs={{0,8},{8,16},{16,24},{24,0},{1,9},{9,17},{17,25},{25,1},{2,10},{10... | collective-permute-start | bytes 196616 | tf_op jit(solution)/shard_map/ppermute | solution.py:13
  7.7 7.1 %collective-permute-start.1 = (f32[1,1,2,8,1024]{4,3,2,1,0:T(8,128)}, f32[1,1,2,8,1024]{4,3,2,1,0:T(8,128)S(1)}, u32[]{:S(2)}, u32[]{:S(2)}) collective-permute-start(f32[1,1,2,8,1024]{4,3,2,1,0:T(8,128)} %param.5), channel_id=1, source_target_pairs={{0,2},{2,4},{4,6},{6,0},{1,3},{3,5},{5,7},{7,1},{8,10},{10,12},{12... | collective-permute-start | bytes 196616 | tf_op jit(solution)/shard_map/ppermute | solution.py:13
  48.7 24.8 %collective-permute-start.2 = (f32[1,1,4,2,8,4096]{5,4,3,2,1,0:T(8,128)S(1)}, f32[1,1,4,2,8,4096]{5,4,3,2,1,0:T(8,128)S(1)}, u32[]{:S(2)}, u32[]{:S(2)}) collective-permute-start(f32[1,1,4,2,8,4096]{5,4,3,2,1,0:T(8,128)S(1)} %bitcast.75), channel_id=1, source_target_pairs={{8,0},{16,8},{24,16},{0,24},{9,1},{17,9},{25,17},{1,25},{10,2},{18... | collective-permute-start | bytes 3145736 | tf_op jit(solution)/shard_map/ppermute | solution.py:25
  50.3 24.8 %collective-permute-start.3 = (f32[1,1,4,2,8,4096]{5,4,3,2,1,0:T(8,128)S(1)}, f32[1,1,4,2,8,4096]{5,4,3,2,1,0:T(8,128)S(1)}, u32[]{:S(2)}, u32[]{:S(2)}) collective-permute-start(f32[1,1,4,2,8,4096]{5,4,3,2,1,0:T(8,128)S(1)} %bitcast.76), channel_id=1, source_target_pairs={{0,8},{8,16},{16,24},{24,0},{1,9},{9,17},{17,25},{25,1},{2,10},{10... | collective-permute-start | bytes 3145736 | tf_op jit(solution)/shard_map/ppermute | solution.py:22
  75.4 72.9 %collective-permute-start.5 = (f32[3,1,4,2,8,4096]{5,4,3,2,1,0:T(8,128)S(1)}, f32[3,1,4,2,8,4096]{5,4,3,2,1,0:T(8,128)S(1)}, u32[]{:S(2)}, u32[]{:S(2)}) collective-permute-start(f32[3,1,4,2,8,4096]{5,4,3,2,1,0:T(8,128)S(1)} %pad_maximum_fusion), channel_id=1, source_target_pairs={{0,2},{2,4},{4,6},{6,0},{1,3},{3,5},{5,7},{7,1},{8,10},{10,12},{12... | collective-permute-start | bytes 9437192 | tf_op jit(solution)/shard_map/ppermute | solution.py:22
  75.5 137.0 %collective-permute-start.4 = (f32[3,1,4,2,8,4096]{5,4,3,2,1,0:T(8,128)S(1)}, f32[3,1,4,2,8,4096]{5,4,3,2,1,0:T(8,128)S(1)}, u32[]{:S(2)}, u32[]{:S(2)}) collective-permute-start(f32[3,1,4,2,8,4096]{5,4,3,2,1,0:T(8,128)S(1)} %pad_maximum_fusion), channel_id=1, source_target_pairs={{2,0},{4,2},{6,4},{0,6},{3,1},{5,3},{7,5},{1,7},{10,8},{12,10},{14... | collective-permute-start | bytes 9437192 | tf_op jit(solution)/shard_map/ppermute | solution.py:25
  271.0 4.8 %collective-permute-start.6 = (f32[1,1,4,2,8,512]{5,4,3,2,1,0:T(8,128)S(1)}, f32[1,1,4,2,8,512]{5,4,3,2,1,0:T(8,128)S(1)}, u32[]{:S(2)}, u32[]{:S(2)}) collective-permute-start(f32[1,1,4,2,8,512]{5,4,3,2,1,0:T(8,128)S(1)} %bitcast.78), channel_id=1, source_target_pairs={{8,0},{16,8},{24,16},{0,24},{9,1},{17,9},{25,17},{1,25},{10,2},{18... | collective-permute-start | bytes 393224 | tf_op jit(solution)/shard_map/ppermute | solution.py:25
  272.0 4.9 %collective-permute-start.7 = (f32[1,1,4,2,8,512]{5,4,3,2,1,0:T(8,128)S(1)}, f32[1,1,4,2,8,512]{5,4,3,2,1,0:T(8,128)S(1)}, u32[]{:S(2)}, u32[]{:S(2)}) collective-permute-start(f32[1,1,4,2,8,512]{5,4,3,2,1,0:T(8,128)S(1)} %bitcast.79), channel_id=1, source_target_pairs={{0,8},{8,16},{16,24},{24,0},{1,9},{9,17},{17,25},{25,1},{2,10},{10... | collective-permute-start | bytes 393224 | tf_op jit(solution)/shard_map/ppermute | solution.py:22
  276.9 13.9 %collective-permute-start.9 = (f32[3,1,4,2,8,512]{5,4,3,2,1,0:T(8,128)S(1)}, f32[3,1,4,2,8,512]{5,4,3,2,1,0:T(8,128)S(1)}, u32[]{:S(2)}, u32[]{:S(2)}) collective-permute-start(f32[3,1,4,2,8,512]{5,4,3,2,1,0:T(8,128)S(1)} %pad_maximum_fusion.1), channel_id=1, source_target_pairs={{0,2},{2,4},{4,6},{6,0},{1,3},{3,5},{5,7},{7,1},{8,10},{10,12},{12... | collective-permute-start | bytes 1179656 | tf_op jit(solution)/shard_map/ppermute | solution.py:22
  278.5 18.4 %collective-permute-start.8 = (f32[3,1,4,2,8,512]{5,4,3,2,1,0:T(8,128)S(1)}, f32[3,1,4,2,8,512]{5,4,3,2,1,0:T(8,128)S(1)}, u32[]{:S(2)}, u32[]{:S(2)}) collective-permute-start(f32[3,1,4,2,8,512]{5,4,3,2,1,0:T(8,128)S(1)} %pad_maximum_fusion.1), channel_id=1, source_target_pairs={{2,0},{4,2},{6,4},{0,6},{3,1},{5,3},{7,5},{1,7},{10,8},{12,10},{14... | collective-permute-start | bytes 1179656 | tf_op jit(solution)/shard_map/ppermute | solution.py:25
Sparse Core Ops, SparseCore 0:
  259.6 10.5 reduce-scatter.1
where the time goes:
time: 345 us; the launch traced here: 344 us
  waiting for transfers between devices  194 us (56%)
  matrix products  94.2 us (27%)
  blocking collectives  14.3 us (4%)
  between operations  14.1 us (4%)
  starting transfers between devices  13.4 us (4%)
  other arithmetic  12.4 us (4%)
    ppermute x4, waiting for transfers between devices, with_halo(): lax.ppermute(lax.slice_in_dim(block, 0, width, axis=dim), axis, backward)  97.3 us
    ppermute x4, waiting for transfers between devices, with_halo(): lax.ppermute(lax.slice_in_dim(block, block.shape[dim] - width, None, axis...  81.6 us
    dot_general x1, matrix products, per_device(): jnp.einsum('emrk,mdk->emrd', factor_set, local_rows, precision=highest)  33.8 us
    dot_general x1, matrix products, per_device(): jnp.einsum('emrd,emrk->mdk', normalised, updated, precision=highest)  33.5 us
    dot_general x1, matrix products, per_device(): jnp.einsum('emrd,mdk->emrk', normalised, local_rows, precision=highest)  23.5 us
    reduce_scatter x1, waiting for transfers between devices, per_device(): shares = lax.psum_scatter(back_terms, 'tp', scatter_dimension=3, tiled=True)  10.7 us
    psum x1, blocking collectives, per_device(): gram_total = lax.psum(gram_local, 'tp')  8.7 us
    ppermute x4, starting transfers between devices, with_halo(): lax.ppermute(lax.slice_in_dim(block, 0, width, axis=dim), axis, backward)  8.62 us
  transfers between devices with their start and end apart: 11, of which 11 were waited for; matrix products, arithmetic and copies ran while one was open for 0% of the time, Pallas kernels for 0%

commit v1 on v0

v1 whole, which is shorter than its diff:
```python
import functools

import jax
import jax.numpy as jnp
from jax import lax
from jax.experimental import pallas as pl
from jax.experimental.pallas import tpu as pltpu
from jax.sharding import PartitionSpec as P

f32 = jnp.float32
bf16 = jnp.bfloat16
mixing = 0.2
edges = 4
mib = 1 << 20

NN = (((1,), (0,)), ((), ()))
NT = (((1,), (1,)), ((), ()))
TN = (((0,), (0,)), ((), ()))

in_vmem = pl.BlockSpec(memory_space=pltpu.VMEM)
in_hbm = pl.BlockSpec(memory_space=pltpu.HBM)


def vmem(value):
    return pltpu.with_memory_space_constraint(value, pltpu.VMEM)


def hbm(value):
    return pltpu.with_memory_space_constraint(value, pltpu.HBM)


def dot(a, b, dims):
    return lax.dot_general(a, b, dims, preferred_element_type=f32)


def split(value):
    high = value.astype(bf16)
    return high, (value - high.astype(f32)).astype(bf16)


def chunk_of(rows, most):
    size = min(rows, most)
    while rows % size:
        size //= 2
    return size


def shifted(value, axis, steps):
    count = lax.axis_size(axis)
    pairs = [(source, (source + steps) % count) for source in range(count)]
    return lax.ppermute(value, axis, pairs)


def from_partner(value, axis, distance):
    count = lax.axis_size(axis)
    return lax.ppermute(value, axis, [(i, i ^ distance) for i in range(count)])


def load_kernel(weights, held, sems):
    rows = held.shape[1]
    parts = sems.shape[0]
    size = rows // parts
    copies = [
        pltpu.make_async_copy(
            weights.at[0, 0, 0, pl.ds(i * size, size)], held.at[0, pl.ds(i * size, size)], sems.at[i]
        )
        for i in range(parts)
    ]
    for copy in copies:
        copy.start()
    for copy in copies:
        copy.wait()


def load(weights):
    return pl.pallas_call(
        load_kernel,
        name="load",
        out_shape=jax.ShapeDtypeStruct(weights.shape[2:], f32),
        in_specs=[in_hbm],
        out_specs=in_vmem,
        scratch_shapes=[pltpu.SemaphoreType.DMA((4,))],
        compiler_params=pltpu.CompilerParams(vmem_limit_bytes=4 * mib),
    )(hbm(weights))


def project_kernel(mat, chunk, following, same, f0, f1, f2, f3, *rest):
    if following:
        weights, o0, o1, o2, o3, held, sem = rest
        copy = pltpu.make_async_copy(weights.at[0, 0, mat + 1], held.at[mat + 1], sem)
        copy.start()
    else:
        o0, o1, o2, o3, held = rest
    rank = f0.shape[-2]
    high, low = split(jnp.concatenate([f[0, 0, mat] for f in (f0, f1, f2, f3)], 0))
    stack = jnp.concatenate(
        [jnp.concatenate([high, high], 1), jnp.concatenate([low, low], 1)], 0
    )
    width = edges * rank

    @pl.loop(0, held.shape[1] // chunk)
    def _(step):
        here = pl.ds(pl.multiple_of(step * chunk, chunk), chunk)
        w_high, w_low = split(held[mat, here, :])
        both = dot(stack, jnp.concatenate([w_high, w_low], 1), NT)
        total = both[:width] + both[width:]
        for edge, out in enumerate((o0, o1, o2, o3)):
            out[:, here] = total[edge * rank : (edge + 1) * rank]

    if following:
        copy.wait()


def project(held, factors, mat, weights=None):
    rows = held.shape[1]
    rank = factors[0].shape[-2]
    following = weights is not None
    shapes = [jax.ShapeDtypeStruct((rank, rows), f32)] * edges
    shapes = shapes + [jax.ShapeDtypeStruct(held.shape, f32)]
    scratch = []
    args = [vmem(held), *factors]
    in_specs = [in_vmem] * 5
    if following:
        args.append(hbm(weights))
        in_specs.append(in_hbm)
        scratch = [pltpu.SemaphoreType.DMA]
    return pl.pallas_call(
        functools.partial(project_kernel, mat, chunk_of(rows, 1024), following),
        name=f"project{mat}",
        out_shape=shapes,
        in_specs=in_specs,
        out_specs=[in_vmem] * (edges + 1),
        scratch_shapes=scratch,
        input_output_aliases={0: edges},
        compiler_params=pltpu.CompilerParams(vmem_limit_bytes=4 * mib),
    )(*args)


def back_kernel(mat, chunk, same, o0, o1, o2, o3, n0, n1, n2, n3, differ, sums, held):
    rank = o0.shape[0]
    width = edges * rank
    features = held.shape[2]
    sums[...] = jnp.zeros_like(sums)

    def body(step, gram):
        here = pl.ds(pl.multiple_of(step * chunk, chunk), chunk)
        p = jnp.concatenate(
            [o[:, here] - n[:, here] for o, n in zip((o0, o1, o2, o3), (n0, n1, n2, n3))], 0
        )
        differ[:, here] = p
        high, low = split(p)
        w_high, w_low = split(held[mat, here, :])
        pair = jnp.concatenate([high, low], 0)
        stack = jnp.concatenate([pair, pair], 1)
        both = dot(stack, jnp.concatenate([w_high, w_low], 0), NN)
        sums[:, :features] += both[:width] + both[width:]
        return gram + dot(pair, pair, NT)

    gram = lax.fori_loop(
        0, held.shape[1] // chunk, body, jnp.zeros((2 * width, 2 * width), f32)
    )
    total = (gram[:width, :width] + gram[width:, width:]) + (
        gram[:width, width:] + gram[width:, :width]
    )
    for edge in range(edges):
        here = slice(edge * rank, (edge + 1) * rank)
        sums[here, features : features + rank] = total[here, here]


def back(held, own, near, mat):
    _, rows, features = held.shape
    rank = own[0].shape[0]
    return pl.pallas_call(
        functools.partial(back_kernel, mat, chunk_of(rows, 1024)),
        name=f"back{mat}",
        out_shape=[
            jax.ShapeDtypeStruct((edges * rank, rows), f32),
            jax.ShapeDtypeStruct((edges * rank, features + 128), f32),
            jax.ShapeDtypeStruct(held.shape, f32),
        ],
        in_specs=[in_vmem] * 9,
        out_specs=[in_vmem] * 3,
        input_output_aliases={0: 2},
        compiler_params=pltpu.CompilerParams(vmem_limit_bytes=4 * mib),
    )(vmem(held), *own, *near)


def add_kernel(same, mine, other, b0, b1, b2, b3, gram, held):
    rank, features = b0.shape
    for edge, out in enumerate((b0, b1, b2, b3)):
        here = slice(edge * rank, (edge + 1) * rank)
        out[...] = mine[here, :features] + other[here, :features]
    gram[...] = mine[:, features:] + other[:, features:]


def add(held, mine, other, rank, mat):
    width, wide = mine.shape
    features = wide - 128
    return pl.pallas_call(
        add_kernel,
        name=f"add{mat}",
        out_shape=[jax.ShapeDtypeStruct((rank, features), f32)] * edges
        + [jax.ShapeDtypeStruct((width, 128), f32), jax.ShapeDtypeStruct(held.shape, f32)],
        in_specs=[in_vmem] * 3,
        out_specs=[in_vmem] * 6,
        input_output_aliases={0: 5},
        compiler_params=pltpu.CompilerParams(vmem_limit_bytes=4 * mib),
    )(vmem(held), mine, other)


def inverse_kernel(rank, same, gram, inverse, held):
    width = gram.shape[0]
    shape = (edges, rank, 128)
    row = lax.broadcasted_iota(jnp.int32, shape, 1)
    lane = lax.broadcasted_iota(jnp.int32, shape, 2)
    edge = lax.broadcasted_iota(jnp.int32, shape, 0)
    value = gram[...].reshape(shape)
    value = jnp.where(lane < rank, value, (lane == width + edge * rank + row).astype(f32))
    pivots = jnp.ones((edges, rank, 1), f32)
    for j in range(rank):
        pivot = value[:, j : j + 1, j : j + 1]
        pivots = jnp.where(row[:, :, :1] == j, pivot, pivots)
        factor = jnp.where(row > j, value[:, :, j : j + 1] / pivot, 0.0)
        value = value - factor * value[:, j : j + 1, :]
    value = value / jnp.sqrt(pivots)
    inverse[...] = value.reshape(width, 128)


def inverse_factor(held, gram, rank, mat):
    return pl.pallas_call(
        functools.partial(inverse_kernel, rank),
        name=f"inverse{mat}",
        out_shape=[
            jax.ShapeDtypeStruct(gram.shape, f32),
            jax.ShapeDtypeStruct(held.shape, f32),
        ],
        in_specs=[in_vmem] * 2,
        out_specs=[in_vmem] * 2,
        input_output_aliases={0: 1},
        compiler_params=pltpu.CompilerParams(vmem_limit_bytes=4 * mib),
    )(vmem(held), gram)


def mix_kernel(
    mat, chunk, slots, same, differ, inverse, b0, b1, b2, b3, n0, n1, n2, n3, *rest
):
    mixed, next_rx, next_ry, held, buffer, sems = rest[-6:]
    rank = b0.shape[0]
    width = edges * rank
    factor = inverse[:, width : 2 * width]
    sums = jnp.concatenate(
        [b[...] + n[...] for b, n in zip((b0, b1, b2, b3), (n0, n1, n2, n3))], 0
    )
    updated = lax.dot_general(
        factor, sums, NN, precision=lax.Precision.HIGHEST, preferred_element_type=f32
    )
    next_rx[...] = updated[:rank]
    next_ry[...] = updated[2 * rank : 3 * rank]
    right = mixing * lax.dot_general(
        factor, updated, TN, precision=lax.Precision.HIGHEST, preferred_element_type=f32
    )
    r_high, r_low = split(right)
    terms = jnp.concatenate([r_high, r_high, r_low, r_low], 0)
    steps = held.shape[1] // chunk

    def copy(step):
        slot = lax.rem(step, slots)
        return pltpu.make_async_copy(
            buffer.at[slot],
            mixed.at[0, 0, mat, pl.ds(pl.multiple_of(step * chunk, chunk), chunk)],
            sems.at[slot],
        )

    @pl.loop(0, steps)
    def _(step):
        here = pl.ds(pl.multiple_of(step * chunk, chunk), chunk)

        @pl.when(step >= slots)
        def _():
            copy(step - slots).wait()

        high, low = split(differ[:, here])
        lhs = jnp.concatenate([high, low, high, low], 0)
        buffer[lax.rem(step, slots)] = held[mat, here, :] - dot(lhs, terms, TN)
        copy(step).start()

    for step in range(max(steps - slots, 0), steps):
        copy(step).wait()


def mix(held, differ, inverse, sums, near, mat, shape, previous=None):
    _, rows, features = held.shape
    rank = sums[0].shape[0]
    chunk = chunk_of(rows, 256)
    slots = 3
    args = [vmem(held), differ, inverse, *sums, *near]
    specs = [in_vmem] * 11
    aliases = {0: 3}
    if previous is not None:
        args.append(hbm(previous))
        specs.append(in_hbm)
        aliases = {0: 3, 11: 0}
    return pl.pallas_call(
        functools.partial(mix_kernel, mat, chunk, slots),
        name=f"mix{mat}",
        out_shape=[
            jax.ShapeDtypeStruct(shape, f32),
            jax.ShapeDtypeStruct((rank, features), f32),
            jax.ShapeDtypeStruct((rank, features), f32),
            jax.ShapeDtypeStruct(held.shape, f32),
        ],
        in_specs=specs,
        out_specs=[in_hbm, in_vmem, in_vmem, in_vmem],
        scratch_shapes=[
            pltpu.VMEM((slots, chunk, features), f32),
            pltpu.SemaphoreType.DMA((slots,)),
        ],
        input_output_aliases=aliases,
        compiler_params=pltpu.CompilerParams(vmem_limit_bytes=8 * mib),
    )(*args)


def exchange(values):
    return [
        shifted(values[1], "rx", -1),
        shifted(values[0], "rx", 1),
        shifted(values[3], "ry", -1),
        shifted(values[2], "ry", 1),
    ]


def per_device(weights, factors_rx, factors_ry):
    mats = weights.shape[2]
    rank = factors_rx.shape[-2]
    factors = [
        factors_rx,
        shifted(factors_rx, "rx", 1),
        factors_ry,
        shifted(factors_ry, "ry", 1),
    ]
    held = load(weights)
    own = []
    for mat in range(mats):
        *own_mat, held = project(held, factors, mat, weights if mat + 1 < mats else None)
        own.append(own_mat)
    near = [exchange(own_mat) for own_mat in own]
    differ, sums, inverse, near_sums = [], [], [], []
    tp = lax.axis_size("tp")
    pairs = []
    for mat in range(mats):
        p, terms, held = back(held, own[mat], near[mat], mat)
        distance = 1
        while 2 * distance < tp:
            terms = terms + from_partner(terms, "tp", distance)
            distance *= 2
        other = from_partner(terms, "tp", distance) if tp > 1 else jnp.zeros_like(terms)
        differ.append(p)
        pairs.append((terms, other))
    grams = []
    for mat in range(mats):
        *sum_mat, gram, held = add(held, *pairs[mat], rank, mat)
        sums.append(sum_mat)
        near_sums.append(exchange(sum_mat))
        grams.append(gram)
    for mat in range(mats):
        factor, held = inverse_factor(held, grams[mat], rank, mat)
        inverse.append(factor)
    mixed = None
    next_rx, next_ry = [], []
    for mat in range(mats):
        mixed, rx, ry, held = mix(
            held,
            differ[mat],
            inverse[mat],
            sums[mat],
            near_sums[mat],
            mat,
            weights.shape,
            mixed,
        )
        next_rx.append(rx)
        next_ry.append(ry)
    return mixed, jnp.stack(next_rx)[None, None], jnp.stack(next_ry)[None, None]


def solution(mesh):
    return jax.shard_map(
        per_device,
        mesh=mesh,
        in_specs=(
            P("rx", "ry", None, "tp", None),
            P("rx", "ry", None, None, None),
            P("rx", "ry", None, None, None),
        ),
        out_specs=(
            P("rx", "ry", None, "tp", None),
            P("rx", "ry", None, None, None),
            P("rx", "ry", None, None, None),
        ),
        check_vma=False,
    )
```

time: 345 us -> 94.9 us (0.28)
  waiting for transfers between devices: 194 us -> 2.21 us
  matrix products: 94.2 us -> 0 us
  Pallas kernels: 0 us -> 43.5 us
  local copies, waits for them, and re-layouts: 1.8 us -> 22.2 us
  blocking collectives: 14.3 us -> 0 us
  between operations: 14.1 us -> 0.82 us
  starting transfers between devices: 13.4 us -> 25.3 us
  other arithmetic: 12.4 us -> 0.66 us
    ppermute x8 -> x2, waiting for transfers between devices: 179 us -> 2.16 us  [from_partner(): return lax.ppermute(value, axis, [(i, i ^ distance) for i in range(count)])]
    dot_general x4 -> x0, matrix products: 93.1 us -> none  [the longest x1 33.8 us: per_device(): jnp.einsum('emrk,mdk->emrd', factor_set, local_rows, precision=highest)]
    pallas_call x0 -> x11, Pallas kernels: none -> 43.5 us  [the longest x2 16.5 us: mix(): pl.pallas_call(functools.partial(mix_kernel, mat, chunk, slots), name=f'm...]
    unnamed x0 -> x8, local copies, waits for them, and re-layouts: none -> 22.2 us
    ppermute x2 -> x18, starting transfers between devices: 3.14 us -> 23.2 us  [shifted(): return lax.ppermute(value, axis, pairs)]
    another operation x7 -> x0, other arithmetic: 11.2 us -> none  [the longest x4 6.07 us: per_device(): lower_factor = jnp.linalg.cholesky(gram_total)]
    reduce_scatter x1 -> x0, waiting for transfers between devices: 10.7 us -> none  [per_device(): shares = lax.psum_scatter(back_terms, 'tp', scatter_dimension=3, tiled=True)]
    psum x1 -> x0, blocking collectives: 8.7 us -> none  [per_device(): gram_total = lax.psum(gram_local, 'tp')]
  transfers between devices with their start and end apart: 11 -> 20, of which waited for: 11 -> 1; matrix products, arithmetic and copies ran while one was open for 0% -> 0% of each run, Pallas kernels for 0% -> 31%
where the time goes in v1:
time: 94.9 us; the launch traced here: 94.7 us
  Pallas kernels  43.5 us (46%)
  starting transfers between devices  25.3 us (27%)
  local copies, waits for them, and re-layouts  22.2 us (23%)
  waiting for transfers between devices  2.21 us (2%)
    ppermute x18, starting transfers between devices, shifted(): return lax.ppermute(value, axis, pairs)  23.2 us
    unnamed x8, local copies, waits for them, and re-layouts  22.2 us
    pallas_call x2, Pallas kernels, mix(): pl.pallas_call(functools.partial(mix_kernel, mat, chunk, slots), name=f'm...  16.5 us
    pallas_call x2, Pallas kernels, project(): pl.pallas_call(functools.partial(project_kernel, mat, chunk_of(rows, 1024...  11.4 us
    pallas_call x2, Pallas kernels, back(): pl.pallas_call(functools.partial(back_kernel, mat, chunk_of(rows, 1024)),...  8.37 us
    pallas_call x1, Pallas kernels, load(): pl.pallas_call(load_kernel, name='load', out_shape=jax.ShapeDtypeStruct(w...  5.89 us
    ppermute x2, waiting for transfers between devices, from_partner(): return lax.ppermute(value, axis, [(i, i ^ distance) for i in range(count)])  2.16 us
    ppermute x2, starting transfers between devices, from_partner(): return lax.ppermute(value, axis, [(i, i ^ distance) for i in range(count)])  2.04 us
  transfers between devices with their start and end apart: 20, of which 1 were waited for; matrix products, arithmetic and copies ran while one was open for 0% of the time, Pallas kernels for 31%

profile of v1, /device:TPU:0, one launch (start us, length us, event | category | flops | bytes accessed | tf_op | source)
XLA Modules:
  0.0 94.7 jit_solution(5840287584533852513)
XLA Ops:
  0.7 0.5 collective-permute-start
  1.2 2.6 %collective-permute-start.1 = (f32[1,1,2,8,1024]{4,3,2,1,0:T(8,128)}, f32[1,1,2,8,1024]{4,3,2,1,0:T(8,128)S(1)}, u32[]{:S(2)}, u32[]{:S(2)}) collective-permute-start(f32[1,1,2,8,1024]{4,3,2,1,0:T(8,128)} %f2.3), channel_id=1, source_target_pairs={{0,2},{2,4},{4,6},{6,0},{1,3},{3,5},{5,7},{7,1},{8,10},{10,12},{12... | collective-permute-start | bytes 196616 | tf_op jit(solution)/shard_map/ppermute | solution.py:51
  3.8 5.9 %load.1.same = f32[2,4096,1024]{2,1,0:T(8,128)S(1)} custom-call(f32[1,1,2,4096,1024]{4,3,2,1,0:T(8,128)} %rest_0_.1), custom_call_target="tpu_custom_call" | custom-call | tf_op jit(solution)/shard_map/load/pallas_call | solution.py:76
  9.7 0.0 collective-permute-done.1.f3
  9.7 5.8 %project0.1 = (f32[8,4096]{1,0:T(8,128)S(1)}, f32[8,4096]{1,0:T(8,128)S(1)}, f32[8,4096]{1,0:T(8,128)S(1)}, f32[8,4096]{1,0:T(8,128)S(1)}, f32[2,4096,1024]{2,1,0:T(8,128)S(1)}) custom-call(f32[2,4096,1024]{2,1,0:T(8,128)S(1)} %load.1.same, f32[1,1,2,8,1024]{4,3,2,1,0:T(8,128)S(1)} %copy-done.2, ...), custom_call_target="tpu_custom_call", output_to_operand_aliasing={{4}: (0, {})} | custom-call | tf_op jit(solution)/shard_map/project0/pallas_call | solution.py:127
  15.5 1.3 %collective-permute-start.3 = (f32[8,4096]{1,0:T(8,128)S(1)}, f32[8,4096]{1,0:T(8,128)S(1)}, u32[]{:S(2)}, u32[]{:S(2)}) collective-permute-start(f32[8,4096]{1,0:T(8,128)S(1)} %get-tuple-element.44.o0), channel_id=1, source_target_pairs={{0,8},{8,16},{16,24},{24,0},{1,9},{9,17},{17,25},{25,1},{2,10},{10... | collective-permute-start | bytes 393224 | tf_op jit(solution)/shard_map/ppermute | solution.py:51
  16.8 0.5 collective-permute-start.2
  17.3 1.6 %collective-permute-start.5 = (f32[8,4096]{1,0:T(8,128)S(1)}, f32[8,4096]{1,0:T(8,128)S(1)}, u32[]{:S(2)}, u32[]{:S(2)}) collective-permute-start(f32[8,4096]{1,0:T(8,128)S(1)} %get-tuple-element.46.o2), channel_id=1, source_target_pairs={{0,2},{2,4},{4,6},{6,0},{1,3},{3,5},{5,7},{7,1},{8,10},{10,12},{12... | collective-permute-start | bytes 393224 | tf_op jit(solution)/shard_map/ppermute | solution.py:51
  18.9 2.2 %collective-permute-start.4 = (f32[8,4096]{1,0:T(8,128)S(1)}, f32[8,4096]{1,0:T(8,128)S(1)}, u32[]{:S(2)}, u32[]{:S(2)}) collective-permute-start(f32[8,4096]{1,0:T(8,128)S(1)} %get-tuple-element.47.o3), channel_id=1, source_target_pairs={{0,6},{2,0},{4,2},{6,4},{1,7},{3,1},{5,3},{7,5},{8,14},{10,8},{12,... | collective-permute-start | bytes 393224 | tf_op jit(solution)/shard_map/ppermute | solution.py:51
  21.1 5.6 %project1.1 = (f32[8,4096]{1,0:T(8,128)S(1)}, f32[8,4096]{1,0:T(8,128)S(1)}, f32[8,4096]{1,0:T(8,128)S(1)}, f32[8,4096]{1,0:T(8,128)S(1)}, f32[2,4096,1024]{2,1,0:T(8,128)S(1)}) custom-call(f32[2,4096,1024]{2,1,0:T(8,128)S(1)} %get-tuple-element.42.same, f32[1,1,2,8,1024]{4,3,2,1,0:T(8,128)S(1)} %copy-done.2, ...), custom_call_target="tpu_custom_call", output_to_operand_aliasing={{4}: (0, {})} | custom-call | tf_op jit(solution)/shard_map/project1/pallas_call | solution.py:127
  26.7 0.0 collective-permute-start.7
  26.8 0.0 collective-permute-done.3.n1
  26.8 1.7 %collective-permute-start.6 = (f32[8,4096]{1,0:T(8,128)S(1)}, f32[8,4096]{1,0:T(8,128)S(1)}, u32[]{:S(2)}, u32[]{:S(2)}) collective-permute-start(f32[8,4096]{1,0:T(8,128)S(1)} %get-tuple-element.50.o1), channel_id=1, source_target_pairs={{0,24},{8,0},{16,8},{24,16},{1,25},{9,1},{17,9},{25,17},{2,26},{10... | collective-permute-start | bytes 393224 | tf_op jit(solution)/shard_map/ppermute | solution.py:51
  28.5 0.0 collective-permute-done.2.n0
  28.5 0.0 collective-permute-start.9
  28.5 0.0 collective-permute-done.5.n3
  28.5 3.8 %collective-permute-start.8 = (f32[8,4096]{1,0:T(8,128)S(1)}, f32[8,4096]{1,0:T(8,128)S(1)}, u32[]{:S(2)}, u32[]{:S(2)}) collective-permute-start(f32[8,4096]{1,0:T(8,128)S(1)} %get-tuple-element.52.o3), channel_id=1, source_target_pairs={{0,6},{2,0},{4,2},{6,4},{1,7},{3,1},{5,3},{7,5},{8,14},{10,8},{12,... | collective-permute-start | bytes 393224 | tf_op jit(solution)/shard_map/ppermute | solution.py:51
  32.3 0.0 collective-permute-done.4.n2
  32.3 4.2 %back0.1 = (f32[32,4096]{1,0:T(8,128)S(1)}, f32[32,1152]{1,0:T(8,128)S(1)}, f32[2,4096,1024]{2,1,0:T(8,128)S(1)}) custom-call(f32[2,4096,1024]{2,1,0:T(8,128)S(1)} %get-tuple-element.43.same, f32[8,4096]{1,0:T(8,128)S(1)} %get-tuple-element.44.o0, f32[8,4096]{1,0:T(8,128)S(1)} %get-tuple-element.45.o1, ...), custom_call_target="tpu_custom_call", output_to_operand_aliasing={{2}: (0, {})} | custom-call | tf_op jit(solution)/shard_map/back0/pallas_call | solution.py:173
  36.5 1.5 %collective-permute-start.10 = (f32[32,1152]{1,0:T(8,128)S(1)}, f32[32,1152]{1,0:T(8,128)S(1)}, u32[]{:S(2)}, u32[]{:S(2)}) collective-permute-start(f32[32,1152]{1,0:T(8,128)S(1)} %get-tuple-element.54.mine), channel_id=1, source_target_pairs={{0,1},{1,0},{2,3},{3,2},{4,5},{5,4},{6,7},{7,6},{8,9},{9,8},{10,11... | collective-permute-start | bytes 442376 | tf_op jit(solution)/shard_map/ppermute | solution.py:56
  38.1 0.0 collective-permute-done.7.n1
  38.1 0.0 collective-permute-done.6.n0
  38.1 0.0 collective-permute-done.9.n3
  38.1 0.0 collective-permute-done.8.n2
  38.1 4.2 %back1.1 = (f32[32,4096]{1,0:T(8,128)S(1)}, f32[32,1152]{1,0:T(8,128)S(1)}, f32[2,4096,1024]{2,1,0:T(8,128)S(1)}) custom-call(f32[2,4096,1024]{2,1,0:T(8,128)S(1)} %get-tuple-element.48.same, f32[8,4096]{1,0:T(8,128)S(1)} %get-tuple-element.49.o0, f32[8,4096]{1,0:T(8,128)S(1)} %get-tuple-element.50.o1, ...), custom_call_target="tpu_custom_call", output_to_operand_aliasing={{2}: (0, {})} | custom-call | tf_op jit(solution)/shard_map/back1/pallas_call | solution.py:173
  42.3 0.5 collective-permute-start.11
  42.8 0.1 collective-permute-start.13
  42.9 1.7 %collective-permute-start.12 = (f32[8,1024]{1,0:T(8,128)S(1)}, f32[8,1024]{1,0:T(8,128)S(1)}, u32[]{:S(2)}, u32[]{:S(2)}) collective-permute-start(f32[8,1024]{1,0:T(8,128)S(1)} %get-tuple-element.65.b1), channel_id=1, source_target_pairs={{0,24},{8,0},{16,8},{24,16},{1,25},{9,1},{17,9},{25,17},{2,26},{10... | collective-permute-start | bytes 98312 | tf_op jit(solution)/shard_map/ppermute | solution.py:51
  44.6 0.7 collective-permute-start.15
  45.3 2.2 %collective-permute-done.11.other = f32[32,1152]{1,0:T(8,128)S(1)} collective-permute-done((f32[32,1152]{1,0:T(8,128)S(1)}, f32[32,1152]{1,0:T(8,128)S(1)}, u32[]{:S(2)}, u32[]{:S(2)}) %collective-permute-start.11) | collective-permute-done | bytes 147488 | tf_op jit(solution)/shard_map/ppermute | solution.py:56
  47.4 0.1 collective-permute-start.17
  47.5 1.2 %collective-permute-start.14 = (f32[8,1024]{1,0:T(8,128)S(1)}, f32[8,1024]{1,0:T(8,128)S(1)}, u32[]{:S(2)}, u32[]{:S(2)}) collective-permute-start(f32[8,1024]{1,0:T(8,128)S(1)} %get-tuple-element.67.b3), channel_id=1, source_target_pairs={{0,6},{2,0},{4,2},{6,4},{1,7},{3,1},{5,3},{7,5},{8,14},{10,8},{12,... | collective-permute-start | bytes 98312 | tf_op jit(solution)/shard_map/ppermute | solution.py:51
  48.7 0.0 collective-permute-done.13.n1
  48.7 1.4 %collective-permute-start.16 = (f32[8,1024]{1,0:T(8,128)S(1)}, f32[8,1024]{1,0:T(8,128)S(1)}, u32[]{:S(2)}, u32[]{:S(2)}) collective-permute-start(f32[8,1024]{1,0:T(8,128)S(1)} %get-tuple-element.72.b1), channel_id=1, source_target_pairs={{0,24},{8,0},{16,8},{24,16},{1,25},{9,1},{17,9},{25,17},{2,26},{10... | collective-permute-start | bytes 98312 | tf_op jit(solution)/shard_map/ppermute | solution.py:51
  50.1 0.9 collective-permute-start.19
  51.0 0.0 collective-permute-done.15.n3
  51.0 2.9 %collective-permute-start.18 = (f32[8,1024]{1,0:T(8,128)S(1)}, f32[8,1024]{1,0:T(8,128)S(1)}, u32[]{:S(2)}, u32[]{:S(2)}) collective-permute-start(f32[8,1024]{1,0:T(8,128)S(1)} %get-tuple-element.74.b3), channel_id=1, source_target_pairs={{0,6},{2,0},{4,2},{6,4},{1,7},{3,1},{5,3},{7,5},{8,14},{10,8},{12,... | collective-permute-start | bytes 98312 | tf_op jit(solution)/shard_map/ppermute | solution.py:51
  53.9 0.7 inverse0.1
  54.6 0.7 inverse1.1
  55.2 0.0 copy-start
  55.2 11.7 %copy-done = f32[2,4096,1024]{2,1,0:T(8,128)} copy-done((f32[2,4096,1024]{2,1,0:T(8,128)}, f32[2,4096,1024]{2,1,0:T(8,128)S(1)}, u32[]{:S(2)}) %copy-start) | copy-done | bytes 33554456
  66.9 0.0 collective-permute-done.14.n2
  66.9 10.5 %copy-done.1 = f32[2,4096,1024]{2,1,0:T(8,128)S(1)} copy-done((f32[2,4096,1024]{2,1,0:T(8,128)S(1)}, f32[2,4096,1024]{2,1,0:T(8,128)}, u32[]{:S(2)}) %copy-start.1) | copy-done | bytes 33554456
  77.5 8.3 %mix0.1 = (f32[1,1,2,4096,1024]{4,3,2,1,0:T(8,128)}, f32[8,1024]{1,0:T(8,128)S(1)}, f32[8,1024]{1,0:T(8,128)S(1)}, f32[2,4096,1024]{2,1,0:T(8,128)S(1)}) custom-call(f32[2,4096,1024]{2,1,0:T(8,128)S(1)} %copy-done.1, f32[32,4096]{1,0:T(8,128)S(1)} %get-tuple-element.62.differ, ...), custom_call_target="tpu_custom_call", output_to_operand_aliasing={{3}: (0, {})} | custom-call | tf_op jit(solution)/shard_map/mix0/pallas_call | solution.py:303
  85.7 0.0 collective-permute-done.17.n1
  85.8 0.0 collective-permute-done.19.n3
  85.8 8.3 %mix1.1 = (f32[1,1,2,4096,1024]{4,3,2,1,0:T(8,128)}, f32[8,1024]{1,0:T(8,128)S(1)}, f32[8,1024]{1,0:T(8,128)S(1)}, f32[2,4096,1024]{2,1,0:T(8,128)S(1)}) custom-call(f32[2,4096,1024]{2,1,0:T(8,128)S(1)} %get-tuple-element.68.same, f32[32,4096]{1,0:T(8,128)S(1)} %get-tuple-element.69.differ, ...), custom_call_target="tpu_custom_call", output_to_operand_aliasing={{3}: (0, {}), {0}: (11, {})} | custom-call | tf_op jit(solution)/shard_map/mix1/pallas_call | solution.py:303
  94.1 0.7 maximum_bitcast_fusion
  (12 shorter events, 0.1 us)
Async XLA Ops:
  0.6 9.1 %copy-start.2 = (f32[1,1,2,8,1024]{4,3,2,1,0:T(8,128)S(1)}, f32[1,1,2,8,1024]{4,3,2,1,0:T(8,128)}, u32[]{:S(2)}) copy-start(f32[1,1,2,8,1024]{4,3,2,1,0:T(8,128)} %f0.3) | copy-start | bytes 196612
  0.6 9.1 %copy-start.3 = (f32[1,1,2,8,1024]{4,3,2,1,0:T(8,128)S(1)}, f32[1,1,2,8,1024]{4,3,2,1,0:T(8,128)}, u32[]{:S(2)}) copy-start(f32[1,1,2,8,1024]{4,3,2,1,0:T(8,128)} %f2.3) | copy-start | bytes 196612
  0.7 9.0 %collective-permute-start = (f32[1,1,2,8,1024]{4,3,2,1,0:T(8,128)}, f32[1,1,2,8,1024]{4,3,2,1,0:T(8,128)S(1)}, u32[]{:S(2)}, u32[]{:S(2)}) collective-permute-start(f32[1,1,2,8,1024]{4,3,2,1,0:T(8,128)} %f0.3), channel_id=1, source_target_pairs={{0,8},{8,16},{16,24},{24,0},{1,9},{9,17},{17,25},{25,1},{2,10},{10... | collective-permute-start | bytes 196616 | tf_op jit(solution)/shard_map/ppermute | solution.py:51
  1.2 8.5 %collective-permute-start.1 = (f32[1,1,2,8,1024]{4,3,2,1,0:T(8,128)}, f32[1,1,2,8,1024]{4,3,2,1,0:T(8,128)S(1)}, u32[]{:S(2)}, u32[]{:S(2)}) collective-permute-start(f32[1,1,2,8,1024]{4,3,2,1,0:T(8,128)} %f2.3), channel_id=1, source_target_pairs={{0,2},{2,4},{4,6},{6,0},{1,3},{3,5},{5,7},{7,1},{8,10},{10,12},{12... | collective-permute-start | bytes 196616 | tf_op jit(solution)/shard_map/ppermute | solution.py:51
  15.5 11.2 %collective-permute-start.3 = (f32[8,4096]{1,0:T(8,128)S(1)}, f32[8,4096]{1,0:T(8,128)S(1)}, u32[]{:S(2)}, u32[]{:S(2)}) collective-permute-start(f32[8,4096]{1,0:T(8,128)S(1)} %get-tuple-element.44.o0), channel_id=1, source_target_pairs={{0,8},{8,16},{16,24},{24,0},{1,9},{9,17},{17,25},{25,1},{2,10},{10... | collective-permute-start | bytes 393224 | tf_op jit(solution)/shard_map/ppermute | solution.py:51
  16.8 11.7 %collective-permute-start.2 = (f32[8,4096]{1,0:T(8,128)S(1)}, f32[8,4096]{1,0:T(8,128)S(1)}, u32[]{:S(2)}, u32[]{:S(2)}) collective-permute-start(f32[8,4096]{1,0:T(8,128)S(1)} %get-tuple-element.45.o1), channel_id=1, source_target_pairs={{0,24},{8,0},{16,8},{24,16},{1,25},{9,1},{17,9},{25,17},{2,26},{10... | collective-permute-start | bytes 393224 | tf_op jit(solution)/shard_map/ppermute | solution.py:51
  17.3 11.2 %collective-permute-start.5 = (f32[8,4096]{1,0:T(8,128)S(1)}, f32[8,4096]{1,0:T(8,128)S(1)}, u32[]{:S(2)}, u32[]{:S(2)}) collective-permute-start(f32[8,4096]{1,0:T(8,128)S(1)} %get-tuple-element.46.o2), channel_id=1, source_target_pairs={{0,2},{2,4},{4,6},{6,0},{1,3},{3,5},{5,7},{7,1},{8,10},{10,12},{12... | collective-permute-start | bytes 393224 | tf_op jit(solution)/shard_map/ppermute | solution.py:51
  18.9 13.4 %collective-permute-start.4 = (f32[8,4096]{1,0:T(8,128)S(1)}, f32[8,4096]{1,0:T(8,128)S(1)}, u32[]{:S(2)}, u32[]{:S(2)}) collective-permute-start(f32[8,4096]{1,0:T(8,128)S(1)} %get-tuple-element.47.o3), channel_id=1, source_target_pairs={{0,6},{2,0},{4,2},{6,4},{1,7},{3,1},{5,3},{7,5},{8,14},{10,8},{12,... | collective-permute-start | bytes 393224 | tf_op jit(solution)/shard_map/ppermute | solution.py:51
  26.7 11.3 %collective-permute-start.7 = (f32[8,4096]{1,0:T(8,128)S(1)}, f32[8,4096]{1,0:T(8,128)S(1)}, u32[]{:S(2)}, u32[]{:S(2)}) collective-permute-start(f32[8,4096]{1,0:T(8,128)S(1)} %get-tuple-element.49.o0), channel_id=1, source_target_pairs={{0,8},{8,16},{16,24},{24,0},{1,9},{9,17},{17,25},{25,1},{2,10},{10... | collective-permute-start | bytes 393224 | tf_op jit(solution)/shard_map/ppermute | solution.py:51
  26.8 11.3 %collective-permute-start.6 = (f32[8,4096]{1,0:T(8,128)S(1)}, f32[8,4096]{1,0:T(8,128)S(1)}, u32[]{:S(2)}, u32[]{:S(2)}) collective-permute-start(f32[8,4096]{1,0:T(8,128)S(1)} %get-tuple-element.50.o1), channel_id=1, source_target_pairs={{0,24},{8,0},{16,8},{24,16},{1,25},{9,1},{17,9},{25,17},{2,26},{10... | collective-permute-start | bytes 393224 | tf_op jit(solution)/shard_map/ppermute | solution.py:51
  28.5 9.6 %collective-permute-start.9 = (f32[8,4096]{1,0:T(8,128)S(1)}, f32[8,4096]{1,0:T(8,128)S(1)}, u32[]{:S(2)}, u32[]{:S(2)}) collective-permute-start(f32[8,4096]{1,0:T(8,128)S(1)} %get-tuple-element.51.o2), channel_id=1, source_target_pairs={{0,2},{2,4},{4,6},{6,0},{1,3},{3,5},{5,7},{7,1},{8,10},{10,12},{12... | collective-permute-start | bytes 393224 | tf_op jit(solution)/shard_map/ppermute | solution.py:51
  28.5 9.6 %collective-permute-start.8 = (f32[8,4096]{1,0:T(8,128)S(1)}, f32[8,4096]{1,0:T(8,128)S(1)}, u32[]{:S(2)}, u32[]{:S(2)}) collective-permute-start(f32[8,4096]{1,0:T(8,128)S(1)} %get-tuple-element.52.o3), channel_id=1, source_target_pairs={{0,6},{2,0},{4,2},{6,4},{1,7},{3,1},{5,3},{7,5},{8,14},{10,8},{12,... | collective-permute-start | bytes 393224 | tf_op jit(solution)/shard_map/ppermute | solution.py:51
  36.5 6.3 %collective-permute-start.10 = (f32[32,1152]{1,0:T(8,128)S(1)}, f32[32,1152]{1,0:T(8,128)S(1)}, u32[]{:S(2)}, u32[]{:S(2)}) collective-permute-start(f32[32,1152]{1,0:T(8,128)S(1)} %get-tuple-element.54.mine), channel_id=1, source_target_pairs={{0,1},{1,0},{2,3},{3,2},{4,5},{5,4},{6,7},{7,6},{8,9},{9,8},{10,11... | collective-permute-start | bytes 442376 | tf_op jit(solution)/shard_map/ppermute | solution.py:56
  42.3 5.2 %collective-permute-start.11 = (f32[32,1152]{1,0:T(8,128)S(1)}, f32[32,1152]{1,0:T(8,128)S(1)}, u32[]{:S(2)}, u32[]{:S(2)}) collective-permute-start(f32[32,1152]{1,0:T(8,128)S(1)} %get-tuple-element.56.mine), channel_id=1, source_target_pairs={{0,1},{1,0},{2,3},{3,2},{4,5},{5,4},{6,7},{7,6},{8,9},{9,8},{10,11... | collective-permute-start | bytes 442376 | tf_op jit(solution)/shard_map/ppermute | solution.py:56
  42.8 5.9 %collective-permute-start.13 = (f32[8,1024]{1,0:T(8,128)S(1)}, f32[8,1024]{1,0:T(8,128)S(1)}, u32[]{:S(2)}, u32[]{:S(2)}) collective-permute-start(f32[8,1024]{1,0:T(8,128)S(1)} %get-tuple-element.64.b0), channel_id=1, source_target_pairs={{0,8},{8,16},{16,24},{24,0},{1,9},{9,17},{17,25},{25,1},{2,10},{10... | collective-permute-start | bytes 98312 | tf_op jit(solution)/shard_map/ppermute | solution.py:51
  42.9 7.2 %collective-permute-start.12 = (f32[8,1024]{1,0:T(8,128)S(1)}, f32[8,1024]{1,0:T(8,128)S(1)}, u32[]{:S(2)}, u32[]{:S(2)}) collective-permute-start(f32[8,1024]{1,0:T(8,128)S(1)} %get-tuple-element.65.b1), channel_id=1, source_target_pairs={{0,24},{8,0},{16,8},{24,16},{1,25},{9,1},{17,9},{25,17},{2,26},{10... | collective-permute-start | bytes 98312 | tf_op jit(solution)/shard_map/ppermute | solution.py:51
  44.6 6.4 %collective-permute-start.15 = (f32[8,1024]{1,0:T(8,128)S(1)}, f32[8,1024]{1,0:T(8,128)S(1)}, u32[]{:S(2)}, u32[]{:S(2)}) collective-permute-start(f32[8,1024]{1,0:T(8,128)S(1)} %get-tuple-element.66.b2), channel_id=1, source_target_pairs={{0,2},{2,4},{4,6},{6,0},{1,3},{3,5},{5,7},{7,1},{8,10},{10,12},{12... | collective-permute-start | bytes 98312 | tf_op jit(solution)/shard_map/ppermute | solution.py:51
  47.4 38.3 %collective-permute-start.17 = (f32[8,1024]{1,0:T(8,128)S(1)}, f32[8,1024]{1,0:T(8,128)S(1)}, u32[]{:S(2)}, u32[]{:S(2)}) collective-permute-start(f32[8,1024]{1,0:T(8,128)S(1)} %get-tuple-element.71.b0), channel_id=1, source_target_pairs={{0,8},{8,16},{16,24},{24,0},{1,9},{9,17},{17,25},{25,1},{2,10},{10... | collective-permute-start | bytes 98312 | tf_op jit(solution)/shard_map/ppermute | solution.py:51
  47.5 19.4 %collective-permute-start.14 = (f32[8,1024]{1,0:T(8,128)S(1)}, f32[8,1024]{1,0:T(8,128)S(1)}, u32[]{:S(2)}, u32[]{:S(2)}) collective-permute-start(f32[8,1024]{1,0:T(8,128)S(1)} %get-tuple-element.67.b3), channel_id=1, source_target_pairs={{0,6},{2,0},{4,2},{6,4},{1,7},{3,1},{5,3},{7,5},{8,14},{10,8},{12,... | collective-permute-start | bytes 98312 | tf_op jit(solution)/shard_map/ppermute | solution.py:51
  48.7 37.1 %collective-permute-start.16 = (f32[8,1024]{1,0:T(8,128)S(1)}, f32[8,1024]{1,0:T(8,128)S(1)}, u32[]{:S(2)}, u32[]{:S(2)}) collective-permute-start(f32[8,1024]{1,0:T(8,128)S(1)} %get-tuple-element.72.b1), channel_id=1, source_target_pairs={{0,24},{8,0},{16,8},{24,16},{1,25},{9,1},{17,9},{25,17},{2,26},{10... | collective-permute-start | bytes 98312 | tf_op jit(solution)/shard_map/ppermute | solution.py:51
  50.1 35.7 %collective-permute-start.19 = (f32[8,1024]{1,0:T(8,128)S(1)}, f32[8,1024]{1,0:T(8,128)S(1)}, u32[]{:S(2)}, u32[]{:S(2)}) collective-permute-start(f32[8,1024]{1,0:T(8,128)S(1)} %get-tuple-element.73.b2), channel_id=1, source_target_pairs={{0,2},{2,4},{4,6},{6,0},{1,3},{3,5},{5,7},{7,1},{8,10},{10,12},{12... | collective-permute-start | bytes 98312 | tf_op jit(solution)/shard_map/ppermute | solution.py:51
  51.0 34.8 %collective-permute-start.18 = (f32[8,1024]{1,0:T(8,128)S(1)}, f32[8,1024]{1,0:T(8,128)S(1)}, u32[]{:S(2)}, u32[]{:S(2)}) collective-permute-start(f32[8,1024]{1,0:T(8,128)S(1)} %get-tuple-element.74.b3), channel_id=1, source_target_pairs={{0,6},{2,0},{4,2},{6,4},{1,7},{3,1},{5,3},{7,5},{8,14},{10,8},{12,... | collective-permute-start | bytes 98312 | tf_op jit(solution)/shard_map/ppermute | solution.py:51
  55.2 11.7 %copy-start = (f32[2,4096,1024]{2,1,0:T(8,128)}, f32[2,4096,1024]{2,1,0:T(8,128)S(1)}, u32[]{:S(2)}) copy-start(f32[2,4096,1024]{2,1,0:T(8,128)S(1)} %get-tuple-element.61.same) | copy-start | bytes 100663296
  66.9 10.5 %copy-start.1 = (f32[2,4096,1024]{2,1,0:T(8,128)S(1)}, f32[2,4096,1024]{2,1,0:T(8,128)}, u32[]{:S(2)}) copy-start(f32[2,4096,1024]{2,1,0:T(8,128)} %copy-done) | copy-start | bytes 100663296

commit v2 on v1

v2 whole, which is shorter than its diff:
```python
import functools

import jax
import jax.numpy as jnp
from jax import lax
from jax.experimental import pallas as pl
from jax.experimental.pallas import tpu as pltpu
from jax.sharding import PartitionSpec as P

f32 = jnp.float32
bf16 = jnp.bfloat16
mixing = 0.2
edges = 4
mib = 1 << 20

NN = (((1,), (0,)), ((), ()))
NT = (((1,), (1,)), ((), ()))
TN = (((0,), (0,)), ((), ()))

in_vmem = pl.BlockSpec(memory_space=pltpu.VMEM)
in_hbm = pl.BlockSpec(memory_space=pltpu.HBM)


def vmem(value):
    return pltpu.with_memory_space_constraint(value, pltpu.VMEM)


def hbm(value):
    return pltpu.with_memory_space_constraint(value, pltpu.HBM)


def dot(a, b, dims):
    return lax.dot_general(a, b, dims, preferred_element_type=f32)


def split(value):
    high = value.astype(bf16)
    return high, (value - high.astype(f32)).astype(bf16)


def chunk_of(rows, most):
    size = min(rows, most)
    while rows % size:
        size //= 2
    return size


def shifted(value, axis, steps):
    count = lax.axis_size(axis)
    pairs = [(source, (source + steps) % count) for source in range(count)]
    return lax.ppermute(value, axis, pairs)


def from_partner(value, axis, distance):
    count = lax.axis_size(axis)
    return lax.ppermute(value, axis, [(i, i ^ distance) for i in range(count)])


def exchange(values):
    swapped = []
    for slot, value in enumerate(values):
        axis = ("rx", "ry")[slot // 2]
        count = lax.axis_size(axis)
        pairs = [(i, (i + (1 if i % 2 == slot % 2 else -1)) % count) for i in range(count)]
        swapped.append(lax.ppermute(value, axis, pairs))
    return swapped


def odd(axis):
    return lax.rem(lax.axis_index(axis), 2) == 1


def piece_copy(weights, held, sems, size, piece, first):
    rows = held.shape[1]
    mat, row = divmod(piece * size, rows)
    here = pl.ds(row, size)
    return pltpu.make_async_copy(
        weights.at[0, 0, mat, here], held.at[mat, here], sems.at[piece - first]
    )


def load_kernel(size, until, weights, held, sems):
    copies = [piece_copy(weights, held, sems, size, piece, 0) for piece in range(until)]
    for copy in copies:
        copy.start()
    for copy in copies:
        copy.wait()


def load(weights, size, until):
    return pl.pallas_call(
        functools.partial(load_kernel, size, until),
        name="load",
        out_shape=jax.ShapeDtypeStruct(weights.shape[2:], f32),
        in_specs=[in_hbm],
        out_specs=in_vmem,
        scratch_shapes=[pltpu.SemaphoreType.DMA((until,))],
        compiler_params=pltpu.CompilerParams(vmem_limit_bytes=4 * mib),
    )(hbm(weights))


def project_kernel(
    mat, chunk, size, first, until, same, f0, f1, f2, f3, weights, o0, o1, o2, o3, held, sems
):
    rows = held.shape[1]
    copies = {
        piece: piece_copy(weights, held, sems, size, piece, first)
        for piece in range(first, until)
    }
    for copy in copies.values():
        copy.start()
    rank = f0.shape[-2]
    slots = []
    for axis, own, lower in (("rx", f0, f1), ("ry", f2, f3)):
        own, lower, swap = own[0, 0, mat], lower[0, 0, mat], odd(axis)
        slots += [jnp.where(swap, lower, own), jnp.where(swap, own, lower)]
    high, low = split(jnp.concatenate(slots, 0))
    stack = jnp.concatenate(
        [jnp.concatenate([high, high], 1), jnp.concatenate([low, low], 1)], 0
    )
    width = edges * rank
    for row in range(0, rows, chunk):
        here = pl.ds(row, chunk)
        start = mat * rows + row
        for piece in range(start // size, (start + chunk) // size):
            if piece in copies:
                copies.pop(piece).wait()
        w_high, w_low = split(held[mat, here, :])
        both = dot(stack, jnp.concatenate([w_high, w_low], 1), NT)
        total = both[:width] + both[width:]
        for slot, out in enumerate((o0, o1, o2, o3)):
            out[:, here] = total[slot * rank : (slot + 1) * rank]
    for copy in copies.values():
        copy.wait()


def project(held, factors, weights, mat, size, first, until):
    rows = held.shape[1]
    rank = factors[0].shape[-2]
    return pl.pallas_call(
        functools.partial(project_kernel, mat, chunk_of(rows, 1024), size, first, until),
        name=f"project{mat}",
        out_shape=[jax.ShapeDtypeStruct((rank, rows), f32)] * edges
        + [jax.ShapeDtypeStruct(held.shape, f32)],
        in_specs=[in_vmem] * 5 + [in_hbm],
        out_specs=[in_vmem] * (edges + 1),
        scratch_shapes=[pltpu.SemaphoreType.DMA((until - first,))],
        input_output_aliases={0: edges},
        compiler_params=pltpu.CompilerParams(vmem_limit_bytes=4 * mib),
    )(vmem(held), *factors, hbm(weights))


def back_kernel(mat, chunk, same, o0, o1, o2, o3, n0, n1, n2, n3, differ, sums, held):
    rank = o0.shape[0]
    width = edges * rank
    features = held.shape[2]
    sums[...] = jnp.zeros_like(sums)

    def body(step, gram):
        here = pl.ds(pl.multiple_of(step * chunk, chunk), chunk)
        p = jnp.concatenate(
            [o[:, here] - n[:, here] for o, n in zip((o0, o1, o2, o3), (n0, n1, n2, n3))], 0
        )
        differ[:, here] = p
        high, low = split(p)
        w_high, w_low = split(held[mat, here, :])
        pair = jnp.concatenate([high, low], 0)
        stack = jnp.concatenate([pair, pair], 1)
        both = dot(stack, jnp.concatenate([w_high, w_low], 0), NN)
        sums[:, :features] += both[:width] + both[width:]
        return gram + dot(pair, pair, NT)

    gram = lax.fori_loop(
        0, held.shape[1] // chunk, body, jnp.zeros((2 * width, 2 * width), f32)
    )
    total = (gram[:width, :width] + gram[width:, width:]) + (
        gram[:width, width:] + gram[width:, :width]
    )
    for edge in range(edges):
        here = slice(edge * rank, (edge + 1) * rank)
        sums[here, features : features + rank] = total[here, here]


def back(held, own, near, mat):
    _, rows, features = held.shape
    rank = own[0].shape[0]
    return pl.pallas_call(
        functools.partial(back_kernel, mat, chunk_of(rows, 1024)),
        name=f"back{mat}",
        out_shape=[
            jax.ShapeDtypeStruct((edges * rank, rows), f32),
            jax.ShapeDtypeStruct((edges * rank, features + 128), f32),
            jax.ShapeDtypeStruct(held.shape, f32),
        ],
        in_specs=[in_vmem] * 9,
        out_specs=[in_vmem] * 3,
        input_output_aliases={0: 2},
        compiler_params=pltpu.CompilerParams(vmem_limit_bytes=4 * mib),
    )(vmem(held), *own, *near)


def add_kernel(same, mine, other, b0, b1, b2, b3, gram, held):
    rank, features = b0.shape
    for edge, out in enumerate((b0, b1, b2, b3)):
        here = slice(edge * rank, (edge + 1) * rank)
        out[...] = mine[here, :features] + other[here, :features]
    gram[...] = mine[:, features:] + other[:, features:]


def add(held, mine, other, rank, mat):
    width, wide = mine.shape
    features = wide - 128
    return pl.pallas_call(
        add_kernel,
        name=f"add{mat}",
        out_shape=[jax.ShapeDtypeStruct((rank, features), f32)] * edges
        + [jax.ShapeDtypeStruct((width, 128), f32), jax.ShapeDtypeStruct(held.shape, f32)],
        in_specs=[in_vmem] * 3,
        out_specs=[in_vmem] * 6,
        input_output_aliases={0: 5},
        compiler_params=pltpu.CompilerParams(vmem_limit_bytes=4 * mib),
    )(vmem(held), mine, other)


def inverse_kernel(rank, same, *refs):
    count = len(refs) // 2
    grams, inverses = refs[:count], refs[count : 2 * count]
    width = grams[0].shape[0]
    shape = (len(grams) * edges, rank, 128)
    row = lax.broadcasted_iota(jnp.int32, shape, 1)
    lane = lax.broadcasted_iota(jnp.int32, shape, 2)
    slot = lax.rem(lax.broadcasted_iota(jnp.int32, shape, 0), edges)
    value = jnp.concatenate([gram[...] for gram in grams], 0).reshape(shape)
    value = jnp.where(lane < rank, value, (lane == width + slot * rank + row).astype(f32))
    pivots = jnp.ones((shape[0], rank, 1), f32)
    for j in range(rank):
        pivot = value[:, j : j + 1, j : j + 1]
        pivots = jnp.where(row[:, :, :1] == j, pivot, pivots)
        factor = jnp.where(row > j, value[:, :, j : j + 1] / pivot, 0.0)
        value = value - factor * value[:, j : j + 1, :]
    value = (value / jnp.sqrt(pivots)).reshape(len(grams) * width, 128)
    for mat, inverse in enumerate(inverses):
        inverse[...] = value[mat * width : (mat + 1) * width]


def inverse_factors(held, grams, rank):
    return pl.pallas_call(
        functools.partial(inverse_kernel, rank),
        name="inverse",
        out_shape=[jax.ShapeDtypeStruct(gram.shape, f32) for gram in grams]
        + [jax.ShapeDtypeStruct(held.shape, f32)],
        in_specs=[in_vmem] * (len(grams) + 1),
        out_specs=[in_vmem] * (len(grams) + 1),
        input_output_aliases={0: len(grams)},
        compiler_params=pltpu.CompilerParams(vmem_limit_bytes=4 * mib),
    )(vmem(held), *grams)


def mix_kernel(mat, chunk, same, differ, inverse, b0, b1, b2, b3, n0, n1, n2, n3, *rest):
    mixed, next_rx, next_ry, held, new_rx, new_ry, sems, new_sems = rest[-8:]
    rank = b0.shape[0]
    width = edges * rank
    factor = inverse[:, width : 2 * width]
    sums = jnp.concatenate(
        [b[...] + n[...] for b, n in zip((b0, b1, b2, b3), (n0, n1, n2, n3))], 0
    )
    updated = lax.dot_general(
        factor, sums, NN, precision=lax.Precision.HIGHEST, preferred_element_type=f32
    )
    parts = [updated[slot * rank : (slot + 1) * rank] for slot in range(edges)]
    new_rx[...] = jnp.where(odd("rx"), parts[1], parts[0])
    new_ry[...] = jnp.where(odd("ry"), parts[3], parts[2])
    new_copies = [
        pltpu.make_async_copy(new_rx, next_rx.at[0, 0, mat], new_sems.at[0]),
        pltpu.make_async_copy(new_ry, next_ry.at[0, 0, mat], new_sems.at[1]),
    ]
    for copy in new_copies:
        copy.start()
    right = mixing * lax.dot_general(
        factor, updated, TN, precision=lax.Precision.HIGHEST, preferred_element_type=f32
    )
    r_high, r_low = split(right)
    terms = jnp.concatenate([r_high, r_high, r_low, r_low], 0)
    steps = held.shape[1] // chunk

    def copy(step):
        here = pl.ds(pl.multiple_of(step * chunk, chunk), chunk)
        return pltpu.make_async_copy(
            held.at[mat, here], mixed.at[0, 0, mat, here], sems.at[step]
        )

    @pl.loop(0, steps)
    def _(step):
        here = pl.ds(pl.multiple_of(step * chunk, chunk), chunk)
        high, low = split(differ[:, here])
        lhs = jnp.concatenate([high, low, high, low], 0)
        held[mat, here, :] -= dot(lhs, terms, TN)
        copy(step).start()

    @pl.loop(0, steps)
    def _(step):
        copy(step).wait()

    for copy in new_copies:
        copy.wait()


def mix(held, differ, inverse, sums, near, mat, shapes, previous=None):
    _, rows, features = held.shape
    rank = sums[0].shape[0]
    chunk = chunk_of(rows, 256)
    args = [vmem(held), differ, inverse, *sums, *near]
    specs = [in_vmem] * 11
    aliases = {0: 3}
    if previous is not None:
        args += [hbm(array) for array in previous]
        specs += [in_hbm] * 3
        aliases |= {11: 0, 12: 1, 13: 2}
    return pl.pallas_call(
        functools.partial(mix_kernel, mat, chunk),
        name=f"mix{mat}",
        out_shape=[jax.ShapeDtypeStruct(shape, f32) for shape in (*shapes, held.shape)],
        in_specs=specs,
        out_specs=[in_hbm] * 3 + [in_vmem],
        scratch_shapes=[
            pltpu.VMEM((rank, features), f32),
            pltpu.VMEM((rank, features), f32),
            pltpu.SemaphoreType.DMA((rows // chunk,)),
            pltpu.SemaphoreType.DMA((2,)),
        ],
        input_output_aliases=aliases,
        compiler_params=pltpu.CompilerParams(vmem_limit_bytes=4 * mib),
    )(*args)


def per_device(weights, factors_rx, factors_ry):
    mats, rows = weights.shape[2:4]
    rank = factors_rx.shape[-2]
    factors = [
        factors_rx,
        shifted(factors_rx, "rx", 1),
        factors_ry,
        shifted(factors_ry, "ry", 1),
    ]
    size = chunk_of(rows, 512)
    pieces = rows // size
    ahead = max(pieces // 4, 1)
    held = load(weights, size, ahead)
    own = []
    for mat in range(mats):
        first = mat * pieces + ahead
        until = min((mat + 1) * pieces + ahead, mats * pieces)
        *own_mat, held = project(held, factors, weights, mat, size, first, until)
        own.append(own_mat)
    near = [exchange(own_mat) for own_mat in own]
    differ, sums, grams, near_sums, pairs = [], [], [], [], []
    tp = lax.axis_size("tp")
    for mat in range(mats):
        p, terms, held = back(held, own[mat], near[mat], mat)
        distance = 1
        while 2 * distance < tp:
            terms = terms + from_partner(terms, "tp", distance)
            distance *= 2
        other = from_partner(terms, "tp", distance) if tp > 1 else jnp.zeros_like(terms)
        differ.append(p)
        pairs.append((terms, other))
    for mat in range(mats):
        *sum_mat, gram, held = add(held, *pairs[mat], rank, mat)
        sums.append(sum_mat)
        near_sums.append(exchange(sum_mat))
        grams.append(gram)
    *inverse, held = inverse_factors(held, grams, rank)
    results = None
    shapes = (weights.shape, factors_rx.shape, factors_ry.shape)
    for mat in range(mats):
        *results, held = mix(
            held, differ[mat], inverse[mat], sums[mat], near_sums[mat], mat, shapes, results
        )
    return tuple(results)


def solution(mesh):
    return jax.shard_map(
        per_device,
        mesh=mesh,
        in_specs=(
            P("rx", "ry", None, "tp", None),
            P("rx", "ry", None, None, None),
            P("rx", "ry", None, None, None),
        ),
        out_specs=(
            P("rx", "ry", None, "tp", None),
            P("rx", "ry", None, None, None),
            P("rx", "ry", None, None, None),
        ),
        check_vma=False,
    )
```

time: 94.9 us -> 64.9 us (0.68)
  local copies, waits for them, and re-layouts: 22.2 us -> 0.01 us
  Pallas kernels: 43.5 us -> 38.1 us
  starting transfers between devices: 25.3 us -> 22 us
  waiting for transfers between devices: 2.21 us -> 3.71 us
    unnamed x8 -> x4, local copies, waits for them, and re-layouts: 22.2 us -> 0.01 us
    ppermute x18 -> x2, starting transfers between devices: 23.2 us -> 3.14 us  [shifted(): return lax.ppermute(value, axis, pairs)]
    ppermute x0 -> x16, starting transfers between devices: none -> 15.7 us  [exchange(): swapped.append(lax.ppermute(value, axis, pairs))]
    pallas_call x5 -> x4, Pallas kernels: 23.8 us -> 16.5 us  [the longest x2 13.6 us: mix(): pl.pallas_call(functools.partial(mix_kernel, mat, chunk), name=f'mix{mat}...]
    ppermute x18 -> x2, waiting for transfers between devices: 0.05 us -> 2.23 us  [shifted(): return lax.ppermute(value, axis, pairs)]
    pallas_call x2, Pallas kernels: 11.4 us -> 13 us  [project(): pl.pallas_call(functools.partial(project_kernel, mat, chunk_of(rows, 1024...]
    ppermute x2, waiting for transfers between devices: 2.16 us -> 0.87 us  [from_partner(): return lax.ppermute(value, axis, [(i, i ^ distance) for i in range(count)])]
    ppermute x2, starting transfers between devices: 2.04 us -> 3.16 us  [from_partner(): return lax.ppermute(value, axis, [(i, i ^ distance) for i in range(count)])]
  transfers between devices with their start and end apart: 20 -> 20, of which waited for: 1 -> 3; matrix products, arithmetic and copies ran while one was open for 0% -> 0% of each run, Pallas kernels for 31% -> 38%
where the time goes in v2:
time: 64.9 us; the launch traced here: 64.8 us
  Pallas kernels  38.1 us (59%)
  starting transfers between devices  22 us (34%)
  waiting for transfers between devices  3.71 us (6%)
  between operations  0.96 us (1%)
    ppermute x16, starting transfers between devices, exchange(): swapped.append(lax.ppermute(value, axis, pairs))  15.7 us
    pallas_call x2, Pallas kernels, mix(): pl.pallas_call(functools.partial(mix_kernel, mat, chunk), name=f'mix{mat}...  13.6 us
    pallas_call x2, Pallas kernels, project(): pl.pallas_call(functools.partial(project_kernel, mat, chunk_of(rows, 1024...  13 us
    pallas_call x2, Pallas kernels, back(): pl.pallas_call(functools.partial(back_kernel, mat, chunk_of(rows, 1024)),...  8.54 us
    ppermute x2, starting transfers between devices, from_partner(): return lax.ppermute(value, axis, [(i, i ^ distance) for i in range(count)])  3.16 us
    ppermute x2, starting transfers between devices, shifted(): return lax.ppermute(value, axis, pairs)  3.14 us
    pallas_call x1, Pallas kernels, load(): pl.pallas_call(functools.partial(load_kernel, size, until), name='load',...  2.24 us
    ppermute x2, waiting for transfers between devices, shifted(): return lax.ppermute(value, axis, pairs)  2.23 us
  transfers between devices with their start and end apart: 20, of which 3 were waited for; matrix products, arithmetic and copies ran while one was open for 0% of the time, Pallas kernels for 38%

profile of v2, /device:TPU:0, one launch (start us, length us, event | category | flops | bytes accessed | tf_op | source)
XLA Modules:
  0.0 64.8 jit_solution(7280472472432832467)
XLA Ops:
  0.7 0.5 collective-permute-start
  1.2 2.6 %collective-permute-start.1 = (f32[1,1,2,8,1024]{4,3,2,1,0:T(8,128)}, f32[1,1,2,8,1024]{4,3,2,1,0:T(8,128)S(1)}, u32[]{:S(2)}, u32[]{:S(2)}) collective-permute-start(f32[1,1,2,8,1024]{4,3,2,1,0:T(8,128)} %f2.3), channel_id=1, source_target_pairs={{0,2},{2,4},{4,6},{6,0},{1,3},{3,5},{5,7},{7,1},{8,10},{10,12},{12... | collective-permute-start | bytes 196616 | tf_op jit(solution)/shard_map/ppermute | solution.py:51
  3.8 2.2 %load.1.same = f32[2,4096,1024]{2,1,0:T(8,128)S(1)} custom-call(f32[1,1,2,4096,1024]{4,3,2,1,0:T(8,128)} %weights.5), custom_call_target="tpu_custom_call" | custom-call | tf_op jit(solution)/shard_map/load/pallas_call | solution.py:91
  6.0 0.0 collective-permute-done.f1
  6.0 2.2 %collective-permute-done.1.f3 = f32[1,1,2,8,1024]{4,3,2,1,0:T(8,128)S(1)} collective-permute-done((f32[1,1,2,8,1024]{4,3,2,1,0:T(8,128)}, f32[1,1,2,8,1024]{4,3,2,1,0:T(8,128)S(1)}, u32[]{:S(2)}, u32[]{:S(2)}) %collective-permute-start.1) | collective-permute-done | bytes 65568 | tf_op jit(solution)/shard_map/ppermute | solution.py:51
  8.3 6.5 %project0.1 = (f32[8,4096]{1,0:T(8,128)S(1)}, f32[8,4096]{1,0:T(8,128)S(1)}, f32[8,4096]{1,0:T(8,128)S(1)}, f32[8,4096]{1,0:T(8,128)S(1)}, f32[2,4096,1024]{2,1,0:T(8,128)S(1)}) custom-call(f32[2,4096,1024]{2,1,0:T(8,128)S(1)} %load.1.same, f32[1,1,2,8,1024]{4,3,2,1,0:T(8,128)S(1)} %copy-done, ...), custom_call_target="tpu_custom_call", output_to_operand_aliasing={{4}: (0, {})} | custom-call | tf_op jit(solution)/shard_map/project0/pallas_call | solution.py:140
  14.8 0.7 %collective-permute-start.2 = (f32[8,4096]{1,0:T(8,128)S(1)}, f32[8,4096]{1,0:T(8,128)S(1)}, u32[]{:S(2)}, u32[]{:S(2)}) collective-permute-start(f32[8,4096]{1,0:T(8,128)S(1)} %get-tuple-element.43.o0), channel_id=1, source_target_pairs={{0,8},{8,0},{16,24},{24,16},{1,9},{9,1},{17,25},{25,17},{2,10},{10... | collective-permute-start | bytes 393224 | tf_op jit(solution)/shard_map/ppermute | solution.py:65
  15.5 1.5 %collective-permute-start.3 = (f32[8,4096]{1,0:T(8,128)S(1)}, f32[8,4096]{1,0:T(8,128)S(1)}, u32[]{:S(2)}, u32[]{:S(2)}) collective-permute-start(f32[8,4096]{1,0:T(8,128)S(1)} %get-tuple-element.44.o1), channel_id=1, source_target_pairs={{0,24},{8,16},{16,8},{24,0},{1,25},{9,17},{17,9},{25,1},{2,26},{10... | collective-permute-start | bytes 393224 | tf_op jit(solution)/shard_map/ppermute | solution.py:65
  17.1 0.0 collective-permute-start.4
  17.1 2.2 %collective-permute-start.5 = (f32[8,4096]{1,0:T(8,128)S(1)}, f32[8,4096]{1,0:T(8,128)S(1)}, u32[]{:S(2)}, u32[]{:S(2)}) collective-permute-start(f32[8,4096]{1,0:T(8,128)S(1)} %get-tuple-element.46.o3), channel_id=1, source_target_pairs={{0,6},{2,4},{4,2},{6,0},{1,7},{3,5},{5,3},{7,1},{8,14},{10,12},{12... | collective-permute-start | bytes 393224 | tf_op jit(solution)/shard_map/ppermute | solution.py:65
  19.3 6.5 %project1.1 = (f32[8,4096]{1,0:T(8,128)S(1)}, f32[8,4096]{1,0:T(8,128)S(1)}, f32[8,4096]{1,0:T(8,128)S(1)}, f32[8,4096]{1,0:T(8,128)S(1)}, f32[2,4096,1024]{2,1,0:T(8,128)S(1)}) custom-call(f32[2,4096,1024]{2,1,0:T(8,128)S(1)} %get-tuple-element.41.same, f32[1,1,2,8,1024]{4,3,2,1,0:T(8,128)S(1)} %copy-done, ...), custom_call_target="tpu_custom_call", output_to_operand_aliasing={{4}: (0, {})} | custom-call | tf_op jit(solution)/shard_map/project1/pallas_call | solution.py:140
  25.7 0.1 collective-permute-start.6
  25.8 0.0 collective-permute-done.2.n0
  25.8 0.5 collective-permute-start.7
  26.3 0.0 collective-permute-done.3.n1
  26.4 0.6 %collective-permute-start.8 = (f32[8,4096]{1,0:T(8,128)S(1)}, f32[8,4096]{1,0:T(8,128)S(1)}, u32[]{:S(2)}, u32[]{:S(2)}) collective-permute-start(f32[8,4096]{1,0:T(8,128)S(1)} %get-tuple-element.50.o2), channel_id=1, source_target_pairs={{0,2},{2,0},{4,6},{6,4},{1,3},{3,1},{5,7},{7,5},{8,10},{10,8},{12,... | collective-permute-start | bytes 393224 | tf_op jit(solution)/shard_map/ppermute | solution.py:65
  27.0 0.0 collective-permute-done.4.n2
  27.0 1.9 %collective-permute-start.9 = (f32[8,4096]{1,0:T(8,128)S(1)}, f32[8,4096]{1,0:T(8,128)S(1)}, u32[]{:S(2)}, u32[]{:S(2)}) collective-permute-start(f32[8,4096]{1,0:T(8,128)S(1)} %get-tuple-element.51.o3), channel_id=1, source_target_pairs={{0,6},{2,4},{4,2},{6,0},{1,7},{3,5},{5,3},{7,1},{8,14},{10,12},{12... | collective-permute-start | bytes 393224 | tf_op jit(solution)/shard_map/ppermute | solution.py:65
  28.9 0.0 collective-permute-done.5.n3
  28.9 4.4 %back0.1 = (f32[32,4096]{1,0:T(8,128)S(1)}, f32[32,1152]{1,0:T(8,128)S(1)}, f32[2,4096,1024]{2,1,0:T(8,128)S(1)}) custom-call(f32[2,4096,1024]{2,1,0:T(8,128)S(1)} %get-tuple-element.42.same, f32[8,4096]{1,0:T(8,128)S(1)} %get-tuple-element.43.o0, f32[8,4096]{1,0:T(8,128)S(1)} %get-tuple-element.44.o1, ...), custom_call_target="tpu_custom_call", output_to_operand_aliasing={{2}: (0, {})} | custom-call | tf_op jit(solution)/shard_map/back0/pallas_call | solution.py:187
  33.2 1.6 %collective-permute-start.10 = (f32[32,1152]{1,0:T(8,128)S(1)}, f32[32,1152]{1,0:T(8,128)S(1)}, u32[]{:S(2)}, u32[]{:S(2)}) collective-permute-start(f32[32,1152]{1,0:T(8,128)S(1)} %get-tuple-element.53.mine), channel_id=1, source_target_pairs={{0,1},{1,0},{2,3},{3,2},{4,5},{5,4},{6,7},{7,6},{8,9},{9,8},{10,11... | collective-permute-start | bytes 442376 | tf_op jit(solution)/shard_map/ppermute | solution.py:56
  34.8 0.0 collective-permute-done.6.n0
  34.8 0.0 collective-permute-done.7.n1
  34.9 0.0 collective-permute-done.8.n2
  34.9 0.6 collective-permute-done.9.n3
  35.4 4.2 %back1.1 = (f32[32,4096]{1,0:T(8,128)S(1)}, f32[32,1152]{1,0:T(8,128)S(1)}, f32[2,4096,1024]{2,1,0:T(8,128)S(1)}) custom-call(f32[2,4096,1024]{2,1,0:T(8,128)S(1)} %get-tuple-element.47.same, f32[8,4096]{1,0:T(8,128)S(1)} %get-tuple-element.48.o0, f32[8,4096]{1,0:T(8,128)S(1)} %get-tuple-element.49.o1, ...), custom_call_target="tpu_custom_call", output_to_operand_aliasing={{2}: (0, {})} | custom-call | tf_op jit(solution)/shard_map/back1/pallas_call | solution.py:187
  39.6 1.5 %collective-permute-start.11 = (f32[32,1152]{1,0:T(8,128)S(1)}, f32[32,1152]{1,0:T(8,128)S(1)}, u32[]{:S(2)}, u32[]{:S(2)}) collective-permute-start(f32[32,1152]{1,0:T(8,128)S(1)} %get-tuple-element.55.mine), channel_id=1, source_target_pairs={{0,1},{1,0},{2,3},{3,2},{4,5},{5,4},{6,7},{7,6},{8,9},{9,8},{10,11... | collective-permute-start | bytes 442376 | tf_op jit(solution)/shard_map/ppermute | solution.py:56
  41.1 0.0 collective-permute-done.10.other
  41.2 0.1 collective-permute-start.12
  41.2 1.8 %collective-permute-start.13 = (f32[8,1024]{1,0:T(8,128)S(1)}, f32[8,1024]{1,0:T(8,128)S(1)}, u32[]{:S(2)}, u32[]{:S(2)}) collective-permute-start(f32[8,1024]{1,0:T(8,128)S(1)} %get-tuple-element.63.b1), channel_id=1, source_target_pairs={{0,24},{8,16},{16,8},{24,0},{1,25},{9,17},{17,9},{25,1},{2,26},{10... | collective-permute-start | bytes 98312 | tf_op jit(solution)/shard_map/ppermute | solution.py:65
  43.0 0.9 %collective-permute-start.14 = (f32[8,1024]{1,0:T(8,128)S(1)}, f32[8,1024]{1,0:T(8,128)S(1)}, u32[]{:S(2)}, u32[]{:S(2)}) collective-permute-start(f32[8,1024]{1,0:T(8,128)S(1)} %get-tuple-element.64.b2), channel_id=1, source_target_pairs={{0,2},{2,0},{4,6},{6,4},{1,3},{3,1},{5,7},{7,5},{8,10},{10,8},{12,... | collective-permute-start | bytes 98312 | tf_op jit(solution)/shard_map/ppermute | solution.py:65
  43.9 0.9 %collective-permute-done.11.other = f32[32,1152]{1,0:T(8,128)S(1)} collective-permute-done((f32[32,1152]{1,0:T(8,128)S(1)}, f32[32,1152]{1,0:T(8,128)S(1)}, u32[]{:S(2)}, u32[]{:S(2)}) %collective-permute-start.11) | collective-permute-done | bytes 147488 | tf_op jit(solution)/shard_map/ppermute | solution.py:56
  44.8 0.1 collective-permute-start.16
  44.9 1.8 %collective-permute-start.15 = (f32[8,1024]{1,0:T(8,128)S(1)}, f32[8,1024]{1,0:T(8,128)S(1)}, u32[]{:S(2)}, u32[]{:S(2)}) collective-permute-start(f32[8,1024]{1,0:T(8,128)S(1)} %get-tuple-element.65.b3), channel_id=1, source_target_pairs={{0,6},{2,4},{4,2},{6,0},{1,7},{3,5},{5,3},{7,1},{8,14},{10,12},{12... | collective-permute-start | bytes 98312 | tf_op jit(solution)/shard_map/ppermute | solution.py:65
  46.7 0.0 collective-permute-done.12.n0
  46.7 1.4 %collective-permute-start.17 = (f32[8,1024]{1,0:T(8,128)S(1)}, f32[8,1024]{1,0:T(8,128)S(1)}, u32[]{:S(2)}, u32[]{:S(2)}) collective-permute-start(f32[8,1024]{1,0:T(8,128)S(1)} %get-tuple-element.70.b1), channel_id=1, source_target_pairs={{0,24},{8,16},{16,8},{24,0},{1,25},{9,17},{17,9},{25,1},{2,26},{10... | collective-permute-start | bytes 98312 | tf_op jit(solution)/shard_map/ppermute | solution.py:65
  48.1 0.0 collective-permute-done.13.n1
  48.1 0.0 collective-permute-start.18
  48.1 0.0 collective-permute-done.14.n2
  48.1 2.1 %collective-permute-start.19 = (f32[8,1024]{1,0:T(8,128)S(1)}, f32[8,1024]{1,0:T(8,128)S(1)}, u32[]{:S(2)}, u32[]{:S(2)}) collective-permute-start(f32[8,1024]{1,0:T(8,128)S(1)} %get-tuple-element.72.b3), channel_id=1, source_target_pairs={{0,6},{2,4},{4,2},{6,0},{1,7},{3,5},{5,3},{7,1},{8,14},{10,12},{12... | collective-permute-start | bytes 98312 | tf_op jit(solution)/shard_map/ppermute | solution.py:65
  50.3 0.7 %inverse.1 = (f32[32,128]{1,0:T(8,128)S(1)}, f32[32,128]{1,0:T(8,128)S(1)}, f32[2,4096,1024]{2,1,0:T(8,128)S(1)}) custom-call(f32[2,4096,1024]{2,1,0:T(8,128)S(1)} %get-tuple-element.56.same, f32[32,128]{1,0:T(8,128)S(1)} %get-tuple-element.57.refs_0_, f32[32,128]{1,0:T(8,128)S(1)} %get-tuple-element.58.refs_1_), custom_call_target="tpu_custom_call", output_to_operand_aliasing={{2}: (0, {})} | custom-call | tf_op jit(solution)/shard_map/inverse/pallas_call | solution.py:247
  50.9 0.0 collective-permute-done.15.n3
  51.0 6.8 %mix0.1 = (f32[1,1,2,4096,1024]{4,3,2,1,0:T(8,128)}, f32[1,1,2,8,1024]{4,3,2,1,0:T(8,128)}, f32[1,1,2,8,1024]{4,3,2,1,0:T(8,128)}, f32[2,4096,1024]{2,1,0:T(8,128)S(1)}) custom-call(f32[2,4096,1024]{2,1,0:T(8,128)S(1)} %get-tuple-element.59.same, f32[32,4096]{1,0:T(8,128)S(1)} %get-tuple-element.60.differ, ...), custom_call_target="tpu_custom_call", output_to_operand_aliasing={{3}: (0, {})} | custom-call | tf_op jit(solution)/shard_map/mix0/pallas_call | solution.py:319
  57.8 0.0 collective-permute-done.16.n0
  57.8 0.0 collective-permute-done.17.n1
  57.8 0.0 collective-permute-done.18.n2
  57.8 0.0 collective-permute-done.19.n3
  57.8 6.8 %mix1.1 = (f32[1,1,2,4096,1024]{4,3,2,1,0:T(8,128)}, f32[1,1,2,8,1024]{4,3,2,1,0:T(8,128)}, f32[1,1,2,8,1024]{4,3,2,1,0:T(8,128)}, f32[2,4096,1024]{2,1,0:T(8,128)S(1)}) custom-call(f32[2,4096,1024]{2,1,0:T(8,128)S(1)} %get-tuple-element.66.same, ...), custom_call_target="tpu_custom_call", output_to_operand_aliasing={{3}: (0, {}), {0}: (11, {}), {1}: (12, {}), {2}: (13, {})} | custom-call | tf_op jit(solution)/shard_map/mix1/pallas_call | solution.py:319
  (6 shorter events, 0.0 us)
Async XLA Ops:
  0.6 7.6 %copy-start = (f32[1,1,2,8,1024]{4,3,2,1,0:T(8,128)S(1)}, f32[1,1,2,8,1024]{4,3,2,1,0:T(8,128)}, u32[]{:S(2)}) copy-start(f32[1,1,2,8,1024]{4,3,2,1,0:T(8,128)} %f0.3) | copy-start | bytes 196612
  0.6 7.6 %copy-start.1 = (f32[1,1,2,8,1024]{4,3,2,1,0:T(8,128)S(1)}, f32[1,1,2,8,1024]{4,3,2,1,0:T(8,128)}, u32[]{:S(2)}) copy-start(f32[1,1,2,8,1024]{4,3,2,1,0:T(8,128)} %f2.3) | copy-start | bytes 196612
  0.7 5.4 %collective-permute-start = (f32[1,1,2,8,1024]{4,3,2,1,0:T(8,128)}, f32[1,1,2,8,1024]{4,3,2,1,0:T(8,128)S(1)}, u32[]{:S(2)}, u32[]{:S(2)}) collective-permute-start(f32[1,1,2,8,1024]{4,3,2,1,0:T(8,128)} %f0.3), channel_id=1, source_target_pairs={{0,8},{8,16},{16,24},{24,0},{1,9},{9,17},{17,25},{25,1},{2,10},{10... | collective-permute-start | bytes 196616 | tf_op jit(solution)/shard_map/ppermute | solution.py:51
  1.2 7.1 %collective-permute-start.1 = (f32[1,1,2,8,1024]{4,3,2,1,0:T(8,128)}, f32[1,1,2,8,1024]{4,3,2,1,0:T(8,128)S(1)}, u32[]{:S(2)}, u32[]{:S(2)}) collective-permute-start(f32[1,1,2,8,1024]{4,3,2,1,0:T(8,128)} %f2.3), channel_id=1, source_target_pairs={{0,2},{2,4},{4,6},{6,0},{1,3},{3,5},{5,7},{7,1},{8,10},{10,12},{12... | collective-permute-start | bytes 196616 | tf_op jit(solution)/shard_map/ppermute | solution.py:51
  14.8 11.0 %collective-permute-start.2 = (f32[8,4096]{1,0:T(8,128)S(1)}, f32[8,4096]{1,0:T(8,128)S(1)}, u32[]{:S(2)}, u32[]{:S(2)}) collective-permute-start(f32[8,4096]{1,0:T(8,128)S(1)} %get-tuple-element.43.o0), channel_id=1, source_target_pairs={{0,8},{8,0},{16,24},{24,16},{1,9},{9,1},{17,25},{25,17},{2,10},{10... | collective-permute-start | bytes 393224 | tf_op jit(solution)/shard_map/ppermute | solution.py:65
  15.5 10.8 %collective-permute-start.3 = (f32[8,4096]{1,0:T(8,128)S(1)}, f32[8,4096]{1,0:T(8,128)S(1)}, u32[]{:S(2)}, u32[]{:S(2)}) collective-permute-start(f32[8,4096]{1,0:T(8,128)S(1)} %get-tuple-element.44.o1), channel_id=1, source_target_pairs={{0,24},{8,16},{16,8},{24,0},{1,25},{9,17},{17,9},{25,1},{2,26},{10... | collective-permute-start | bytes 393224 | tf_op jit(solution)/shard_map/ppermute | solution.py:65
  17.1 9.9 %collective-permute-start.4 = (f32[8,4096]{1,0:T(8,128)S(1)}, f32[8,4096]{1,0:T(8,128)S(1)}, u32[]{:S(2)}, u32[]{:S(2)}) collective-permute-start(f32[8,4096]{1,0:T(8,128)S(1)} %get-tuple-element.45.o2), channel_id=1, source_target_pairs={{0,2},{2,0},{4,6},{6,4},{1,3},{3,1},{5,7},{7,5},{8,10},{10,8},{12,... | collective-permute-start | bytes 393224 | tf_op jit(solution)/shard_map/ppermute | solution.py:65
  17.1 11.8 %collective-permute-start.5 = (f32[8,4096]{1,0:T(8,128)S(1)}, f32[8,4096]{1,0:T(8,128)S(1)}, u32[]{:S(2)}, u32[]{:S(2)}) collective-permute-start(f32[8,4096]{1,0:T(8,128)S(1)} %get-tuple-element.46.o3), channel_id=1, source_target_pairs={{0,6},{2,4},{4,2},{6,0},{1,7},{3,5},{5,3},{7,1},{8,14},{10,12},{12... | collective-permute-start | bytes 393224 | tf_op jit(solution)/shard_map/ppermute | solution.py:65
  25.7 9.1 %collective-permute-start.6 = (f32[8,4096]{1,0:T(8,128)S(1)}, f32[8,4096]{1,0:T(8,128)S(1)}, u32[]{:S(2)}, u32[]{:S(2)}) collective-permute-start(f32[8,4096]{1,0:T(8,128)S(1)} %get-tuple-element.48.o0), channel_id=1, source_target_pairs={{0,8},{8,0},{16,24},{24,16},{1,9},{9,1},{17,25},{25,17},{2,10},{10... | collective-permute-start | bytes 393224 | tf_op jit(solution)/shard_map/ppermute | solution.py:65
  25.8 9.0 %collective-permute-start.7 = (f32[8,4096]{1,0:T(8,128)S(1)}, f32[8,4096]{1,0:T(8,128)S(1)}, u32[]{:S(2)}, u32[]{:S(2)}) collective-permute-start(f32[8,4096]{1,0:T(8,128)S(1)} %get-tuple-element.49.o1), channel_id=1, source_target_pairs={{0,24},{8,16},{16,8},{24,0},{1,25},{9,17},{17,9},{25,1},{2,26},{10... | collective-permute-start | bytes 393224 | tf_op jit(solution)/shard_map/ppermute | solution.py:65
  26.4 8.5 %collective-permute-start.8 = (f32[8,4096]{1,0:T(8,128)S(1)}, f32[8,4096]{1,0:T(8,128)S(1)}, u32[]{:S(2)}, u32[]{:S(2)}) collective-permute-start(f32[8,4096]{1,0:T(8,128)S(1)} %get-tuple-element.50.o2), channel_id=1, source_target_pairs={{0,2},{2,0},{4,6},{6,4},{1,3},{3,1},{5,7},{7,5},{8,10},{10,8},{12,... | collective-permute-start | bytes 393224 | tf_op jit(solution)/shard_map/ppermute | solution.py:65
  27.0 8.4 %collective-permute-start.9 = (f32[8,4096]{1,0:T(8,128)S(1)}, f32[8,4096]{1,0:T(8,128)S(1)}, u32[]{:S(2)}, u32[]{:S(2)}) collective-permute-start(f32[8,4096]{1,0:T(8,128)S(1)} %get-tuple-element.51.o3), channel_id=1, source_target_pairs={{0,6},{2,4},{4,2},{6,0},{1,7},{3,5},{5,3},{7,1},{8,14},{10,12},{12... | collective-permute-start | bytes 393224 | tf_op jit(solution)/shard_map/ppermute | solution.py:65
  33.2 7.9 %collective-permute-start.10 = (f32[32,1152]{1,0:T(8,128)S(1)}, f32[32,1152]{1,0:T(8,128)S(1)}, u32[]{:S(2)}, u32[]{:S(2)}) collective-permute-start(f32[32,1152]{1,0:T(8,128)S(1)} %get-tuple-element.53.mine), channel_id=1, source_target_pairs={{0,1},{1,0},{2,3},{3,2},{4,5},{5,4},{6,7},{7,6},{8,9},{9,8},{10,11... | collective-permute-start | bytes 442376 | tf_op jit(solution)/shard_map/ppermute | solution.py:56
  39.6 5.2 %collective-permute-start.11 = (f32[32,1152]{1,0:T(8,128)S(1)}, f32[32,1152]{1,0:T(8,128)S(1)}, u32[]{:S(2)}, u32[]{:S(2)}) collective-permute-start(f32[32,1152]{1,0:T(8,128)S(1)} %get-tuple-element.55.mine), channel_id=1, source_target_pairs={{0,1},{1,0},{2,3},{3,2},{4,5},{5,4},{6,7},{7,6},{8,9},{9,8},{10,11... | collective-permute-start | bytes 442376 | tf_op jit(solution)/shard_map/ppermute | solution.py:56
  41.2 5.5 %collective-permute-start.12 = (f32[8,1024]{1,0:T(8,128)S(1)}, f32[8,1024]{1,0:T(8,128)S(1)}, u32[]{:S(2)}, u32[]{:S(2)}) collective-permute-start(f32[8,1024]{1,0:T(8,128)S(1)} %get-tuple-element.62.b0), channel_id=1, source_target_pairs={{0,8},{8,0},{16,24},{24,16},{1,9},{9,1},{17,25},{25,17},{2,10},{10... | collective-permute-start | bytes 98312 | tf_op jit(solution)/shard_map/ppermute | solution.py:65
  41.2 6.9 %collective-permute-start.13 = (f32[8,1024]{1,0:T(8,128)S(1)}, f32[8,1024]{1,0:T(8,128)S(1)}, u32[]{:S(2)}, u32[]{:S(2)}) collective-permute-start(f32[8,1024]{1,0:T(8,128)S(1)} %get-tuple-element.63.b1), channel_id=1, source_target_pairs={{0,24},{8,16},{16,8},{24,0},{1,25},{9,17},{17,9},{25,1},{2,26},{10... | collective-permute-start | bytes 98312 | tf_op jit(solution)/shard_map/ppermute | solution.py:65
  43.0 5.1 %collective-permute-start.14 = (f32[8,1024]{1,0:T(8,128)S(1)}, f32[8,1024]{1,0:T(8,128)S(1)}, u32[]{:S(2)}, u32[]{:S(2)}) collective-permute-start(f32[8,1024]{1,0:T(8,128)S(1)} %get-tuple-element.64.b2), channel_id=1, source_target_pairs={{0,2},{2,0},{4,6},{6,4},{1,3},{3,1},{5,7},{7,5},{8,10},{10,8},{12,... | collective-permute-start | bytes 98312 | tf_op jit(solution)/shard_map/ppermute | solution.py:65
  44.8 13.0 %collective-permute-start.16 = (f32[8,1024]{1,0:T(8,128)S(1)}, f32[8,1024]{1,0:T(8,128)S(1)}, u32[]{:S(2)}, u32[]{:S(2)}) collective-permute-start(f32[8,1024]{1,0:T(8,128)S(1)} %get-tuple-element.69.b0), channel_id=1, source_target_pairs={{0,8},{8,0},{16,24},{24,16},{1,9},{9,1},{17,25},{25,17},{2,10},{10... | collective-permute-start | bytes 98312 | tf_op jit(solution)/shard_map/ppermute | solution.py:65
  44.9 6.1 %collective-permute-start.15 = (f32[8,1024]{1,0:T(8,128)S(1)}, f32[8,1024]{1,0:T(8,128)S(1)}, u32[]{:S(2)}, u32[]{:S(2)}) collective-permute-start(f32[8,1024]{1,0:T(8,128)S(1)} %get-tuple-element.65.b3), channel_id=1, source_target_pairs={{0,6},{2,4},{4,2},{6,0},{1,7},{3,5},{5,3},{7,1},{8,14},{10,12},{12... | collective-permute-start | bytes 98312 | tf_op jit(solution)/shard_map/ppermute | solution.py:65
  46.7 11.1 %collective-permute-start.17 = (f32[8,1024]{1,0:T(8,128)S(1)}, f32[8,1024]{1,0:T(8,128)S(1)}, u32[]{:S(2)}, u32[]{:S(2)}) collective-permute-start(f32[8,1024]{1,0:T(8,128)S(1)} %get-tuple-element.70.b1), channel_id=1, source_target_pairs={{0,24},{8,16},{16,8},{24,0},{1,25},{9,17},{17,9},{25,1},{2,26},{10... | collective-permute-start | bytes 98312 | tf_op jit(solution)/shard_map/ppermute | solution.py:65
  48.1 9.7 %collective-permute-start.18 = (f32[8,1024]{1,0:T(8,128)S(1)}, f32[8,1024]{1,0:T(8,128)S(1)}, u32[]{:S(2)}, u32[]{:S(2)}) collective-permute-start(f32[8,1024]{1,0:T(8,128)S(1)} %get-tuple-element.71.b2), channel_id=1, source_target_pairs={{0,2},{2,0},{4,6},{6,4},{1,3},{3,1},{5,7},{7,5},{8,10},{10,8},{12,... | collective-permute-start | bytes 98312 | tf_op jit(solution)/shard_map/ppermute | solution.py:65
  48.1 9.7 %collective-permute-start.19 = (f32[8,1024]{1,0:T(8,128)S(1)}, f32[8,1024]{1,0:T(8,128)S(1)}, u32[]{:S(2)}, u32[]{:S(2)}) collective-permute-start(f32[8,1024]{1,0:T(8,128)S(1)} %get-tuple-element.72.b3), channel_id=1, source_target_pairs={{0,6},{2,4},{4,2},{6,0},{1,7},{3,5},{5,3},{7,1},{8,14},{10,12},{12... | collective-permute-start | bytes 98312 | tf_op jit(solution)/shard_map/ppermute | solution.py:65

commit v3 on v2

v3 whole, which is shorter than its diff:
```python
import functools

import jax
import jax.numpy as jnp
from jax import lax
from jax.experimental import pallas as pl
from jax.experimental.pallas import tpu as pltpu
from jax.sharding import PartitionSpec as P

f32 = jnp.float32
bf16 = jnp.bfloat16
mixing = 0.2
edges = 4
grant = 6 << 20

NN = (((1,), (0,)), ((), ()))
NT = (((1,), (1,)), ((), ()))
TN = (((0,), (0,)), ((), ()))

in_vmem = pl.BlockSpec(memory_space=pltpu.VMEM)
in_hbm = pl.BlockSpec(memory_space=pltpu.HBM)


def vmem(value):
    return pltpu.with_memory_space_constraint(value, pltpu.VMEM)


def hbm(value):
    return pltpu.with_memory_space_constraint(value, pltpu.HBM)


def cost(held, passes):
    _, rows, features = held.shape
    flops = passes * 2 * 256 * rows * features
    return pl.CostEstimate(flops=flops, bytes_accessed=8 * rows * features, transcendentals=0)


def dot(a, b, dims):
    return lax.dot_general(a, b, dims, preferred_element_type=f32)


def split(value):
    high = value.astype(bf16)
    return high, (value - high.astype(f32)).astype(bf16)


def chunk_of(rows, most):
    size = min(rows, most)
    while rows % size:
        size //= 2
    return size


def shifted(value, axis, steps):
    count = lax.axis_size(axis)
    pairs = [(source, (source + steps) % count) for source in range(count)]
    return lax.ppermute(value, axis, pairs)


def from_partner(value, axis, distance):
    count = lax.axis_size(axis)
    return lax.ppermute(value, axis, [(i, i ^ distance) for i in range(count)])


def exchange(values):
    swapped = []
    for slot, value in enumerate(values):
        axis, colour = ("ry", "rx")[slot // 2], 1 - slot % 2
        count = lax.axis_size(axis)
        pairs = [(i, (i + (1 if i % 2 == colour else -1)) % count) for i in range(count)]
        swapped.append(lax.ppermute(value, axis, pairs))
    return swapped


def odd(axis):
    return lax.rem(lax.axis_index(axis), 2) == 1


def piece_copy(weights, held, sems, size, mat, row, sem):
    here = pl.ds(row, size)
    return pltpu.make_async_copy(weights.at[0, 0, mat, here], held.at[mat, here], sems.at[sem])


def piece_copies(weights, held, sems, size, first, until):
    rows = held.shape[1]
    places = [divmod(piece * size, rows) for piece in range(first, until)]
    return [
        piece_copy(weights, held, sems, size, mat, row, sem)
        for sem, (mat, row) in enumerate(places)
    ]


def load_kernel(size, until, weights, held, sems):
    copies = piece_copies(weights, held, sems, size, 0, until)
    for copy in copies:
        copy.start()
    for copy in copies:
        copy.wait()


def load(weights, size, until):
    return pl.pallas_call(
        functools.partial(load_kernel, size, until),
        name="load",
        out_shape=jax.ShapeDtypeStruct(weights.shape[2:], f32),
        in_specs=[in_hbm],
        out_specs=in_vmem,
        scratch_shapes=[pltpu.SemaphoreType.DMA((until,))],
        compiler_params=pltpu.CompilerParams(vmem_limit_bytes=grant),
    )(hbm(weights))


def project_kernel(
    mat, chunk, size, first, until, same, f0, f1, f2, f3, weights, o0, o1, o2, o3, held, sems
):
    rows = held.shape[1]
    pieces = rows // size
    copies = piece_copies(weights, held, sems, size, first, until)
    for copy in copies:
        copy.start()
    rank = f0.shape[-2]
    slots = []
    for axis, own, lower in (("ry", f0, f1), ("rx", f2, f3)):
        own, lower, swap = own[0, 0, mat], lower[0, 0, mat], odd(axis)
        slots += [jnp.where(swap, own, lower), jnp.where(swap, lower, own)]
    high, low = split(jnp.concatenate(slots, 0))
    stack = jnp.concatenate(
        [jnp.concatenate([high, high], 1), jnp.concatenate([low, low], 1)], 0
    )
    width = edges * rank

    @pl.loop(0, rows // chunk)
    def _(step):
        here = pl.ds(pl.multiple_of(step * chunk, chunk), chunk)
        for part in range(chunk // size):
            piece = step * (chunk // size) + part

            @pl.when(mat * pieces + piece >= first)
            def _():
                row = pl.multiple_of(piece * size, size)
                sem = mat * pieces + piece - first
                piece_copy(weights, held, sems, size, mat, row, sem).wait()

        w_high, w_low = split(held[mat, here, :])
        both = dot(stack, jnp.concatenate([w_high, w_low], 1), NT)
        total = both[:width] + both[width:]
        for slot, out in enumerate((o0, o1, o2, o3)):
            out[:, here] = total[slot * rank : (slot + 1) * rank]

    for copy in copies[(mat + 1) * pieces - first :]:
        copy.wait()


def project(held, factors, weights, mat, size, first, until):
    rows = held.shape[1]
    rank = factors[0].shape[-2]
    return pl.pallas_call(
        functools.partial(project_kernel, mat, chunk_of(rows, 1024), size, first, until),
        name=f"project{mat}",
        out_shape=[jax.ShapeDtypeStruct((rank, rows), f32)] * edges
        + [jax.ShapeDtypeStruct(held.shape, f32)],
        in_specs=[in_vmem] * 5 + [in_hbm],
        out_specs=[in_vmem] * (edges + 1),
        scratch_shapes=[pltpu.SemaphoreType.DMA((max(until - first, 1),))],
        input_output_aliases={0: edges},
        cost_estimate=cost(held, 2),
        compiler_params=pltpu.CompilerParams(vmem_limit_bytes=grant),
    )(vmem(held), *factors, hbm(weights))


def back_kernel(mat, chunk, same, o0, o1, o2, o3, n0, n1, n2, n3, differ, sums, held):
    rank = o0.shape[0]
    width = edges * rank
    features = held.shape[2]
    sums[...] = jnp.zeros_like(sums)

    def body(step, gram):
        here = pl.ds(pl.multiple_of(step * chunk, chunk), chunk)
        p = jnp.concatenate(
            [o[:, here] - n[:, here] for o, n in zip((o0, o1, o2, o3), (n0, n1, n2, n3))], 0
        )
        differ[:, here] = p
        high, low = split(p)
        w_high, w_low = split(held[mat, here, :])
        pair = jnp.concatenate([high, low], 0)
        stack = jnp.concatenate([pair, pair], 1)
        both = dot(stack, jnp.concatenate([w_high, w_low], 0), NN)
        sums[:, :features] += both[:width] + both[width:]
        return gram + dot(pair, pair, NT)

    gram = lax.fori_loop(
        0, held.shape[1] // chunk, body, jnp.zeros((2 * width, 2 * width), f32)
    )
    total = (gram[:width, :width] + gram[width:, width:]) + (
        gram[:width, width:] + gram[width:, :width]
    )
    for edge in range(edges):
        here = slice(edge * rank, (edge + 1) * rank)
        sums[here, features : features + rank] = total[here, here]


def back(held, own, near, mat):
    _, rows, features = held.shape
    rank = own[0].shape[0]
    return pl.pallas_call(
        functools.partial(back_kernel, mat, chunk_of(rows, 1024)),
        name=f"back{mat}",
        out_shape=[
            jax.ShapeDtypeStruct((edges * rank, rows), f32),
            jax.ShapeDtypeStruct((edges * rank, features + 128), f32),
            jax.ShapeDtypeStruct(held.shape, f32),
        ],
        in_specs=[in_vmem] * 9,
        out_specs=[in_vmem] * 3,
        input_output_aliases={0: 2},
        cost_estimate=cost(held, 2),
        compiler_params=pltpu.CompilerParams(vmem_limit_bytes=grant),
    )(vmem(held), *own, *near)


def add_kernel(same, *refs):
    *refs, held = refs
    pairs, outs = refs[:-edges], refs[-edges:]
    mats, rank, features = outs[0].shape
    for mat in range(mats):
        mine, other = pairs[2 * mat], pairs[2 * mat + 1]
        for slot, out in enumerate(outs):
            here = slice(slot * rank, (slot + 1) * rank)
            out[mat] = mine[here, :features] + other[here, :features]


def add(held, pairs, rank):
    mats = len(pairs)
    pairs = [terms for pair in pairs for terms in pair]
    sums = jax.ShapeDtypeStruct((mats, rank, held.shape[-1]), f32)
    return pl.pallas_call(
        add_kernel,
        name="add",
        out_shape=[sums] * edges + [jax.ShapeDtypeStruct(held.shape, f32)],
        in_specs=[in_vmem] * (1 + len(pairs)),
        out_specs=[in_vmem] * (edges + 1),
        input_output_aliases={0: edges},
        compiler_params=pltpu.CompilerParams(vmem_limit_bytes=grant),
    )(vmem(held), *pairs)


def inverse_kernel(rank, same, mine, other, inverse, held):
    width = edges * rank
    shape = (edges, rank, 128)
    row = lax.broadcasted_iota(jnp.int32, shape, 1)
    lane = lax.broadcasted_iota(jnp.int32, shape, 2)
    slot = lax.broadcasted_iota(jnp.int32, shape, 0)
    value = (mine[:, -128:] + other[:, -128:]).reshape(shape)
    value = jnp.where(lane < rank, value, (lane == width + slot * rank + row).astype(f32))
    pivots = jnp.ones((edges, rank, 1), f32)
    for j in range(rank):
        pivot = value[:, j : j + 1, j : j + 1]
        pivots = jnp.where(row[:, :, :1] == j, pivot, pivots)
        factor = jnp.where(row > j, value[:, :, j : j + 1] / pivot, 0.0)
        value = value - factor * value[:, j : j + 1, :]
    inverse[...] = (value / jnp.sqrt(pivots)).reshape(width, 128)


def inverse_factor(held, pair, rank, mat):
    return pl.pallas_call(
        functools.partial(inverse_kernel, rank),
        name=f"inverse{mat}",
        out_shape=[
            jax.ShapeDtypeStruct((edges * rank, 128), f32),
            jax.ShapeDtypeStruct(held.shape, f32),
        ],
        in_specs=[in_vmem] * 3,
        out_specs=[in_vmem] * 2,
        input_output_aliases={0: 1},
        compiler_params=pltpu.CompilerParams(vmem_limit_bytes=grant),
    )(vmem(held), *pair)


def mix_kernel(chunk, same, *refs):
    *refs, mixed, next_rx, next_ry, held, new_rx, new_ry, sems, new_sems = refs
    mats, rows, _ = held.shape
    differs, inverses = refs[:mats], refs[mats : 2 * mats]
    sums, near = refs[2 * mats : 2 * mats + edges], refs[2 * mats + edges :]
    rank = sums[0].shape[1]
    width = edges * rank
    steps = rows // chunk

    def copy(mat, step):
        here = pl.ds(pl.multiple_of(step * chunk, chunk), chunk)
        return pltpu.make_async_copy(
            held.at[mat, here], mixed.at[0, 0, mat, here], sems.at[mat, step]
        )

    for mat in range(mats):
        factor = inverses[mat][:, width : 2 * width]
        total = jnp.concatenate([b[mat] + n[mat] for b, n in zip(sums, near)], 0)
        updated = lax.dot_general(
            factor, total, NN, precision=lax.Precision.HIGHEST, preferred_element_type=f32
        )
        parts = [updated[slot * rank : (slot + 1) * rank] for slot in range(edges)]
        new_rx[mat] = jnp.where(odd("rx"), parts[2], parts[3])
        new_ry[mat] = jnp.where(odd("ry"), parts[0], parts[1])
        right = mixing * lax.dot_general(
            factor, updated, TN, precision=lax.Precision.HIGHEST, preferred_element_type=f32
        )
        r_high, r_low = split(right)
        terms = jnp.concatenate([r_high, r_high, r_low, r_low], 0)

        @pl.loop(0, steps)
        def _(step):
            here = pl.ds(pl.multiple_of(step * chunk, chunk), chunk)
            high, low = split(differs[mat][:, here])
            lhs = jnp.concatenate([high, low, high, low], 0)
            held[mat, here, :] -= dot(lhs, terms, TN)
            copy(mat, step).start()

    new_copies = [
        pltpu.make_async_copy(new_rx, next_rx.at[0, 0], new_sems.at[0]),
        pltpu.make_async_copy(new_ry, next_ry.at[0, 0], new_sems.at[1]),
    ]
    for new_copy in new_copies:
        new_copy.start()
    for mat in range(mats):

        @pl.loop(0, steps)
        def _(step):
            copy(mat, step).wait()

    for new_copy in new_copies:
        new_copy.wait()


def mix(held, differs, inverses, sums, near, shapes):
    mats, rows, features = held.shape
    rank = sums[0].shape[1]
    chunk = chunk_of(rows, 512)
    args = [vmem(held), *differs, *inverses, *sums, *near]
    return pl.pallas_call(
        functools.partial(mix_kernel, chunk),
        name="mix",
        out_shape=[jax.ShapeDtypeStruct(shape, f32) for shape in (*shapes, held.shape)],
        in_specs=[in_vmem] * len(args),
        out_specs=[in_hbm] * 3 + [in_vmem],
        scratch_shapes=[
            pltpu.VMEM((mats, rank, features), f32),
            pltpu.VMEM((mats, rank, features), f32),
            pltpu.SemaphoreType.DMA((mats, rows // chunk)),
            pltpu.SemaphoreType.DMA((2,)),
        ],
        input_output_aliases={0: 3},
        cost_estimate=cost(held, 4),
        compiler_params=pltpu.CompilerParams(vmem_limit_bytes=grant),
    )(*args)


def per_device(weights, factors_rx, factors_ry):
    mats, rows = weights.shape[2:4]
    rank = factors_rx.shape[-2]
    lower_ry = shifted(factors_ry, "ry", 1)
    lower_rx = shifted(factors_rx, "rx", 1)
    factors = [factors_ry, lower_ry, factors_rx, lower_rx]
    size = chunk_of(rows, 512)
    pieces = rows // size
    until = max(3 * pieces // 8, 1)
    held = load(weights, size, until)
    own = []
    for mat in range(mats):
        first, until = until, min((mat + 1) * pieces + pieces // 4, mats * pieces)
        *own_mat, held = project(held, factors, weights, mat, size, first, until)
        own.append(own_mat)
    near = [exchange(own_mat) for own_mat in own]
    differs, pairs = [], []
    tp = lax.axis_size("tp")
    for mat in range(mats):
        p, terms, held = back(held, own[mat], near[mat], mat)
        distance = 1
        while 2 * distance < tp:
            terms = terms + from_partner(terms, "tp", distance)
            distance *= 2
        other = from_partner(terms, "tp", distance) if tp > 1 else jnp.zeros_like(terms)
        differs.append(p)
        pairs.append((terms, other))
    inverses = [None] * mats
    for mat in range(mats - 1):
        inverses[mat], held = inverse_factor(held, pairs[mat], rank, mat)
    *sums, held = add(held, pairs, rank)
    near_sums = exchange(sums)
    inverses[-1], held = inverse_factor(held, pairs[-1], rank, mats - 1)
    shapes = (weights.shape, factors_rx.shape, factors_ry.shape)
    *results, held = mix(held, differs, inverses, sums, near_sums, shapes)
    return tuple(results)


def solution(mesh):
    return jax.shard_map(
        per_device,
        mesh=mesh,
        in_specs=(
            P("rx", "ry", None, "tp", None),
            P("rx", "ry", None, None, None),
            P("rx", "ry", None, None, None),
        ),
        out_specs=(
            P("rx", "ry", None, "tp", None),
            P("rx", "ry", None, None, None),
            P("rx", "ry", None, None, None),
        ),
        check_vma=False,
    )
```

time: 64.9 us -> 63.3 us (0.975)
  starting transfers between devices: 22 us -> 16.7 us
  waiting for transfers between devices: 3.71 us -> 8.78 us
  Pallas kernels: 38.1 us -> 37 us
    ppermute x16 -> x12, starting transfers between devices: 15.7 us -> 10.2 us  [exchange(): swapped.append(lax.ppermute(value, axis, pairs))]
    ppermute x16 -> x12, waiting for transfers between devices: 0.61 us -> 3.7 us  [exchange(): swapped.append(lax.ppermute(value, axis, pairs))]
    ppermute x2, waiting for transfers between devices: 0.87 us -> 3.49 us  [from_partner(): return lax.ppermute(value, axis, [(i, i ^ distance) for i in range(count)])]
    pallas_call x5 -> x4, Pallas kernels: 14.3 us -> 13.4 us  [the longest x1 12.1 us: mix(): pl.pallas_call(functools.partial(mix_kernel, chunk), name='mix', out_shap...]
  transfers between devices with their start and end apart: 20 -> 16, of which waited for: 3 -> 5; matrix products, arithmetic and copies ran while one was open for 0% -> 0% of each run, Pallas kernels for 38% -> 30%
where the time goes in v3:
time: 63.3 us; the launch traced here: 63.2 us
  Pallas kernels  37 us (58%)
  starting transfers between devices  16.7 us (26%)
  waiting for transfers between devices  8.78 us (14%)
  between operations  0.71 us (1%)
    pallas_call x2, Pallas kernels, project(): pl.pallas_call(functools.partial(project_kernel, mat, chunk_of(rows, 1024...  12.3 us
    pallas_call x1, Pallas kernels, mix(): pl.pallas_call(functools.partial(mix_kernel, chunk), name='mix', out_shap...  12.1 us
    ppermute x12, starting transfers between devices, exchange(): swapped.append(lax.ppermute(value, axis, pairs))  10.2 us
    pallas_call x2, Pallas kernels, back(): pl.pallas_call(functools.partial(back_kernel, mat, chunk_of(rows, 1024)),...  8.37 us
    ppermute x12, waiting for transfers between devices, exchange(): swapped.append(lax.ppermute(value, axis, pairs))  3.7 us
    ppermute x2, waiting for transfers between devices, from_partner(): return lax.ppermute(value, axis, [(i, i ^ distance) for i in range(count)])  3.49 us
    ppermute x2, starting transfers between devices, from_partner(): return lax.ppermute(value, axis, [(i, i ^ distance) for i in range(count)])  3.35 us
    ppermute x2, starting transfers between devices, shifted(): return lax.ppermute(value, axis, pairs)  3.14 us
  transfers between devices with their start and end apart: 16, of which 5 were waited for; matrix products, arithmetic and copies ran while one was open for 0% of the time, Pallas kernels for 30%

profile of v3, /device:TPU:0, one launch (start us, length us, event | category | flops | bytes accessed | tf_op | source)
XLA Modules:
  0.0 63.2 jit_solution(16587425995913455845)
XLA Ops:
  0.6 0.0 copy-start.1
  0.6 0.0 copy-start
  0.7 0.5 collective-permute-start.1
  1.2 2.6 %collective-permute-start = (f32[1,1,2,8,1024]{4,3,2,1,0:T(8,128)}, f32[1,1,2,8,1024]{4,3,2,1,0:T(8,128)S(1)}, u32[]{:S(2)}, u32[]{:S(2)}) collective-permute-start(f32[1,1,2,8,1024]{4,3,2,1,0:T(8,128)} %f0.3), channel_id=1, source_target_pairs={{0,2},{2,4},{4,6},{6,0},{1,3},{3,5},{5,7},{7,1},{8,10},{10,12},{12... | collective-permute-start | bytes 196616 | tf_op jit(solution)/shard_map/ppermute | solution.py:57
  3.8 2.9 %load.1.same = f32[2,4096,1024]{2,1,0:T(8,128)S(1)} custom-call(f32[1,1,2,4096,1024]{4,3,2,1,0:T(8,128)} %weights.5), custom_call_target="tpu_custom_call" | custom-call | tf_op jit(solution)/shard_map/load/pallas_call | solution.py:102
  6.7 0.0 collective-permute-done.1.f3
  6.7 1.6 %collective-permute-done.f1 = f32[1,1,2,8,1024]{4,3,2,1,0:T(8,128)S(1)} collective-permute-done((f32[1,1,2,8,1024]{4,3,2,1,0:T(8,128)}, f32[1,1,2,8,1024]{4,3,2,1,0:T(8,128)S(1)}, u32[]{:S(2)}, u32[]{:S(2)}) %collective-permute-start) | collective-permute-done | bytes 65568 | tf_op jit(solution)/shard_map/ppermute | solution.py:57
  8.3 0.0 copy-done.1
  8.3 0.0 copy-done
  8.3 5.9 %project0.1 = (f32[8,4096]{1,0:T(8,128)S(1)}, f32[8,4096]{1,0:T(8,128)S(1)}, f32[8,4096]{1,0:T(8,128)S(1)}, f32[8,4096]{1,0:T(8,128)S(1)}, f32[2,4096,1024]{2,1,0:T(8,128)S(1)}) custom-call(f32[2,4096,1024]{2,1,0:T(8,128)S(1)} %load.1.same, f32[1,1,2,8,1024]{4,3,2,1,0:T(8,128)S(1)} %copy-done, ...), custom_call_target="tpu_custom_call", output_to_operand_aliasing={{4}: (0, {})} | custom-call | flops 4294967296 | bytes 33554432 | tf_op jit(solution)/shard_map/project0/pallas_call | solution.py:157
  14.1 2.3 %collective-permute-start.2 = (f32[8,4096]{1,0:T(8,128)S(1)}, f32[8,4096]{1,0:T(8,128)S(1)}, u32[]{:S(2)}, u32[]{:S(2)}) collective-permute-start(f32[8,4096]{1,0:T(8,128)S(1)} %get-tuple-element.33.o0), channel_id=1, source_target_pairs={{0,6},{2,4},{4,2},{6,0},{1,7},{3,5},{5,3},{7,1},{8,14},{10,12},{12... | collective-permute-start | bytes 393224 | tf_op jit(solution)/shard_map/ppermute | solution.py:71
  16.4 0.0 collective-permute-start.3
  16.4 0.8 %collective-permute-start.4 = (f32[8,4096]{1,0:T(8,128)S(1)}, f32[8,4096]{1,0:T(8,128)S(1)}, u32[]{:S(2)}, u32[]{:S(2)}) collective-permute-start(f32[8,4096]{1,0:T(8,128)S(1)} %get-tuple-element.35.o2), channel_id=1, source_target_pairs={{0,24},{8,16},{16,8},{24,0},{1,25},{9,17},{17,9},{25,1},{2,26},{10... | collective-permute-start | bytes 393224 | tf_op jit(solution)/shard_map/ppermute | solution.py:71
  17.2 1.0 %collective-permute-start.5 = (f32[8,4096]{1,0:T(8,128)S(1)}, f32[8,4096]{1,0:T(8,128)S(1)}, u32[]{:S(2)}, u32[]{:S(2)}) collective-permute-start(f32[8,4096]{1,0:T(8,128)S(1)} %get-tuple-element.36.o3), channel_id=1, source_target_pairs={{0,8},{8,0},{16,24},{24,16},{1,9},{9,1},{17,25},{25,17},{2,10},{10... | collective-permute-start | bytes 393224 | tf_op jit(solution)/shard_map/ppermute | solution.py:71
  18.2 6.5 %project1.1 = (f32[8,4096]{1,0:T(8,128)S(1)}, f32[8,4096]{1,0:T(8,128)S(1)}, f32[8,4096]{1,0:T(8,128)S(1)}, f32[8,4096]{1,0:T(8,128)S(1)}, f32[2,4096,1024]{2,1,0:T(8,128)S(1)}) custom-call(f32[2,4096,1024]{2,1,0:T(8,128)S(1)} %get-tuple-element.31.same, f32[1,1,2,8,1024]{4,3,2,1,0:T(8,128)S(1)} %copy-done, ...), custom_call_target="tpu_custom_call", output_to_operand_aliasing={{4}: (0, {})} | custom-call | flops 4294967296 | bytes 33554432 | tf_op jit(solution)/shard_map/project1/pallas_call | solution.py:157
  24.7 2.1 %collective-permute-start.6 = (f32[8,4096]{1,0:T(8,128)S(1)}, f32[8,4096]{1,0:T(8,128)S(1)}, u32[]{:S(2)}, u32[]{:S(2)}) collective-permute-start(f32[8,4096]{1,0:T(8,128)S(1)} %get-tuple-element.38.o0), channel_id=1, source_target_pairs={{0,6},{2,4},{4,2},{6,0},{1,7},{3,5},{5,3},{7,1},{8,14},{10,12},{12... | collective-permute-start | bytes 393224 | tf_op jit(solution)/shard_map/ppermute | solution.py:71
  26.8 0.0 collective-permute-done.2.n0
  26.8 1.1 %collective-permute-start.7 = (f32[8,4096]{1,0:T(8,128)S(1)}, f32[8,4096]{1,0:T(8,128)S(1)}, u32[]{:S(2)}, u32[]{:S(2)}) collective-permute-start(f32[8,4096]{1,0:T(8,128)S(1)} %get-tuple-element.39.o1), channel_id=1, source_target_pairs={{0,2},{2,0},{4,6},{6,4},{1,3},{3,1},{5,7},{7,5},{8,10},{10,8},{12,... | collective-permute-start | bytes 393224 | tf_op jit(solution)/shard_map/ppermute | solution.py:71
  27.9 0.0 collective-permute-done.3.n1
  27.9 0.0 collective-permute-start.8
  27.9 0.0 collective-permute-done.4.n2
  27.9 0.1 collective-permute-start.9
  28.0 0.0 collective-permute-done.5.n3
  28.0 4.2 %back0.1 = (f32[32,4096]{1,0:T(8,128)S(1)}, f32[32,1152]{1,0:T(8,128)S(1)}, f32[2,4096,1024]{2,1,0:T(8,128)S(1)}) custom-call(f32[2,4096,1024]{2,1,0:T(8,128)S(1)} %get-tuple-element.32.same, f32[8,4096]{1,0:T(8,128)S(1)} %get-tuple-element.33.o0, f32[8,4096]{1,0:T(8,128)S(1)} %get-tuple-element.34.o1, ...), custom_call_target="tpu_custom_call", output_to_operand_aliasing={{2}: (0, {})} | custom-call | flops 4294967296 | bytes 33554432 | tf_op jit(solution)/shard_map/back0/pallas_call | solution.py:205
  32.2 1.8 %collective-permute-start.10 = (f32[32,1152]{1,0:T(8,128)S(1)}, f32[32,1152]{1,0:T(8,128)S(1)}, u32[]{:S(2)}, u32[]{:S(2)}) collective-permute-start(f32[32,1152]{1,0:T(8,128)S(1)} %get-tuple-element.43.mine.refs_0_), channel_id=1, source_target_pairs={{0,1},{1,0},{2,3},{3,2},{4,5},{5,4},{6,7},{7,6},{8,9},{9,8},{10,11... | collective-permute-start | bytes 442376 | tf_op jit(solution)/shard_map/ppermute | solution.py:62
  34.0 0.0 collective-permute-done.6.n0
  34.0 0.7 %collective-permute-done.7.n1 = f32[8,4096]{1,0:T(8,128)S(1)} collective-permute-done((f32[8,4096]{1,0:T(8,128)S(1)}, f32[8,4096]{1,0:T(8,128)S(1)}, u32[]{:S(2)}, u32[]{:S(2)}) %collective-permute-start.7) | collective-permute-done | bytes 131104 | tf_op jit(solution)/shard_map/ppermute | solution.py:71
  34.7 0.0 collective-permute-done.8.n2
  34.7 0.0 collective-permute-done.9.n3
  34.7 4.2 %back1.1 = (f32[32,4096]{1,0:T(8,128)S(1)}, f32[32,1152]{1,0:T(8,128)S(1)}, f32[2,4096,1024]{2,1,0:T(8,128)S(1)}) custom-call(f32[2,4096,1024]{2,1,0:T(8,128)S(1)} %get-tuple-element.37.same, f32[8,4096]{1,0:T(8,128)S(1)} %get-tuple-element.38.o0, f32[8,4096]{1,0:T(8,128)S(1)} %get-tuple-element.39.o1, ...), custom_call_target="tpu_custom_call", output_to_operand_aliasing={{2}: (0, {})} | custom-call | flops 4294967296 | bytes 33554432 | tf_op jit(solution)/shard_map/back1/pallas_call | solution.py:205
  38.9 1.5 %collective-permute-start.11 = (f32[32,1152]{1,0:T(8,128)S(1)}, f32[32,1152]{1,0:T(8,128)S(1)}, u32[]{:S(2)}, u32[]{:S(2)}) collective-permute-start(f32[32,1152]{1,0:T(8,128)S(1)} %get-tuple-element.45.refs_2_.mine), channel_id=1, source_target_pairs={{0,1},{1,0},{2,3},{3,2},{4,5},{5,4},{6,7},{7,6},{8,9},{9,8},{10,11... | collective-permute-start | bytes 442376 | tf_op jit(solution)/shard_map/ppermute | solution.py:62
  40.4 0.0 collective-permute-done.10.other.refs_1_
  40.5 0.7 %inverse0.1 = (f32[32,128]{1,0:T(8,128)S(1)}, f32[2,4096,1024]{2,1,0:T(8,128)S(1)}) custom-call(f32[2,4096,1024]{2,1,0:T(8,128)S(1)} %get-tuple-element.42.same, f32[32,1152]{1,0:T(8,128)S(1)} %get-tuple-element.43.mine.refs_0_, f32[32,1152]{1,0:T(8,128)S(1)} %collective-permute-done.10.other.refs_1_), custom_call_target="tpu_custom_call", output_to_operand_aliasing={{1}: (0, {})} | custom-call | tf_op jit(solution)/shard_map/inverse0/pallas_call | solution.py:265
  41.1 3.5 %collective-permute-done.11.refs_3_.other = f32[32,1152]{1,0:T(8,128)S(1)} collective-permute-done((f32[32,1152]{1,0:T(8,128)S(1)}, f32[32,1152]{1,0:T(8,128)S(1)}, u32[]{:S(2)}, u32[]{:S(2)}) %collective-permute-start.11) | collective-permute-done | bytes 147488 | tf_op jit(solution)/shard_map/ppermute | solution.py:62
  44.6 1.5 %collective-permute-start.12 = (f32[2,8,1024]{2,1,0:T(8,128)S(1)}, f32[2,8,1024]{2,1,0:T(8,128)S(1)}, u32[]{:S(2)}, u32[]{:S(2)}) collective-permute-start(f32[2,8,1024]{2,1,0:T(8,128)S(1)} %get-tuple-element.52.refs_4_), channel_id=1, source_target_pairs={{0,6},{2,4},{4,2},{6,0},{1,7},{3,5},{5,3},{7,1},{8,14},{10,12},{12... | collective-permute-start | bytes 196616 | tf_op jit(solution)/shard_map/ppermute | solution.py:71
  46.1 0.0 collective-permute-start.13
  46.1 0.0 collective-permute-start.14
  46.1 1.3 %collective-permute-start.15 = (f32[2,8,1024]{2,1,0:T(8,128)S(1)}, f32[2,8,1024]{2,1,0:T(8,128)S(1)}, u32[]{:S(2)}, u32[]{:S(2)}) collective-permute-start(f32[2,8,1024]{2,1,0:T(8,128)S(1)} %get-tuple-element.55.refs_7_), channel_id=1, source_target_pairs={{0,8},{8,0},{16,24},{24,16},{1,9},{9,1},{17,25},{25,17},{2,10},{10... | collective-permute-start | bytes 196616 | tf_op jit(solution)/shard_map/ppermute | solution.py:71
  47.4 0.7 %inverse1.1 = (f32[32,128]{1,0:T(8,128)S(1)}, f32[2,4096,1024]{2,1,0:T(8,128)S(1)}) custom-call(f32[2,4096,1024]{2,1,0:T(8,128)S(1)} %get-tuple-element.46.same, f32[32,1152]{1,0:T(8,128)S(1)} %get-tuple-element.45.refs_2_.mine, f32[32,1152]{1,0:T(8,128)S(1)} %collective-permute-done.11.refs_3_.other), custom_call_target="tpu_custom_call", output_to_operand_aliasing={{1}: (0, {})} | custom-call | tf_op jit(solution)/shard_map/inverse1/pallas_call | solution.py:265
  48.1 2.8 %collective-permute-done.12.refs_8_ = f32[2,8,1024]{2,1,0:T(8,128)S(1)} collective-permute-done((f32[2,8,1024]{2,1,0:T(8,128)S(1)}, f32[2,8,1024]{2,1,0:T(8,128)S(1)}, u32[]{:S(2)}, u32[]{:S(2)}) %collective-permute-start.12) | collective-permute-done | bytes 65568 | tf_op jit(solution)/shard_map/ppermute | solution.py:71
  50.9 0.2 collective-permute-done.13.refs_9_
  51.1 0.0 collective-permute-done.14.refs_10_
  51.1 0.0 collective-permute-done.15.refs_11_
  51.1 12.1 %mix.1 = (f32[1,1,2,4096,1024]{4,3,2,1,0:T(8,128)}, f32[1,1,2,8,1024]{4,3,2,1,0:T(8,128)}, f32[1,1,2,8,1024]{4,3,2,1,0:T(8,128)}, f32[2,4096,1024]{2,1,0:T(8,128)S(1)}) custom-call(f32[2,4096,1024]{2,1,0:T(8,128)S(1)} %get-tuple-element.47.same, f32[32,4096]{1,0:T(8,128)S(1)} %get-tuple-element.48.refs_0_, ...), custom_call_target="tpu_custom_call", output_to_operand_aliasing={{3}: (0, {})} | custom-call | flops 8589934592 | bytes 33554432 | tf_op jit(solution)/shard_map/mix/pallas_call | solution.py:338
  (1 shorter events, 0.0 us)
Async XLA Ops:
  0.6 7.6 %copy-start.1 = (f32[1,1,2,8,1024]{4,3,2,1,0:T(8,128)S(1)}, f32[1,1,2,8,1024]{4,3,2,1,0:T(8,128)}, u32[]{:S(2)}) copy-start(f32[1,1,2,8,1024]{4,3,2,1,0:T(8,128)} %f2.3) | copy-start | bytes 196612
  0.6 7.6 %copy-start = (f32[1,1,2,8,1024]{4,3,2,1,0:T(8,128)S(1)}, f32[1,1,2,8,1024]{4,3,2,1,0:T(8,128)}, u32[]{:S(2)}) copy-start(f32[1,1,2,8,1024]{4,3,2,1,0:T(8,128)} %f0.3) | copy-start | bytes 196612
  0.7 6.0 %collective-permute-start.1 = (f32[1,1,2,8,1024]{4,3,2,1,0:T(8,128)}, f32[1,1,2,8,1024]{4,3,2,1,0:T(8,128)S(1)}, u32[]{:S(2)}, u32[]{:S(2)}) collective-permute-start(f32[1,1,2,8,1024]{4,3,2,1,0:T(8,128)} %f2.3), channel_id=1, source_target_pairs={{0,8},{8,16},{16,24},{24,0},{1,9},{9,17},{17,25},{25,1},{2,10},{10... | collective-permute-start | bytes 196616 | tf_op jit(solution)/shard_map/ppermute | solution.py:57
  1.2 7.1 %collective-permute-start = (f32[1,1,2,8,1024]{4,3,2,1,0:T(8,128)}, f32[1,1,2,8,1024]{4,3,2,1,0:T(8,128)S(1)}, u32[]{:S(2)}, u32[]{:S(2)}) collective-permute-start(f32[1,1,2,8,1024]{4,3,2,1,0:T(8,128)} %f0.3), channel_id=1, source_target_pairs={{0,2},{2,4},{4,6},{6,0},{1,3},{3,5},{5,7},{7,1},{8,10},{10,12},{12... | collective-permute-start | bytes 196616 | tf_op jit(solution)/shard_map/ppermute | solution.py:57
  14.1 12.7 %collective-permute-start.2 = (f32[8,4096]{1,0:T(8,128)S(1)}, f32[8,4096]{1,0:T(8,128)S(1)}, u32[]{:S(2)}, u32[]{:S(2)}) collective-permute-start(f32[8,4096]{1,0:T(8,128)S(1)} %get-tuple-element.33.o0), channel_id=1, source_target_pairs={{0,6},{2,4},{4,2},{6,0},{1,7},{3,5},{5,3},{7,1},{8,14},{10,12},{12... | collective-permute-start | bytes 393224 | tf_op jit(solution)/shard_map/ppermute | solution.py:71
  16.4 11.5 %collective-permute-start.3 = (f32[8,4096]{1,0:T(8,128)S(1)}, f32[8,4096]{1,0:T(8,128)S(1)}, u32[]{:S(2)}, u32[]{:S(2)}) collective-permute-start(f32[8,4096]{1,0:T(8,128)S(1)} %get-tuple-element.34.o1), channel_id=1, source_target_pairs={{0,2},{2,0},{4,6},{6,4},{1,3},{3,1},{5,7},{7,5},{8,10},{10,8},{12,... | collective-permute-start | bytes 393224 | tf_op jit(solution)/shard_map/ppermute | solution.py:71
  16.4 11.5 %collective-permute-start.4 = (f32[8,4096]{1,0:T(8,128)S(1)}, f32[8,4096]{1,0:T(8,128)S(1)}, u32[]{:S(2)}, u32[]{:S(2)}) collective-permute-start(f32[8,4096]{1,0:T(8,128)S(1)} %get-tuple-element.35.o2), channel_id=1, source_target_pairs={{0,24},{8,16},{16,8},{24,0},{1,25},{9,17},{17,9},{25,1},{2,26},{10... | collective-permute-start | bytes 393224 | tf_op jit(solution)/shard_map/ppermute | solution.py:71
  17.2 10.8 %collective-permute-start.5 = (f32[8,4096]{1,0:T(8,128)S(1)}, f32[8,4096]{1,0:T(8,128)S(1)}, u32[]{:S(2)}, u32[]{:S(2)}) collective-permute-start(f32[8,4096]{1,0:T(8,128)S(1)} %get-tuple-element.36.o3), channel_id=1, source_target_pairs={{0,8},{8,0},{16,24},{24,16},{1,9},{9,1},{17,25},{25,17},{2,10},{10... | collective-permute-start | bytes 393224 | tf_op jit(solution)/shard_map/ppermute | solution.py:71
  24.7 9.4 %collective-permute-start.6 = (f32[8,4096]{1,0:T(8,128)S(1)}, f32[8,4096]{1,0:T(8,128)S(1)}, u32[]{:S(2)}, u32[]{:S(2)}) collective-permute-start(f32[8,4096]{1,0:T(8,128)S(1)} %get-tuple-element.38.o0), channel_id=1, source_target_pairs={{0,6},{2,4},{4,2},{6,0},{1,7},{3,5},{5,3},{7,1},{8,14},{10,12},{12... | collective-permute-start | bytes 393224 | tf_op jit(solution)/shard_map/ppermute | solution.py:71
  26.8 7.9 %collective-permute-start.7 = (f32[8,4096]{1,0:T(8,128)S(1)}, f32[8,4096]{1,0:T(8,128)S(1)}, u32[]{:S(2)}, u32[]{:S(2)}) collective-permute-start(f32[8,4096]{1,0:T(8,128)S(1)} %get-tuple-element.39.o1), channel_id=1, source_target_pairs={{0,2},{2,0},{4,6},{6,4},{1,3},{3,1},{5,7},{7,5},{8,10},{10,8},{12,... | collective-permute-start | bytes 393224 | tf_op jit(solution)/shard_map/ppermute | solution.py:71
  27.9 6.8 %collective-permute-start.8 = (f32[8,4096]{1,0:T(8,128)S(1)}, f32[8,4096]{1,0:T(8,128)S(1)}, u32[]{:S(2)}, u32[]{:S(2)}) collective-permute-start(f32[8,4096]{1,0:T(8,128)S(1)} %get-tuple-element.40.o2), channel_id=1, source_target_pairs={{0,24},{8,16},{16,8},{24,0},{1,25},{9,17},{17,9},{25,1},{2,26},{10... | collective-permute-start | bytes 393224 | tf_op jit(solution)/shard_map/ppermute | solution.py:71
  27.9 6.8 %collective-permute-start.9 = (f32[8,4096]{1,0:T(8,128)S(1)}, f32[8,4096]{1,0:T(8,128)S(1)}, u32[]{:S(2)}, u32[]{:S(2)}) collective-permute-start(f32[8,4096]{1,0:T(8,128)S(1)} %get-tuple-element.41.o3), channel_id=1, source_target_pairs={{0,8},{8,0},{16,24},{24,16},{1,9},{9,1},{17,25},{25,17},{2,10},{10... | collective-permute-start | bytes 393224 | tf_op jit(solution)/shard_map/ppermute | solution.py:71
  32.2 8.2 %collective-permute-start.10 = (f32[32,1152]{1,0:T(8,128)S(1)}, f32[32,1152]{1,0:T(8,128)S(1)}, u32[]{:S(2)}, u32[]{:S(2)}) collective-permute-start(f32[32,1152]{1,0:T(8,128)S(1)} %get-tuple-element.43.mine.refs_0_), channel_id=1, source_target_pairs={{0,1},{1,0},{2,3},{3,2},{4,5},{5,4},{6,7},{7,6},{8,9},{9,8},{10,11... | collective-permute-start | bytes 442376 | tf_op jit(solution)/shard_map/ppermute | solution.py:62
  38.9 5.7 %collective-permute-start.11 = (f32[32,1152]{1,0:T(8,128)S(1)}, f32[32,1152]{1,0:T(8,128)S(1)}, u32[]{:S(2)}, u32[]{:S(2)}) collective-permute-start(f32[32,1152]{1,0:T(8,128)S(1)} %get-tuple-element.45.refs_2_.mine), channel_id=1, source_target_pairs={{0,1},{1,0},{2,3},{3,2},{4,5},{5,4},{6,7},{7,6},{8,9},{9,8},{10,11... | collective-permute-start | bytes 442376 | tf_op jit(solution)/shard_map/ppermute | solution.py:62
  44.6 6.2 %collective-permute-start.12 = (f32[2,8,1024]{2,1,0:T(8,128)S(1)}, f32[2,8,1024]{2,1,0:T(8,128)S(1)}, u32[]{:S(2)}, u32[]{:S(2)}) collective-permute-start(f32[2,8,1024]{2,1,0:T(8,128)S(1)} %get-tuple-element.52.refs_4_), channel_id=1, source_target_pairs={{0,6},{2,4},{4,2},{6,0},{1,7},{3,5},{5,3},{7,1},{8,14},{10,12},{12... | collective-permute-start | bytes 196616 | tf_op jit(solution)/shard_map/ppermute | solution.py:71
  46.1 5.0 %collective-permute-start.13 = (f32[2,8,1024]{2,1,0:T(8,128)S(1)}, f32[2,8,1024]{2,1,0:T(8,128)S(1)}, u32[]{:S(2)}, u32[]{:S(2)}) collective-permute-start(f32[2,8,1024]{2,1,0:T(8,128)S(1)} %get-tuple-element.53.refs_5_), channel_id=1, source_target_pairs={{0,2},{2,0},{4,6},{6,4},{1,3},{3,1},{5,7},{7,5},{8,10},{10,8},{12,... | collective-permute-start | bytes 196616 | tf_op jit(solution)/shard_map/ppermute | solution.py:71
  46.1 5.0 %collective-permute-start.14 = (f32[2,8,1024]{2,1,0:T(8,128)S(1)}, f32[2,8,1024]{2,1,0:T(8,128)S(1)}, u32[]{:S(2)}, u32[]{:S(2)}) collective-permute-start(f32[2,8,1024]{2,1,0:T(8,128)S(1)} %get-tuple-element.54.refs_6_), channel_id=1, source_target_pairs={{0,24},{8,16},{16,8},{24,0},{1,25},{9,17},{17,9},{25,1},{2,26},{10... | collective-permute-start | bytes 196616 | tf_op jit(solution)/shard_map/ppermute | solution.py:71
  46.1 5.0 %collective-permute-start.15 = (f32[2,8,1024]{2,1,0:T(8,128)S(1)}, f32[2,8,1024]{2,1,0:T(8,128)S(1)}, u32[]{:S(2)}, u32[]{:S(2)}) collective-permute-start(f32[2,8,1024]{2,1,0:T(8,128)S(1)} %get-tuple-element.55.refs_7_), channel_id=1, source_target_pairs={{0,8},{8,0},{16,24},{24,16},{1,9},{9,1},{17,25},{25,17},{2,10},{10... | collective-permute-start | bytes 196616 | tf_op jit(solution)/shard_map/ppermute | solution.py:71

commit v4 on v3

--- a/solution.py
+++ b/solution.py
@@ -218,137 +218,136 @@
     )(vmem(held), *own, *near)
 
 
-def add_kernel(same, *refs):
-    *refs, held = refs
-    pairs, outs = refs[:-edges], refs[-edges:]
-    mats, rank, features = outs[0].shape
-    for mat in range(mats):
-        mine, other = pairs[2 * mat], pairs[2 * mat + 1]
-        for slot, out in enumerate(outs):
-            here = slice(slot * rank, (slot + 1) * rank)
-            out[mat] = mine[here, :features] + other[here, :features]
-
-
-def add(held, pairs, rank):
-    mats = len(pairs)
-    pairs = [terms for pair in pairs for terms in pair]
-    sums = jax.ShapeDtypeStruct((mats, rank, held.shape[-1]), f32)
+def add_kernel(same, mine, other, *refs):
+    *outs, held = refs
+    rank, features = outs[0].shape
+    for slot, out in enumerate(outs):
+        here = slice(slot * rank, (slot + 1) * rank)
+        out[...] = mine[here, :features] + other[here, :features]
+
+
+def add(held, pair, rank, mat):
+    sums = jax.ShapeDtypeStruct((rank, held.shape[-1]), f32)
     return pl.pallas_call(
         add_kernel,
-        name="add",
+        name=f"add{mat}",
         out_shape=[sums] * edges + [jax.ShapeDtypeStruct(held.shape, f32)],
-        in_specs=[in_vmem] * (1 + len(pairs)),
+        in_specs=[in_vmem] * 3,
         out_specs=[in_vmem] * (edges + 1),
         input_output_aliases={0: edges},
         compiler_params=pltpu.CompilerParams(vmem_limit_bytes=grant),
-    )(vmem(held), *pairs)
-
-
-def inverse_kernel(rank, same, mine, other, inverse, held):
+    )(vmem(held), *pair)
+
+
+def inverse_kernel(rank, same, *refs):
+    *refs, held = refs
+    mats = len(refs) // 3
     width = edges * rank
-    shape = (edges, rank, 128)
+    shape = (mats * edges, rank, 128)
     row = lax.broadcasted_iota(jnp.int32, shape, 1)
     lane = lax.broadcasted_iota(jnp.int32, shape, 2)
-    slot = lax.broadcasted_iota(jnp.int32, shape, 0)
-    value = (mine[:, -128:] + other[:, -128:]).reshape(shape)
+    slot = lax.rem(lax.broadcasted_iota(jnp.int32, shape, 0), edges)
+    grams = [refs[2 * mat][:, -128:] + refs[2 * mat + 1][:, -128:] for mat in range(mats)]
+    value = jnp.concatenate(grams, 0).reshape(shape)
     value = jnp.where(lane < rank, value, (lane == width + slot * rank + row).astype(f32))
-    pivots = jnp.ones((edges, rank, 1), f32)
+    pivots = jnp.ones((shape[0], rank, 1), f32)
     for j in range(rank):
         pivot = value[:, j : j + 1, j : j + 1]
         pivots = jnp.where(row[:, :, :1] == j, pivot, pivots)
         factor = jnp.where(row > j, value[:, :, j : j + 1] / pivot, 0.0)
         value = value - factor * value[:, j : j + 1, :]
-    inverse[...] = (value / jnp.sqrt(pivots)).reshape(width, 128)
-
-
-def inverse_factor(held, pair, rank, mat):
+    value = (value / jnp.sqrt(pivots)).reshape(mats * width, 128)
+    for mat, inverse in enumerate(refs[2 * mats :]):
+        inverse[...] = value[mat * width : (mat + 1) * width]
+
+
+def inverse_factors(held, pairs, rank):
+    mats = len(pairs)
+    pairs = [terms for pair in pairs for terms in pair]
     return pl.pallas_call(
         functools.partial(inverse_kernel, rank),
-        name=f"inverse{mat}",
-        out_shape=[
-            jax.ShapeDtypeStruct((edges * rank, 128), f32),
-            jax.ShapeDtypeStruct(held.shape, f32),
-        ],
-        in_specs=[in_vmem] * 3,
-        out_specs=[in_vmem] * 2,
-        input_output_aliases={0: 1},
-        compiler_params=pltpu.CompilerParams(vmem_limit_bytes=grant),
-    )(vmem(held), *pair)
-
-
-def mix_kernel(chunk, same, *refs):
-    *refs, mixed, next_rx, next_ry, held, new_rx, new_ry, sems, new_sems = refs
-    mats, rows, _ = held.shape
-    differs, inverses = refs[:mats], refs[mats : 2 * mats]
-    sums, near = refs[2 * mats : 2 * mats + edges], refs[2 * mats + edges :]
-    rank = sums[0].shape[1]
+        name="inverse",
+        out_shape=[jax.ShapeDtypeStruct((edges * rank, 128), f32)] * mats
+        + [jax.ShapeDtypeStruct(held.shape, f32)],
+        in_specs=[in_vmem] * (1 + 2 * mats),
+        out_specs=[in_vmem] * (1 + mats),
+        input_output_aliases={0: mats},
+        compiler_params=pltpu.CompilerParams(vmem_limit_bytes=grant),
+    )(vmem(held), *pairs)
+
+
+def mix_kernel(mat, chunk, same, differ, inverse, *refs):
+    sums, near = refs[:edges], refs[edges : 2 * edges]
+    mixed, next_rx, next_ry, held, new_rx, new_ry, sems, new_sems = refs[-8:]
+    rank = sums[0].shape[0]
     width = edges * rank
-    steps = rows // chunk
-
-    def copy(mat, step):
+    steps = held.shape[1] // chunk
+
+    def copy(step):
         here = pl.ds(pl.multiple_of(step * chunk, chunk), chunk)
         return pltpu.make_async_copy(
-            held.at[mat, here], mixed.at[0, 0, mat, here], sems.at[mat, step]
+            held.at[mat, here], mixed.at[0, 0, mat, here], sems.at[step]
         )
 
-    for mat in range(mats):
-        factor = inverses[mat][:, width : 2 * width]
-        total = jnp.concatenate([b[mat] + n[mat] for b, n in zip(sums, near)], 0)
-        updated = lax.dot_general(
-            factor, total, NN, precision=lax.Precision.HIGHEST, preferred_element_type=f32
-        )
-        parts = [updated[slot * rank : (slot + 1) * rank] for slot in range(edges)]
-        new_rx[mat] = jnp.where(odd("rx"), parts[2], parts[3])
-        new_ry[mat] = jnp.where(odd("ry"), parts[0], parts[1])
-        right = mixing * lax.dot_general(
-            factor, updated, TN, precision=lax.Precision.HIGHEST, preferred_element_type=f32
-        )
-        r_high, r_low = split(right)
-        terms = jnp.concatenate([r_high, r_high, r_low, r_low], 0)
-
-        @pl.loop(0, steps)
-        def _(step):
-            here = pl.ds(pl.multiple_of(step * chunk, chunk), chunk)
-            high, low = split(differs[mat][:, here])
-            lhs = jnp.concatenate([high, low, high, low], 0)
-            held[mat, here, :] -= dot(lhs, terms, TN)
-            copy(mat, step).start()
-
+    factor = inverse[:, width : 2 * width]
+    total = jnp.concatenate([b[...] + n[...] for b, n in zip(sums, near)], 0)
+    updated = lax.dot_general(
+        factor, total, NN, precision=lax.Precision.HIGHEST, preferred_element_type=f32
+    )
+    right = mixing * lax.dot_general(
+        factor, updated, TN, precision=lax.Precision.HIGHEST, preferred_element_type=f32
+    )
+    r_high, r_low = split(right)
+    terms = jnp.concatenate([r_high, r_high, r_low, r_low], 0)
+
+    @pl.loop(0, steps)
+    def _(step):
+        here = pl.ds(pl.multiple_of(step * chunk, chunk), chunk)
+        high, low = split(differ[:, here])
+        lhs = jnp.concatenate([high, low, high, low], 0)
+        held[mat, here, :] -= dot(lhs, terms, TN)
+        copy(step).start()
+
+    parts = [updated[slot * rank : (slot + 1) * rank] for slot in range(edges)]
+    new_rx[...] = jnp.where(odd("rx"), parts[2], parts[3])
+    new_ry[...] = jnp.where(odd("ry"), parts[0], parts[1])
     new_copies = [
-        pltpu.make_async_copy(new_rx, next_rx.at[0, 0], new_sems.at[0]),
-        pltpu.make_async_copy(new_ry, next_ry.at[0, 0], new_sems.at[1]),
+        pltpu.make_async_copy(new_rx, next_rx.at[0, 0, mat], new_sems.at[0]),
+        pltpu.make_async_copy(new_ry, next_ry.at[0, 0, mat], new_sems.at[1]),
     ]
     for new_copy in new_copies:
         new_copy.start()
-    for mat in range(mats):
-
-        @pl.loop(0, steps)
-        def _(step):
-            copy(mat, step).wait()
+
+    @pl.loop(0, steps)
+    def _(step):
+        copy(step).wait()
 
     for new_copy in new_copies:
         new_copy.wait()
 
 
-def mix(held, differs, inverses, sums, near, shapes):
-    mats, rows, features = held.shape
-    rank = sums[0].shape[1]
+def mix(held, differ, inverse, sums, near, mat, shapes, previous):
+    _, rows, features = held.shape
+    rank = sums[0].shape[0]
     chunk = chunk_of(rows, 512)
-    args = [vmem(held), *differs, *inverses, *sums, *near]
-    return pl.pallas_call(
-        functools.partial(mix_kernel, chunk),
-        name="mix",
+    args = [vmem(held), differ, inverse, *sums, *near]
+    specs = [in_vmem] * len(args) + [in_hbm] * len(previous)
+    aliases = {0: 3} | {len(args) + place: place for place in range(len(previous))}
+    args += [hbm(array) for array in previous]
+    return pl.pallas_call(
+        functools.partial(mix_kernel, mat, chunk),
+        name=f"mix{mat}",
         out_shape=[jax.ShapeDtypeStruct(shape, f32) for shape in (*shapes, held.shape)],
-        in_specs=[in_vmem] * len(args),
+        in_specs=specs,
         out_specs=[in_hbm] * 3 + [in_vmem],
         scratch_shapes=[
-            pltpu.VMEM((mats, rank, features), f32),
-            pltpu.VMEM((mats, rank, features), f32),
-            pltpu.SemaphoreType.DMA((mats, rows // chunk)),
+            pltpu.VMEM((rank, features), f32),
+            pltpu.VMEM((rank, features), f32),
+            pltpu.SemaphoreType.DMA((rows // chunk,)),
             pltpu.SemaphoreType.DMA((2,)),
         ],
-        input_output_aliases={0: 3},
-        cost_estimate=cost(held, 4),
+        input_output_aliases=aliases,
+        cost_estimate=cost(held, 2),
         compiler_params=pltpu.CompilerParams(vmem_limit_bytes=grant),
     )(*args)
 
@@ -361,11 +360,12 @@
     factors = [factors_ry, lower_ry, factors_rx, lower_rx]
     size = chunk_of(rows, 512)
     pieces = rows // size
-    until = max(3 * pieces // 8, 1)
+    ahead = max(pieces // 2, 1)
+    until = ahead
     held = load(weights, size, until)
     own = []
     for mat in range(mats):
-        first, until = until, min((mat + 1) * pieces + pieces // 4, mats * pieces)
+        first, until = until, min((mat + 1) * pieces + ahead, mats * pieces)
         *own_mat, held = project(held, factors, weights, mat, size, first, until)
         own.append(own_mat)
     near = [exchange(own_mat) for own_mat in own]
@@ -380,14 +380,18 @@
         other = from_partner(terms, "tp", distance) if tp > 1 else jnp.zeros_like(terms)
         differs.append(p)
         pairs.append((terms, other))
-    inverses = [None] * mats
-    for mat in range(mats - 1):
-        inverses[mat], held = inverse_factor(held, pairs[mat], rank, mat)
-    *sums, held = add(held, pairs, rank)
-    near_sums = exchange(sums)
-    inverses[-1], held = inverse_factor(held, pairs[-1], rank, mats - 1)
+    sums, near_sums = [], []
+    for mat in range(mats):
+        *sum_mat, held = add(held, pairs[mat], rank, mat)
+        sums.append(sum_mat)
+        near_sums.append(exchange(sum_mat))
+    *inverses, held = inverse_factors(held, pairs, rank)
+    results = []
     shapes = (weights.shape, factors_rx.shape, factors_ry.shape)
-    *results, held = mix(held, differs, inverses, sums, near_sums, shapes)
+    for mat in range(mats):
+        *results, held = mix(
+            held, differs[mat], inverses[mat], sums[mat], near_sums[mat], mat, shapes, results
+        )
     return tuple(results)
 
 

time: 63.3 us -> 61.9 us (0.978)
  waiting for transfers between devices: 8.78 us -> 3.05 us
  starting transfers between devices: 16.7 us -> 19.9 us
  Pallas kernels: 37 us -> 38 us
    ppermute x12 -> x16, starting transfers between devices: 10.2 us -> 13.4 us  [exchange(): swapped.append(lax.ppermute(value, axis, pairs))]
    ppermute x12 -> x16, waiting for transfers between devices: 3.7 us -> 0.73 us  [exchange(): swapped.append(lax.ppermute(value, axis, pairs))]
    ppermute x2, waiting for transfers between devices: 3.49 us -> 1.35 us  [from_partner(): return lax.ppermute(value, axis, [(i, i ^ distance) for i in range(count)])]
    pallas_call x4 -> x5, Pallas kernels: 13.4 us -> 14.5 us  [the longest x2 13.8 us: mix(): pl.pallas_call(functools.partial(mix_kernel, mat, chunk), name=f'mix{mat}...]
    pallas_call x2, Pallas kernels: 12.3 us -> 11.6 us  [project(): pl.pallas_call(functools.partial(project_kernel, mat, chunk_of(rows, 1024...]
  transfers between devices with their start and end apart: 16 -> 20, of which waited for: 5 -> 3; matrix products, arithmetic and copies ran while one was open for 0% -> 0% of each run, Pallas kernels for 30% -> 41%
where the time goes in v4:
time: 61.9 us; the launch traced here: 61.8 us
  Pallas kernels  38 us (61%)
  starting transfers between devices  19.9 us (32%)
  waiting for transfers between devices  3.05 us (5%)
  between operations  0.78 us (1%)
    pallas_call x2, Pallas kernels, mix(): pl.pallas_call(functools.partial(mix_kernel, mat, chunk), name=f'mix{mat}...  13.8 us
    ppermute x16, starting transfers between devices, exchange(): swapped.append(lax.ppermute(value, axis, pairs))  13.4 us
    pallas_call x2, Pallas kernels, project(): pl.pallas_call(functools.partial(project_kernel, mat, chunk_of(rows, 1024...  11.6 us
    pallas_call x2, Pallas kernels, back(): pl.pallas_call(functools.partial(back_kernel, mat, chunk_of(rows, 1024)),...  8.37 us
    pallas_call x1, Pallas kernels, load(): pl.pallas_call(functools.partial(load_kernel, size, until), name='load',...  3.5 us
    ppermute x2, starting transfers between devices, from_partner(): return lax.ppermute(value, axis, [(i, i ^ distance) for i in range(count)])  3.35 us
    ppermute x2, starting transfers between devices, shifted(): return lax.ppermute(value, axis, pairs)  3.14 us
    ppermute x2, waiting for transfers between devices, from_partner(): return lax.ppermute(value, axis, [(i, i ^ distance) for i in range(count)])  1.35 us
  transfers between devices with their start and end apart: 20, of which 3 were waited for; matrix products, arithmetic and copies ran while one was open for 0% of the time, Pallas kernels for 41%

profile of v4, /device:TPU:0, one launch (start us, length us, event | category | flops | bytes accessed | tf_op | source)
XLA Modules:
  0.0 61.8 jit_solution(8161237298830125664)
XLA Ops:
  0.7 0.5 collective-permute-start.1
  1.2 2.6 %collective-permute-start = (f32[1,1,2,8,1024]{4,3,2,1,0:T(8,128)}, f32[1,1,2,8,1024]{4,3,2,1,0:T(8,128)S(1)}, u32[]{:S(2)}, u32[]{:S(2)}) collective-permute-start(f32[1,1,2,8,1024]{4,3,2,1,0:T(8,128)} %f0.3), channel_id=1, source_target_pairs={{0,2},{2,4},{4,6},{6,0},{1,3},{3,5},{5,7},{7,1},{8,10},{10,12},{12... | collective-permute-start | bytes 196616 | tf_op jit(solution)/shard_map/ppermute | solution.py:57
  3.8 3.5 %load.1.same = f32[2,4096,1024]{2,1,0:T(8,128)S(1)} custom-call(f32[1,1,2,4096,1024]{4,3,2,1,0:T(8,128)} %weights.5), custom_call_target="tpu_custom_call" | custom-call | tf_op jit(solution)/shard_map/load/pallas_call | solution.py:102
  7.3 0.0 collective-permute-done.1.f3
  7.3 1.0 %collective-permute-done.f1 = f32[1,1,2,8,1024]{4,3,2,1,0:T(8,128)S(1)} collective-permute-done((f32[1,1,2,8,1024]{4,3,2,1,0:T(8,128)}, f32[1,1,2,8,1024]{4,3,2,1,0:T(8,128)S(1)}, u32[]{:S(2)}, u32[]{:S(2)}) %collective-permute-start) | collective-permute-done | bytes 65568 | tf_op jit(solution)/shard_map/ppermute | solution.py:57
  8.3 5.9 %project0.1 = (f32[8,4096]{1,0:T(8,128)S(1)}, f32[8,4096]{1,0:T(8,128)S(1)}, f32[8,4096]{1,0:T(8,128)S(1)}, f32[8,4096]{1,0:T(8,128)S(1)}, f32[2,4096,1024]{2,1,0:T(8,128)S(1)}) custom-call(f32[2,4096,1024]{2,1,0:T(8,128)S(1)} %load.1.same, f32[1,1,2,8,1024]{4,3,2,1,0:T(8,128)S(1)} %copy-done, ...), custom_call_target="tpu_custom_call", output_to_operand_aliasing={{4}: (0, {})} | custom-call | flops 4294967296 | bytes 33554432 | tf_op jit(solution)/shard_map/project0/pallas_call | solution.py:157
  14.2 2.3 %collective-permute-start.2 = (f32[8,4096]{1,0:T(8,128)S(1)}, f32[8,4096]{1,0:T(8,128)S(1)}, u32[]{:S(2)}, u32[]{:S(2)}) collective-permute-start(f32[8,4096]{1,0:T(8,128)S(1)} %get-tuple-element.41.o0), channel_id=1, source_target_pairs={{0,6},{2,4},{4,2},{6,0},{1,7},{3,5},{5,3},{7,1},{8,14},{10,12},{12... | collective-permute-start | bytes 393224 | tf_op jit(solution)/shard_map/ppermute | solution.py:71
  16.5 0.0 collective-permute-start.3
  16.5 0.8 %collective-permute-start.4 = (f32[8,4096]{1,0:T(8,128)S(1)}, f32[8,4096]{1,0:T(8,128)S(1)}, u32[]{:S(2)}, u32[]{:S(2)}) collective-permute-start(f32[8,4096]{1,0:T(8,128)S(1)} %get-tuple-element.43.o2), channel_id=1, source_target_pairs={{0,24},{8,16},{16,8},{24,0},{1,25},{9,17},{17,9},{25,1},{2,26},{10... | collective-permute-start | bytes 393224 | tf_op jit(solution)/shard_map/ppermute | solution.py:71
  17.3 0.9 %collective-permute-start.5 = (f32[8,4096]{1,0:T(8,128)S(1)}, f32[8,4096]{1,0:T(8,128)S(1)}, u32[]{:S(2)}, u32[]{:S(2)}) collective-permute-start(f32[8,4096]{1,0:T(8,128)S(1)} %get-tuple-element.44.o3), channel_id=1, source_target_pairs={{0,8},{8,0},{16,24},{24,16},{1,9},{9,1},{17,25},{25,17},{2,10},{10... | collective-permute-start | bytes 393224 | tf_op jit(solution)/shard_map/ppermute | solution.py:71
  18.2 5.7 %project1.1 = (f32[8,4096]{1,0:T(8,128)S(1)}, f32[8,4096]{1,0:T(8,128)S(1)}, f32[8,4096]{1,0:T(8,128)S(1)}, f32[8,4096]{1,0:T(8,128)S(1)}, f32[2,4096,1024]{2,1,0:T(8,128)S(1)}) custom-call(f32[2,4096,1024]{2,1,0:T(8,128)S(1)} %get-tuple-element.39.same, f32[1,1,2,8,1024]{4,3,2,1,0:T(8,128)S(1)} %copy-done, ...), custom_call_target="tpu_custom_call", output_to_operand_aliasing={{4}: (0, {})} | custom-call | flops 4294967296 | bytes 33554432 | tf_op jit(solution)/shard_map/project1/pallas_call | solution.py:157
  23.9 2.1 %collective-permute-start.6 = (f32[8,4096]{1,0:T(8,128)S(1)}, f32[8,4096]{1,0:T(8,128)S(1)}, u32[]{:S(2)}, u32[]{:S(2)}) collective-permute-start(f32[8,4096]{1,0:T(8,128)S(1)} %get-tuple-element.46.o0), channel_id=1, source_target_pairs={{0,6},{2,4},{4,2},{6,0},{1,7},{3,5},{5,3},{7,1},{8,14},{10,12},{12... | collective-permute-start | bytes 393224 | tf_op jit(solution)/shard_map/ppermute | solution.py:71
  26.1 0.0 collective-permute-done.2.n0
  26.1 1.1 %collective-permute-start.7 = (f32[8,4096]{1,0:T(8,128)S(1)}, f32[8,4096]{1,0:T(8,128)S(1)}, u32[]{:S(2)}, u32[]{:S(2)}) collective-permute-start(f32[8,4096]{1,0:T(8,128)S(1)} %get-tuple-element.47.o1), channel_id=1, source_target_pairs={{0,2},{2,0},{4,6},{6,4},{1,3},{3,1},{5,7},{7,5},{8,10},{10,8},{12,... | collective-permute-start | bytes 393224 | tf_op jit(solution)/shard_map/ppermute | solution.py:71
  27.2 0.0 collective-permute-done.3.n1
  27.2 0.0 collective-permute-start.8
  27.2 0.0 collective-permute-done.4.n2
  27.2 0.1 collective-permute-start.9
  27.3 0.0 collective-permute-done.5.n3
  27.3 4.2 %back0.1 = (f32[32,4096]{1,0:T(8,128)S(1)}, f32[32,1152]{1,0:T(8,128)S(1)}, f32[2,4096,1024]{2,1,0:T(8,128)S(1)}) custom-call(f32[2,4096,1024]{2,1,0:T(8,128)S(1)} %get-tuple-element.40.same, f32[8,4096]{1,0:T(8,128)S(1)} %get-tuple-element.41.o0, f32[8,4096]{1,0:T(8,128)S(1)} %get-tuple-element.42.o1, ...), custom_call_target="tpu_custom_call", output_to_operand_aliasing={{2}: (0, {})} | custom-call | flops 4294967296 | bytes 33554432 | tf_op jit(solution)/shard_map/back0/pallas_call | solution.py:205
  31.5 1.8 %collective-permute-start.10 = (f32[32,1152]{1,0:T(8,128)S(1)}, f32[32,1152]{1,0:T(8,128)S(1)}, u32[]{:S(2)}, u32[]{:S(2)}) collective-permute-start(f32[32,1152]{1,0:T(8,128)S(1)} %get-tuple-element.51.mine.refs_0_), channel_id=1, source_target_pairs={{0,1},{1,0},{2,3},{3,2},{4,5},{5,4},{6,7},{7,6},{8,9},{9,8},{10,11... | collective-permute-start | bytes 442376 | tf_op jit(solution)/shard_map/ppermute | solution.py:62
  33.3 0.0 collective-permute-done.6.n0
  33.3 0.7 %collective-permute-done.7.n1 = f32[8,4096]{1,0:T(8,128)S(1)} collective-permute-done((f32[8,4096]{1,0:T(8,128)S(1)}, f32[8,4096]{1,0:T(8,128)S(1)}, u32[]{:S(2)}, u32[]{:S(2)}) %collective-permute-start.7) | collective-permute-done | bytes 131104 | tf_op jit(solution)/shard_map/ppermute | solution.py:71
  34.0 0.0 collective-permute-done.8.n2
  34.0 0.0 collective-permute-done.9.n3
  34.0 4.2 %back1.1 = (f32[32,4096]{1,0:T(8,128)S(1)}, f32[32,1152]{1,0:T(8,128)S(1)}, f32[2,4096,1024]{2,1,0:T(8,128)S(1)}) custom-call(f32[2,4096,1024]{2,1,0:T(8,128)S(1)} %get-tuple-element.45.same, f32[8,4096]{1,0:T(8,128)S(1)} %get-tuple-element.46.o0, f32[8,4096]{1,0:T(8,128)S(1)} %get-tuple-element.47.o1, ...), custom_call_target="tpu_custom_call", output_to_operand_aliasing={{2}: (0, {})} | custom-call | flops 4294967296 | bytes 33554432 | tf_op jit(solution)/shard_map/back1/pallas_call | solution.py:205
  38.2 1.5 %collective-permute-start.11 = (f32[32,1152]{1,0:T(8,128)S(1)}, f32[32,1152]{1,0:T(8,128)S(1)}, u32[]{:S(2)}, u32[]{:S(2)}) collective-permute-start(f32[32,1152]{1,0:T(8,128)S(1)} %get-tuple-element.53.mine.refs_2_), channel_id=1, source_target_pairs={{0,1},{1,0},{2,3},{3,2},{4,5},{5,4},{6,7},{7,6},{8,9},{9,8},{10,11... | collective-permute-start | bytes 442376 | tf_op jit(solution)/shard_map/ppermute | solution.py:62
  39.7 0.0 collective-permute-done.10.other.refs_1_
  39.7 1.8 %collective-permute-start.12 = (f32[8,1024]{1,0:T(8,128)S(1)}, f32[8,1024]{1,0:T(8,128)S(1)}, u32[]{:S(2)}, u32[]{:S(2)}) collective-permute-start(f32[8,1024]{1,0:T(8,128)S(1)} %get-tuple-element.58.refs_0_), channel_id=1, source_target_pairs={{0,6},{2,4},{4,2},{6,0},{1,7},{3,5},{5,3},{7,1},{8,14},{10,12},{12... | collective-permute-start | bytes 98312 | tf_op jit(solution)/shard_map/ppermute | solution.py:71
  41.5 0.0 collective-permute-start.13
  41.5 0.0 collective-permute-start.14
  41.6 1.0 %collective-permute-start.15 = (f32[8,1024]{1,0:T(8,128)S(1)}, f32[8,1024]{1,0:T(8,128)S(1)}, u32[]{:S(2)}, u32[]{:S(2)}) collective-permute-start(f32[8,1024]{1,0:T(8,128)S(1)} %get-tuple-element.61.refs_3_), channel_id=1, source_target_pairs={{0,8},{8,0},{16,24},{24,16},{1,9},{9,1},{17,25},{25,17},{2,10},{10... | collective-permute-start | bytes 98312 | tf_op jit(solution)/shard_map/ppermute | solution.py:71
  42.5 1.3 %collective-permute-done.11.other.refs_3_ = f32[32,1152]{1,0:T(8,128)S(1)} collective-permute-done((f32[32,1152]{1,0:T(8,128)S(1)}, f32[32,1152]{1,0:T(8,128)S(1)}, u32[]{:S(2)}, u32[]{:S(2)}) %collective-permute-start.11) | collective-permute-done | bytes 147488 | tf_op jit(solution)/shard_map/ppermute | solution.py:62
  43.9 1.5 %collective-permute-start.16 = (f32[8,1024]{1,0:T(8,128)S(1)}, f32[8,1024]{1,0:T(8,128)S(1)}, u32[]{:S(2)}, u32[]{:S(2)}) collective-permute-start(f32[8,1024]{1,0:T(8,128)S(1)} %get-tuple-element.65.refs_0_), channel_id=1, source_target_pairs={{0,6},{2,4},{4,2},{6,0},{1,7},{3,5},{5,3},{7,1},{8,14},{10,12},{12... | collective-permute-start | bytes 98312 | tf_op jit(solution)/shard_map/ppermute | solution.py:71
  45.4 0.7 %inverse.1 = (f32[32,128]{1,0:T(8,128)S(1)}, f32[32,128]{1,0:T(8,128)S(1)}, f32[2,4096,1024]{2,1,0:T(8,128)S(1)}) custom-call(f32[2,4096,1024]{2,1,0:T(8,128)S(1)} %get-tuple-element.54.same, f32[32,1152]{1,0:T(8,128)S(1)} %get-tuple-element.51.mine.refs_0_, f32[32,1152]{1,0:T(8,128)S(1)} %collective-permute-done.10.other.refs_1_, ...), custom_call_target="tpu_custom_call", output_to_operand_aliasing={{2}: (0, {})} | custom-call | tf_op jit(solution)/shard_map/inverse/pallas_call | solution.py:267
  46.1 0.0 collective-permute-done.12.refs_4_
  46.1 0.1 collective-permute-start.17
  46.2 0.0 collective-permute-done.13.refs_5_
  46.2 0.6 %collective-permute-start.18 = (f32[8,1024]{1,0:T(8,128)S(1)}, f32[8,1024]{1,0:T(8,128)S(1)}, u32[]{:S(2)}, u32[]{:S(2)}) collective-permute-start(f32[8,1024]{1,0:T(8,128)S(1)} %get-tuple-element.67.refs_2_), channel_id=1, source_target_pairs={{0,24},{8,16},{16,8},{24,0},{1,25},{9,17},{17,9},{25,1},{2,26},{10... | collective-permute-start | bytes 98312 | tf_op jit(solution)/shard_map/ppermute | solution.py:71
  46.8 0.0 collective-permute-done.14.refs_6_
  46.8 1.1 %collective-permute-start.19 = (f32[8,1024]{1,0:T(8,128)S(1)}, f32[8,1024]{1,0:T(8,128)S(1)}, u32[]{:S(2)}, u32[]{:S(2)}) collective-permute-start(f32[8,1024]{1,0:T(8,128)S(1)} %get-tuple-element.68.refs_3_), channel_id=1, source_target_pairs={{0,8},{8,0},{16,24},{24,16},{1,9},{9,1},{17,25},{25,17},{2,10},{10... | collective-permute-start | bytes 98312 | tf_op jit(solution)/shard_map/ppermute | solution.py:71
  47.9 0.0 collective-permute-done.15.refs_7_
  47.9 6.9 %mix0.1 = (f32[1,1,2,4096,1024]{4,3,2,1,0:T(8,128)}, f32[1,1,2,8,1024]{4,3,2,1,0:T(8,128)}, f32[1,1,2,8,1024]{4,3,2,1,0:T(8,128)}, f32[2,4096,1024]{2,1,0:T(8,128)S(1)}) custom-call(f32[2,4096,1024]{2,1,0:T(8,128)S(1)} %get-tuple-element.55.same, f32[32,4096]{1,0:T(8,128)S(1)} %get-tuple-element.56.differ, ...), custom_call_target="tpu_custom_call", output_to_operand_aliasing={{3}: (0, {})} | custom-call | flops 4294967296 | bytes 33554432 | tf_op jit(solution)/shard_map/mix0/pallas_call | solution.py:337
  54.8 0.0 collective-permute-done.16.refs_4_
  54.8 0.0 collective-permute-done.17.refs_5_
  54.8 0.0 collective-permute-done.18.refs_6_
  54.8 0.0 collective-permute-done.19.refs_7_
  54.8 6.9 %mix1.1 = (f32[1,1,2,4096,1024]{4,3,2,1,0:T(8,128)}, f32[1,1,2,8,1024]{4,3,2,1,0:T(8,128)}, f32[1,1,2,8,1024]{4,3,2,1,0:T(8,128)}, f32[2,4096,1024]{2,1,0:T(8,128)S(1)}) custom-call(f32[2,4096,1024]{2,1,0:T(8,128)S(1)} %get-tuple-element.62.same, ...), custom_call_target="tpu_custom_call", output_to_operand_aliasing={{3}: (0, {}), {0}: (11, {}), {1}: (12, {}), {2}: (13, {})} | custom-call | flops 4294967296 | bytes 33554432 | tf_op jit(solution)/shard_map/mix1/pallas_call | solution.py:337
  (6 shorter events, 0.0 us)
Async XLA Ops:
  0.6 7.6 %copy-start.1 = (f32[1,1,2,8,1024]{4,3,2,1,0:T(8,128)S(1)}, f32[1,1,2,8,1024]{4,3,2,1,0:T(8,128)}, u32[]{:S(2)}) copy-start(f32[1,1,2,8,1024]{4,3,2,1,0:T(8,128)} %f2.3) | copy-start | bytes 196612
  0.6 7.6 %copy-start = (f32[1,1,2,8,1024]{4,3,2,1,0:T(8,128)S(1)}, f32[1,1,2,8,1024]{4,3,2,1,0:T(8,128)}, u32[]{:S(2)}) copy-start(f32[1,1,2,8,1024]{4,3,2,1,0:T(8,128)} %f0.3) | copy-start | bytes 196612
  0.7 6.7 %collective-permute-start.1 = (f32[1,1,2,8,1024]{4,3,2,1,0:T(8,128)}, f32[1,1,2,8,1024]{4,3,2,1,0:T(8,128)S(1)}, u32[]{:S(2)}, u32[]{:S(2)}) collective-permute-start(f32[1,1,2,8,1024]{4,3,2,1,0:T(8,128)} %f2.3), channel_id=1, source_target_pairs={{0,8},{8,16},{16,24},{24,0},{1,9},{9,17},{17,25},{25,1},{2,10},{10... | collective-permute-start | bytes 196616 | tf_op jit(solution)/shard_map/ppermute | solution.py:57
  1.2 7.1 %collective-permute-start = (f32[1,1,2,8,1024]{4,3,2,1,0:T(8,128)}, f32[1,1,2,8,1024]{4,3,2,1,0:T(8,128)S(1)}, u32[]{:S(2)}, u32[]{:S(2)}) collective-permute-start(f32[1,1,2,8,1024]{4,3,2,1,0:T(8,128)} %f0.3), channel_id=1, source_target_pairs={{0,2},{2,4},{4,6},{6,0},{1,3},{3,5},{5,7},{7,1},{8,10},{10,12},{12... | collective-permute-start | bytes 196616 | tf_op jit(solution)/shard_map/ppermute | solution.py:57
  14.2 11.8 %collective-permute-start.2 = (f32[8,4096]{1,0:T(8,128)S(1)}, f32[8,4096]{1,0:T(8,128)S(1)}, u32[]{:S(2)}, u32[]{:S(2)}) collective-permute-start(f32[8,4096]{1,0:T(8,128)S(1)} %get-tuple-element.41.o0), channel_id=1, source_target_pairs={{0,6},{2,4},{4,2},{6,0},{1,7},{3,5},{5,3},{7,1},{8,14},{10,12},{12... | collective-permute-start | bytes 393224 | tf_op jit(solution)/shard_map/ppermute | solution.py:71
  16.5 10.7 %collective-permute-start.3 = (f32[8,4096]{1,0:T(8,128)S(1)}, f32[8,4096]{1,0:T(8,128)S(1)}, u32[]{:S(2)}, u32[]{:S(2)}) collective-permute-start(f32[8,4096]{1,0:T(8,128)S(1)} %get-tuple-element.42.o1), channel_id=1, source_target_pairs={{0,2},{2,0},{4,6},{6,4},{1,3},{3,1},{5,7},{7,5},{8,10},{10,8},{12,... | collective-permute-start | bytes 393224 | tf_op jit(solution)/shard_map/ppermute | solution.py:71
  16.5 10.7 %collective-permute-start.4 = (f32[8,4096]{1,0:T(8,128)S(1)}, f32[8,4096]{1,0:T(8,128)S(1)}, u32[]{:S(2)}, u32[]{:S(2)}) collective-permute-start(f32[8,4096]{1,0:T(8,128)S(1)} %get-tuple-element.43.o2), channel_id=1, source_target_pairs={{0,24},{8,16},{16,8},{24,0},{1,25},{9,17},{17,9},{25,1},{2,26},{10... | collective-permute-start | bytes 393224 | tf_op jit(solution)/shard_map/ppermute | solution.py:71
  17.3 9.9 %collective-permute-start.5 = (f32[8,4096]{1,0:T(8,128)S(1)}, f32[8,4096]{1,0:T(8,128)S(1)}, u32[]{:S(2)}, u32[]{:S(2)}) collective-permute-start(f32[8,4096]{1,0:T(8,128)S(1)} %get-tuple-element.44.o3), channel_id=1, source_target_pairs={{0,8},{8,0},{16,24},{24,16},{1,9},{9,1},{17,25},{25,17},{2,10},{10... | collective-permute-start | bytes 393224 | tf_op jit(solution)/shard_map/ppermute | solution.py:71
  23.9 9.4 %collective-permute-start.6 = (f32[8,4096]{1,0:T(8,128)S(1)}, f32[8,4096]{1,0:T(8,128)S(1)}, u32[]{:S(2)}, u32[]{:S(2)}) collective-permute-start(f32[8,4096]{1,0:T(8,128)S(1)} %get-tuple-element.46.o0), channel_id=1, source_target_pairs={{0,6},{2,4},{4,2},{6,0},{1,7},{3,5},{5,3},{7,1},{8,14},{10,12},{12... | collective-permute-start | bytes 393224 | tf_op jit(solution)/shard_map/ppermute | solution.py:71
  26.1 7.9 %collective-permute-start.7 = (f32[8,4096]{1,0:T(8,128)S(1)}, f32[8,4096]{1,0:T(8,128)S(1)}, u32[]{:S(2)}, u32[]{:S(2)}) collective-permute-start(f32[8,4096]{1,0:T(8,128)S(1)} %get-tuple-element.47.o1), channel_id=1, source_target_pairs={{0,2},{2,0},{4,6},{6,4},{1,3},{3,1},{5,7},{7,5},{8,10},{10,8},{12,... | collective-permute-start | bytes 393224 | tf_op jit(solution)/shard_map/ppermute | solution.py:71
  27.2 6.8 %collective-permute-start.8 = (f32[8,4096]{1,0:T(8,128)S(1)}, f32[8,4096]{1,0:T(8,128)S(1)}, u32[]{:S(2)}, u32[]{:S(2)}) collective-permute-start(f32[8,4096]{1,0:T(8,128)S(1)} %get-tuple-element.48.o2), channel_id=1, source_target_pairs={{0,24},{8,16},{16,8},{24,0},{1,25},{9,17},{17,9},{25,1},{2,26},{10... | collective-permute-start | bytes 393224 | tf_op jit(solution)/shard_map/ppermute | solution.py:71
  27.2 6.8 %collective-permute-start.9 = (f32[8,4096]{1,0:T(8,128)S(1)}, f32[8,4096]{1,0:T(8,128)S(1)}, u32[]{:S(2)}, u32[]{:S(2)}) collective-permute-start(f32[8,4096]{1,0:T(8,128)S(1)} %get-tuple-element.49.o3), channel_id=1, source_target_pairs={{0,8},{8,0},{16,24},{24,16},{1,9},{9,1},{17,25},{25,17},{2,10},{10... | collective-permute-start | bytes 393224 | tf_op jit(solution)/shard_map/ppermute | solution.py:71
  31.5 8.3 %collective-permute-start.10 = (f32[32,1152]{1,0:T(8,128)S(1)}, f32[32,1152]{1,0:T(8,128)S(1)}, u32[]{:S(2)}, u32[]{:S(2)}) collective-permute-start(f32[32,1152]{1,0:T(8,128)S(1)} %get-tuple-element.51.mine.refs_0_), channel_id=1, source_target_pairs={{0,1},{1,0},{2,3},{3,2},{4,5},{5,4},{6,7},{7,6},{8,9},{9,8},{10,11... | collective-permute-start | bytes 442376 | tf_op jit(solution)/shard_map/ppermute | solution.py:62
  38.2 5.7 %collective-permute-start.11 = (f32[32,1152]{1,0:T(8,128)S(1)}, f32[32,1152]{1,0:T(8,128)S(1)}, u32[]{:S(2)}, u32[]{:S(2)}) collective-permute-start(f32[32,1152]{1,0:T(8,128)S(1)} %get-tuple-element.53.mine.refs_2_), channel_id=1, source_target_pairs={{0,1},{1,0},{2,3},{3,2},{4,5},{5,4},{6,7},{7,6},{8,9},{9,8},{10,11... | collective-permute-start | bytes 442376 | tf_op jit(solution)/shard_map/ppermute | solution.py:62
  39.7 6.3 %collective-permute-start.12 = (f32[8,1024]{1,0:T(8,128)S(1)}, f32[8,1024]{1,0:T(8,128)S(1)}, u32[]{:S(2)}, u32[]{:S(2)}) collective-permute-start(f32[8,1024]{1,0:T(8,128)S(1)} %get-tuple-element.58.refs_0_), channel_id=1, source_target_pairs={{0,6},{2,4},{4,2},{6,0},{1,7},{3,5},{5,3},{7,1},{8,14},{10,12},{12... | collective-permute-start | bytes 98312 | tf_op jit(solution)/shard_map/ppermute | solution.py:71
  41.5 4.6 %collective-permute-start.13 = (f32[8,1024]{1,0:T(8,128)S(1)}, f32[8,1024]{1,0:T(8,128)S(1)}, u32[]{:S(2)}, u32[]{:S(2)}) collective-permute-start(f32[8,1024]{1,0:T(8,128)S(1)} %get-tuple-element.59.refs_1_), channel_id=1, source_target_pairs={{0,2},{2,0},{4,6},{6,4},{1,3},{3,1},{5,7},{7,5},{8,10},{10,8},{12,... | collective-permute-start | bytes 98312 | tf_op jit(solution)/shard_map/ppermute | solution.py:71
  41.5 5.3 %collective-permute-start.14 = (f32[8,1024]{1,0:T(8,128)S(1)}, f32[8,1024]{1,0:T(8,128)S(1)}, u32[]{:S(2)}, u32[]{:S(2)}) collective-permute-start(f32[8,1024]{1,0:T(8,128)S(1)} %get-tuple-element.60.refs_2_), channel_id=1, source_target_pairs={{0,24},{8,16},{16,8},{24,0},{1,25},{9,17},{17,9},{25,1},{2,26},{10... | collective-permute-start | bytes 98312 | tf_op jit(solution)/shard_map/ppermute | solution.py:71
  41.6 6.3 %collective-permute-start.15 = (f32[8,1024]{1,0:T(8,128)S(1)}, f32[8,1024]{1,0:T(8,128)S(1)}, u32[]{:S(2)}, u32[]{:S(2)}) collective-permute-start(f32[8,1024]{1,0:T(8,128)S(1)} %get-tuple-element.61.refs_3_), channel_id=1, source_target_pairs={{0,8},{8,0},{16,24},{24,16},{1,9},{9,1},{17,25},{25,17},{2,10},{10... | collective-permute-start | bytes 98312 | tf_op jit(solution)/shard_map/ppermute | solution.py:71
  43.9 10.9 %collective-permute-start.16 = (f32[8,1024]{1,0:T(8,128)S(1)}, f32[8,1024]{1,0:T(8,128)S(1)}, u32[]{:S(2)}, u32[]{:S(2)}) collective-permute-start(f32[8,1024]{1,0:T(8,128)S(1)} %get-tuple-element.65.refs_0_), channel_id=1, source_target_pairs={{0,6},{2,4},{4,2},{6,0},{1,7},{3,5},{5,3},{7,1},{8,14},{10,12},{12... | collective-permute-start | bytes 98312 | tf_op jit(solution)/shard_map/ppermute | solution.py:71
  46.1 8.7 %collective-permute-start.17 = (f32[8,1024]{1,0:T(8,128)S(1)}, f32[8,1024]{1,0:T(8,128)S(1)}, u32[]{:S(2)}, u32[]{:S(2)}) collective-permute-start(f32[8,1024]{1,0:T(8,128)S(1)} %get-tuple-element.66.refs_1_), channel_id=1, source_target_pairs={{0,2},{2,0},{4,6},{6,4},{1,3},{3,1},{5,7},{7,5},{8,10},{10,8},{12,... | collective-permute-start | bytes 98312 | tf_op jit(solution)/shard_map/ppermute | solution.py:71
  46.2 8.6 %collective-permute-start.18 = (f32[8,1024]{1,0:T(8,128)S(1)}, f32[8,1024]{1,0:T(8,128)S(1)}, u32[]{:S(2)}, u32[]{:S(2)}) collective-permute-start(f32[8,1024]{1,0:T(8,128)S(1)} %get-tuple-element.67.refs_2_), channel_id=1, source_target_pairs={{0,24},{8,16},{16,8},{24,0},{1,25},{9,17},{17,9},{25,1},{2,26},{10... | collective-permute-start | bytes 98312 | tf_op jit(solution)/shard_map/ppermute | solution.py:71
  46.8 8.0 %collective-permute-start.19 = (f32[8,1024]{1,0:T(8,128)S(1)}, f32[8,1024]{1,0:T(8,128)S(1)}, u32[]{:S(2)}, u32[]{:S(2)}) collective-permute-start(f32[8,1024]{1,0:T(8,128)S(1)} %get-tuple-element.68.refs_3_), channel_id=1, source_target_pairs={{0,8},{8,0},{16,24},{24,16},{1,9},{9,1},{17,25},{25,17},{2,10},{10... | collective-permute-start | bytes 98312 | tf_op jit(solution)/shard_map/ppermute | solution.py:71

commit v5 on v3

--- a/solution.py
+++ b/solution.py
@@ -62,14 +62,11 @@
     return lax.ppermute(value, axis, [(i, i ^ distance) for i in range(count)])
 
 
-def exchange(values):
-    swapped = []
-    for slot, value in enumerate(values):
-        axis, colour = ("ry", "rx")[slot // 2], 1 - slot % 2
-        count = lax.axis_size(axis)
-        pairs = [(i, (i + (1 if i % 2 == colour else -1)) % count) for i in range(count)]
-        swapped.append(lax.ppermute(value, axis, pairs))
-    return swapped
+def swapped(value, slot):
+    axis, colour = ("ry", "rx")[slot // 2], 1 - slot % 2
+    count = lax.axis_size(axis)
+    pairs = [(i, (i + (1 if i % 2 == colour else -1)) % count) for i in range(count)]
+    return lax.ppermute(value, axis, pairs)
 
 
 def odd(axis):
@@ -218,30 +215,46 @@
     )(vmem(held), *own, *near)
 
 
-def add_kernel(same, *refs):
-    *refs, held = refs
-    pairs, outs = refs[:-edges], refs[-edges:]
-    mats, rank, features = outs[0].shape
-    for mat in range(mats):
-        mine, other = pairs[2 * mat], pairs[2 * mat + 1]
-        for slot, out in enumerate(outs):
-            here = slice(slot * rank, (slot + 1) * rank)
-            out[mat] = mine[here, :features] + other[here, :features]
-
-
-def add(held, pairs, rank):
-    mats = len(pairs)
-    pairs = [terms for pair in pairs for terms in pair]
-    sums = jax.ShapeDtypeStruct((mats, rank, held.shape[-1]), f32)
-    return pl.pallas_call(
-        add_kernel,
-        name="add",
-        out_shape=[sums] * edges + [jax.ShapeDtypeStruct(held.shape, f32)],
-        in_specs=[in_vmem] * (1 + len(pairs)),
-        out_specs=[in_vmem] * (edges + 1),
-        input_output_aliases={0: edges},
-        compiler_params=pltpu.CompilerParams(vmem_limit_bytes=grant),
-    )(vmem(held), *pairs)
+def add_kernel(rank, width, same, *refs):
+    count = 2 * width
+    pairs, refs = refs[:count], refs[count:-1]
+    whole = 4 * (width - 1)
+    ends, outs = refs[:whole], refs[whole:]
+
+    def total(mat, slot):
+        here = slice(slot * rank, (slot + 1) * rank)
+        return pairs[2 * mat][here, :-128] + pairs[2 * mat + 1][here, :-128]
+
+    for slot in range(2):
+        outs[slot][...] = total(width - 1, slot)
+    for mat in range(width - 1):
+        for slot in range(2):
+            outs[edges + mat][slot] = ends[4 * mat + slot][...] + ends[4 * mat + 2 + slot][...]
+    if len(outs) > 2:
+        for slot in range(2, edges):
+            for mat in range(width):
+                outs[slot][mat] = total(mat, slot)
+
+
+def add(held, pairs, rank, mat, ends=()):
+    mats, _, features = held.shape
+    outs = [jax.ShapeDtypeStruct((rank, features), f32)] * 2
+    if mat == mats - 1:
+        outs = outs + [jax.ShapeDtypeStruct((mats, rank, features), f32)] * 2
+        outs = outs + [jax.ShapeDtypeStruct((2, rank, features), f32)] * (mats - 1)
+    else:
+        pairs = pairs[mat : mat + 1]
+    args = [vmem(held), *(terms for pair in pairs for terms in pair), *ends]
+    outs = outs + [jax.ShapeDtypeStruct(held.shape, f32)]
+    return pl.pallas_call(
+        functools.partial(add_kernel, rank, len(pairs)),
+        name=f"add{mat}",
+        out_shape=outs,
+        in_specs=[in_vmem] * len(args),
+        out_specs=[in_vmem] * len(outs),
+        input_output_aliases={0: len(outs) - 1},
+        compiler_params=pltpu.CompilerParams(vmem_limit_bytes=grant),
+    )(*args)
 
 
 def inverse_kernel(rank, same, mine, other, inverse, held):
@@ -280,8 +293,8 @@
     *refs, mixed, next_rx, next_ry, held, new_rx, new_ry, sems, new_sems = refs
     mats, rows, _ = held.shape
     differs, inverses = refs[:mats], refs[mats : 2 * mats]
-    sums, near = refs[2 * mats : 2 * mats + edges], refs[2 * mats + edges :]
-    rank = sums[0].shape[1]
+    ends = refs[2 * mats :]
+    rank = new_rx.shape[1]
     width = edges * rank
     steps = rows // chunk
 
@@ -291,9 +304,15 @@
             held.at[mat, here], mixed.at[0, 0, mat, here], sems.at[mat, step]
         )
 
+    done, last, rx_ends = ends[: mats - 1], ends[mats - 1 : mats + 3], ends[mats + 3 :]
     for mat in range(mats):
         factor = inverses[mat][:, width : 2 * width]
-        total = jnp.concatenate([b[mat] + n[mat] for b, n in zip(sums, near)], 0)
+        if mat < mats - 1:
+            total = [done[mat][0], done[mat][1]]
+        else:
+            total = [last[0][...] + last[2][...], last[1][...] + last[3][...]]
+        total += [rx_ends[0][mat] + rx_ends[2][mat], rx_ends[1][mat] + rx_ends[3][mat]]
+        total = jnp.concatenate(total, 0)
         updated = lax.dot_general(
             factor, total, NN, precision=lax.Precision.HIGHEST, preferred_element_type=f32
         )
@@ -330,11 +349,10 @@
         new_copy.wait()
 
 
-def mix(held, differs, inverses, sums, near, shapes):
+def mix(held, differs, inverses, ends, rank, shapes):
     mats, rows, features = held.shape
-    rank = sums[0].shape[1]
     chunk = chunk_of(rows, 512)
-    args = [vmem(held), *differs, *inverses, *sums, *near]
+    args = [vmem(held), *differs, *inverses, *ends]
     return pl.pallas_call(
         functools.partial(mix_kernel, chunk),
         name="mix",
@@ -361,14 +379,15 @@
     factors = [factors_ry, lower_ry, factors_rx, lower_rx]
     size = chunk_of(rows, 512)
     pieces = rows // size
-    until = max(3 * pieces // 8, 1)
+    ahead = max(pieces // 2, 1)
+    until = ahead
     held = load(weights, size, until)
-    own = []
+    own, near = [], []
     for mat in range(mats):
-        first, until = until, min((mat + 1) * pieces + pieces // 4, mats * pieces)
+        first, until = until, min((mat + 1) * pieces + ahead, mats * pieces)
         *own_mat, held = project(held, factors, weights, mat, size, first, until)
         own.append(own_mat)
-    near = [exchange(own_mat) for own_mat in own]
+        near.append([swapped(value, slot) for slot, value in enumerate(own_mat)])
     differs, pairs = [], []
     tp = lax.axis_size("tp")
     for mat in range(mats):
@@ -380,14 +399,20 @@
         other = from_partner(terms, "tp", distance) if tp > 1 else jnp.zeros_like(terms)
         differs.append(p)
         pairs.append((terms, other))
-    inverses = [None] * mats
+    inverses, ends = [], []
     for mat in range(mats - 1):
-        inverses[mat], held = inverse_factor(held, pairs[mat], rank, mat)
-    *sums, held = add(held, pairs, rank)
-    near_sums = exchange(sums)
-    inverses[-1], held = inverse_factor(held, pairs[-1], rank, mats - 1)
+        *sums, held = add(held, pairs, rank, mat)
+        ends += [*sums, *(swapped(value, slot) for slot, value in enumerate(sums))]
+        inverse, held = inverse_factor(held, pairs[mat], rank, mat)
+        inverses.append(inverse)
+    *sums, held = add(held, pairs, rank, mats - 1, ends)
+    sums, done = sums[:edges], sums[edges:]
+    near_sums = [swapped(value, slot) for slot, value in enumerate(sums)]
+    ends = [*done, *sums[:2], *near_sums[:2], *sums[2:], *near_sums[2:]]
+    inverse, held = inverse_factor(held, pairs[-1], rank, mats - 1)
+    inverses.append(inverse)
     shapes = (weights.shape, factors_rx.shape, factors_ry.shape)
-    *results, held = mix(held, differs, inverses, sums, near_sums, shapes)
+    *results, held = mix(held, differs, inverses, ends, rank, shapes)
     return tuple(results)
 
 

time: 63.3 us -> 64.8 us (1.024)
  starting transfers between devices: 16.7 us -> 18.3 us
    ppermute x12 -> x14, waiting for transfers between devices: 3.7 us -> 6.06 us  [swapped(): return lax.ppermute(value, axis, pairs)]
    ppermute x2, waiting for transfers between devices: 3.49 us -> 1.66 us  [from_partner(): return lax.ppermute(value, axis, [(i, i ^ distance) for i in range(count)])]
    ppermute x12 -> x14, starting transfers between devices: 10.2 us -> 11.9 us  [swapped(): return lax.ppermute(value, axis, pairs)]
    pallas_call x2, Pallas kernels: 12.3 us -> 11.6 us  [project(): pl.pallas_call(functools.partial(project_kernel, mat, chunk_of(rows, 1024...]
  transfers between devices with their start and end apart: 16 -> 18, of which waited for: 5 -> 7; matrix products, arithmetic and copies ran while one was open for 0% -> 0% of each run, Pallas kernels for 30% -> 29%
where the time goes in v5:
time: 64.8 us; the launch traced here: 64.7 us
  Pallas kernels  36.9 us (57%)
  starting transfers between devices  18.3 us (28%)
  waiting for transfers between devices  8.69 us (13%)
  between operations  0.72 us (1%)
    pallas_call x1, Pallas kernels, mix(): pl.pallas_call(functools.partial(mix_kernel, chunk), name='mix', out_shap...  12.1 us
    ppermute x14, starting transfers between devices, swapped(): return lax.ppermute(value, axis, pairs)  11.9 us
    pallas_call x2, Pallas kernels, project(): pl.pallas_call(functools.partial(project_kernel, mat, chunk_of(rows, 1024...  11.6 us
    pallas_call x2, Pallas kernels, back(): pl.pallas_call(functools.partial(back_kernel, mat, chunk_of(rows, 1024)),...  8.37 us
    ppermute x14, waiting for transfers between devices, swapped(): return lax.ppermute(value, axis, pairs)  6.06 us
    pallas_call x1, Pallas kernels, load(): pl.pallas_call(functools.partial(load_kernel, size, until), name='load',...  3.5 us
    ppermute x2, starting transfers between devices, from_partner(): return lax.ppermute(value, axis, [(i, i ^ distance) for i in range(count)])  3.35 us
    ppermute x2, starting transfers between devices, shifted(): return lax.ppermute(value, axis, pairs)  3.14 us
  transfers between devices with their start and end apart: 18, of which 7 were waited for; matrix products, arithmetic and copies ran while one was open for 0% of the time, Pallas kernels for 29%

profile of v5, /device:TPU:0, one launch (start us, length us, event | category | flops | bytes accessed | tf_op | source)
XLA Modules:
  0.0 64.7 jit_solution(7891444533179515141)
XLA Ops:
  0.6 0.0 copy-start.1
  0.6 0.0 copy-start
  0.7 0.5 collective-permute-start.1
  1.2 2.6 %collective-permute-start = (f32[1,1,2,8,1024]{4,3,2,1,0:T(8,128)}, f32[1,1,2,8,1024]{4,3,2,1,0:T(8,128)S(1)}, u32[]{:S(2)}, u32[]{:S(2)}) collective-permute-start(f32[1,1,2,8,1024]{4,3,2,1,0:T(8,128)} %f0.3), channel_id=1, source_target_pairs={{0,2},{2,4},{4,6},{6,0},{1,3},{3,5},{5,7},{7,1},{8,10},{10,12},{12... | collective-permute-start | bytes 196616 | tf_op jit(solution)/shard_map/ppermute | solution.py:57
  3.8 3.5 %load.1.same = f32[2,4096,1024]{2,1,0:T(8,128)S(1)} custom-call(f32[1,1,2,4096,1024]{4,3,2,1,0:T(8,128)} %weights.5), custom_call_target="tpu_custom_call" | custom-call | tf_op jit(solution)/shard_map/load/pallas_call | solution.py:99
  7.3 0.0 collective-permute-done.1.f3
  7.3 1.0 %collective-permute-done.f1 = f32[1,1,2,8,1024]{4,3,2,1,0:T(8,128)S(1)} collective-permute-done((f32[1,1,2,8,1024]{4,3,2,1,0:T(8,128)}, f32[1,1,2,8,1024]{4,3,2,1,0:T(8,128)S(1)}, u32[]{:S(2)}, u32[]{:S(2)}) %collective-permute-start) | collective-permute-done | bytes 65568 | tf_op jit(solution)/shard_map/ppermute | solution.py:57
  8.3 0.0 copy-done.1
  8.3 0.0 copy-done
  8.3 5.9 %project0.1 = (f32[8,4096]{1,0:T(8,128)S(1)}, f32[8,4096]{1,0:T(8,128)S(1)}, f32[8,4096]{1,0:T(8,128)S(1)}, f32[8,4096]{1,0:T(8,128)S(1)}, f32[2,4096,1024]{2,1,0:T(8,128)S(1)}) custom-call(f32[2,4096,1024]{2,1,0:T(8,128)S(1)} %load.1.same, f32[1,1,2,8,1024]{4,3,2,1,0:T(8,128)S(1)} %copy-done, ...), custom_call_target="tpu_custom_call", output_to_operand_aliasing={{4}: (0, {})} | custom-call | flops 4294967296 | bytes 33554432 | tf_op jit(solution)/shard_map/project0/pallas_call | solution.py:154
  14.2 2.3 %collective-permute-start.2 = (f32[8,4096]{1,0:T(8,128)S(1)}, f32[8,4096]{1,0:T(8,128)S(1)}, u32[]{:S(2)}, u32[]{:S(2)}) collective-permute-start(f32[8,4096]{1,0:T(8,128)S(1)} %get-tuple-element.37.o0), channel_id=1, source_target_pairs={{0,6},{2,4},{4,2},{6,0},{1,7},{3,5},{5,3},{7,1},{8,14},{10,12},{12... | collective-permute-start | bytes 393224 | tf_op jit(solution)/shard_map/ppermute | solution.py:69
  16.5 0.0 collective-permute-start.3
  16.5 0.8 %collective-permute-start.4 = (f32[8,4096]{1,0:T(8,128)S(1)}, f32[8,4096]{1,0:T(8,128)S(1)}, u32[]{:S(2)}, u32[]{:S(2)}) collective-permute-start(f32[8,4096]{1,0:T(8,128)S(1)} %get-tuple-element.39.o2), channel_id=1, source_target_pairs={{0,24},{8,16},{16,8},{24,0},{1,25},{9,17},{17,9},{25,1},{2,26},{10... | collective-permute-start | bytes 393224 | tf_op jit(solution)/shard_map/ppermute | solution.py:69
  17.3 0.9 %collective-permute-start.5 = (f32[8,4096]{1,0:T(8,128)S(1)}, f32[8,4096]{1,0:T(8,128)S(1)}, u32[]{:S(2)}, u32[]{:S(2)}) collective-permute-start(f32[8,4096]{1,0:T(8,128)S(1)} %get-tuple-element.40.o3), channel_id=1, source_target_pairs={{0,8},{8,0},{16,24},{24,16},{1,9},{9,1},{17,25},{25,17},{2,10},{10... | collective-permute-start | bytes 393224 | tf_op jit(solution)/shard_map/ppermute | solution.py:69
  18.2 5.7 %project1.1 = (f32[8,4096]{1,0:T(8,128)S(1)}, f32[8,4096]{1,0:T(8,128)S(1)}, f32[8,4096]{1,0:T(8,128)S(1)}, f32[8,4096]{1,0:T(8,128)S(1)}, f32[2,4096,1024]{2,1,0:T(8,128)S(1)}) custom-call(f32[2,4096,1024]{2,1,0:T(8,128)S(1)} %get-tuple-element.35.same, f32[1,1,2,8,1024]{4,3,2,1,0:T(8,128)S(1)} %copy-done, ...), custom_call_target="tpu_custom_call", output_to_operand_aliasing={{4}: (0, {})} | custom-call | flops 4294967296 | bytes 33554432 | tf_op jit(solution)/shard_map/project1/pallas_call | solution.py:154
  23.9 2.1 %collective-permute-start.6 = (f32[8,4096]{1,0:T(8,128)S(1)}, f32[8,4096]{1,0:T(8,128)S(1)}, u32[]{:S(2)}, u32[]{:S(2)}) collective-permute-start(f32[8,4096]{1,0:T(8,128)S(1)} %get-tuple-element.42.o0), channel_id=1, source_target_pairs={{0,6},{2,4},{4,2},{6,0},{1,7},{3,5},{5,3},{7,1},{8,14},{10,12},{12... | collective-permute-start | bytes 393224 | tf_op jit(solution)/shard_map/ppermute | solution.py:69
  26.1 0.0 collective-permute-done.2.n0
  26.1 1.1 %collective-permute-start.7 = (f32[8,4096]{1,0:T(8,128)S(1)}, f32[8,4096]{1,0:T(8,128)S(1)}, u32[]{:S(2)}, u32[]{:S(2)}) collective-permute-start(f32[8,4096]{1,0:T(8,128)S(1)} %get-tuple-element.43.o1), channel_id=1, source_target_pairs={{0,2},{2,0},{4,6},{6,4},{1,3},{3,1},{5,7},{7,5},{8,10},{10,8},{12,... | collective-permute-start | bytes 393224 | tf_op jit(solution)/shard_map/ppermute | solution.py:69
  27.2 0.0 collective-permute-done.3.n1
  27.2 0.0 collective-permute-start.8
  27.2 0.0 collective-permute-done.4.n2
  27.2 0.1 collective-permute-start.9
  27.3 0.0 collective-permute-done.5.n3
  27.3 4.2 %back0.1 = (f32[32,4096]{1,0:T(8,128)S(1)}, f32[32,1152]{1,0:T(8,128)S(1)}, f32[2,4096,1024]{2,1,0:T(8,128)S(1)}) custom-call(f32[2,4096,1024]{2,1,0:T(8,128)S(1)} %get-tuple-element.36.same, f32[8,4096]{1,0:T(8,128)S(1)} %get-tuple-element.37.o0, f32[8,4096]{1,0:T(8,128)S(1)} %get-tuple-element.38.o1, ...), custom_call_target="tpu_custom_call", output_to_operand_aliasing={{2}: (0, {})} | custom-call | flops 4294967296 | bytes 33554432 | tf_op jit(solution)/shard_map/back0/pallas_call | solution.py:202
  31.5 1.8 %collective-permute-start.10 = (f32[32,1152]{1,0:T(8,128)S(1)}, f32[32,1152]{1,0:T(8,128)S(1)}, u32[]{:S(2)}, u32[]{:S(2)}) collective-permute-start(f32[32,1152]{1,0:T(8,128)S(1)} %get-tuple-element.47.refs_0_.mine), channel_id=1, source_target_pairs={{0,1},{1,0},{2,3},{3,2},{4,5},{5,4},{6,7},{7,6},{8,9},{9,8},{10,11... | collective-permute-start | bytes 442376 | tf_op jit(solution)/shard_map/ppermute | solution.py:62
  33.3 0.0 collective-permute-done.6.n0
  33.3 0.7 %collective-permute-done.7.n1 = f32[8,4096]{1,0:T(8,128)S(1)} collective-permute-done((f32[8,4096]{1,0:T(8,128)S(1)}, f32[8,4096]{1,0:T(8,128)S(1)}, u32[]{:S(2)}, u32[]{:S(2)}) %collective-permute-start.7) | collective-permute-done | bytes 131104 | tf_op jit(solution)/shard_map/ppermute | solution.py:69
  34.0 0.0 collective-permute-done.8.n2
  34.0 0.0 collective-permute-done.9.n3
  34.0 4.2 %back1.1 = (f32[32,4096]{1,0:T(8,128)S(1)}, f32[32,1152]{1,0:T(8,128)S(1)}, f32[2,4096,1024]{2,1,0:T(8,128)S(1)}) custom-call(f32[2,4096,1024]{2,1,0:T(8,128)S(1)} %get-tuple-element.41.same, f32[8,4096]{1,0:T(8,128)S(1)} %get-tuple-element.42.o0, f32[8,4096]{1,0:T(8,128)S(1)} %get-tuple-element.43.o1, ...), custom_call_target="tpu_custom_call", output_to_operand_aliasing={{2}: (0, {})} | custom-call | flops 4294967296 | bytes 33554432 | tf_op jit(solution)/shard_map/back1/pallas_call | solution.py:202
  38.2 1.5 %collective-permute-start.11 = (f32[32,1152]{1,0:T(8,128)S(1)}, f32[32,1152]{1,0:T(8,128)S(1)}, u32[]{:S(2)}, u32[]{:S(2)}) collective-permute-start(f32[32,1152]{1,0:T(8,128)S(1)} %get-tuple-element.50.refs_2_.mine), channel_id=1, source_target_pairs={{0,1},{1,0},{2,3},{3,2},{4,5},{5,4},{6,7},{7,6},{8,9},{9,8},{10,11... | collective-permute-start | bytes 442376 | tf_op jit(solution)/shard_map/ppermute | solution.py:62
  39.7 0.0 collective-permute-done.10.refs_1_.other
  39.7 1.8 %collective-permute-start.12 = (f32[8,1024]{1,0:T(8,128)S(1)}, f32[8,1024]{1,0:T(8,128)S(1)}, u32[]{:S(2)}, u32[]{:S(2)}) collective-permute-start(f32[8,1024]{1,0:T(8,128)S(1)} %get-tuple-element.51.refs_4_), channel_id=1, source_target_pairs={{0,6},{2,4},{4,2},{6,0},{1,7},{3,5},{5,3},{7,1},{8,14},{10,12},{12... | collective-permute-start | bytes 98312 | tf_op jit(solution)/shard_map/ppermute | solution.py:69
  41.5 0.0 collective-permute-start.13
  41.5 0.7 %inverse0.1 = (f32[32,128]{1,0:T(8,128)S(1)}, f32[2,4096,1024]{2,1,0:T(8,128)S(1)}) custom-call(f32[2,4096,1024]{2,1,0:T(8,128)S(1)} %get-tuple-element.48.same, f32[32,1152]{1,0:T(8,128)S(1)} %get-tuple-element.47.refs_0_.mine, f32[32,1152]{1,0:T(8,128)S(1)} %collective-permute-done.10.refs_1_.other), custom_call_target="tpu_custom_call", output_to_operand_aliasing={{1}: (0, {})} | custom-call | tf_op jit(solution)/shard_map/inverse0/pallas_call | solution.py:278
  42.2 1.7 %collective-permute-done.11.refs_3_.other = f32[32,1152]{1,0:T(8,128)S(1)} collective-permute-done((f32[32,1152]{1,0:T(8,128)S(1)}, f32[32,1152]{1,0:T(8,128)S(1)}, u32[]{:S(2)}, u32[]{:S(2)}) %collective-permute-start.11) | collective-permute-done | bytes 147488 | tf_op jit(solution)/shard_map/ppermute | solution.py:62
  43.9 1.8 %collective-permute-done.12.refs_6_ = f32[8,1024]{1,0:T(8,128)S(1)} collective-permute-done((f32[8,1024]{1,0:T(8,128)S(1)}, f32[8,1024]{1,0:T(8,128)S(1)}, u32[]{:S(2)}, u32[]{:S(2)}) %collective-permute-start.12) | collective-permute-done | bytes 32800 | tf_op jit(solution)/shard_map/ppermute | solution.py:69
  45.6 0.2 collective-permute-done.13.refs_7_
  45.8 0.1 collective-permute-start.16
  45.9 0.6 collective-permute-start.17
  46.5 2.0 %collective-permute-start.14 = (f32[8,1024]{1,0:T(8,128)S(1)}, f32[8,1024]{1,0:T(8,128)S(1)}, u32[]{:S(2)}, u32[]{:S(2)}) collective-permute-start(f32[8,1024]{1,0:T(8,128)S(1)} %get-tuple-element.60.refs_5_), channel_id=1, source_target_pairs={{0,6},{2,4},{4,2},{6,0},{1,7},{3,5},{5,3},{7,1},{8,14},{10,12},{12... | collective-permute-start | bytes 98312 | tf_op jit(solution)/shard_map/ppermute | solution.py:69
  48.5 0.0 collective-permute-start.15
  48.5 0.7 %inverse1.1 = (f32[32,128]{1,0:T(8,128)S(1)}, f32[2,4096,1024]{2,1,0:T(8,128)S(1)}) custom-call(f32[2,4096,1024]{2,1,0:T(8,128)S(1)} %get-tuple-element.53.same, f32[32,1152]{1,0:T(8,128)S(1)} %get-tuple-element.50.refs_2_.mine, f32[32,1152]{1,0:T(8,128)S(1)} %collective-permute-done.11.refs_3_.other), custom_call_target="tpu_custom_call", output_to_operand_aliasing={{1}: (0, {})} | custom-call | tf_op jit(solution)/shard_map/inverse1/pallas_call | solution.py:278
  49.2 3.1 %collective-permute-done.14.refs_7_ = f32[8,1024]{1,0:T(8,128)S(1)} collective-permute-done((f32[8,1024]{1,0:T(8,128)S(1)}, f32[8,1024]{1,0:T(8,128)S(1)}, u32[]{:S(2)}, u32[]{:S(2)}) %collective-permute-start.14) | collective-permute-done | bytes 32800 | tf_op jit(solution)/shard_map/ppermute | solution.py:69
  52.2 0.3 collective-permute-done.15.refs_8_
  52.6 0.0 collective-permute-done.16.refs_11_
  52.6 0.0 collective-permute-done.17.refs_12_
  52.6 12.1 %mix.1 = (f32[1,1,2,4096,1024]{4,3,2,1,0:T(8,128)}, f32[1,1,2,8,1024]{4,3,2,1,0:T(8,128)}, f32[1,1,2,8,1024]{4,3,2,1,0:T(8,128)}, f32[2,4096,1024]{2,1,0:T(8,128)S(1)}) custom-call(f32[2,4096,1024]{2,1,0:T(8,128)S(1)} %get-tuple-element.54.same, f32[32,4096]{1,0:T(8,128)S(1)} %get-tuple-element.55.refs_0_, ...), custom_call_target="tpu_custom_call", output_to_operand_aliasing={{3}: (0, {})} | custom-call | flops 8589934592 | bytes 33554432 | tf_op jit(solution)/shard_map/mix/pallas_call | solution.py:356
  (2 shorter events, 0.0 us)
Async XLA Ops:
  0.6 7.6 %copy-start.1 = (f32[1,1,2,8,1024]{4,3,2,1,0:T(8,128)S(1)}, f32[1,1,2,8,1024]{4,3,2,1,0:T(8,128)}, u32[]{:S(2)}) copy-start(f32[1,1,2,8,1024]{4,3,2,1,0:T(8,128)} %f2.3) | copy-start | bytes 196612
  0.6 7.6 %copy-start = (f32[1,1,2,8,1024]{4,3,2,1,0:T(8,128)S(1)}, f32[1,1,2,8,1024]{4,3,2,1,0:T(8,128)}, u32[]{:S(2)}) copy-start(f32[1,1,2,8,1024]{4,3,2,1,0:T(8,128)} %f0.3) | copy-start | bytes 196612
  0.7 6.7 %collective-permute-start.1 = (f32[1,1,2,8,1024]{4,3,2,1,0:T(8,128)}, f32[1,1,2,8,1024]{4,3,2,1,0:T(8,128)S(1)}, u32[]{:S(2)}, u32[]{:S(2)}) collective-permute-start(f32[1,1,2,8,1024]{4,3,2,1,0:T(8,128)} %f2.3), channel_id=1, source_target_pairs={{0,8},{8,16},{16,24},{24,0},{1,9},{9,17},{17,25},{25,1},{2,10},{10... | collective-permute-start | bytes 196616 | tf_op jit(solution)/shard_map/ppermute | solution.py:57
  1.2 7.1 %collective-permute-start = (f32[1,1,2,8,1024]{4,3,2,1,0:T(8,128)}, f32[1,1,2,8,1024]{4,3,2,1,0:T(8,128)S(1)}, u32[]{:S(2)}, u32[]{:S(2)}) collective-permute-start(f32[1,1,2,8,1024]{4,3,2,1,0:T(8,128)} %f0.3), channel_id=1, source_target_pairs={{0,2},{2,4},{4,6},{6,0},{1,3},{3,5},{5,7},{7,1},{8,10},{10,12},{12... | collective-permute-start | bytes 196616 | tf_op jit(solution)/shard_map/ppermute | solution.py:57
  14.2 11.8 %collective-permute-start.2 = (f32[8,4096]{1,0:T(8,128)S(1)}, f32[8,4096]{1,0:T(8,128)S(1)}, u32[]{:S(2)}, u32[]{:S(2)}) collective-permute-start(f32[8,4096]{1,0:T(8,128)S(1)} %get-tuple-element.37.o0), channel_id=1, source_target_pairs={{0,6},{2,4},{4,2},{6,0},{1,7},{3,5},{5,3},{7,1},{8,14},{10,12},{12... | collective-permute-start | bytes 393224 | tf_op jit(solution)/shard_map/ppermute | solution.py:69
  16.5 10.7 %collective-permute-start.3 = (f32[8,4096]{1,0:T(8,128)S(1)}, f32[8,4096]{1,0:T(8,128)S(1)}, u32[]{:S(2)}, u32[]{:S(2)}) collective-permute-start(f32[8,4096]{1,0:T(8,128)S(1)} %get-tuple-element.38.o1), channel_id=1, source_target_pairs={{0,2},{2,0},{4,6},{6,4},{1,3},{3,1},{5,7},{7,5},{8,10},{10,8},{12,... | collective-permute-start | bytes 393224 | tf_op jit(solution)/shard_map/ppermute | solution.py:69
  16.5 10.7 %collective-permute-start.4 = (f32[8,4096]{1,0:T(8,128)S(1)}, f32[8,4096]{1,0:T(8,128)S(1)}, u32[]{:S(2)}, u32[]{:S(2)}) collective-permute-start(f32[8,4096]{1,0:T(8,128)S(1)} %get-tuple-element.39.o2), channel_id=1, source_target_pairs={{0,24},{8,16},{16,8},{24,0},{1,25},{9,17},{17,9},{25,1},{2,26},{10... | collective-permute-start | bytes 393224 | tf_op jit(solution)/shard_map/ppermute | solution.py:69
  17.3 9.9 %collective-permute-start.5 = (f32[8,4096]{1,0:T(8,128)S(1)}, f32[8,4096]{1,0:T(8,128)S(1)}, u32[]{:S(2)}, u32[]{:S(2)}) collective-permute-start(f32[8,4096]{1,0:T(8,128)S(1)} %get-tuple-element.40.o3), channel_id=1, source_target_pairs={{0,8},{8,0},{16,24},{24,16},{1,9},{9,1},{17,25},{25,17},{2,10},{10... | collective-permute-start | bytes 393224 | tf_op jit(solution)/shard_map/ppermute | solution.py:69
  23.9 9.4 %collective-permute-start.6 = (f32[8,4096]{1,0:T(8,128)S(1)}, f32[8,4096]{1,0:T(8,128)S(1)}, u32[]{:S(2)}, u32[]{:S(2)}) collective-permute-start(f32[8,4096]{1,0:T(8,128)S(1)} %get-tuple-element.42.o0), channel_id=1, source_target_pairs={{0,6},{2,4},{4,2},{6,0},{1,7},{3,5},{5,3},{7,1},{8,14},{10,12},{12... | collective-permute-start | bytes 393224 | tf_op jit(solution)/shard_map/ppermute | solution.py:69
  26.1 7.9 %collective-permute-start.7 = (f32[8,4096]{1,0:T(8,128)S(1)}, f32[8,4096]{1,0:T(8,128)S(1)}, u32[]{:S(2)}, u32[]{:S(2)}) collective-permute-start(f32[8,4096]{1,0:T(8,128)S(1)} %get-tuple-element.43.o1), channel_id=1, source_target_pairs={{0,2},{2,0},{4,6},{6,4},{1,3},{3,1},{5,7},{7,5},{8,10},{10,8},{12,... | collective-permute-start | bytes 393224 | tf_op jit(solution)/shard_map/ppermute | solution.py:69
  27.2 6.8 %collective-permute-start.8 = (f32[8,4096]{1,0:T(8,128)S(1)}, f32[8,4096]{1,0:T(8,128)S(1)}, u32[]{:S(2)}, u32[]{:S(2)}) collective-permute-start(f32[8,4096]{1,0:T(8,128)S(1)} %get-tuple-element.44.o2), channel_id=1, source_target_pairs={{0,24},{8,16},{16,8},{24,0},{1,25},{9,17},{17,9},{25,1},{2,26},{10... | collective-permute-start | bytes 393224 | tf_op jit(solution)/shard_map/ppermute | solution.py:69
  27.2 6.8 %collective-permute-start.9 = (f32[8,4096]{1,0:T(8,128)S(1)}, f32[8,4096]{1,0:T(8,128)S(1)}, u32[]{:S(2)}, u32[]{:S(2)}) collective-permute-start(f32[8,4096]{1,0:T(8,128)S(1)} %get-tuple-element.45.o3), channel_id=1, source_target_pairs={{0,8},{8,0},{16,24},{24,16},{1,9},{9,1},{17,25},{25,17},{2,10},{10... | collective-permute-start | bytes 393224 | tf_op jit(solution)/shard_map/ppermute | solution.py:69
  31.5 8.2 %collective-permute-start.10 = (f32[32,1152]{1,0:T(8,128)S(1)}, f32[32,1152]{1,0:T(8,128)S(1)}, u32[]{:S(2)}, u32[]{:S(2)}) collective-permute-start(f32[32,1152]{1,0:T(8,128)S(1)} %get-tuple-element.47.refs_0_.mine), channel_id=1, source_target_pairs={{0,1},{1,0},{2,3},{3,2},{4,5},{5,4},{6,7},{7,6},{8,9},{9,8},{10,11... | collective-permute-start | bytes 442376 | tf_op jit(solution)/shard_map/ppermute | solution.py:62
  38.2 5.7 %collective-permute-start.11 = (f32[32,1152]{1,0:T(8,128)S(1)}, f32[32,1152]{1,0:T(8,128)S(1)}, u32[]{:S(2)}, u32[]{:S(2)}) collective-permute-start(f32[32,1152]{1,0:T(8,128)S(1)} %get-tuple-element.50.refs_2_.mine), channel_id=1, source_target_pairs={{0,1},{1,0},{2,3},{3,2},{4,5},{5,4},{6,7},{7,6},{8,9},{9,8},{10,11... | collective-permute-start | bytes 442376 | tf_op jit(solution)/shard_map/ppermute | solution.py:62
  39.7 5.9 %collective-permute-start.12 = (f32[8,1024]{1,0:T(8,128)S(1)}, f32[8,1024]{1,0:T(8,128)S(1)}, u32[]{:S(2)}, u32[]{:S(2)}) collective-permute-start(f32[8,1024]{1,0:T(8,128)S(1)} %get-tuple-element.51.refs_4_), channel_id=1, source_target_pairs={{0,6},{2,4},{4,2},{6,0},{1,7},{3,5},{5,3},{7,1},{8,14},{10,12},{12... | collective-permute-start | bytes 98312 | tf_op jit(solution)/shard_map/ppermute | solution.py:69
  41.5 4.3 %collective-permute-start.13 = (f32[8,1024]{1,0:T(8,128)S(1)}, f32[8,1024]{1,0:T(8,128)S(1)}, u32[]{:S(2)}, u32[]{:S(2)}) collective-permute-start(f32[8,1024]{1,0:T(8,128)S(1)} %get-tuple-element.52.refs_5_), channel_id=1, source_target_pairs={{0,2},{2,0},{4,6},{6,4},{1,3},{3,1},{5,7},{7,5},{8,10},{10,8},{12,... | collective-permute-start | bytes 98312 | tf_op jit(solution)/shard_map/ppermute | solution.py:69
  45.8 6.7 %collective-permute-start.16 = (f32[2,8,1024]{2,1,0:T(8,128)S(1)}, f32[2,8,1024]{2,1,0:T(8,128)S(1)}, u32[]{:S(2)}, u32[]{:S(2)}) collective-permute-start(f32[2,8,1024]{2,1,0:T(8,128)S(1)} %get-tuple-element.62.refs_9_), channel_id=1, source_target_pairs={{0,24},{8,16},{16,8},{24,0},{1,25},{9,17},{17,9},{25,1},{2,26},{10... | collective-permute-start | bytes 196616 | tf_op jit(solution)/shard_map/ppermute | solution.py:69
  45.9 6.7 %collective-permute-start.17 = (f32[2,8,1024]{2,1,0:T(8,128)S(1)}, f32[2,8,1024]{2,1,0:T(8,128)S(1)}, u32[]{:S(2)}, u32[]{:S(2)}) collective-permute-start(f32[2,8,1024]{2,1,0:T(8,128)S(1)} %get-tuple-element.63.refs_10_), channel_id=1, source_target_pairs={{0,8},{8,0},{16,24},{24,16},{1,9},{9,1},{17,25},{25,17},{2,10},{10... | collective-permute-start | bytes 196616 | tf_op jit(solution)/shard_map/ppermute | solution.py:69
  46.5 5.7 %collective-permute-start.14 = (f32[8,1024]{1,0:T(8,128)S(1)}, f32[8,1024]{1,0:T(8,128)S(1)}, u32[]{:S(2)}, u32[]{:S(2)}) collective-permute-start(f32[8,1024]{1,0:T(8,128)S(1)} %get-tuple-element.60.refs_5_), channel_id=1, source_target_pairs={{0,6},{2,4},{4,2},{6,0},{1,7},{3,5},{5,3},{7,1},{8,14},{10,12},{12... | collective-permute-start | bytes 98312 | tf_op jit(solution)/shard_map/ppermute | solution.py:69
  48.5 4.1 %collective-permute-start.15 = (f32[8,1024]{1,0:T(8,128)S(1)}, f32[8,1024]{1,0:T(8,128)S(1)}, u32[]{:S(2)}, u32[]{:S(2)}) collective-permute-start(f32[8,1024]{1,0:T(8,128)S(1)} %get-tuple-element.61.refs_6_), channel_id=1, source_target_pairs={{0,2},{2,0},{4,6},{6,4},{1,3},{3,1},{5,7},{7,5},{8,10},{10,8},{12,... | collective-permute-start | bytes 98312 | tf_op jit(solution)/shard_map/ppermute | solution.py:69

commit v6 on v4

--- a/solution.py
+++ b/solution.py
@@ -11,7 +11,7 @@
 bf16 = jnp.bfloat16
 mixing = 0.2
 edges = 4
-grant = 6 << 20
+grant = 8 << 20
 
 NN = (((1,), (0,)), ((), ()))
 NT = (((1,), (1,)), ((), ()))
@@ -203,7 +203,7 @@
     _, rows, features = held.shape
     rank = own[0].shape[0]
     return pl.pallas_call(
-        functools.partial(back_kernel, mat, chunk_of(rows, 1024)),
+        functools.partial(back_kernel, mat, chunk_of(rows, 4096)),
         name=f"back{mat}",
         out_shape=[
             jax.ShapeDtypeStruct((edges * rank, rows), f32),
@@ -239,56 +239,60 @@
     )(vmem(held), *pair)
 
 
-def inverse_kernel(rank, same, *refs):
-    *refs, held = refs
-    mats = len(refs) // 3
+def inverse_of(gram, rank):
     width = edges * rank
-    shape = (mats * edges, rank, 128)
+    shape = (edges, rank, 128)
     row = lax.broadcasted_iota(jnp.int32, shape, 1)
     lane = lax.broadcasted_iota(jnp.int32, shape, 2)
-    slot = lax.rem(lax.broadcasted_iota(jnp.int32, shape, 0), edges)
-    grams = [refs[2 * mat][:, -128:] + refs[2 * mat + 1][:, -128:] for mat in range(mats)]
-    value = jnp.concatenate(grams, 0).reshape(shape)
+    slot = lax.broadcasted_iota(jnp.int32, shape, 0)
+    value = gram.reshape(shape)
     value = jnp.where(lane < rank, value, (lane == width + slot * rank + row).astype(f32))
-    pivots = jnp.ones((shape[0], rank, 1), f32)
+    pivots = jnp.ones((edges, rank, 1), f32)
     for j in range(rank):
         pivot = value[:, j : j + 1, j : j + 1]
         pivots = jnp.where(row[:, :, :1] == j, pivot, pivots)
         factor = jnp.where(row > j, value[:, :, j : j + 1] / pivot, 0.0)
         value = value - factor * value[:, j : j + 1, :]
-    value = (value / jnp.sqrt(pivots)).reshape(mats * width, 128)
-    for mat, inverse in enumerate(refs[2 * mats :]):
-        inverse[...] = value[mat * width : (mat + 1) * width]
-
-
-def inverse_factors(held, pairs, rank):
-    mats = len(pairs)
-    pairs = [terms for pair in pairs for terms in pair]
+    return (value / jnp.sqrt(pivots)).reshape(width, 128)
+
+
+def inverse_kernel(rank, same, mine, other, inverse, held):
+    inverse[...] = inverse_of(mine[:, -128:] + other[:, -128:], rank)
+
+
+def inverse_factor(held, pair, rank):
     return pl.pallas_call(
         functools.partial(inverse_kernel, rank),
         name="inverse",
-        out_shape=[jax.ShapeDtypeStruct((edges * rank, 128), f32)] * mats
-        + [jax.ShapeDtypeStruct(held.shape, f32)],
-        in_specs=[in_vmem] * (1 + 2 * mats),
-        out_specs=[in_vmem] * (1 + mats),
-        input_output_aliases={0: mats},
-        compiler_params=pltpu.CompilerParams(vmem_limit_bytes=grant),
-    )(vmem(held), *pairs)
-
-
-def mix_kernel(mat, chunk, same, differ, inverse, *refs):
+        out_shape=[
+            jax.ShapeDtypeStruct((edges * rank, 128), f32),
+            jax.ShapeDtypeStruct(held.shape, f32),
+        ],
+        in_specs=[in_vmem] * 3,
+        out_specs=[in_vmem] * 2,
+        input_output_aliases={0: 1},
+        compiler_params=pltpu.CompilerParams(vmem_limit_bytes=grant),
+    )(vmem(held), *pair)
+
+
+def mix_kernel(mat, chunk, late, same, differ, inverse, *refs):
     sums, near = refs[:edges], refs[edges : 2 * edges]
-    mixed, next_rx, next_ry, held, new_rx, new_ry, sems, new_sems = refs[-8:]
+    mixed, next_rx, next_ry, held, following, new_rx, new_ry, sems, new_sems = refs[-9:]
     rank = sums[0].shape[0]
     width = edges * rank
-    steps = held.shape[1] // chunk
-
-    def copy(step):
-        here = pl.ds(pl.multiple_of(step * chunk, chunk), chunk)
+    mats, rows, _ = held.shape
+    steps = rows // chunk
+    mine = steps - (late if mat < mats - 1 else 0)
+
+    def copy(which, row, size, sem):
+        here = pl.ds(row, size)
         return pltpu.make_async_copy(
-            held.at[mat, here], mixed.at[0, 0, mat, here], sems.at[step]
+            held.at[which, here], mixed.at[0, 0, which, here], sems.at[sem]
         )
 
+    left = [copy(mat - 1, rows - late * chunk, late * chunk, steps)] if mat and late else []
+    for other in left:
+        other.start()
     factor = inverse[:, width : 2 * width]
     total = jnp.concatenate([b[...] + n[...] for b, n in zip(sums, near)], 0)
     updated = lax.dot_general(
@@ -300,13 +304,28 @@
     r_high, r_low = split(right)
     terms = jnp.concatenate([r_high, r_high, r_low, r_low], 0)
 
-    @pl.loop(0, steps)
-    def _(step):
-        here = pl.ds(pl.multiple_of(step * chunk, chunk), chunk)
+    def correct(row, size):
+        here = pl.ds(row, size)
         high, low = split(differ[:, here])
         lhs = jnp.concatenate([high, low, high, low], 0)
         held[mat, here, :] -= dot(lhs, terms, TN)
-        copy(step).start()
+
+    halves = [copy(mat, 0, chunk // 2, 0), copy(mat, chunk // 2, chunk // 2, steps + 1)]
+    for half in range(2):
+        correct(half * (chunk // 2), chunk // 2)
+        halves[half].start()
+
+    def place(step):
+        return pl.multiple_of(step * chunk, chunk)
+
+    @pl.loop(1, mine)
+    def _(step):
+        correct(place(step), chunk)
+        copy(mat, place(step), chunk, step).start()
+
+    @pl.loop(mine, steps)
+    def _(step):
+        correct(place(step), chunk)
 
     parts = [updated[slot * rank : (slot + 1) * rank] for slot in range(edges)]
     new_rx[...] = jnp.where(odd("rx"), parts[2], parts[3])
@@ -317,33 +336,42 @@
     ]
     for new_copy in new_copies:
         new_copy.start()
-
-    @pl.loop(0, steps)
+    if mat < mats - 1:
+        gram, gram_other = refs[2 * edges : 2 * edges + 2]
+        following[...] = inverse_of(gram[:, -128:] + gram_other[:, -128:], rank)
+    else:
+        following[...] = inverse[...]
+    for half in halves:
+        half.wait()
+
+    @pl.loop(1, mine)
     def _(step):
-        copy(step).wait()
-
-    for new_copy in new_copies:
-        new_copy.wait()
-
-
-def mix(held, differ, inverse, sums, near, mat, shapes, previous):
-    _, rows, features = held.shape
+        copy(mat, place(step), chunk, step).wait()
+
+    for other in left + new_copies:
+        other.wait()
+
+
+def mix(held, differ, inverse, sums, near, mat, shapes, pair, previous):
+    mats, rows, features = held.shape
     rank = sums[0].shape[0]
     chunk = chunk_of(rows, 512)
-    args = [vmem(held), differ, inverse, *sums, *near]
+    steps = rows // chunk
+    args = [vmem(held), differ, inverse, *sums, *near, *pair]
     specs = [in_vmem] * len(args) + [in_hbm] * len(previous)
     aliases = {0: 3} | {len(args) + place: place for place in range(len(previous))}
     args += [hbm(array) for array in previous]
-    return pl.pallas_call(
-        functools.partial(mix_kernel, mat, chunk),
+    shapes = (*shapes, held.shape, inverse.shape)
+    return pl.pallas_call(
+        functools.partial(mix_kernel, mat, chunk, 3 * steps // 8),
         name=f"mix{mat}",
-        out_shape=[jax.ShapeDtypeStruct(shape, f32) for shape in (*shapes, held.shape)],
+        out_shape=[jax.ShapeDtypeStruct(shape, f32) for shape in shapes],
         in_specs=specs,
-        out_specs=[in_hbm] * 3 + [in_vmem],
+        out_specs=[in_hbm] * 3 + [in_vmem] * 2,
         scratch_shapes=[
             pltpu.VMEM((rank, features), f32),
             pltpu.VMEM((rank, features), f32),
-            pltpu.SemaphoreType.DMA((rows // chunk,)),
+            pltpu.SemaphoreType.DMA((steps + 2,)),
             pltpu.SemaphoreType.DMA((2,)),
         ],
         input_output_aliases=aliases,
@@ -385,12 +413,14 @@
         *sum_mat, held = add(held, pairs[mat], rank, mat)
         sums.append(sum_mat)
         near_sums.append(exchange(sum_mat))
-    *inverses, held = inverse_factors(held, pairs, rank)
+        if mat == 0:
+            inverse, held = inverse_factor(held, pairs[0], rank)
     results = []
     shapes = (weights.shape, factors_rx.shape, factors_ry.shape)
     for mat in range(mats):
-        *results, held = mix(
-            held, differs[mat], inverses[mat], sums[mat], near_sums[mat], mat, shapes, results
+        pair = pairs[mat + 1] if mat + 1 < mats else ()
+        *results, held, inverse = mix(
+            held, differs[mat], inverse, sums[mat], near_sums[mat], mat, shapes, pair, results
         )
     return tuple(results)
 

time: 61.9 us -> 61.6 us (level)
  Pallas kernels: 38 us -> 37.3 us
    pallas_call x5, Pallas kernels: 22.9 us -> 22.2 us  [the longest x2 13.9 us: mix(): pl.pallas_call(functools.partial(mix_kernel, mat, chunk, 3 * steps // 8),...]
    ppermute x2, waiting for transfers between devices: 1.35 us -> 0.69 us  [from_partner(): return lax.ppermute(value, axis, [(i, i ^ distance) for i in range(count)])]
  transfers between devices with their start and end apart: 20 -> 20, of which waited for: 3 -> 4; matrix products, arithmetic and copies ran while one was open for 0% -> 0% of each run, Pallas kernels for 41% -> 37%
where the time goes in v6:
time: 61.6 us; the launch traced here: 61.4 us
  Pallas kernels  37.3 us (61%)
  starting transfers between devices  20.3 us (33%)
  waiting for transfers between devices  2.99 us (5%)
  between operations  0.75 us (1%)
    pallas_call x2, Pallas kernels, mix(): pl.pallas_call(functools.partial(mix_kernel, mat, chunk, 3 * steps // 8),...  13.9 us
    ppermute x16, starting transfers between devices, exchange(): swapped.append(lax.ppermute(value, axis, pairs))  13.8 us
    pallas_call x2, Pallas kernels, project(): pl.pallas_call(functools.partial(project_kernel, mat, chunk_of(rows, 1024...  11.6 us
    pallas_call x2, Pallas kernels, back(): pl.pallas_call(functools.partial(back_kernel, mat, chunk_of(rows, 4096)),...  7.62 us
    pallas_call x1, Pallas kernels, load(): pl.pallas_call(functools.partial(load_kernel, size, until), name='load',...  3.5 us
    ppermute x2, starting transfers between devices, from_partner(): return lax.ppermute(value, axis, [(i, i ^ distance) for i in range(count)])  3.35 us
    ppermute x2, starting transfers between devices, shifted(): return lax.ppermute(value, axis, pairs)  3.14 us
    ppermute x16, waiting for transfers between devices, exchange(): swapped.append(lax.ppermute(value, axis, pairs))  1.34 us
  transfers between devices with their start and end apart: 20, of which 4 were waited for; matrix products, arithmetic and copies ran while one was open for 0% of the time, Pallas kernels for 37%

profile of v6, /device:TPU:0, one launch (start us, length us, event | category | flops | bytes accessed | tf_op | source)
XLA Modules:
  0.0 61.4 jit_solution(5801408166844415474)
XLA Ops:
  0.7 0.5 collective-permute-start.1
  1.2 2.6 %collective-permute-start = (f32[1,1,2,8,1024]{4,3,2,1,0:T(8,128)}, f32[1,1,2,8,1024]{4,3,2,1,0:T(8,128)S(1)}, u32[]{:S(2)}, u32[]{:S(2)}) collective-permute-start(f32[1,1,2,8,1024]{4,3,2,1,0:T(8,128)} %f0.3), channel_id=1, source_target_pairs={{0,2},{2,4},{4,6},{6,0},{1,3},{3,5},{5,7},{7,1},{8,10},{10,12},{12... | collective-permute-start | bytes 196616 | tf_op jit(solution)/shard_map/ppermute | solution.py:57
  3.8 3.5 %load.1.same = f32[2,4096,1024]{2,1,0:T(8,128)S(1)} custom-call(f32[1,1,2,4096,1024]{4,3,2,1,0:T(8,128)} %weights.5), custom_call_target="tpu_custom_call" | custom-call | tf_op jit(solution)/shard_map/load/pallas_call | solution.py:102
  7.3 0.0 collective-permute-done.1.f3
  7.3 1.0 %collective-permute-done.f1 = f32[1,1,2,8,1024]{4,3,2,1,0:T(8,128)S(1)} collective-permute-done((f32[1,1,2,8,1024]{4,3,2,1,0:T(8,128)}, f32[1,1,2,8,1024]{4,3,2,1,0:T(8,128)S(1)}, u32[]{:S(2)}, u32[]{:S(2)}) %collective-permute-start) | collective-permute-done | bytes 65568 | tf_op jit(solution)/shard_map/ppermute | solution.py:57
  8.3 5.9 %project0.1 = (f32[8,4096]{1,0:T(8,128)S(1)}, f32[8,4096]{1,0:T(8,128)S(1)}, f32[8,4096]{1,0:T(8,128)S(1)}, f32[8,4096]{1,0:T(8,128)S(1)}, f32[2,4096,1024]{2,1,0:T(8,128)S(1)}) custom-call(f32[2,4096,1024]{2,1,0:T(8,128)S(1)} %load.1.same, f32[1,1,2,8,1024]{4,3,2,1,0:T(8,128)S(1)} %copy-done, ...), custom_call_target="tpu_custom_call", output_to_operand_aliasing={{4}: (0, {})} | custom-call | flops 4294967296 | bytes 33554432 | tf_op jit(solution)/shard_map/project0/pallas_call | solution.py:157
  14.2 2.3 %collective-permute-start.2 = (f32[8,4096]{1,0:T(8,128)S(1)}, f32[8,4096]{1,0:T(8,128)S(1)}, u32[]{:S(2)}, u32[]{:S(2)}) collective-permute-start(f32[8,4096]{1,0:T(8,128)S(1)} %get-tuple-element.41.o0), channel_id=1, source_target_pairs={{0,6},{2,4},{4,2},{6,0},{1,7},{3,5},{5,3},{7,1},{8,14},{10,12},{12... | collective-permute-start | bytes 393224 | tf_op jit(solution)/shard_map/ppermute | solution.py:71
  16.5 0.0 collective-permute-start.3
  16.5 0.8 %collective-permute-start.4 = (f32[8,4096]{1,0:T(8,128)S(1)}, f32[8,4096]{1,0:T(8,128)S(1)}, u32[]{:S(2)}, u32[]{:S(2)}) collective-permute-start(f32[8,4096]{1,0:T(8,128)S(1)} %get-tuple-element.43.o2), channel_id=1, source_target_pairs={{0,24},{8,16},{16,8},{24,0},{1,25},{9,17},{17,9},{25,1},{2,26},{10... | collective-permute-start | bytes 393224 | tf_op jit(solution)/shard_map/ppermute | solution.py:71
  17.3 0.9 %collective-permute-start.5 = (f32[8,4096]{1,0:T(8,128)S(1)}, f32[8,4096]{1,0:T(8,128)S(1)}, u32[]{:S(2)}, u32[]{:S(2)}) collective-permute-start(f32[8,4096]{1,0:T(8,128)S(1)} %get-tuple-element.44.o3), channel_id=1, source_target_pairs={{0,8},{8,0},{16,24},{24,16},{1,9},{9,1},{17,25},{25,17},{2,10},{10... | collective-permute-start | bytes 393224 | tf_op jit(solution)/shard_map/ppermute | solution.py:71
  18.2 5.7 %project1.1 = (f32[8,4096]{1,0:T(8,128)S(1)}, f32[8,4096]{1,0:T(8,128)S(1)}, f32[8,4096]{1,0:T(8,128)S(1)}, f32[8,4096]{1,0:T(8,128)S(1)}, f32[2,4096,1024]{2,1,0:T(8,128)S(1)}) custom-call(f32[2,4096,1024]{2,1,0:T(8,128)S(1)} %get-tuple-element.39.same, f32[1,1,2,8,1024]{4,3,2,1,0:T(8,128)S(1)} %copy-done, ...), custom_call_target="tpu_custom_call", output_to_operand_aliasing={{4}: (0, {})} | custom-call | flops 4294967296 | bytes 33554432 | tf_op jit(solution)/shard_map/project1/pallas_call | solution.py:157
  23.9 2.1 %collective-permute-start.6 = (f32[8,4096]{1,0:T(8,128)S(1)}, f32[8,4096]{1,0:T(8,128)S(1)}, u32[]{:S(2)}, u32[]{:S(2)}) collective-permute-start(f32[8,4096]{1,0:T(8,128)S(1)} %get-tuple-element.46.o0), channel_id=1, source_target_pairs={{0,6},{2,4},{4,2},{6,0},{1,7},{3,5},{5,3},{7,1},{8,14},{10,12},{12... | collective-permute-start | bytes 393224 | tf_op jit(solution)/shard_map/ppermute | solution.py:71
  26.1 0.0 collective-permute-done.2.n0
  26.1 1.1 %collective-permute-start.7 = (f32[8,4096]{1,0:T(8,128)S(1)}, f32[8,4096]{1,0:T(8,128)S(1)}, u32[]{:S(2)}, u32[]{:S(2)}) collective-permute-start(f32[8,4096]{1,0:T(8,128)S(1)} %get-tuple-element.47.o1), channel_id=1, source_target_pairs={{0,2},{2,0},{4,6},{6,4},{1,3},{3,1},{5,7},{7,5},{8,10},{10,8},{12,... | collective-permute-start | bytes 393224 | tf_op jit(solution)/shard_map/ppermute | solution.py:71
  27.2 0.0 collective-permute-done.3.n1
  27.2 0.0 collective-permute-start.8
  27.2 0.0 collective-permute-done.4.n2
  27.2 0.1 collective-permute-start.9
  27.3 0.0 collective-permute-done.5.n3
  27.3 3.8 %back0.1 = (f32[32,4096]{1,0:T(8,128)S(1)}, f32[32,1152]{1,0:T(8,128)S(1)}, f32[2,4096,1024]{2,1,0:T(8,128)S(1)}) custom-call(f32[2,4096,1024]{2,1,0:T(8,128)S(1)} %get-tuple-element.40.same, f32[8,4096]{1,0:T(8,128)S(1)} %get-tuple-element.41.o0, f32[8,4096]{1,0:T(8,128)S(1)} %get-tuple-element.42.o1, ...), custom_call_target="tpu_custom_call", output_to_operand_aliasing={{2}: (0, {})} | custom-call | flops 4294967296 | bytes 33554432 | tf_op jit(solution)/shard_map/back0/pallas_call | solution.py:205
  31.1 1.8 %collective-permute-start.10 = (f32[32,1152]{1,0:T(8,128)S(1)}, f32[32,1152]{1,0:T(8,128)S(1)}, u32[]{:S(2)}, u32[]{:S(2)}) collective-permute-start(f32[32,1152]{1,0:T(8,128)S(1)} %get-tuple-element.51.mine), channel_id=1, source_target_pairs={{0,1},{1,0},{2,3},{3,2},{4,5},{5,4},{6,7},{7,6},{8,9},{9,8},{10,11... | collective-permute-start | bytes 442376 | tf_op jit(solution)/shard_map/ppermute | solution.py:62
  32.9 0.0 collective-permute-done.6.n0
  32.9 1.1 %collective-permute-done.7.n1 = f32[8,4096]{1,0:T(8,128)S(1)} collective-permute-done((f32[8,4096]{1,0:T(8,128)S(1)}, f32[8,4096]{1,0:T(8,128)S(1)}, u32[]{:S(2)}, u32[]{:S(2)}) %collective-permute-start.7) | collective-permute-done | bytes 131104 | tf_op jit(solution)/shard_map/ppermute | solution.py:71
  34.0 0.0 collective-permute-done.8.n2
  34.0 0.0 collective-permute-done.9.n3
  34.0 3.8 %back1.1 = (f32[32,4096]{1,0:T(8,128)S(1)}, f32[32,1152]{1,0:T(8,128)S(1)}, f32[2,4096,1024]{2,1,0:T(8,128)S(1)}) custom-call(f32[2,4096,1024]{2,1,0:T(8,128)S(1)} %get-tuple-element.45.same, f32[8,4096]{1,0:T(8,128)S(1)} %get-tuple-element.46.o0, f32[8,4096]{1,0:T(8,128)S(1)} %get-tuple-element.47.o1, ...), custom_call_target="tpu_custom_call", output_to_operand_aliasing={{2}: (0, {})} | custom-call | flops 4294967296 | bytes 33554432 | tf_op jit(solution)/shard_map/back1/pallas_call | solution.py:205
  37.8 1.5 %collective-permute-start.11 = (f32[32,1152]{1,0:T(8,128)S(1)}, f32[32,1152]{1,0:T(8,128)S(1)}, u32[]{:S(2)}, u32[]{:S(2)}) collective-permute-start(f32[32,1152]{1,0:T(8,128)S(1)} %get-tuple-element.54.mine.refs_8_), channel_id=1, source_target_pairs={{0,1},{1,0},{2,3},{3,2},{4,5},{5,4},{6,7},{7,6},{8,9},{9,8},{10,11... | collective-permute-start | bytes 442376 | tf_op jit(solution)/shard_map/ppermute | solution.py:62
  39.3 0.0 collective-permute-done.10.other
  39.4 1.8 %collective-permute-start.12 = (f32[8,1024]{1,0:T(8,128)S(1)}, f32[8,1024]{1,0:T(8,128)S(1)}, u32[]{:S(2)}, u32[]{:S(2)}) collective-permute-start(f32[8,1024]{1,0:T(8,128)S(1)} %get-tuple-element.58.refs_0_), channel_id=1, source_target_pairs={{0,6},{2,4},{4,2},{6,0},{1,7},{3,5},{5,3},{7,1},{8,14},{10,12},{12... | collective-permute-start | bytes 98312 | tf_op jit(solution)/shard_map/ppermute | solution.py:71
  41.2 0.0 collective-permute-start.13
  41.2 0.0 collective-permute-start.14
  41.2 1.0 %collective-permute-start.15 = (f32[8,1024]{1,0:T(8,128)S(1)}, f32[8,1024]{1,0:T(8,128)S(1)}, u32[]{:S(2)}, u32[]{:S(2)}) collective-permute-start(f32[8,1024]{1,0:T(8,128)S(1)} %get-tuple-element.61.refs_3_), channel_id=1, source_target_pairs={{0,8},{8,0},{16,24},{24,16},{1,9},{9,1},{17,25},{25,17},{2,10},{10... | collective-permute-start | bytes 98312 | tf_op jit(solution)/shard_map/ppermute | solution.py:71
  42.1 0.7 %inverse.1 = (f32[32,128]{1,0:T(8,128)S(1)}, f32[2,4096,1024]{2,1,0:T(8,128)S(1)}) custom-call(f32[2,4096,1024]{2,1,0:T(8,128)S(1)} %get-tuple-element.52.same, f32[32,1152]{1,0:T(8,128)S(1)} %get-tuple-element.51.mine, f32[32,1152]{1,0:T(8,128)S(1)} %collective-permute-done.10.other), custom_call_target="tpu_custom_call", output_to_operand_aliasing={{1}: (0, {})} | custom-call | tf_op jit(solution)/shard_map/inverse/pallas_call | solution.py:264
  42.8 0.7 %collective-permute-done.11.other.refs_9_ = f32[32,1152]{1,0:T(8,128)S(1)} collective-permute-done((f32[32,1152]{1,0:T(8,128)S(1)}, f32[32,1152]{1,0:T(8,128)S(1)}, u32[]{:S(2)}, u32[]{:S(2)}) %collective-permute-start.11) | collective-permute-done | bytes 147488 | tf_op jit(solution)/shard_map/ppermute | solution.py:62
  43.5 1.5 %collective-permute-start.16 = (f32[8,1024]{1,0:T(8,128)S(1)}, f32[8,1024]{1,0:T(8,128)S(1)}, u32[]{:S(2)}, u32[]{:S(2)}) collective-permute-start(f32[8,1024]{1,0:T(8,128)S(1)} %get-tuple-element.65.refs_0_), channel_id=1, source_target_pairs={{0,6},{2,4},{4,2},{6,0},{1,7},{3,5},{5,3},{7,1},{8,14},{10,12},{12... | collective-permute-start | bytes 98312 | tf_op jit(solution)/shard_map/ppermute | solution.py:71
  45.0 0.2 collective-permute-done.12.refs_4_
  45.2 0.4 collective-permute-start.17
  45.7 0.0 collective-permute-done.13.refs_5_
  45.7 0.6 %collective-permute-start.18 = (f32[8,1024]{1,0:T(8,128)S(1)}, f32[8,1024]{1,0:T(8,128)S(1)}, u32[]{:S(2)}, u32[]{:S(2)}) collective-permute-start(f32[8,1024]{1,0:T(8,128)S(1)} %get-tuple-element.67.refs_2_), channel_id=1, source_target_pairs={{0,24},{8,16},{16,8},{24,0},{1,25},{9,17},{17,9},{25,1},{2,26},{10... | collective-permute-start | bytes 98312 | tf_op jit(solution)/shard_map/ppermute | solution.py:71
  46.3 0.0 collective-permute-done.14.refs_6_
  46.3 1.1 %collective-permute-start.19 = (f32[8,1024]{1,0:T(8,128)S(1)}, f32[8,1024]{1,0:T(8,128)S(1)}, u32[]{:S(2)}, u32[]{:S(2)}) collective-permute-start(f32[8,1024]{1,0:T(8,128)S(1)} %get-tuple-element.68.refs_3_), channel_id=1, source_target_pairs={{0,8},{8,0},{16,24},{24,16},{1,9},{9,1},{17,25},{25,17},{2,10},{10... | collective-permute-start | bytes 98312 | tf_op jit(solution)/shard_map/ppermute | solution.py:71
  47.4 0.0 collective-permute-done.15.refs_7_
  47.4 5.4 %mix0.1 = (f32[1,1,2,4096,1024]{4,3,2,1,0:T(8,128)}, f32[1,1,2,8,1024]{4,3,2,1,0:T(8,128)}, f32[1,1,2,8,1024]{4,3,2,1,0:T(8,128)}, f32[2,4096,1024]{2,1,0:T(8,128)S(1)}, f32[32,128]{1,0:T(8,128)S(1)}) custom-call(f32[2,4096,1024]{2,1,0:T(8,128)S(1)} %get-tuple-element.55.same, ...), custom_call_target="tpu_custom_call", output_to_operand_aliasing={{3}: (0, {})} | custom-call | flops 4294967296 | bytes 33554432 | tf_op jit(solution)/shard_map/mix0/pallas_call | solution.py:365
  52.8 0.0 collective-permute-done.16.refs_4_
  52.8 0.0 collective-permute-done.17.refs_5_
  52.9 0.0 collective-permute-done.18.refs_6_
  52.9 0.0 collective-permute-done.19.refs_7_
  52.9 8.5 %mix1.1 = (f32[1,1,2,4096,1024]{4,3,2,1,0:T(8,128)}, f32[1,1,2,8,1024]{4,3,2,1,0:T(8,128)}, f32[1,1,2,8,1024]{4,3,2,1,0:T(8,128)}, f32[2,4096,1024]{2,1,0:T(8,128)S(1)}, f32[32,128]{1,0:T(8,128)}) custom-call(f32[2,4096,1024]{2,1,0:T(8,128)S(1)} %get-tuple-element.62.same, ...), custom_call_target="tpu_custom_call", output_to_operand_aliasing={{3}: (0, {}), {0}: (11, {}), {1}: (12, {}), {2}: (13, {})} | custom-call | flops 4294967296 | bytes 33554432 | tf_op jit(solution)/shard_map/mix1/pallas_call | solution.py:365
  (6 shorter events, 0.0 us)
Async XLA Ops:
  0.6 7.6 %copy-start.1 = (f32[1,1,2,8,1024]{4,3,2,1,0:T(8,128)S(1)}, f32[1,1,2,8,1024]{4,3,2,1,0:T(8,128)}, u32[]{:S(2)}) copy-start(f32[1,1,2,8,1024]{4,3,2,1,0:T(8,128)} %f2.3) | copy-start | bytes 196612
  0.6 7.6 %copy-start = (f32[1,1,2,8,1024]{4,3,2,1,0:T(8,128)S(1)}, f32[1,1,2,8,1024]{4,3,2,1,0:T(8,128)}, u32[]{:S(2)}) copy-start(f32[1,1,2,8,1024]{4,3,2,1,0:T(8,128)} %f0.3) | copy-start | bytes 196612
  0.7 6.7 %collective-permute-start.1 = (f32[1,1,2,8,1024]{4,3,2,1,0:T(8,128)}, f32[1,1,2,8,1024]{4,3,2,1,0:T(8,128)S(1)}, u32[]{:S(2)}, u32[]{:S(2)}) collective-permute-start(f32[1,1,2,8,1024]{4,3,2,1,0:T(8,128)} %f2.3), channel_id=1, source_target_pairs={{0,8},{8,16},{16,24},{24,0},{1,9},{9,17},{17,25},{25,1},{2,10},{10... | collective-permute-start | bytes 196616 | tf_op jit(solution)/shard_map/ppermute | solution.py:57
  1.2 7.1 %collective-permute-start = (f32[1,1,2,8,1024]{4,3,2,1,0:T(8,128)}, f32[1,1,2,8,1024]{4,3,2,1,0:T(8,128)S(1)}, u32[]{:S(2)}, u32[]{:S(2)}) collective-permute-start(f32[1,1,2,8,1024]{4,3,2,1,0:T(8,128)} %f0.3), channel_id=1, source_target_pairs={{0,2},{2,4},{4,6},{6,0},{1,3},{3,5},{5,7},{7,1},{8,10},{10,12},{12... | collective-permute-start | bytes 196616 | tf_op jit(solution)/shard_map/ppermute | solution.py:57
  14.2 11.8 %collective-permute-start.2 = (f32[8,4096]{1,0:T(8,128)S(1)}, f32[8,4096]{1,0:T(8,128)S(1)}, u32[]{:S(2)}, u32[]{:S(2)}) collective-permute-start(f32[8,4096]{1,0:T(8,128)S(1)} %get-tuple-element.41.o0), channel_id=1, source_target_pairs={{0,6},{2,4},{4,2},{6,0},{1,7},{3,5},{5,3},{7,1},{8,14},{10,12},{12... | collective-permute-start | bytes 393224 | tf_op jit(solution)/shard_map/ppermute | solution.py:71
  16.5 10.7 %collective-permute-start.3 = (f32[8,4096]{1,0:T(8,128)S(1)}, f32[8,4096]{1,0:T(8,128)S(1)}, u32[]{:S(2)}, u32[]{:S(2)}) collective-permute-start(f32[8,4096]{1,0:T(8,128)S(1)} %get-tuple-element.42.o1), channel_id=1, source_target_pairs={{0,2},{2,0},{4,6},{6,4},{1,3},{3,1},{5,7},{7,5},{8,10},{10,8},{12,... | collective-permute-start | bytes 393224 | tf_op jit(solution)/shard_map/ppermute | solution.py:71
  16.5 10.7 %collective-permute-start.4 = (f32[8,4096]{1,0:T(8,128)S(1)}, f32[8,4096]{1,0:T(8,128)S(1)}, u32[]{:S(2)}, u32[]{:S(2)}) collective-permute-start(f32[8,4096]{1,0:T(8,128)S(1)} %get-tuple-element.43.o2), channel_id=1, source_target_pairs={{0,24},{8,16},{16,8},{24,0},{1,25},{9,17},{17,9},{25,1},{2,26},{10... | collective-permute-start | bytes 393224 | tf_op jit(solution)/shard_map/ppermute | solution.py:71
  17.3 9.9 %collective-permute-start.5 = (f32[8,4096]{1,0:T(8,128)S(1)}, f32[8,4096]{1,0:T(8,128)S(1)}, u32[]{:S(2)}, u32[]{:S(2)}) collective-permute-start(f32[8,4096]{1,0:T(8,128)S(1)} %get-tuple-element.44.o3), channel_id=1, source_target_pairs={{0,8},{8,0},{16,24},{24,16},{1,9},{9,1},{17,25},{25,17},{2,10},{10... | collective-permute-start | bytes 393224 | tf_op jit(solution)/shard_map/ppermute | solution.py:71
  23.9 9.0 %collective-permute-start.6 = (f32[8,4096]{1,0:T(8,128)S(1)}, f32[8,4096]{1,0:T(8,128)S(1)}, u32[]{:S(2)}, u32[]{:S(2)}) collective-permute-start(f32[8,4096]{1,0:T(8,128)S(1)} %get-tuple-element.46.o0), channel_id=1, source_target_pairs={{0,6},{2,4},{4,2},{6,0},{1,7},{3,5},{5,3},{7,1},{8,14},{10,12},{12... | collective-permute-start | bytes 393224 | tf_op jit(solution)/shard_map/ppermute | solution.py:71
  26.1 7.9 %collective-permute-start.7 = (f32[8,4096]{1,0:T(8,128)S(1)}, f32[8,4096]{1,0:T(8,128)S(1)}, u32[]{:S(2)}, u32[]{:S(2)}) collective-permute-start(f32[8,4096]{1,0:T(8,128)S(1)} %get-tuple-element.47.o1), channel_id=1, source_target_pairs={{0,2},{2,0},{4,6},{6,4},{1,3},{3,1},{5,7},{7,5},{8,10},{10,8},{12,... | collective-permute-start | bytes 393224 | tf_op jit(solution)/shard_map/ppermute | solution.py:71
  27.2 6.8 %collective-permute-start.8 = (f32[8,4096]{1,0:T(8,128)S(1)}, f32[8,4096]{1,0:T(8,128)S(1)}, u32[]{:S(2)}, u32[]{:S(2)}) collective-permute-start(f32[8,4096]{1,0:T(8,128)S(1)} %get-tuple-element.48.o2), channel_id=1, source_target_pairs={{0,24},{8,16},{16,8},{24,0},{1,25},{9,17},{17,9},{25,1},{2,26},{10... | collective-permute-start | bytes 393224 | tf_op jit(solution)/shard_map/ppermute | solution.py:71
  27.2 6.8 %collective-permute-start.9 = (f32[8,4096]{1,0:T(8,128)S(1)}, f32[8,4096]{1,0:T(8,128)S(1)}, u32[]{:S(2)}, u32[]{:S(2)}) collective-permute-start(f32[8,4096]{1,0:T(8,128)S(1)} %get-tuple-element.49.o3), channel_id=1, source_target_pairs={{0,8},{8,0},{16,24},{24,16},{1,9},{9,1},{17,25},{25,17},{2,10},{10... | collective-permute-start | bytes 393224 | tf_op jit(solution)/shard_map/ppermute | solution.py:71
  31.1 8.2 %collective-permute-start.10 = (f32[32,1152]{1,0:T(8,128)S(1)}, f32[32,1152]{1,0:T(8,128)S(1)}, u32[]{:S(2)}, u32[]{:S(2)}) collective-permute-start(f32[32,1152]{1,0:T(8,128)S(1)} %get-tuple-element.51.mine), channel_id=1, source_target_pairs={{0,1},{1,0},{2,3},{3,2},{4,5},{5,4},{6,7},{7,6},{8,9},{9,8},{10,11... | collective-permute-start | bytes 442376 | tf_op jit(solution)/shard_map/ppermute | solution.py:62
  37.8 5.7 %collective-permute-start.11 = (f32[32,1152]{1,0:T(8,128)S(1)}, f32[32,1152]{1,0:T(8,128)S(1)}, u32[]{:S(2)}, u32[]{:S(2)}) collective-permute-start(f32[32,1152]{1,0:T(8,128)S(1)} %get-tuple-element.54.mine.refs_8_), channel_id=1, source_target_pairs={{0,1},{1,0},{2,3},{3,2},{4,5},{5,4},{6,7},{7,6},{8,9},{9,8},{10,11... | collective-permute-start | bytes 442376 | tf_op jit(solution)/shard_map/ppermute | solution.py:62
  39.4 5.9 %collective-permute-start.12 = (f32[8,1024]{1,0:T(8,128)S(1)}, f32[8,1024]{1,0:T(8,128)S(1)}, u32[]{:S(2)}, u32[]{:S(2)}) collective-permute-start(f32[8,1024]{1,0:T(8,128)S(1)} %get-tuple-element.58.refs_0_), channel_id=1, source_target_pairs={{0,6},{2,4},{4,2},{6,0},{1,7},{3,5},{5,3},{7,1},{8,14},{10,12},{12... | collective-permute-start | bytes 98312 | tf_op jit(solution)/shard_map/ppermute | solution.py:71
  41.2 4.5 %collective-permute-start.13 = (f32[8,1024]{1,0:T(8,128)S(1)}, f32[8,1024]{1,0:T(8,128)S(1)}, u32[]{:S(2)}, u32[]{:S(2)}) collective-permute-start(f32[8,1024]{1,0:T(8,128)S(1)} %get-tuple-element.59.refs_1_), channel_id=1, source_target_pairs={{0,2},{2,0},{4,6},{6,4},{1,3},{3,1},{5,7},{7,5},{8,10},{10,8},{12,... | collective-permute-start | bytes 98312 | tf_op jit(solution)/shard_map/ppermute | solution.py:71
  41.2 5.2 %collective-permute-start.14 = (f32[8,1024]{1,0:T(8,128)S(1)}, f32[8,1024]{1,0:T(8,128)S(1)}, u32[]{:S(2)}, u32[]{:S(2)}) collective-permute-start(f32[8,1024]{1,0:T(8,128)S(1)} %get-tuple-element.60.refs_2_), channel_id=1, source_target_pairs={{0,24},{8,16},{16,8},{24,0},{1,25},{9,17},{17,9},{25,1},{2,26},{10... | collective-permute-start | bytes 98312 | tf_op jit(solution)/shard_map/ppermute | solution.py:71
  41.2 6.2 %collective-permute-start.15 = (f32[8,1024]{1,0:T(8,128)S(1)}, f32[8,1024]{1,0:T(8,128)S(1)}, u32[]{:S(2)}, u32[]{:S(2)}) collective-permute-start(f32[8,1024]{1,0:T(8,128)S(1)} %get-tuple-element.61.refs_3_), channel_id=1, source_target_pairs={{0,8},{8,0},{16,24},{24,16},{1,9},{9,1},{17,25},{25,17},{2,10},{10... | collective-permute-start | bytes 98312 | tf_op jit(solution)/shard_map/ppermute | solution.py:71
  43.5 9.3 %collective-permute-start.16 = (f32[8,1024]{1,0:T(8,128)S(1)}, f32[8,1024]{1,0:T(8,128)S(1)}, u32[]{:S(2)}, u32[]{:S(2)}) collective-permute-start(f32[8,1024]{1,0:T(8,128)S(1)} %get-tuple-element.65.refs_0_), channel_id=1, source_target_pairs={{0,6},{2,4},{4,2},{6,0},{1,7},{3,5},{5,3},{7,1},{8,14},{10,12},{12... | collective-permute-start | bytes 98312 | tf_op jit(solution)/shard_map/ppermute | solution.py:71
  45.2 7.6 %collective-permute-start.17 = (f32[8,1024]{1,0:T(8,128)S(1)}, f32[8,1024]{1,0:T(8,128)S(1)}, u32[]{:S(2)}, u32[]{:S(2)}) collective-permute-start(f32[8,1024]{1,0:T(8,128)S(1)} %get-tuple-element.66.refs_1_), channel_id=1, source_target_pairs={{0,2},{2,0},{4,6},{6,4},{1,3},{3,1},{5,7},{7,5},{8,10},{10,8},{12,... | collective-permute-start | bytes 98312 | tf_op jit(solution)/shard_map/ppermute | solution.py:71
  45.7 7.2 %collective-permute-start.18 = (f32[8,1024]{1,0:T(8,128)S(1)}, f32[8,1024]{1,0:T(8,128)S(1)}, u32[]{:S(2)}, u32[]{:S(2)}) collective-permute-start(f32[8,1024]{1,0:T(8,128)S(1)} %get-tuple-element.67.refs_2_), channel_id=1, source_target_pairs={{0,24},{8,16},{16,8},{24,0},{1,25},{9,17},{17,9},{25,1},{2,26},{10... | collective-permute-start | bytes 98312 | tf_op jit(solution)/shard_map/ppermute | solution.py:71
  46.3 6.5 %collective-permute-start.19 = (f32[8,1024]{1,0:T(8,128)S(1)}, f32[8,1024]{1,0:T(8,128)S(1)}, u32[]{:S(2)}, u32[]{:S(2)}) collective-permute-start(f32[8,1024]{1,0:T(8,128)S(1)} %get-tuple-element.68.refs_3_), channel_id=1, source_target_pairs={{0,8},{8,0},{16,24},{24,16},{1,9},{9,1},{17,25},{25,17},{2,10},{10... | collective-permute-start | bytes 98312 | tf_op jit(solution)/shard_map/ppermute | solution.py:71

commit v7 on v6

--- a/solution.py
+++ b/solution.py
@@ -49,6 +49,12 @@
     while rows % size:
         size //= 2
     return size
+
+
+def chunks_of(rows, size):
+    if rows % (4 * size):
+        return [(0, rows)]
+    return [(0, rows // 2), (rows // 2, rows // 4), (3 * rows // 4, rows // 4)]
 
 
 def shifted(value, axis, steps):
@@ -275,9 +281,9 @@
     )(vmem(held), *pair)
 
 
-def mix_kernel(mat, chunk, late, same, differ, inverse, *refs):
-    sums, near = refs[:edges], refs[edges : 2 * edges]
-    mixed, next_rx, next_ry, held, following, new_rx, new_ry, sems, new_sems = refs[-9:]
+def mix_kernel(mat, chunk, late, same, differ, *refs):
+    sums, near, factors = refs[:edges], refs[edges : 2 * edges], refs[2 * edges :]
+    mixed, next_rx, next_ry, held, new_rx, new_ry, sems, new_sems = refs[-8:]
     rank = sums[0].shape[0]
     width = edges * rank
     mats, rows, _ = held.shape
@@ -293,7 +299,11 @@
     left = [copy(mat - 1, rows - late * chunk, late * chunk, steps)] if mat and late else []
     for other in left:
         other.start()
-    factor = inverse[:, width : 2 * width]
+    if mat:
+        factor = inverse_of(factors[0][:, -128:] + factors[1][:, -128:], rank)
+    else:
+        factor = factors[0][...]
+    factor = factor[:, width : 2 * width]
     total = jnp.concatenate([b[...] + n[...] for b, n in zip(sums, near)], 0)
     updated = lax.dot_general(
         factor, total, NN, precision=lax.Precision.HIGHEST, preferred_element_type=f32
@@ -336,11 +346,6 @@
     ]
     for new_copy in new_copies:
         new_copy.start()
-    if mat < mats - 1:
-        gram, gram_other = refs[2 * edges : 2 * edges + 2]
-        following[...] = inverse_of(gram[:, -128:] + gram_other[:, -128:], rank)
-    else:
-        following[...] = inverse[...]
     for half in halves:
         half.wait()
 
@@ -352,22 +357,22 @@
         other.wait()
 
 
-def mix(held, differ, inverse, sums, near, mat, shapes, pair, previous):
+def mix(held, differ, factors, sums, near, mat, shapes, previous):
     mats, rows, features = held.shape
     rank = sums[0].shape[0]
     chunk = chunk_of(rows, 512)
     steps = rows // chunk
-    args = [vmem(held), differ, inverse, *sums, *near, *pair]
+    args = [vmem(held), differ, *sums, *near, *factors]
     specs = [in_vmem] * len(args) + [in_hbm] * len(previous)
     aliases = {0: 3} | {len(args) + place: place for place in range(len(previous))}
     args += [hbm(array) for array in previous]
-    shapes = (*shapes, held.shape, inverse.shape)
+    shapes = (*shapes, held.shape)
     return pl.pallas_call(
         functools.partial(mix_kernel, mat, chunk, 3 * steps // 8),
         name=f"mix{mat}",
         out_shape=[jax.ShapeDtypeStruct(shape, f32) for shape in shapes],
         in_specs=specs,
-        out_specs=[in_hbm] * 3 + [in_vmem] * 2,
+        out_specs=[in_hbm] * 3 + [in_vmem],
         scratch_shapes=[
             pltpu.VMEM((rank, features), f32),
             pltpu.VMEM((rank, features), f32),
@@ -418,9 +423,9 @@
     results = []
     shapes = (weights.shape, factors_rx.shape, factors_ry.shape)
     for mat in range(mats):
-        pair = pairs[mat + 1] if mat + 1 < mats else ()
-        *results, held, inverse = mix(
-            held, differs[mat], inverse, sums[mat], near_sums[mat], mat, shapes, pair, results
+        factor = pairs[mat] if mat else [inverse]
+        *results, held = mix(
+            held, differs[mat], factor, sums[mat], near_sums[mat], mat, shapes, results
         )
     return tuple(results)
 

time: 61.6 us -> 60.4 us (0.981)
  Pallas kernels: 37.3 us -> 36.2 us
    pallas_call x2, Pallas kernels: 13.9 us -> 12.8 us  [mix(): pl.pallas_call(functools.partial(mix_kernel, mat, chunk, 3 * steps // 8),...]
where the time goes in v7:
time: 60.4 us; the launch traced here: 60.2 us
  Pallas kernels  36.2 us (60%)
  starting transfers between devices  20.3 us (34%)
  waiting for transfers between devices  2.99 us (5%)
  between operations  0.75 us (1%)
    ppermute x16, starting transfers between devices, exchange(): swapped.append(lax.ppermute(value, axis, pairs))  13.8 us
    pallas_call x2, Pallas kernels, mix(): pl.pallas_call(functools.partial(mix_kernel, mat, chunk, 3 * steps // 8),...  12.8 us
    pallas_call x2, Pallas kernels, project(): pl.pallas_call(functools.partial(project_kernel, mat, chunk_of(rows, 1024...  11.6 us
    pallas_call x2, Pallas kernels, back(): pl.pallas_call(functools.partial(back_kernel, mat, chunk_of(rows, 4096)),...  7.62 us
    pallas_call x1, Pallas kernels, load(): pl.pallas_call(functools.partial(load_kernel, size, until), name='load',...  3.5 us
    ppermute x2, starting transfers between devices, from_partner(): return lax.ppermute(value, axis, [(i, i ^ distance) for i in range(count)])  3.35 us
    ppermute x2, starting transfers between devices, shifted(): return lax.ppermute(value, axis, pairs)  3.14 us
    ppermute x16, waiting for transfers between devices, exchange(): swapped.append(lax.ppermute(value, axis, pairs))  1.34 us
  transfers between devices with their start and end apart: 20, of which 4 were waited for; matrix products, arithmetic and copies ran while one was open for 0% of the time, Pallas kernels for 37%

profile of v7, /device:TPU:0, one launch (start us, length us, event | category | flops | bytes accessed | tf_op | source)
XLA Modules:
  0.0 60.2 jit_solution(4533400584971773967)
XLA Ops:
  0.7 0.5 collective-permute-start.1
  1.2 2.6 %collective-permute-start = (f32[1,1,2,8,1024]{4,3,2,1,0:T(8,128)}, f32[1,1,2,8,1024]{4,3,2,1,0:T(8,128)S(1)}, u32[]{:S(2)}, u32[]{:S(2)}) collective-permute-start(f32[1,1,2,8,1024]{4,3,2,1,0:T(8,128)} %f0.3), channel_id=1, source_target_pairs={{0,2},{2,4},{4,6},{6,0},{1,3},{3,5},{5,7},{7,1},{8,10},{10,12},{12... | collective-permute-start | bytes 196616 | tf_op jit(solution)/shard_map/ppermute | solution.py:63
  3.8 3.5 %load.1.same = f32[2,4096,1024]{2,1,0:T(8,128)S(1)} custom-call(f32[1,1,2,4096,1024]{4,3,2,1,0:T(8,128)} %weights.5), custom_call_target="tpu_custom_call" | custom-call | tf_op jit(solution)/shard_map/load/pallas_call | solution.py:108
  7.3 0.0 collective-permute-done.1.f3
  7.3 1.0 %collective-permute-done.f1 = f32[1,1,2,8,1024]{4,3,2,1,0:T(8,128)S(1)} collective-permute-done((f32[1,1,2,8,1024]{4,3,2,1,0:T(8,128)}, f32[1,1,2,8,1024]{4,3,2,1,0:T(8,128)S(1)}, u32[]{:S(2)}, u32[]{:S(2)}) %collective-permute-start) | collective-permute-done | bytes 65568 | tf_op jit(solution)/shard_map/ppermute | solution.py:63
  8.3 5.9 %project0.1 = (f32[8,4096]{1,0:T(8,128)S(1)}, f32[8,4096]{1,0:T(8,128)S(1)}, f32[8,4096]{1,0:T(8,128)S(1)}, f32[8,4096]{1,0:T(8,128)S(1)}, f32[2,4096,1024]{2,1,0:T(8,128)S(1)}) custom-call(f32[2,4096,1024]{2,1,0:T(8,128)S(1)} %load.1.same, f32[1,1,2,8,1024]{4,3,2,1,0:T(8,128)S(1)} %copy-done, ...), custom_call_target="tpu_custom_call", output_to_operand_aliasing={{4}: (0, {})} | custom-call | flops 4294967296 | bytes 33554432 | tf_op jit(solution)/shard_map/project0/pallas_call | solution.py:163
  14.2 2.3 %collective-permute-start.2 = (f32[8,4096]{1,0:T(8,128)S(1)}, f32[8,4096]{1,0:T(8,128)S(1)}, u32[]{:S(2)}, u32[]{:S(2)}) collective-permute-start(f32[8,4096]{1,0:T(8,128)S(1)} %get-tuple-element.40.o0), channel_id=1, source_target_pairs={{0,6},{2,4},{4,2},{6,0},{1,7},{3,5},{5,3},{7,1},{8,14},{10,12},{12... | collective-permute-start | bytes 393224 | tf_op jit(solution)/shard_map/ppermute | solution.py:77
  16.5 0.0 collective-permute-start.3
  16.5 0.8 %collective-permute-start.4 = (f32[8,4096]{1,0:T(8,128)S(1)}, f32[8,4096]{1,0:T(8,128)S(1)}, u32[]{:S(2)}, u32[]{:S(2)}) collective-permute-start(f32[8,4096]{1,0:T(8,128)S(1)} %get-tuple-element.42.o2), channel_id=1, source_target_pairs={{0,24},{8,16},{16,8},{24,0},{1,25},{9,17},{17,9},{25,1},{2,26},{10... | collective-permute-start | bytes 393224 | tf_op jit(solution)/shard_map/ppermute | solution.py:77
  17.3 0.9 %collective-permute-start.5 = (f32[8,4096]{1,0:T(8,128)S(1)}, f32[8,4096]{1,0:T(8,128)S(1)}, u32[]{:S(2)}, u32[]{:S(2)}) collective-permute-start(f32[8,4096]{1,0:T(8,128)S(1)} %get-tuple-element.43.o3), channel_id=1, source_target_pairs={{0,8},{8,0},{16,24},{24,16},{1,9},{9,1},{17,25},{25,17},{2,10},{10... | collective-permute-start | bytes 393224 | tf_op jit(solution)/shard_map/ppermute | solution.py:77
  18.2 5.7 %project1.1 = (f32[8,4096]{1,0:T(8,128)S(1)}, f32[8,4096]{1,0:T(8,128)S(1)}, f32[8,4096]{1,0:T(8,128)S(1)}, f32[8,4096]{1,0:T(8,128)S(1)}, f32[2,4096,1024]{2,1,0:T(8,128)S(1)}) custom-call(f32[2,4096,1024]{2,1,0:T(8,128)S(1)} %get-tuple-element.38.same, f32[1,1,2,8,1024]{4,3,2,1,0:T(8,128)S(1)} %copy-done, ...), custom_call_target="tpu_custom_call", output_to_operand_aliasing={{4}: (0, {})} | custom-call | flops 4294967296 | bytes 33554432 | tf_op jit(solution)/shard_map/project1/pallas_call | solution.py:163
  23.9 2.1 %collective-permute-start.6 = (f32[8,4096]{1,0:T(8,128)S(1)}, f32[8,4096]{1,0:T(8,128)S(1)}, u32[]{:S(2)}, u32[]{:S(2)}) collective-permute-start(f32[8,4096]{1,0:T(8,128)S(1)} %get-tuple-element.45.o0), channel_id=1, source_target_pairs={{0,6},{2,4},{4,2},{6,0},{1,7},{3,5},{5,3},{7,1},{8,14},{10,12},{12... | collective-permute-start | bytes 393224 | tf_op jit(solution)/shard_map/ppermute | solution.py:77
  26.1 0.0 collective-permute-done.2.n0
  26.1 1.1 %collective-permute-start.7 = (f32[8,4096]{1,0:T(8,128)S(1)}, f32[8,4096]{1,0:T(8,128)S(1)}, u32[]{:S(2)}, u32[]{:S(2)}) collective-permute-start(f32[8,4096]{1,0:T(8,128)S(1)} %get-tuple-element.46.o1), channel_id=1, source_target_pairs={{0,2},{2,0},{4,6},{6,4},{1,3},{3,1},{5,7},{7,5},{8,10},{10,8},{12,... | collective-permute-start | bytes 393224 | tf_op jit(solution)/shard_map/ppermute | solution.py:77
  27.2 0.0 collective-permute-done.3.n1
  27.2 0.0 collective-permute-start.8
  27.2 0.0 collective-permute-done.4.n2
  27.2 0.1 collective-permute-start.9
  27.3 0.0 collective-permute-done.5.n3
  27.3 3.8 %back0.1 = (f32[32,4096]{1,0:T(8,128)S(1)}, f32[32,1152]{1,0:T(8,128)S(1)}, f32[2,4096,1024]{2,1,0:T(8,128)S(1)}) custom-call(f32[2,4096,1024]{2,1,0:T(8,128)S(1)} %get-tuple-element.39.same, f32[8,4096]{1,0:T(8,128)S(1)} %get-tuple-element.40.o0, f32[8,4096]{1,0:T(8,128)S(1)} %get-tuple-element.41.o1, ...), custom_call_target="tpu_custom_call", output_to_operand_aliasing={{2}: (0, {})} | custom-call | flops 4294967296 | bytes 33554432 | tf_op jit(solution)/shard_map/back0/pallas_call | solution.py:211
  31.1 1.8 %collective-permute-start.10 = (f32[32,1152]{1,0:T(8,128)S(1)}, f32[32,1152]{1,0:T(8,128)S(1)}, u32[]{:S(2)}, u32[]{:S(2)}) collective-permute-start(f32[32,1152]{1,0:T(8,128)S(1)} %get-tuple-element.50.mine), channel_id=1, source_target_pairs={{0,1},{1,0},{2,3},{3,2},{4,5},{5,4},{6,7},{7,6},{8,9},{9,8},{10,11... | collective-permute-start | bytes 442376 | tf_op jit(solution)/shard_map/ppermute | solution.py:68
  32.9 0.0 collective-permute-done.6.n0
  32.9 1.1 %collective-permute-done.7.n1 = f32[8,4096]{1,0:T(8,128)S(1)} collective-permute-done((f32[8,4096]{1,0:T(8,128)S(1)}, f32[8,4096]{1,0:T(8,128)S(1)}, u32[]{:S(2)}, u32[]{:S(2)}) %collective-permute-start.7) | collective-permute-done | bytes 131104 | tf_op jit(solution)/shard_map/ppermute | solution.py:77
  34.0 0.0 collective-permute-done.8.n2
  34.0 0.0 collective-permute-done.9.n3
  34.0 3.8 %back1.1 = (f32[32,4096]{1,0:T(8,128)S(1)}, f32[32,1152]{1,0:T(8,128)S(1)}, f32[2,4096,1024]{2,1,0:T(8,128)S(1)}) custom-call(f32[2,4096,1024]{2,1,0:T(8,128)S(1)} %get-tuple-element.44.same, f32[8,4096]{1,0:T(8,128)S(1)} %get-tuple-element.45.o0, f32[8,4096]{1,0:T(8,128)S(1)} %get-tuple-element.46.o1, ...), custom_call_target="tpu_custom_call", output_to_operand_aliasing={{2}: (0, {})} | custom-call | flops 4294967296 | bytes 33554432 | tf_op jit(solution)/shard_map/back1/pallas_call | solution.py:211
  37.8 1.5 %collective-permute-start.11 = (f32[32,1152]{1,0:T(8,128)S(1)}, f32[32,1152]{1,0:T(8,128)S(1)}, u32[]{:S(2)}, u32[]{:S(2)}) collective-permute-start(f32[32,1152]{1,0:T(8,128)S(1)} %get-tuple-element.53.mine.refs_8_), channel_id=1, source_target_pairs={{0,1},{1,0},{2,3},{3,2},{4,5},{5,4},{6,7},{7,6},{8,9},{9,8},{10,11... | collective-permute-start | bytes 442376 | tf_op jit(solution)/shard_map/ppermute | solution.py:68
  39.3 0.0 collective-permute-done.10.other
  39.4 1.8 %collective-permute-start.12 = (f32[8,1024]{1,0:T(8,128)S(1)}, f32[8,1024]{1,0:T(8,128)S(1)}, u32[]{:S(2)}, u32[]{:S(2)}) collective-permute-start(f32[8,1024]{1,0:T(8,128)S(1)} %get-tuple-element.56.refs_0_), channel_id=1, source_target_pairs={{0,6},{2,4},{4,2},{6,0},{1,7},{3,5},{5,3},{7,1},{8,14},{10,12},{12... | collective-permute-start | bytes 98312 | tf_op jit(solution)/shard_map/ppermute | solution.py:77
  41.2 0.0 collective-permute-start.13
  41.2 0.0 collective-permute-start.14
  41.2 1.0 %collective-permute-start.15 = (f32[8,1024]{1,0:T(8,128)S(1)}, f32[8,1024]{1,0:T(8,128)S(1)}, u32[]{:S(2)}, u32[]{:S(2)}) collective-permute-start(f32[8,1024]{1,0:T(8,128)S(1)} %get-tuple-element.59.refs_3_), channel_id=1, source_target_pairs={{0,8},{8,0},{16,24},{24,16},{1,9},{9,1},{17,25},{25,17},{2,10},{10... | collective-permute-start | bytes 98312 | tf_op jit(solution)/shard_map/ppermute | solution.py:77
  42.1 0.7 %inverse.1 = (f32[32,128]{1,0:T(8,128)S(1)}, f32[2,4096,1024]{2,1,0:T(8,128)S(1)}) custom-call(f32[2,4096,1024]{2,1,0:T(8,128)S(1)} %get-tuple-element.51.same, f32[32,1152]{1,0:T(8,128)S(1)} %get-tuple-element.50.mine, f32[32,1152]{1,0:T(8,128)S(1)} %collective-permute-done.10.other), custom_call_target="tpu_custom_call", output_to_operand_aliasing={{1}: (0, {})} | custom-call | tf_op jit(solution)/shard_map/inverse/pallas_call | solution.py:270
  42.8 0.7 %collective-permute-done.11.other.refs_9_ = f32[32,1152]{1,0:T(8,128)S(1)} collective-permute-done((f32[32,1152]{1,0:T(8,128)S(1)}, f32[32,1152]{1,0:T(8,128)S(1)}, u32[]{:S(2)}, u32[]{:S(2)}) %collective-permute-start.11) | collective-permute-done | bytes 147488 | tf_op jit(solution)/shard_map/ppermute | solution.py:68
  43.5 1.5 %collective-permute-start.16 = (f32[8,1024]{1,0:T(8,128)S(1)}, f32[8,1024]{1,0:T(8,128)S(1)}, u32[]{:S(2)}, u32[]{:S(2)}) collective-permute-start(f32[8,1024]{1,0:T(8,128)S(1)} %get-tuple-element.63.refs_0_), channel_id=1, source_target_pairs={{0,6},{2,4},{4,2},{6,0},{1,7},{3,5},{5,3},{7,1},{8,14},{10,12},{12... | collective-permute-start | bytes 98312 | tf_op jit(solution)/shard_map/ppermute | solution.py:77
  45.0 0.2 collective-permute-done.12.refs_4_
  45.2 0.4 collective-permute-start.17
  45.7 0.0 collective-permute-done.13.refs_5_
  45.7 0.6 %collective-permute-start.18 = (f32[8,1024]{1,0:T(8,128)S(1)}, f32[8,1024]{1,0:T(8,128)S(1)}, u32[]{:S(2)}, u32[]{:S(2)}) collective-permute-start(f32[8,1024]{1,0:T(8,128)S(1)} %get-tuple-element.65.refs_2_), channel_id=1, source_target_pairs={{0,24},{8,16},{16,8},{24,0},{1,25},{9,17},{17,9},{25,1},{2,26},{10... | collective-permute-start | bytes 98312 | tf_op jit(solution)/shard_map/ppermute | solution.py:77
  46.3 0.0 collective-permute-done.14.refs_6_
  46.3 1.1 %collective-permute-start.19 = (f32[8,1024]{1,0:T(8,128)S(1)}, f32[8,1024]{1,0:T(8,128)S(1)}, u32[]{:S(2)}, u32[]{:S(2)}) collective-permute-start(f32[8,1024]{1,0:T(8,128)S(1)} %get-tuple-element.66.refs_3_), channel_id=1, source_target_pairs={{0,8},{8,0},{16,24},{24,16},{1,9},{9,1},{17,25},{25,17},{2,10},{10... | collective-permute-start | bytes 98312 | tf_op jit(solution)/shard_map/ppermute | solution.py:77
  47.4 0.0 collective-permute-done.15.refs_7_
  47.4 4.8 %mix0.1 = (f32[1,1,2,4096,1024]{4,3,2,1,0:T(8,128)}, f32[1,1,2,8,1024]{4,3,2,1,0:T(8,128)}, f32[1,1,2,8,1024]{4,3,2,1,0:T(8,128)}, f32[2,4096,1024]{2,1,0:T(8,128)S(1)}) custom-call(f32[2,4096,1024]{2,1,0:T(8,128)S(1)} %get-tuple-element.54.same, f32[32,4096]{1,0:T(8,128)S(1)} %get-tuple-element.55.differ, ...), custom_call_target="tpu_custom_call", output_to_operand_aliasing={{3}: (0, {})} | custom-call | flops 4294967296 | bytes 33554432 | tf_op jit(solution)/shard_map/mix0/pallas_call | solution.py:370
  52.3 0.0 collective-permute-done.16.refs_4_
  52.3 0.0 collective-permute-done.17.refs_5_
  52.3 0.0 collective-permute-done.18.refs_6_
  52.3 0.0 collective-permute-done.19.refs_7_
  52.3 7.9 %mix1.1 = (f32[1,1,2,4096,1024]{4,3,2,1,0:T(8,128)}, f32[1,1,2,8,1024]{4,3,2,1,0:T(8,128)}, f32[1,1,2,8,1024]{4,3,2,1,0:T(8,128)}, f32[2,4096,1024]{2,1,0:T(8,128)S(1)}) custom-call(f32[2,4096,1024]{2,1,0:T(8,128)S(1)} %get-tuple-element.61.same, ...), custom_call_target="tpu_custom_call", output_to_operand_aliasing={{3}: (0, {}), {0}: (12, {}), {1}: (13, {}), {2}: (14, {})} | custom-call | flops 4294967296 | bytes 33554432 | tf_op jit(solution)/shard_map/mix1/pallas_call | solution.py:370
  (6 shorter events, 0.0 us)
Async XLA Ops:
  0.6 7.6 %copy-start.1 = (f32[1,1,2,8,1024]{4,3,2,1,0:T(8,128)S(1)}, f32[1,1,2,8,1024]{4,3,2,1,0:T(8,128)}, u32[]{:S(2)}) copy-start(f32[1,1,2,8,1024]{4,3,2,1,0:T(8,128)} %f2.3) | copy-start | bytes 196612
  0.6 7.6 %copy-start = (f32[1,1,2,8,1024]{4,3,2,1,0:T(8,128)S(1)}, f32[1,1,2,8,1024]{4,3,2,1,0:T(8,128)}, u32[]{:S(2)}) copy-start(f32[1,1,2,8,1024]{4,3,2,1,0:T(8,128)} %f0.3) | copy-start | bytes 196612
  0.7 6.7 %collective-permute-start.1 = (f32[1,1,2,8,1024]{4,3,2,1,0:T(8,128)}, f32[1,1,2,8,1024]{4,3,2,1,0:T(8,128)S(1)}, u32[]{:S(2)}, u32[]{:S(2)}) collective-permute-start(f32[1,1,2,8,1024]{4,3,2,1,0:T(8,128)} %f2.3), channel_id=1, source_target_pairs={{0,8},{8,16},{16,24},{24,0},{1,9},{9,17},{17,25},{25,1},{2,10},{10... | collective-permute-start | bytes 196616 | tf_op jit(solution)/shard_map/ppermute | solution.py:63
  1.2 7.1 %collective-permute-start = (f32[1,1,2,8,1024]{4,3,2,1,0:T(8,128)}, f32[1,1,2,8,1024]{4,3,2,1,0:T(8,128)S(1)}, u32[]{:S(2)}, u32[]{:S(2)}) collective-permute-start(f32[1,1,2,8,1024]{4,3,2,1,0:T(8,128)} %f0.3), channel_id=1, source_target_pairs={{0,2},{2,4},{4,6},{6,0},{1,3},{3,5},{5,7},{7,1},{8,10},{10,12},{12... | collective-permute-start | bytes 196616 | tf_op jit(solution)/shard_map/ppermute | solution.py:63
  14.2 11.8 %collective-permute-start.2 = (f32[8,4096]{1,0:T(8,128)S(1)}, f32[8,4096]{1,0:T(8,128)S(1)}, u32[]{:S(2)}, u32[]{:S(2)}) collective-permute-start(f32[8,4096]{1,0:T(8,128)S(1)} %get-tuple-element.40.o0), channel_id=1, source_target_pairs={{0,6},{2,4},{4,2},{6,0},{1,7},{3,5},{5,3},{7,1},{8,14},{10,12},{12... | collective-permute-start | bytes 393224 | tf_op jit(solution)/shard_map/ppermute | solution.py:77
  16.5 10.7 %collective-permute-start.3 = (f32[8,4096]{1,0:T(8,128)S(1)}, f32[8,4096]{1,0:T(8,128)S(1)}, u32[]{:S(2)}, u32[]{:S(2)}) collective-permute-start(f32[8,4096]{1,0:T(8,128)S(1)} %get-tuple-element.41.o1), channel_id=1, source_target_pairs={{0,2},{2,0},{4,6},{6,4},{1,3},{3,1},{5,7},{7,5},{8,10},{10,8},{12,... | collective-permute-start | bytes 393224 | tf_op jit(solution)/shard_map/ppermute | solution.py:77
  16.5 10.7 %collective-permute-start.4 = (f32[8,4096]{1,0:T(8,128)S(1)}, f32[8,4096]{1,0:T(8,128)S(1)}, u32[]{:S(2)}, u32[]{:S(2)}) collective-permute-start(f32[8,4096]{1,0:T(8,128)S(1)} %get-tuple-element.42.o2), channel_id=1, source_target_pairs={{0,24},{8,16},{16,8},{24,0},{1,25},{9,17},{17,9},{25,1},{2,26},{10... | collective-permute-start | bytes 393224 | tf_op jit(solution)/shard_map/ppermute | solution.py:77
  17.3 9.9 %collective-permute-start.5 = (f32[8,4096]{1,0:T(8,128)S(1)}, f32[8,4096]{1,0:T(8,128)S(1)}, u32[]{:S(2)}, u32[]{:S(2)}) collective-permute-start(f32[8,4096]{1,0:T(8,128)S(1)} %get-tuple-element.43.o3), channel_id=1, source_target_pairs={{0,8},{8,0},{16,24},{24,16},{1,9},{9,1},{17,25},{25,17},{2,10},{10... | collective-permute-start | bytes 393224 | tf_op jit(solution)/shard_map/ppermute | solution.py:77
  23.9 9.0 %collective-permute-start.6 = (f32[8,4096]{1,0:T(8,128)S(1)}, f32[8,4096]{1,0:T(8,128)S(1)}, u32[]{:S(2)}, u32[]{:S(2)}) collective-permute-start(f32[8,4096]{1,0:T(8,128)S(1)} %get-tuple-element.45.o0), channel_id=1, source_target_pairs={{0,6},{2,4},{4,2},{6,0},{1,7},{3,5},{5,3},{7,1},{8,14},{10,12},{12... | collective-permute-start | bytes 393224 | tf_op jit(solution)/shard_map/ppermute | solution.py:77
  26.1 7.9 %collective-permute-start.7 = (f32[8,4096]{1,0:T(8,128)S(1)}, f32[8,4096]{1,0:T(8,128)S(1)}, u32[]{:S(2)}, u32[]{:S(2)}) collective-permute-start(f32[8,4096]{1,0:T(8,128)S(1)} %get-tuple-element.46.o1), channel_id=1, source_target_pairs={{0,2},{2,0},{4,6},{6,4},{1,3},{3,1},{5,7},{7,5},{8,10},{10,8},{12,... | collective-permute-start | bytes 393224 | tf_op jit(solution)/shard_map/ppermute | solution.py:77
  27.2 6.8 %collective-permute-start.8 = (f32[8,4096]{1,0:T(8,128)S(1)}, f32[8,4096]{1,0:T(8,128)S(1)}, u32[]{:S(2)}, u32[]{:S(2)}) collective-permute-start(f32[8,4096]{1,0:T(8,128)S(1)} %get-tuple-element.47.o2), channel_id=1, source_target_pairs={{0,24},{8,16},{16,8},{24,0},{1,25},{9,17},{17,9},{25,1},{2,26},{10... | collective-permute-start | bytes 393224 | tf_op jit(solution)/shard_map/ppermute | solution.py:77
  27.2 6.8 %collective-permute-start.9 = (f32[8,4096]{1,0:T(8,128)S(1)}, f32[8,4096]{1,0:T(8,128)S(1)}, u32[]{:S(2)}, u32[]{:S(2)}) collective-permute-start(f32[8,4096]{1,0:T(8,128)S(1)} %get-tuple-element.48.o3), channel_id=1, source_target_pairs={{0,8},{8,0},{16,24},{24,16},{1,9},{9,1},{17,25},{25,17},{2,10},{10... | collective-permute-start | bytes 393224 | tf_op jit(solution)/shard_map/ppermute | solution.py:77
  31.1 8.2 %collective-permute-start.10 = (f32[32,1152]{1,0:T(8,128)S(1)}, f32[32,1152]{1,0:T(8,128)S(1)}, u32[]{:S(2)}, u32[]{:S(2)}) collective-permute-start(f32[32,1152]{1,0:T(8,128)S(1)} %get-tuple-element.50.mine), channel_id=1, source_target_pairs={{0,1},{1,0},{2,3},{3,2},{4,5},{5,4},{6,7},{7,6},{8,9},{9,8},{10,11... | collective-permute-start | bytes 442376 | tf_op jit(solution)/shard_map/ppermute | solution.py:68
  37.8 5.7 %collective-permute-start.11 = (f32[32,1152]{1,0:T(8,128)S(1)}, f32[32,1152]{1,0:T(8,128)S(1)}, u32[]{:S(2)}, u32[]{:S(2)}) collective-permute-start(f32[32,1152]{1,0:T(8,128)S(1)} %get-tuple-element.53.mine.refs_8_), channel_id=1, source_target_pairs={{0,1},{1,0},{2,3},{3,2},{4,5},{5,4},{6,7},{7,6},{8,9},{9,8},{10,11... | collective-permute-start | bytes 442376 | tf_op jit(solution)/shard_map/ppermute | solution.py:68
  39.4 5.9 %collective-permute-start.12 = (f32[8,1024]{1,0:T(8,128)S(1)}, f32[8,1024]{1,0:T(8,128)S(1)}, u32[]{:S(2)}, u32[]{:S(2)}) collective-permute-start(f32[8,1024]{1,0:T(8,128)S(1)} %get-tuple-element.56.refs_0_), channel_id=1, source_target_pairs={{0,6},{2,4},{4,2},{6,0},{1,7},{3,5},{5,3},{7,1},{8,14},{10,12},{12... | collective-permute-start | bytes 98312 | tf_op jit(solution)/shard_map/ppermute | solution.py:77
  41.2 4.5 %collective-permute-start.13 = (f32[8,1024]{1,0:T(8,128)S(1)}, f32[8,1024]{1,0:T(8,128)S(1)}, u32[]{:S(2)}, u32[]{:S(2)}) collective-permute-start(f32[8,1024]{1,0:T(8,128)S(1)} %get-tuple-element.57.refs_1_), channel_id=1, source_target_pairs={{0,2},{2,0},{4,6},{6,4},{1,3},{3,1},{5,7},{7,5},{8,10},{10,8},{12,... | collective-permute-start | bytes 98312 | tf_op jit(solution)/shard_map/ppermute | solution.py:77
  41.2 5.2 %collective-permute-start.14 = (f32[8,1024]{1,0:T(8,128)S(1)}, f32[8,1024]{1,0:T(8,128)S(1)}, u32[]{:S(2)}, u32[]{:S(2)}) collective-permute-start(f32[8,1024]{1,0:T(8,128)S(1)} %get-tuple-element.58.refs_2_), channel_id=1, source_target_pairs={{0,24},{8,16},{16,8},{24,0},{1,25},{9,17},{17,9},{25,1},{2,26},{10... | collective-permute-start | bytes 98312 | tf_op jit(solution)/shard_map/ppermute | solution.py:77
  41.2 6.2 %collective-permute-start.15 = (f32[8,1024]{1,0:T(8,128)S(1)}, f32[8,1024]{1,0:T(8,128)S(1)}, u32[]{:S(2)}, u32[]{:S(2)}) collective-permute-start(f32[8,1024]{1,0:T(8,128)S(1)} %get-tuple-element.59.refs_3_), channel_id=1, source_target_pairs={{0,8},{8,0},{16,24},{24,16},{1,9},{9,1},{17,25},{25,17},{2,10},{10... | collective-permute-start | bytes 98312 | tf_op jit(solution)/shard_map/ppermute | solution.py:77
  43.5 8.8 %collective-permute-start.16 = (f32[8,1024]{1,0:T(8,128)S(1)}, f32[8,1024]{1,0:T(8,128)S(1)}, u32[]{:S(2)}, u32[]{:S(2)}) collective-permute-start(f32[8,1024]{1,0:T(8,128)S(1)} %get-tuple-element.63.refs_0_), channel_id=1, source_target_pairs={{0,6},{2,4},{4,2},{6,0},{1,7},{3,5},{5,3},{7,1},{8,14},{10,12},{12... | collective-permute-start | bytes 98312 | tf_op jit(solution)/shard_map/ppermute | solution.py:77
  45.2 7.0 %collective-permute-start.17 = (f32[8,1024]{1,0:T(8,128)S(1)}, f32[8,1024]{1,0:T(8,128)S(1)}, u32[]{:S(2)}, u32[]{:S(2)}) collective-permute-start(f32[8,1024]{1,0:T(8,128)S(1)} %get-tuple-element.64.refs_1_), channel_id=1, source_target_pairs={{0,2},{2,0},{4,6},{6,4},{1,3},{3,1},{5,7},{7,5},{8,10},{10,8},{12,... | collective-permute-start | bytes 98312 | tf_op jit(solution)/shard_map/ppermute | solution.py:77
  45.7 6.6 %collective-permute-start.18 = (f32[8,1024]{1,0:T(8,128)S(1)}, f32[8,1024]{1,0:T(8,128)S(1)}, u32[]{:S(2)}, u32[]{:S(2)}) collective-permute-start(f32[8,1024]{1,0:T(8,128)S(1)} %get-tuple-element.65.refs_2_), channel_id=1, source_target_pairs={{0,24},{8,16},{16,8},{24,0},{1,25},{9,17},{17,9},{25,1},{2,26},{10... | collective-permute-start | bytes 98312 | tf_op jit(solution)/shard_map/ppermute | solution.py:77
  46.3 6.0 %collective-permute-start.19 = (f32[8,1024]{1,0:T(8,128)S(1)}, f32[8,1024]{1,0:T(8,128)S(1)}, u32[]{:S(2)}, u32[]{:S(2)}) collective-permute-start(f32[8,1024]{1,0:T(8,128)S(1)} %get-tuple-element.66.refs_3_), channel_id=1, source_target_pairs={{0,8},{8,0},{16,24},{24,16},{1,9},{9,1},{17,25},{25,17},{2,10},{10... | collective-permute-start | bytes 98312 | tf_op jit(solution)/shard_map/ppermute | solution.py:77

commit v8 on v7

--- a/solution.py
+++ b/solution.py
@@ -116,54 +116,70 @@
     )(hbm(weights))
 
 
-def project_kernel(
-    mat, chunk, size, first, until, same, f0, f1, f2, f3, weights, o0, o1, o2, o3, held, sems
-):
-    rows = held.shape[1]
+def project_kernel(phase, extra, size, first, until, same, f0, f1, f2, f3, weights, *refs):
+    *outs, held, sems = refs
+    mats, rows, _ = held.shape
     pieces = rows // size
     copies = piece_copies(weights, held, sems, size, first, until)
     for copy in copies:
         copy.start()
     rank = f0.shape[-2]
-    slots = []
-    for axis, own, lower in (("ry", f0, f1), ("rx", f2, f3)):
-        own, lower, swap = own[0, 0, mat], lower[0, 0, mat], odd(axis)
-        slots += [jnp.where(swap, own, lower), jnp.where(swap, lower, own)]
-    high, low = split(jnp.concatenate(slots, 0))
-    stack = jnp.concatenate(
-        [jnp.concatenate([high, high], 1), jnp.concatenate([low, low], 1)], 0
-    )
     width = edges * rank
 
-    @pl.loop(0, rows // chunk)
-    def _(step):
-        here = pl.ds(pl.multiple_of(step * chunk, chunk), chunk)
+    def stack_of(mat):
+        slots = []
+        for axis, own, lower in (("ry", f0, f1), ("rx", f2, f3)):
+            own, lower, swap = own[0, 0, mat], lower[0, 0, mat], odd(axis)
+            slots += [jnp.where(swap, own, lower), jnp.where(swap, lower, own)]
+        high, low = split(jnp.concatenate(slots, 0))
+        return jnp.concatenate(
+            [jnp.concatenate([high, high], 1), jnp.concatenate([low, low], 1)], 0
+        )
+
+    def step(mat, stack, row, chunk, place):
         for part in range(chunk // size):
-            piece = step * (chunk // size) + part
+            piece = row // size + part
 
             @pl.when(mat * pieces + piece >= first)
             def _():
-                row = pl.multiple_of(piece * size, size)
+                start = pl.multiple_of(piece * size, size)
                 sem = mat * pieces + piece - first
-                piece_copy(weights, held, sems, size, mat, row, sem).wait()
-
-        w_high, w_low = split(held[mat, here, :])
+                piece_copy(weights, held, sems, size, mat, start, sem).wait()
+
+        w_high, w_low = split(held[mat, pl.ds(row, chunk), :])
         both = dot(stack, jnp.concatenate([w_high, w_low], 1), NT)
         total = both[:width] + both[width:]
-        for slot, out in enumerate((o0, o1, o2, o3)):
-            out[:, here] = total[slot * rank : (slot + 1) * rank]
-
-    for copy in copies[(mat + 1) * pieces - first :]:
+        for slot, out in enumerate(outs):
+            out[:, pl.ds(place, chunk)] = total[slot * rank : (slot + 1) * rank]
+
+    skip = extra if phase else 0
+    stack = stack_of(phase)
+    chunk = chunk_of(rows, 1024)
+    lead = chunk - skip if skip else 0
+    if lead:
+        step(phase, stack, skip, lead, 0)
+
+    @pl.loop(1 if lead else 0, rows // chunk)
+    def _(index):
+        row = pl.multiple_of(index * chunk, chunk)
+        step(phase, stack, row, chunk, pl.multiple_of(row - skip, min(chunk, extra or chunk)))
+
+    taken = (phase + 1) * pieces
+    if extra and phase < mats - 1:
+        step(phase + 1, stack_of(phase + 1), 0, extra, rows - skip)
+        taken += extra // size
+    for copy in copies[taken - first :]:
         copy.wait()
 
 
-def project(held, factors, weights, mat, size, first, until):
-    rows = held.shape[1]
+def project(held, factors, weights, phase, extra, size, first, until):
+    mats, rows, _ = held.shape
     rank = factors[0].shape[-2]
-    return pl.pallas_call(
-        functools.partial(project_kernel, mat, chunk_of(rows, 1024), size, first, until),
-        name=f"project{mat}",
-        out_shape=[jax.ShapeDtypeStruct((rank, rows), f32)] * edges
+    columns = rows - (extra if phase else 0) + (extra if phase < mats - 1 else 0)
+    return pl.pallas_call(
+        functools.partial(project_kernel, phase, extra, size, first, until),
+        name=f"project{phase}",
+        out_shape=[jax.ShapeDtypeStruct((rank, columns), f32)] * edges
         + [jax.ShapeDtypeStruct(held.shape, f32)],
         in_specs=[in_vmem] * 5 + [in_hbm],
         out_specs=[in_vmem] * (edges + 1),
@@ -174,29 +190,29 @@
     )(vmem(held), *factors, hbm(weights))
 
 
-def back_kernel(mat, chunk, same, o0, o1, o2, o3, n0, n1, n2, n3, differ, sums, held):
-    rank = o0.shape[0]
+def back_kernel(mat, extra, same, *refs):
+    *refs, differ, sums, held = refs
+    ends = list(zip(refs[: len(refs) // 2], refs[len(refs) // 2 :]))
+    rank = ends[0][0].shape[0]
     width = edges * rank
-    features = held.shape[2]
+    _, rows, features = held.shape
+    last = ends[-edges:]
+    parts = []
+    if len(ends) > edges:
+        begin = ends[0][0].shape[1] - extra
+        parts.append([o[:, begin:] - n[:, begin:] for o, n in ends[:edges]])
+    rest = rows - (extra if parts else 0)
+    parts.append([o[:, :rest] - n[:, :rest] for o, n in last])
+    p = jnp.concatenate([jnp.concatenate(part, 0) for part in parts], 1)
+    differ[...] = p
+    high, low = split(p)
+    w_high, w_low = split(held[mat])
+    pair = jnp.concatenate([high, low], 0)
+    stack = jnp.concatenate([pair, pair], 1)
+    both = dot(stack, jnp.concatenate([w_high, w_low], 0), NN)
     sums[...] = jnp.zeros_like(sums)
-
-    def body(step, gram):
-        here = pl.ds(pl.multiple_of(step * chunk, chunk), chunk)
-        p = jnp.concatenate(
-            [o[:, here] - n[:, here] for o, n in zip((o0, o1, o2, o3), (n0, n1, n2, n3))], 0
-        )
-        differ[:, here] = p
-        high, low = split(p)
-        w_high, w_low = split(held[mat, here, :])
-        pair = jnp.concatenate([high, low], 0)
-        stack = jnp.concatenate([pair, pair], 1)
-        both = dot(stack, jnp.concatenate([w_high, w_low], 0), NN)
-        sums[:, :features] += both[:width] + both[width:]
-        return gram + dot(pair, pair, NT)
-
-    gram = lax.fori_loop(
-        0, held.shape[1] // chunk, body, jnp.zeros((2 * width, 2 * width), f32)
-    )
+    sums[:, :features] = both[:width] + both[width:]
+    gram = dot(pair, pair, NT)
     total = (gram[:width, :width] + gram[width:, width:]) + (
         gram[:width, width:] + gram[width:, :width]
     )
@@ -205,23 +221,26 @@
         sums[here, features : features + rank] = total[here, here]
 
 
-def back(held, own, near, mat):
+def back(held, own, near, mat, extra):
     _, rows, features = held.shape
-    rank = own[0].shape[0]
-    return pl.pallas_call(
-        functools.partial(back_kernel, mat, chunk_of(rows, 4096)),
+    rank = own[mat][0].shape[0]
+    phases = [mat - 1, mat] if mat and extra else [mat]
+    ends = [value for phase in phases for value in own[phase]]
+    ends += [value for phase in phases for value in near[phase]]
+    return pl.pallas_call(
+        functools.partial(back_kernel, mat, extra),
         name=f"back{mat}",
         out_shape=[
             jax.ShapeDtypeStruct((edges * rank, rows), f32),
             jax.ShapeDtypeStruct((edges * rank, features + 128), f32),
             jax.ShapeDtypeStruct(held.shape, f32),
         ],
-        in_specs=[in_vmem] * 9,
+        in_specs=[in_vmem] * (1 + len(ends)),
         out_specs=[in_vmem] * 3,
         input_output_aliases={0: 2},
         cost_estimate=cost(held, 2),
         compiler_params=pltpu.CompilerParams(vmem_limit_bytes=grant),
-    )(vmem(held), *own, *near)
+    )(vmem(held), *ends)
 
 
 def add_kernel(same, mine, other, *refs):
@@ -394,18 +413,19 @@
     size = chunk_of(rows, 512)
     pieces = rows // size
     ahead = max(pieces // 2, 1)
+    extra = size if pieces % 8 == 0 else 0
     until = ahead
     held = load(weights, size, until)
     own = []
     for mat in range(mats):
         first, until = until, min((mat + 1) * pieces + ahead, mats * pieces)
-        *own_mat, held = project(held, factors, weights, mat, size, first, until)
+        *own_mat, held = project(held, factors, weights, mat, extra, size, first, until)
         own.append(own_mat)
     near = [exchange(own_mat) for own_mat in own]
     differs, pairs = [], []
     tp = lax.axis_size("tp")
     for mat in range(mats):
-        p, terms, held = back(held, own[mat], near[mat], mat)
+        p, terms, held = back(held, own, near, mat, extra)
         distance = 1
         while 2 * distance < tp:
             terms = terms + from_partner(terms, "tp", distance)

time: 60.4 us -> 59.6 us (0.987)
  waiting for transfers between devices: 2.99 us -> 2.3 us
    ppermute x16, waiting for transfers between devices: 1.34 us -> 0.64 us  [exchange(): swapped.append(lax.ppermute(value, axis, pairs))]
  transfers between devices with their start and end apart: 20 -> 20, of which waited for: 4 -> 4; matrix products, arithmetic and copies ran while one was open for 0% -> 0% of each run, Pallas kernels for 37% -> 36%
where the time goes in v8:
time: 59.6 us; the launch traced here: 59.5 us
  Pallas kernels  36.1 us (61%)
  starting transfers between devices  20.3 us (34%)
  waiting for transfers between devices  2.3 us (4%)
  between operations  0.75 us (1%)
    ppermute x16, starting transfers between devices, exchange(): swapped.append(lax.ppermute(value, axis, pairs))  13.8 us
    pallas_call x2, Pallas kernels, mix(): pl.pallas_call(functools.partial(mix_kernel, mat, chunk, 3 * steps // 8),...  12.8 us
    pallas_call x2, Pallas kernels, project(): pl.pallas_call(functools.partial(project_kernel, phase, extra, size, firs...  11.6 us
    pallas_call x2, Pallas kernels, back(): pl.pallas_call(functools.partial(back_kernel, mat, extra), name=f'back{ma...  7.63 us
    pallas_call x1, Pallas kernels, load(): pl.pallas_call(functools.partial(load_kernel, size, until), name='load',...  3.5 us
    ppermute x2, starting transfers between devices, from_partner(): return lax.ppermute(value, axis, [(i, i ^ distance) for i in range(count)])  3.34 us
    ppermute x2, starting transfers between devices, shifted(): return lax.ppermute(value, axis, pairs)  3.14 us
  transfers between devices with their start and end apart: 20, of which 4 were waited for; matrix products, arithmetic and copies ran while one was open for 0% of the time, Pallas kernels for 36%

profile of v8, /device:TPU:0, one launch (start us, length us, event | category | flops | bytes accessed | tf_op | source)
XLA Modules:
  0.0 59.5 jit_solution(9908667139711743440)
XLA Ops:
  0.7 0.5 collective-permute-start.1
  1.2 2.6 %collective-permute-start = (f32[1,1,2,8,1024]{4,3,2,1,0:T(8,128)}, f32[1,1,2,8,1024]{4,3,2,1,0:T(8,128)S(1)}, u32[]{:S(2)}, u32[]{:S(2)}) collective-permute-start(f32[1,1,2,8,1024]{4,3,2,1,0:T(8,128)} %f0.3), channel_id=1, source_target_pairs={{0,2},{2,4},{4,6},{6,0},{1,3},{3,5},{5,7},{7,1},{8,10},{10,12},{12... | collective-permute-start | bytes 196616 | tf_op jit(solution)/shard_map/ppermute | solution.py:63
  3.8 3.5 %load.1.same = f32[2,4096,1024]{2,1,0:T(8,128)S(1)} custom-call(f32[1,1,2,4096,1024]{4,3,2,1,0:T(8,128)} %weights.5), custom_call_target="tpu_custom_call" | custom-call | tf_op jit(solution)/shard_map/load/pallas_call | solution.py:108
  7.3 0.0 collective-permute-done.1.f3
  7.3 1.0 %collective-permute-done.f1 = f32[1,1,2,8,1024]{4,3,2,1,0:T(8,128)S(1)} collective-permute-done((f32[1,1,2,8,1024]{4,3,2,1,0:T(8,128)}, f32[1,1,2,8,1024]{4,3,2,1,0:T(8,128)S(1)}, u32[]{:S(2)}, u32[]{:S(2)}) %collective-permute-start) | collective-permute-done | bytes 65568 | tf_op jit(solution)/shard_map/ppermute | solution.py:63
  8.3 6.5 %project0.1 = (f32[8,4608]{1,0:T(8,128)S(1)}, f32[8,4608]{1,0:T(8,128)S(1)}, f32[8,4608]{1,0:T(8,128)S(1)}, f32[8,4608]{1,0:T(8,128)S(1)}, f32[2,4096,1024]{2,1,0:T(8,128)S(1)}) custom-call(f32[2,4096,1024]{2,1,0:T(8,128)S(1)} %load.1.same, f32[1,1,2,8,1024]{4,3,2,1,0:T(8,128)S(1)} %copy-done, ...), custom_call_target="tpu_custom_call", output_to_operand_aliasing={{4}: (0, {})} | custom-call | flops 4294967296 | bytes 33554432 | tf_op jit(solution)/shard_map/project0/pallas_call | solution.py:179
  14.8 2.3 %collective-permute-start.2 = (f32[8,4608]{1,0:T(8,128)S(1)}, f32[8,4608]{1,0:T(8,128)S(1)}, u32[]{:S(2)}, u32[]{:S(2)}) collective-permute-start(f32[8,4608]{1,0:T(8,128)S(1)} %get-tuple-element.40.refs_0_), channel_id=1, source_target_pairs={{0,6},{2,4},{4,2},{6,0},{1,7},{3,5},{5,3},{7,1},{8,14},{10,12},{12... | collective-permute-start | bytes 442376 | tf_op jit(solution)/shard_map/ppermute | solution.py:77
  17.1 0.0 collective-permute-start.3
  17.1 0.8 %collective-permute-start.4 = (f32[8,4608]{1,0:T(8,128)S(1)}, f32[8,4608]{1,0:T(8,128)S(1)}, u32[]{:S(2)}, u32[]{:S(2)}) collective-permute-start(f32[8,4608]{1,0:T(8,128)S(1)} %get-tuple-element.42.refs_2_), channel_id=1, source_target_pairs={{0,24},{8,16},{16,8},{24,0},{1,25},{9,17},{17,9},{25,1},{2,26},{10... | collective-permute-start | bytes 442376 | tf_op jit(solution)/shard_map/ppermute | solution.py:77
  17.9 0.9 %collective-permute-start.5 = (f32[8,4608]{1,0:T(8,128)S(1)}, f32[8,4608]{1,0:T(8,128)S(1)}, u32[]{:S(2)}, u32[]{:S(2)}) collective-permute-start(f32[8,4608]{1,0:T(8,128)S(1)} %get-tuple-element.43.refs_3_), channel_id=1, source_target_pairs={{0,8},{8,0},{16,24},{24,16},{1,9},{9,1},{17,25},{25,17},{2,10},{10... | collective-permute-start | bytes 442376 | tf_op jit(solution)/shard_map/ppermute | solution.py:77
  18.8 5.1 %project1.1 = (f32[8,3584]{1,0:T(8,128)S(1)}, f32[8,3584]{1,0:T(8,128)S(1)}, f32[8,3584]{1,0:T(8,128)S(1)}, f32[8,3584]{1,0:T(8,128)S(1)}, f32[2,4096,1024]{2,1,0:T(8,128)S(1)}) custom-call(f32[2,4096,1024]{2,1,0:T(8,128)S(1)} %get-tuple-element.38.same, f32[1,1,2,8,1024]{4,3,2,1,0:T(8,128)S(1)} %copy-done, ...), custom_call_target="tpu_custom_call", output_to_operand_aliasing={{4}: (0, {})} | custom-call | flops 4294967296 | bytes 33554432 | tf_op jit(solution)/shard_map/project1/pallas_call | solution.py:179
  23.9 2.1 %collective-permute-start.6 = (f32[8,3584]{1,0:T(8,128)S(1)}, f32[8,3584]{1,0:T(8,128)S(1)}, u32[]{:S(2)}, u32[]{:S(2)}) collective-permute-start(f32[8,3584]{1,0:T(8,128)S(1)} %get-tuple-element.45.refs_4_), channel_id=1, source_target_pairs={{0,6},{2,4},{4,2},{6,0},{1,7},{3,5},{5,3},{7,1},{8,14},{10,12},{12... | collective-permute-start | bytes 344072 | tf_op jit(solution)/shard_map/ppermute | solution.py:77
  26.0 0.0 collective-permute-done.2.refs_4_.refs_8_
  26.0 1.1 %collective-permute-start.7 = (f32[8,3584]{1,0:T(8,128)S(1)}, f32[8,3584]{1,0:T(8,128)S(1)}, u32[]{:S(2)}, u32[]{:S(2)}) collective-permute-start(f32[8,3584]{1,0:T(8,128)S(1)} %get-tuple-element.46.refs_5_), channel_id=1, source_target_pairs={{0,2},{2,0},{4,6},{6,4},{1,3},{3,1},{5,7},{7,5},{8,10},{10,8},{12,... | collective-permute-start | bytes 344072 | tf_op jit(solution)/shard_map/ppermute | solution.py:77
  27.1 0.0 collective-permute-done.3.refs_5_.refs_9_
  27.2 0.0 collective-permute-start.8
  27.2 0.0 collective-permute-done.4.refs_6_.refs_10_
  27.2 0.1 collective-permute-start.9
  27.3 0.0 collective-permute-done.5.refs_7_.refs_11_
  27.3 3.8 %back0.1 = (f32[32,4096]{1,0:T(8,128)S(1)}, f32[32,1152]{1,0:T(8,128)S(1)}, f32[2,4096,1024]{2,1,0:T(8,128)S(1)}) custom-call(f32[2,4096,1024]{2,1,0:T(8,128)S(1)} %get-tuple-element.39.same, f32[8,4608]{1,0:T(8,128)S(1)} %get-tuple-element.40.refs_0_, f32[8,4608]{1,0:T(8,128)S(1)} %get-tuple-element.41.refs_1_, ...), custom_call_target="tpu_custom_call", output_to_operand_aliasing={{2}: (0, {})} | custom-call | flops 4294967296 | bytes 33554432 | tf_op jit(solution)/shard_map/back0/pallas_call | solution.py:230
  31.1 1.8 %collective-permute-start.10 = (f32[32,1152]{1,0:T(8,128)S(1)}, f32[32,1152]{1,0:T(8,128)S(1)}, u32[]{:S(2)}, u32[]{:S(2)}) collective-permute-start(f32[32,1152]{1,0:T(8,128)S(1)} %get-tuple-element.50.mine), channel_id=1, source_target_pairs={{0,1},{1,0},{2,3},{3,2},{4,5},{5,4},{6,7},{7,6},{8,9},{9,8},{10,11... | collective-permute-start | bytes 442376 | tf_op jit(solution)/shard_map/ppermute | solution.py:68
  32.9 0.0 collective-permute-done.6.refs_12_
  32.9 0.4 collective-permute-done.7.refs_13_
  33.2 0.0 collective-permute-done.8.refs_14_
  33.3 0.0 collective-permute-done.9.refs_15_
  33.3 3.8 %back1.1 = (f32[32,4096]{1,0:T(8,128)S(1)}, f32[32,1152]{1,0:T(8,128)S(1)}, f32[2,4096,1024]{2,1,0:T(8,128)S(1)}) custom-call(f32[2,4096,1024]{2,1,0:T(8,128)S(1)} %get-tuple-element.44.same, f32[8,4608]{1,0:T(8,128)S(1)} %get-tuple-element.40.refs_0_, f32[8,4608]{1,0:T(8,128)S(1)} %get-tuple-element.41.refs_1_, ...), custom_call_target="tpu_custom_call", output_to_operand_aliasing={{2}: (0, {})} | custom-call | flops 4294967296 | bytes 33554432 | tf_op jit(solution)/shard_map/back1/pallas_call | solution.py:230
  37.1 1.5 %collective-permute-start.11 = (f32[32,1152]{1,0:T(8,128)S(1)}, f32[32,1152]{1,0:T(8,128)S(1)}, u32[]{:S(2)}, u32[]{:S(2)}) collective-permute-start(f32[32,1152]{1,0:T(8,128)S(1)} %get-tuple-element.53.mine.refs_8_), channel_id=1, source_target_pairs={{0,1},{1,0},{2,3},{3,2},{4,5},{5,4},{6,7},{7,6},{8,9},{9,8},{10,11... | collective-permute-start | bytes 442376 | tf_op jit(solution)/shard_map/ppermute | solution.py:68
  38.6 0.0 collective-permute-done.10.other
  38.6 1.8 %collective-permute-start.12 = (f32[8,1024]{1,0:T(8,128)S(1)}, f32[8,1024]{1,0:T(8,128)S(1)}, u32[]{:S(2)}, u32[]{:S(2)}) collective-permute-start(f32[8,1024]{1,0:T(8,128)S(1)} %get-tuple-element.56.refs_0_), channel_id=1, source_target_pairs={{0,6},{2,4},{4,2},{6,0},{1,7},{3,5},{5,3},{7,1},{8,14},{10,12},{12... | collective-permute-start | bytes 98312 | tf_op jit(solution)/shard_map/ppermute | solution.py:77
  40.4 0.0 collective-permute-start.13
  40.4 0.0 collective-permute-start.14
  40.4 1.0 %collective-permute-start.15 = (f32[8,1024]{1,0:T(8,128)S(1)}, f32[8,1024]{1,0:T(8,128)S(1)}, u32[]{:S(2)}, u32[]{:S(2)}) collective-permute-start(f32[8,1024]{1,0:T(8,128)S(1)} %get-tuple-element.59.refs_3_), channel_id=1, source_target_pairs={{0,8},{8,0},{16,24},{24,16},{1,9},{9,1},{17,25},{25,17},{2,10},{10... | collective-permute-start | bytes 98312 | tf_op jit(solution)/shard_map/ppermute | solution.py:77
  41.4 0.7 %inverse.1 = (f32[32,128]{1,0:T(8,128)S(1)}, f32[2,4096,1024]{2,1,0:T(8,128)S(1)}) custom-call(f32[2,4096,1024]{2,1,0:T(8,128)S(1)} %get-tuple-element.51.same, f32[32,1152]{1,0:T(8,128)S(1)} %get-tuple-element.50.mine, f32[32,1152]{1,0:T(8,128)S(1)} %collective-permute-done.10.other), custom_call_target="tpu_custom_call", output_to_operand_aliasing={{1}: (0, {})} | custom-call | tf_op jit(solution)/shard_map/inverse/pallas_call | solution.py:289
  42.1 0.7 %collective-permute-done.11.other.refs_9_ = f32[32,1152]{1,0:T(8,128)S(1)} collective-permute-done((f32[32,1152]{1,0:T(8,128)S(1)}, f32[32,1152]{1,0:T(8,128)S(1)}, u32[]{:S(2)}, u32[]{:S(2)}) %collective-permute-start.11) | collective-permute-done | bytes 147488 | tf_op jit(solution)/shard_map/ppermute | solution.py:68
  42.8 1.5 %collective-permute-start.16 = (f32[8,1024]{1,0:T(8,128)S(1)}, f32[8,1024]{1,0:T(8,128)S(1)}, u32[]{:S(2)}, u32[]{:S(2)}) collective-permute-start(f32[8,1024]{1,0:T(8,128)S(1)} %get-tuple-element.63.refs_0_), channel_id=1, source_target_pairs={{0,6},{2,4},{4,2},{6,0},{1,7},{3,5},{5,3},{7,1},{8,14},{10,12},{12... | collective-permute-start | bytes 98312 | tf_op jit(solution)/shard_map/ppermute | solution.py:77
  44.3 0.2 collective-permute-done.12.refs_4_
  44.5 0.4 collective-permute-start.17
  45.0 0.0 collective-permute-done.13.refs_5_
  45.0 0.6 %collective-permute-start.18 = (f32[8,1024]{1,0:T(8,128)S(1)}, f32[8,1024]{1,0:T(8,128)S(1)}, u32[]{:S(2)}, u32[]{:S(2)}) collective-permute-start(f32[8,1024]{1,0:T(8,128)S(1)} %get-tuple-element.65.refs_2_), channel_id=1, source_target_pairs={{0,24},{8,16},{16,8},{24,0},{1,25},{9,17},{17,9},{25,1},{2,26},{10... | collective-permute-start | bytes 98312 | tf_op jit(solution)/shard_map/ppermute | solution.py:77
  45.6 0.0 collective-permute-done.14.refs_6_
  45.6 1.1 %collective-permute-start.19 = (f32[8,1024]{1,0:T(8,128)S(1)}, f32[8,1024]{1,0:T(8,128)S(1)}, u32[]{:S(2)}, u32[]{:S(2)}) collective-permute-start(f32[8,1024]{1,0:T(8,128)S(1)} %get-tuple-element.66.refs_3_), channel_id=1, source_target_pairs={{0,8},{8,0},{16,24},{24,16},{1,9},{9,1},{17,25},{25,17},{2,10},{10... | collective-permute-start | bytes 98312 | tf_op jit(solution)/shard_map/ppermute | solution.py:77
  46.7 0.0 collective-permute-done.15.refs_7_
  46.7 4.8 %mix0.1 = (f32[1,1,2,4096,1024]{4,3,2,1,0:T(8,128)}, f32[1,1,2,8,1024]{4,3,2,1,0:T(8,128)}, f32[1,1,2,8,1024]{4,3,2,1,0:T(8,128)}, f32[2,4096,1024]{2,1,0:T(8,128)S(1)}) custom-call(f32[2,4096,1024]{2,1,0:T(8,128)S(1)} %get-tuple-element.54.same, f32[32,4096]{1,0:T(8,128)S(1)} %get-tuple-element.55.differ, ...), custom_call_target="tpu_custom_call", output_to_operand_aliasing={{3}: (0, {})} | custom-call | flops 4294967296 | bytes 33554432 | tf_op jit(solution)/shard_map/mix0/pallas_call | solution.py:389
  51.5 0.0 collective-permute-done.16.refs_4_
  51.5 0.0 collective-permute-done.17.refs_5_
  51.5 0.0 collective-permute-done.18.refs_6_
  51.5 0.0 collective-permute-done.19.refs_7_
  51.6 7.9 %mix1.1 = (f32[1,1,2,4096,1024]{4,3,2,1,0:T(8,128)}, f32[1,1,2,8,1024]{4,3,2,1,0:T(8,128)}, f32[1,1,2,8,1024]{4,3,2,1,0:T(8,128)}, f32[2,4096,1024]{2,1,0:T(8,128)S(1)}) custom-call(f32[2,4096,1024]{2,1,0:T(8,128)S(1)} %get-tuple-element.61.same, ...), custom_call_target="tpu_custom_call", output_to_operand_aliasing={{3}: (0, {}), {0}: (12, {}), {1}: (13, {}), {2}: (14, {})} | custom-call | flops 4294967296 | bytes 33554432 | tf_op jit(solution)/shard_map/mix1/pallas_call | solution.py:389
  (6 shorter events, 0.0 us)
Async XLA Ops:
  0.6 7.6 %copy-start.1 = (f32[1,1,2,8,1024]{4,3,2,1,0:T(8,128)S(1)}, f32[1,1,2,8,1024]{4,3,2,1,0:T(8,128)}, u32[]{:S(2)}) copy-start(f32[1,1,2,8,1024]{4,3,2,1,0:T(8,128)} %f2.3) | copy-start | bytes 196612
  0.6 7.6 %copy-start = (f32[1,1,2,8,1024]{4,3,2,1,0:T(8,128)S(1)}, f32[1,1,2,8,1024]{4,3,2,1,0:T(8,128)}, u32[]{:S(2)}) copy-start(f32[1,1,2,8,1024]{4,3,2,1,0:T(8,128)} %f0.3) | copy-start | bytes 196612
  0.7 6.7 %collective-permute-start.1 = (f32[1,1,2,8,1024]{4,3,2,1,0:T(8,128)}, f32[1,1,2,8,1024]{4,3,2,1,0:T(8,128)S(1)}, u32[]{:S(2)}, u32[]{:S(2)}) collective-permute-start(f32[1,1,2,8,1024]{4,3,2,1,0:T(8,128)} %f2.3), channel_id=1, source_target_pairs={{0,8},{8,16},{16,24},{24,0},{1,9},{9,17},{17,25},{25,1},{2,10},{10... | collective-permute-start | bytes 196616 | tf_op jit(solution)/shard_map/ppermute | solution.py:63
  1.2 7.1 %collective-permute-start = (f32[1,1,2,8,1024]{4,3,2,1,0:T(8,128)}, f32[1,1,2,8,1024]{4,3,2,1,0:T(8,128)S(1)}, u32[]{:S(2)}, u32[]{:S(2)}) collective-permute-start(f32[1,1,2,8,1024]{4,3,2,1,0:T(8,128)} %f0.3), channel_id=1, source_target_pairs={{0,2},{2,4},{4,6},{6,0},{1,3},{3,5},{5,7},{7,1},{8,10},{10,12},{12... | collective-permute-start | bytes 196616 | tf_op jit(solution)/shard_map/ppermute | solution.py:63
  14.8 11.2 %collective-permute-start.2 = (f32[8,4608]{1,0:T(8,128)S(1)}, f32[8,4608]{1,0:T(8,128)S(1)}, u32[]{:S(2)}, u32[]{:S(2)}) collective-permute-start(f32[8,4608]{1,0:T(8,128)S(1)} %get-tuple-element.40.refs_0_), channel_id=1, source_target_pairs={{0,6},{2,4},{4,2},{6,0},{1,7},{3,5},{5,3},{7,1},{8,14},{10,12},{12... | collective-permute-start | bytes 442376 | tf_op jit(solution)/shard_map/ppermute | solution.py:77
  17.1 10.1 %collective-permute-start.3 = (f32[8,4608]{1,0:T(8,128)S(1)}, f32[8,4608]{1,0:T(8,128)S(1)}, u32[]{:S(2)}, u32[]{:S(2)}) collective-permute-start(f32[8,4608]{1,0:T(8,128)S(1)} %get-tuple-element.41.refs_1_), channel_id=1, source_target_pairs={{0,2},{2,0},{4,6},{6,4},{1,3},{3,1},{5,7},{7,5},{8,10},{10,8},{12,... | collective-permute-start | bytes 442376 | tf_op jit(solution)/shard_map/ppermute | solution.py:77
  17.1 10.1 %collective-permute-start.4 = (f32[8,4608]{1,0:T(8,128)S(1)}, f32[8,4608]{1,0:T(8,128)S(1)}, u32[]{:S(2)}, u32[]{:S(2)}) collective-permute-start(f32[8,4608]{1,0:T(8,128)S(1)} %get-tuple-element.42.refs_2_), channel_id=1, source_target_pairs={{0,24},{8,16},{16,8},{24,0},{1,25},{9,17},{17,9},{25,1},{2,26},{10... | collective-permute-start | bytes 442376 | tf_op jit(solution)/shard_map/ppermute | solution.py:77
  17.9 9.3 %collective-permute-start.5 = (f32[8,4608]{1,0:T(8,128)S(1)}, f32[8,4608]{1,0:T(8,128)S(1)}, u32[]{:S(2)}, u32[]{:S(2)}) collective-permute-start(f32[8,4608]{1,0:T(8,128)S(1)} %get-tuple-element.43.refs_3_), channel_id=1, source_target_pairs={{0,8},{8,0},{16,24},{24,16},{1,9},{9,1},{17,25},{25,17},{2,10},{10... | collective-permute-start | bytes 442376 | tf_op jit(solution)/shard_map/ppermute | solution.py:77
  23.9 9.0 %collective-permute-start.6 = (f32[8,3584]{1,0:T(8,128)S(1)}, f32[8,3584]{1,0:T(8,128)S(1)}, u32[]{:S(2)}, u32[]{:S(2)}) collective-permute-start(f32[8,3584]{1,0:T(8,128)S(1)} %get-tuple-element.45.refs_4_), channel_id=1, source_target_pairs={{0,6},{2,4},{4,2},{6,0},{1,7},{3,5},{5,3},{7,1},{8,14},{10,12},{12... | collective-permute-start | bytes 344072 | tf_op jit(solution)/shard_map/ppermute | solution.py:77
  26.0 7.2 %collective-permute-start.7 = (f32[8,3584]{1,0:T(8,128)S(1)}, f32[8,3584]{1,0:T(8,128)S(1)}, u32[]{:S(2)}, u32[]{:S(2)}) collective-permute-start(f32[8,3584]{1,0:T(8,128)S(1)} %get-tuple-element.46.refs_5_), channel_id=1, source_target_pairs={{0,2},{2,0},{4,6},{6,4},{1,3},{3,1},{5,7},{7,5},{8,10},{10,8},{12,... | collective-permute-start | bytes 344072 | tf_op jit(solution)/shard_map/ppermute | solution.py:77
  27.2 6.1 %collective-permute-start.8 = (f32[8,3584]{1,0:T(8,128)S(1)}, f32[8,3584]{1,0:T(8,128)S(1)}, u32[]{:S(2)}, u32[]{:S(2)}) collective-permute-start(f32[8,3584]{1,0:T(8,128)S(1)} %get-tuple-element.47.refs_6_), channel_id=1, source_target_pairs={{0,24},{8,16},{16,8},{24,0},{1,25},{9,17},{17,9},{25,1},{2,26},{10... | collective-permute-start | bytes 344072 | tf_op jit(solution)/shard_map/ppermute | solution.py:77
  27.2 6.1 %collective-permute-start.9 = (f32[8,3584]{1,0:T(8,128)S(1)}, f32[8,3584]{1,0:T(8,128)S(1)}, u32[]{:S(2)}, u32[]{:S(2)}) collective-permute-start(f32[8,3584]{1,0:T(8,128)S(1)} %get-tuple-element.48.refs_7_), channel_id=1, source_target_pairs={{0,8},{8,0},{16,24},{24,16},{1,9},{9,1},{17,25},{25,17},{2,10},{10... | collective-permute-start | bytes 344072 | tf_op jit(solution)/shard_map/ppermute | solution.py:77
  31.1 7.5 %collective-permute-start.10 = (f32[32,1152]{1,0:T(8,128)S(1)}, f32[32,1152]{1,0:T(8,128)S(1)}, u32[]{:S(2)}, u32[]{:S(2)}) collective-permute-start(f32[32,1152]{1,0:T(8,128)S(1)} %get-tuple-element.50.mine), channel_id=1, source_target_pairs={{0,1},{1,0},{2,3},{3,2},{4,5},{5,4},{6,7},{7,6},{8,9},{9,8},{10,11... | collective-permute-start | bytes 442376 | tf_op jit(solution)/shard_map/ppermute | solution.py:68
  37.1 5.7 %collective-permute-start.11 = (f32[32,1152]{1,0:T(8,128)S(1)}, f32[32,1152]{1,0:T(8,128)S(1)}, u32[]{:S(2)}, u32[]{:S(2)}) collective-permute-start(f32[32,1152]{1,0:T(8,128)S(1)} %get-tuple-element.53.mine.refs_8_), channel_id=1, source_target_pairs={{0,1},{1,0},{2,3},{3,2},{4,5},{5,4},{6,7},{7,6},{8,9},{9,8},{10,11... | collective-permute-start | bytes 442376 | tf_op jit(solution)/shard_map/ppermute | solution.py:68
  38.6 5.9 %collective-permute-start.12 = (f32[8,1024]{1,0:T(8,128)S(1)}, f32[8,1024]{1,0:T(8,128)S(1)}, u32[]{:S(2)}, u32[]{:S(2)}) collective-permute-start(f32[8,1024]{1,0:T(8,128)S(1)} %get-tuple-element.56.refs_0_), channel_id=1, source_target_pairs={{0,6},{2,4},{4,2},{6,0},{1,7},{3,5},{5,3},{7,1},{8,14},{10,12},{12... | collective-permute-start | bytes 98312 | tf_op jit(solution)/shard_map/ppermute | solution.py:77
  40.4 4.5 %collective-permute-start.13 = (f32[8,1024]{1,0:T(8,128)S(1)}, f32[8,1024]{1,0:T(8,128)S(1)}, u32[]{:S(2)}, u32[]{:S(2)}) collective-permute-start(f32[8,1024]{1,0:T(8,128)S(1)} %get-tuple-element.57.refs_1_), channel_id=1, source_target_pairs={{0,2},{2,0},{4,6},{6,4},{1,3},{3,1},{5,7},{7,5},{8,10},{10,8},{12,... | collective-permute-start | bytes 98312 | tf_op jit(solution)/shard_map/ppermute | solution.py:77
  40.4 5.2 %collective-permute-start.14 = (f32[8,1024]{1,0:T(8,128)S(1)}, f32[8,1024]{1,0:T(8,128)S(1)}, u32[]{:S(2)}, u32[]{:S(2)}) collective-permute-start(f32[8,1024]{1,0:T(8,128)S(1)} %get-tuple-element.58.refs_2_), channel_id=1, source_target_pairs={{0,24},{8,16},{16,8},{24,0},{1,25},{9,17},{17,9},{25,1},{2,26},{10... | collective-permute-start | bytes 98312 | tf_op jit(solution)/shard_map/ppermute | solution.py:77
  40.4 6.2 %collective-permute-start.15 = (f32[8,1024]{1,0:T(8,128)S(1)}, f32[8,1024]{1,0:T(8,128)S(1)}, u32[]{:S(2)}, u32[]{:S(2)}) collective-permute-start(f32[8,1024]{1,0:T(8,128)S(1)} %get-tuple-element.59.refs_3_), channel_id=1, source_target_pairs={{0,8},{8,0},{16,24},{24,16},{1,9},{9,1},{17,25},{25,17},{2,10},{10... | collective-permute-start | bytes 98312 | tf_op jit(solution)/shard_map/ppermute | solution.py:77
  42.8 8.7 %collective-permute-start.16 = (f32[8,1024]{1,0:T(8,128)S(1)}, f32[8,1024]{1,0:T(8,128)S(1)}, u32[]{:S(2)}, u32[]{:S(2)}) collective-permute-start(f32[8,1024]{1,0:T(8,128)S(1)} %get-tuple-element.63.refs_0_), channel_id=1, source_target_pairs={{0,6},{2,4},{4,2},{6,0},{1,7},{3,5},{5,3},{7,1},{8,14},{10,12},{12... | collective-permute-start | bytes 98312 | tf_op jit(solution)/shard_map/ppermute | solution.py:77
  44.5 7.0 %collective-permute-start.17 = (f32[8,1024]{1,0:T(8,128)S(1)}, f32[8,1024]{1,0:T(8,128)S(1)}, u32[]{:S(2)}, u32[]{:S(2)}) collective-permute-start(f32[8,1024]{1,0:T(8,128)S(1)} %get-tuple-element.64.refs_1_), channel_id=1, source_target_pairs={{0,2},{2,0},{4,6},{6,4},{1,3},{3,1},{5,7},{7,5},{8,10},{10,8},{12,... | collective-permute-start | bytes 98312 | tf_op jit(solution)/shard_map/ppermute | solution.py:77
  45.0 6.6 %collective-permute-start.18 = (f32[8,1024]{1,0:T(8,128)S(1)}, f32[8,1024]{1,0:T(8,128)S(1)}, u32[]{:S(2)}, u32[]{:S(2)}) collective-permute-start(f32[8,1024]{1,0:T(8,128)S(1)} %get-tuple-element.65.refs_2_), channel_id=1, source_target_pairs={{0,24},{8,16},{16,8},{24,0},{1,25},{9,17},{17,9},{25,1},{2,26},{10... | collective-permute-start | bytes 98312 | tf_op jit(solution)/shard_map/ppermute | solution.py:77
  45.6 5.9 %collective-permute-start.19 = (f32[8,1024]{1,0:T(8,128)S(1)}, f32[8,1024]{1,0:T(8,128)S(1)}, u32[]{:S(2)}, u32[]{:S(2)}) collective-permute-start(f32[8,1024]{1,0:T(8,128)S(1)} %get-tuple-element.66.refs_3_), channel_id=1, source_target_pairs={{0,8},{8,0},{16,24},{24,16},{1,9},{9,1},{17,25},{25,17},{2,10},{10... | collective-permute-start | bytes 98312 | tf_op jit(solution)/shard_map/ppermute | solution.py:77

commit v9 on v8

--- a/solution.py
+++ b/solution.py
@@ -155,11 +155,10 @@
     skip = extra if phase else 0
     stack = stack_of(phase)
     chunk = chunk_of(rows, 1024)
-    lead = chunk - skip if skip else 0
-    if lead:
-        step(phase, stack, skip, lead, 0)
-
-    @pl.loop(1 if lead else 0, rows // chunk)
+    lead = chunk - skip if skip else min(2 * chunk, rows)
+    step(phase, stack, skip, lead, 0)
+
+    @pl.loop((skip + lead) // chunk, rows // chunk)
     def _(index):
         row = pl.multiple_of(index * chunk, chunk)
         step(phase, stack, row, chunk, pl.multiple_of(row - skip, min(chunk, extra or chunk)))

time: 59.6 us -> 59.7 us (level)
  no operation moved by 1% of the time
where the time goes in v9:
time: 59.7 us; the launch traced here: 59.5 us
  Pallas kernels  36 us (60%)
  starting transfers between devices  20.3 us (34%)
  waiting for transfers between devices  2.3 us (4%)
  between operations  0.91 us (2%)
    ppermute x16, starting transfers between devices, exchange(): swapped.append(lax.ppermute(value, axis, pairs))  13.8 us
    pallas_call x2, Pallas kernels, mix(): pl.pallas_call(functools.partial(mix_kernel, mat, chunk, 3 * steps // 8),...  12.8 us
    pallas_call x2, Pallas kernels, project(): pl.pallas_call(functools.partial(project_kernel, phase, extra, size, firs...  11.4 us
    pallas_call x2, Pallas kernels, back(): pl.pallas_call(functools.partial(back_kernel, mat, extra), name=f'back{ma...  7.62 us
    pallas_call x1, Pallas kernels, load(): pl.pallas_call(functools.partial(load_kernel, size, until), name='load',...  3.5 us
    ppermute x2, starting transfers between devices, from_partner(): return lax.ppermute(value, axis, [(i, i ^ distance) for i in range(count)])  3.34 us
    ppermute x2, starting transfers between devices, shifted(): return lax.ppermute(value, axis, pairs)  3.14 us
  transfers between devices with their start and end apart: 20, of which 4 were waited for; matrix products, arithmetic and copies ran while one was open for 0% of the time, Pallas kernels for 36%

profile of v9, /device:TPU:0, one launch (start us, length us, event | category | flops | bytes accessed | tf_op | source)
XLA Modules:
  0.0 59.5 jit_solution(16125629013839690714)
XLA Ops:
  0.7 0.5 collective-permute-start.1
  1.2 2.6 %collective-permute-start = (f32[1,1,2,8,1024]{4,3,2,1,0:T(8,128)}, f32[1,1,2,8,1024]{4,3,2,1,0:T(8,128)S(1)}, u32[]{:S(2)}, u32[]{:S(2)}) collective-permute-start(f32[1,1,2,8,1024]{4,3,2,1,0:T(8,128)} %f0.3), channel_id=1, source_target_pairs={{0,2},{2,4},{4,6},{6,0},{1,3},{3,5},{5,7},{7,1},{8,10},{10,12},{12... | collective-permute-start | bytes 196616 | tf_op jit(solution)/shard_map/ppermute | solution.py:63
  3.8 3.5 %load.1.same = f32[2,4096,1024]{2,1,0:T(8,128)S(1)} custom-call(f32[1,1,2,4096,1024]{4,3,2,1,0:T(8,128)} %weights.5), custom_call_target="tpu_custom_call" | custom-call | tf_op jit(solution)/shard_map/load/pallas_call | solution.py:108
  7.3 0.0 collective-permute-done.1.f3
  7.3 1.0 %collective-permute-done.f1 = f32[1,1,2,8,1024]{4,3,2,1,0:T(8,128)S(1)} collective-permute-done((f32[1,1,2,8,1024]{4,3,2,1,0:T(8,128)}, f32[1,1,2,8,1024]{4,3,2,1,0:T(8,128)S(1)}, u32[]{:S(2)}, u32[]{:S(2)}) %collective-permute-start) | collective-permute-done | bytes 65568 | tf_op jit(solution)/shard_map/ppermute | solution.py:63
  8.3 6.4 %project0.1 = (f32[8,4608]{1,0:T(8,128)S(1)}, f32[8,4608]{1,0:T(8,128)S(1)}, f32[8,4608]{1,0:T(8,128)S(1)}, f32[8,4608]{1,0:T(8,128)S(1)}, f32[2,4096,1024]{2,1,0:T(8,128)S(1)}) custom-call(f32[2,4096,1024]{2,1,0:T(8,128)S(1)} %load.1.same, f32[1,1,2,8,1024]{4,3,2,1,0:T(8,128)S(1)} %copy-done, ...), custom_call_target="tpu_custom_call", output_to_operand_aliasing={{4}: (0, {})} | custom-call | flops 4294967296 | bytes 33554432 | tf_op jit(solution)/shard_map/project0/pallas_call | solution.py:178
  14.7 2.3 %collective-permute-start.2 = (f32[8,4608]{1,0:T(8,128)S(1)}, f32[8,4608]{1,0:T(8,128)S(1)}, u32[]{:S(2)}, u32[]{:S(2)}) collective-permute-start(f32[8,4608]{1,0:T(8,128)S(1)} %get-tuple-element.40.refs_0_), channel_id=1, source_target_pairs={{0,6},{2,4},{4,2},{6,0},{1,7},{3,5},{5,3},{7,1},{8,14},{10,12},{12... | collective-permute-start | bytes 442376 | tf_op jit(solution)/shard_map/ppermute | solution.py:77
  16.9 0.0 collective-permute-start.3
  17.0 0.8 %collective-permute-start.4 = (f32[8,4608]{1,0:T(8,128)S(1)}, f32[8,4608]{1,0:T(8,128)S(1)}, u32[]{:S(2)}, u32[]{:S(2)}) collective-permute-start(f32[8,4608]{1,0:T(8,128)S(1)} %get-tuple-element.42.refs_2_), channel_id=1, source_target_pairs={{0,24},{8,16},{16,8},{24,0},{1,25},{9,17},{17,9},{25,1},{2,26},{10... | collective-permute-start | bytes 442376 | tf_op jit(solution)/shard_map/ppermute | solution.py:77
  17.8 0.9 %collective-permute-start.5 = (f32[8,4608]{1,0:T(8,128)S(1)}, f32[8,4608]{1,0:T(8,128)S(1)}, u32[]{:S(2)}, u32[]{:S(2)}) collective-permute-start(f32[8,4608]{1,0:T(8,128)S(1)} %get-tuple-element.43.refs_3_), channel_id=1, source_target_pairs={{0,8},{8,0},{16,24},{24,16},{1,9},{9,1},{17,25},{25,17},{2,10},{10... | collective-permute-start | bytes 442376 | tf_op jit(solution)/shard_map/ppermute | solution.py:77
  18.7 5.1 %project1.1 = (f32[8,3584]{1,0:T(8,128)S(1)}, f32[8,3584]{1,0:T(8,128)S(1)}, f32[8,3584]{1,0:T(8,128)S(1)}, f32[8,3584]{1,0:T(8,128)S(1)}, f32[2,4096,1024]{2,1,0:T(8,128)S(1)}) custom-call(f32[2,4096,1024]{2,1,0:T(8,128)S(1)} %get-tuple-element.38.same, f32[1,1,2,8,1024]{4,3,2,1,0:T(8,128)S(1)} %copy-done, ...), custom_call_target="tpu_custom_call", output_to_operand_aliasing={{4}: (0, {})} | custom-call | flops 4294967296 | bytes 33554432 | tf_op jit(solution)/shard_map/project1/pallas_call | solution.py:178
  23.8 2.1 %collective-permute-start.6 = (f32[8,3584]{1,0:T(8,128)S(1)}, f32[8,3584]{1,0:T(8,128)S(1)}, u32[]{:S(2)}, u32[]{:S(2)}) collective-permute-start(f32[8,3584]{1,0:T(8,128)S(1)} %get-tuple-element.45.refs_4_), channel_id=1, source_target_pairs={{0,6},{2,4},{4,2},{6,0},{1,7},{3,5},{5,3},{7,1},{8,14},{10,12},{12... | collective-permute-start | bytes 344072 | tf_op jit(solution)/shard_map/ppermute | solution.py:77
  25.9 0.0 collective-permute-done.2.refs_4_.refs_8_
  25.9 1.1 %collective-permute-start.7 = (f32[8,3584]{1,0:T(8,128)S(1)}, f32[8,3584]{1,0:T(8,128)S(1)}, u32[]{:S(2)}, u32[]{:S(2)}) collective-permute-start(f32[8,3584]{1,0:T(8,128)S(1)} %get-tuple-element.46.refs_5_), channel_id=1, source_target_pairs={{0,2},{2,0},{4,6},{6,4},{1,3},{3,1},{5,7},{7,5},{8,10},{10,8},{12,... | collective-permute-start | bytes 344072 | tf_op jit(solution)/shard_map/ppermute | solution.py:77
  27.0 0.0 collective-permute-done.3.refs_5_.refs_9_
  27.0 0.0 collective-permute-start.8
  27.0 0.0 collective-permute-done.4.refs_6_.refs_10_
  27.0 0.1 collective-permute-start.9
  27.1 0.0 collective-permute-done.5.refs_7_.refs_11_
  27.1 3.8 %back0.1 = (f32[32,4096]{1,0:T(8,128)S(1)}, f32[32,1152]{1,0:T(8,128)S(1)}, f32[2,4096,1024]{2,1,0:T(8,128)S(1)}) custom-call(f32[2,4096,1024]{2,1,0:T(8,128)S(1)} %get-tuple-element.39.same, f32[8,4608]{1,0:T(8,128)S(1)} %get-tuple-element.40.refs_0_, f32[8,4608]{1,0:T(8,128)S(1)} %get-tuple-element.41.refs_1_, ...), custom_call_target="tpu_custom_call", output_to_operand_aliasing={{2}: (0, {})} | custom-call | flops 4294967296 | bytes 33554432 | tf_op jit(solution)/shard_map/back0/pallas_call | solution.py:229
  30.9 1.8 %collective-permute-start.10 = (f32[32,1152]{1,0:T(8,128)S(1)}, f32[32,1152]{1,0:T(8,128)S(1)}, u32[]{:S(2)}, u32[]{:S(2)}) collective-permute-start(f32[32,1152]{1,0:T(8,128)S(1)} %get-tuple-element.50.mine), channel_id=1, source_target_pairs={{0,1},{1,0},{2,3},{3,2},{4,5},{5,4},{6,7},{7,6},{8,9},{9,8},{10,11... | collective-permute-start | bytes 442376 | tf_op jit(solution)/shard_map/ppermute | solution.py:68
  32.8 0.0 collective-permute-done.6.refs_12_
  32.8 0.4 collective-permute-done.7.refs_13_
  33.1 0.0 collective-permute-done.8.refs_14_
  33.1 0.0 collective-permute-done.9.refs_15_
  33.1 3.8 %back1.1 = (f32[32,4096]{1,0:T(8,128)S(1)}, f32[32,1152]{1,0:T(8,128)S(1)}, f32[2,4096,1024]{2,1,0:T(8,128)S(1)}) custom-call(f32[2,4096,1024]{2,1,0:T(8,128)S(1)} %get-tuple-element.44.same, f32[8,4608]{1,0:T(8,128)S(1)} %get-tuple-element.40.refs_0_, f32[8,4608]{1,0:T(8,128)S(1)} %get-tuple-element.41.refs_1_, ...), custom_call_target="tpu_custom_call", output_to_operand_aliasing={{2}: (0, {})} | custom-call | flops 4294967296 | bytes 33554432 | tf_op jit(solution)/shard_map/back1/pallas_call | solution.py:229
  36.9 1.5 %collective-permute-start.11 = (f32[32,1152]{1,0:T(8,128)S(1)}, f32[32,1152]{1,0:T(8,128)S(1)}, u32[]{:S(2)}, u32[]{:S(2)}) collective-permute-start(f32[32,1152]{1,0:T(8,128)S(1)} %get-tuple-element.53.mine.refs_8_), channel_id=1, source_target_pairs={{0,1},{1,0},{2,3},{3,2},{4,5},{5,4},{6,7},{7,6},{8,9},{9,8},{10,11... | collective-permute-start | bytes 442376 | tf_op jit(solution)/shard_map/ppermute | solution.py:68
  38.5 0.0 collective-permute-done.10.other
  38.5 1.8 %collective-permute-start.12 = (f32[8,1024]{1,0:T(8,128)S(1)}, f32[8,1024]{1,0:T(8,128)S(1)}, u32[]{:S(2)}, u32[]{:S(2)}) collective-permute-start(f32[8,1024]{1,0:T(8,128)S(1)} %get-tuple-element.56.refs_0_), channel_id=1, source_target_pairs={{0,6},{2,4},{4,2},{6,0},{1,7},{3,5},{5,3},{7,1},{8,14},{10,12},{12... | collective-permute-start | bytes 98312 | tf_op jit(solution)/shard_map/ppermute | solution.py:77
  40.3 0.0 collective-permute-start.13
  40.3 0.0 collective-permute-start.14
  40.3 1.0 %collective-permute-start.15 = (f32[8,1024]{1,0:T(8,128)S(1)}, f32[8,1024]{1,0:T(8,128)S(1)}, u32[]{:S(2)}, u32[]{:S(2)}) collective-permute-start(f32[8,1024]{1,0:T(8,128)S(1)} %get-tuple-element.59.refs_3_), channel_id=1, source_target_pairs={{0,8},{8,0},{16,24},{24,16},{1,9},{9,1},{17,25},{25,17},{2,10},{10... | collective-permute-start | bytes 98312 | tf_op jit(solution)/shard_map/ppermute | solution.py:77
  41.3 0.7 %inverse.1 = (f32[32,128]{1,0:T(8,128)S(1)}, f32[2,4096,1024]{2,1,0:T(8,128)S(1)}) custom-call(f32[2,4096,1024]{2,1,0:T(8,128)S(1)} %get-tuple-element.51.same, f32[32,1152]{1,0:T(8,128)S(1)} %get-tuple-element.50.mine, f32[32,1152]{1,0:T(8,128)S(1)} %collective-permute-done.10.other), custom_call_target="tpu_custom_call", output_to_operand_aliasing={{1}: (0, {})} | custom-call | tf_op jit(solution)/shard_map/inverse/pallas_call | solution.py:288
  41.9 0.7 %collective-permute-done.11.other.refs_9_ = f32[32,1152]{1,0:T(8,128)S(1)} collective-permute-done((f32[32,1152]{1,0:T(8,128)S(1)}, f32[32,1152]{1,0:T(8,128)S(1)}, u32[]{:S(2)}, u32[]{:S(2)}) %collective-permute-start.11) | collective-permute-done | bytes 147488 | tf_op jit(solution)/shard_map/ppermute | solution.py:68
  42.6 1.5 %collective-permute-start.16 = (f32[8,1024]{1,0:T(8,128)S(1)}, f32[8,1024]{1,0:T(8,128)S(1)}, u32[]{:S(2)}, u32[]{:S(2)}) collective-permute-start(f32[8,1024]{1,0:T(8,128)S(1)} %get-tuple-element.63.refs_0_), channel_id=1, source_target_pairs={{0,6},{2,4},{4,2},{6,0},{1,7},{3,5},{5,3},{7,1},{8,14},{10,12},{12... | collective-permute-start | bytes 98312 | tf_op jit(solution)/shard_map/ppermute | solution.py:77
  44.1 0.2 collective-permute-done.12.refs_4_
  44.4 0.4 collective-permute-start.17
  44.8 0.0 collective-permute-done.13.refs_5_
  44.8 0.6 %collective-permute-start.18 = (f32[8,1024]{1,0:T(8,128)S(1)}, f32[8,1024]{1,0:T(8,128)S(1)}, u32[]{:S(2)}, u32[]{:S(2)}) collective-permute-start(f32[8,1024]{1,0:T(8,128)S(1)} %get-tuple-element.65.refs_2_), channel_id=1, source_target_pairs={{0,24},{8,16},{16,8},{24,0},{1,25},{9,17},{17,9},{25,1},{2,26},{10... | collective-permute-start | bytes 98312 | tf_op jit(solution)/shard_map/ppermute | solution.py:77
  45.5 0.0 collective-permute-done.14.refs_6_
  45.5 1.1 %collective-permute-start.19 = (f32[8,1024]{1,0:T(8,128)S(1)}, f32[8,1024]{1,0:T(8,128)S(1)}, u32[]{:S(2)}, u32[]{:S(2)}) collective-permute-start(f32[8,1024]{1,0:T(8,128)S(1)} %get-tuple-element.66.refs_3_), channel_id=1, source_target_pairs={{0,8},{8,0},{16,24},{24,16},{1,9},{9,1},{17,25},{25,17},{2,10},{10... | collective-permute-start | bytes 98312 | tf_op jit(solution)/shard_map/ppermute | solution.py:77
  46.6 0.0 collective-permute-done.15.refs_7_
  46.6 4.8 %mix0.1 = (f32[1,1,2,4096,1024]{4,3,2,1,0:T(8,128)}, f32[1,1,2,8,1024]{4,3,2,1,0:T(8,128)}, f32[1,1,2,8,1024]{4,3,2,1,0:T(8,128)}, f32[2,4096,1024]{2,1,0:T(8,128)S(1)}) custom-call(f32[2,4096,1024]{2,1,0:T(8,128)S(1)} %get-tuple-element.54.same, f32[32,4096]{1,0:T(8,128)S(1)} %get-tuple-element.55.differ, ...), custom_call_target="tpu_custom_call", output_to_operand_aliasing={{3}: (0, {})} | custom-call | flops 4294967296 | bytes 33554432 | tf_op jit(solution)/shard_map/mix0/pallas_call | solution.py:388
  51.4 0.0 collective-permute-done.16.refs_4_
  51.4 0.0 collective-permute-done.17.refs_5_
  51.4 0.0 collective-permute-done.18.refs_6_
  51.4 0.0 collective-permute-done.19.refs_7_
  51.4 7.9 %mix1.1 = (f32[1,1,2,4096,1024]{4,3,2,1,0:T(8,128)}, f32[1,1,2,8,1024]{4,3,2,1,0:T(8,128)}, f32[1,1,2,8,1024]{4,3,2,1,0:T(8,128)}, f32[2,4096,1024]{2,1,0:T(8,128)S(1)}) custom-call(f32[2,4096,1024]{2,1,0:T(8,128)S(1)} %get-tuple-element.61.same, ...), custom_call_target="tpu_custom_call", output_to_operand_aliasing={{3}: (0, {}), {0}: (12, {}), {1}: (13, {}), {2}: (14, {})} | custom-call | flops 4294967296 | bytes 33554432 | tf_op jit(solution)/shard_map/mix1/pallas_call | solution.py:388
  (6 shorter events, 0.0 us)
Async XLA Ops:
  0.6 7.6 %copy-start.1 = (f32[1,1,2,8,1024]{4,3,2,1,0:T(8,128)S(1)}, f32[1,1,2,8,1024]{4,3,2,1,0:T(8,128)}, u32[]{:S(2)}) copy-start(f32[1,1,2,8,1024]{4,3,2,1,0:T(8,128)} %f2.3) | copy-start | bytes 196612
  0.6 7.6 %copy-start = (f32[1,1,2,8,1024]{4,3,2,1,0:T(8,128)S(1)}, f32[1,1,2,8,1024]{4,3,2,1,0:T(8,128)}, u32[]{:S(2)}) copy-start(f32[1,1,2,8,1024]{4,3,2,1,0:T(8,128)} %f0.3) | copy-start | bytes 196612
  0.7 6.7 %collective-permute-start.1 = (f32[1,1,2,8,1024]{4,3,2,1,0:T(8,128)}, f32[1,1,2,8,1024]{4,3,2,1,0:T(8,128)S(1)}, u32[]{:S(2)}, u32[]{:S(2)}) collective-permute-start(f32[1,1,2,8,1024]{4,3,2,1,0:T(8,128)} %f2.3), channel_id=1, source_target_pairs={{0,8},{8,16},{16,24},{24,0},{1,9},{9,17},{17,25},{25,1},{2,10},{10... | collective-permute-start | bytes 196616 | tf_op jit(solution)/shard_map/ppermute | solution.py:63
  1.2 7.1 %collective-permute-start = (f32[1,1,2,8,1024]{4,3,2,1,0:T(8,128)}, f32[1,1,2,8,1024]{4,3,2,1,0:T(8,128)S(1)}, u32[]{:S(2)}, u32[]{:S(2)}) collective-permute-start(f32[1,1,2,8,1024]{4,3,2,1,0:T(8,128)} %f0.3), channel_id=1, source_target_pairs={{0,2},{2,4},{4,6},{6,0},{1,3},{3,5},{5,7},{7,1},{8,10},{10,12},{12... | collective-permute-start | bytes 196616 | tf_op jit(solution)/shard_map/ppermute | solution.py:63
  14.7 11.2 %collective-permute-start.2 = (f32[8,4608]{1,0:T(8,128)S(1)}, f32[8,4608]{1,0:T(8,128)S(1)}, u32[]{:S(2)}, u32[]{:S(2)}) collective-permute-start(f32[8,4608]{1,0:T(8,128)S(1)} %get-tuple-element.40.refs_0_), channel_id=1, source_target_pairs={{0,6},{2,4},{4,2},{6,0},{1,7},{3,5},{5,3},{7,1},{8,14},{10,12},{12... | collective-permute-start | bytes 442376 | tf_op jit(solution)/shard_map/ppermute | solution.py:77
  16.9 10.1 %collective-permute-start.3 = (f32[8,4608]{1,0:T(8,128)S(1)}, f32[8,4608]{1,0:T(8,128)S(1)}, u32[]{:S(2)}, u32[]{:S(2)}) collective-permute-start(f32[8,4608]{1,0:T(8,128)S(1)} %get-tuple-element.41.refs_1_), channel_id=1, source_target_pairs={{0,2},{2,0},{4,6},{6,4},{1,3},{3,1},{5,7},{7,5},{8,10},{10,8},{12,... | collective-permute-start | bytes 442376 | tf_op jit(solution)/shard_map/ppermute | solution.py:77
  17.0 10.1 %collective-permute-start.4 = (f32[8,4608]{1,0:T(8,128)S(1)}, f32[8,4608]{1,0:T(8,128)S(1)}, u32[]{:S(2)}, u32[]{:S(2)}) collective-permute-start(f32[8,4608]{1,0:T(8,128)S(1)} %get-tuple-element.42.refs_2_), channel_id=1, source_target_pairs={{0,24},{8,16},{16,8},{24,0},{1,25},{9,17},{17,9},{25,1},{2,26},{10... | collective-permute-start | bytes 442376 | tf_op jit(solution)/shard_map/ppermute | solution.py:77
  17.8 9.3 %collective-permute-start.5 = (f32[8,4608]{1,0:T(8,128)S(1)}, f32[8,4608]{1,0:T(8,128)S(1)}, u32[]{:S(2)}, u32[]{:S(2)}) collective-permute-start(f32[8,4608]{1,0:T(8,128)S(1)} %get-tuple-element.43.refs_3_), channel_id=1, source_target_pairs={{0,8},{8,0},{16,24},{24,16},{1,9},{9,1},{17,25},{25,17},{2,10},{10... | collective-permute-start | bytes 442376 | tf_op jit(solution)/shard_map/ppermute | solution.py:77
  23.8 9.0 %collective-permute-start.6 = (f32[8,3584]{1,0:T(8,128)S(1)}, f32[8,3584]{1,0:T(8,128)S(1)}, u32[]{:S(2)}, u32[]{:S(2)}) collective-permute-start(f32[8,3584]{1,0:T(8,128)S(1)} %get-tuple-element.45.refs_4_), channel_id=1, source_target_pairs={{0,6},{2,4},{4,2},{6,0},{1,7},{3,5},{5,3},{7,1},{8,14},{10,12},{12... | collective-permute-start | bytes 344072 | tf_op jit(solution)/shard_map/ppermute | solution.py:77
  25.9 7.2 %collective-permute-start.7 = (f32[8,3584]{1,0:T(8,128)S(1)}, f32[8,3584]{1,0:T(8,128)S(1)}, u32[]{:S(2)}, u32[]{:S(2)}) collective-permute-start(f32[8,3584]{1,0:T(8,128)S(1)} %get-tuple-element.46.refs_5_), channel_id=1, source_target_pairs={{0,2},{2,0},{4,6},{6,4},{1,3},{3,1},{5,7},{7,5},{8,10},{10,8},{12,... | collective-permute-start | bytes 344072 | tf_op jit(solution)/shard_map/ppermute | solution.py:77
  27.0 6.1 %collective-permute-start.8 = (f32[8,3584]{1,0:T(8,128)S(1)}, f32[8,3584]{1,0:T(8,128)S(1)}, u32[]{:S(2)}, u32[]{:S(2)}) collective-permute-start(f32[8,3584]{1,0:T(8,128)S(1)} %get-tuple-element.47.refs_6_), channel_id=1, source_target_pairs={{0,24},{8,16},{16,8},{24,0},{1,25},{9,17},{17,9},{25,1},{2,26},{10... | collective-permute-start | bytes 344072 | tf_op jit(solution)/shard_map/ppermute | solution.py:77
  27.0 6.1 %collective-permute-start.9 = (f32[8,3584]{1,0:T(8,128)S(1)}, f32[8,3584]{1,0:T(8,128)S(1)}, u32[]{:S(2)}, u32[]{:S(2)}) collective-permute-start(f32[8,3584]{1,0:T(8,128)S(1)} %get-tuple-element.48.refs_7_), channel_id=1, source_target_pairs={{0,8},{8,0},{16,24},{24,16},{1,9},{9,1},{17,25},{25,17},{2,10},{10... | collective-permute-start | bytes 344072 | tf_op jit(solution)/shard_map/ppermute | solution.py:77
  30.9 7.5 %collective-permute-start.10 = (f32[32,1152]{1,0:T(8,128)S(1)}, f32[32,1152]{1,0:T(8,128)S(1)}, u32[]{:S(2)}, u32[]{:S(2)}) collective-permute-start(f32[32,1152]{1,0:T(8,128)S(1)} %get-tuple-element.50.mine), channel_id=1, source_target_pairs={{0,1},{1,0},{2,3},{3,2},{4,5},{5,4},{6,7},{7,6},{8,9},{9,8},{10,11... | collective-permute-start | bytes 442376 | tf_op jit(solution)/shard_map/ppermute | solution.py:68
  36.9 5.7 %collective-permute-start.11 = (f32[32,1152]{1,0:T(8,128)S(1)}, f32[32,1152]{1,0:T(8,128)S(1)}, u32[]{:S(2)}, u32[]{:S(2)}) collective-permute-start(f32[32,1152]{1,0:T(8,128)S(1)} %get-tuple-element.53.mine.refs_8_), channel_id=1, source_target_pairs={{0,1},{1,0},{2,3},{3,2},{4,5},{5,4},{6,7},{7,6},{8,9},{9,8},{10,11... | collective-permute-start | bytes 442376 | tf_op jit(solution)/shard_map/ppermute | solution.py:68
  38.5 5.9 %collective-permute-start.12 = (f32[8,1024]{1,0:T(8,128)S(1)}, f32[8,1024]{1,0:T(8,128)S(1)}, u32[]{:S(2)}, u32[]{:S(2)}) collective-permute-start(f32[8,1024]{1,0:T(8,128)S(1)} %get-tuple-element.56.refs_0_), channel_id=1, source_target_pairs={{0,6},{2,4},{4,2},{6,0},{1,7},{3,5},{5,3},{7,1},{8,14},{10,12},{12... | collective-permute-start | bytes 98312 | tf_op jit(solution)/shard_map/ppermute | solution.py:77
  40.3 4.5 %collective-permute-start.13 = (f32[8,1024]{1,0:T(8,128)S(1)}, f32[8,1024]{1,0:T(8,128)S(1)}, u32[]{:S(2)}, u32[]{:S(2)}) collective-permute-start(f32[8,1024]{1,0:T(8,128)S(1)} %get-tuple-element.57.refs_1_), channel_id=1, source_target_pairs={{0,2},{2,0},{4,6},{6,4},{1,3},{3,1},{5,7},{7,5},{8,10},{10,8},{12,... | collective-permute-start | bytes 98312 | tf_op jit(solution)/shard_map/ppermute | solution.py:77
  40.3 5.2 %collective-permute-start.14 = (f32[8,1024]{1,0:T(8,128)S(1)}, f32[8,1024]{1,0:T(8,128)S(1)}, u32[]{:S(2)}, u32[]{:S(2)}) collective-permute-start(f32[8,1024]{1,0:T(8,128)S(1)} %get-tuple-element.58.refs_2_), channel_id=1, source_target_pairs={{0,24},{8,16},{16,8},{24,0},{1,25},{9,17},{17,9},{25,1},{2,26},{10... | collective-permute-start | bytes 98312 | tf_op jit(solution)/shard_map/ppermute | solution.py:77
  40.3 6.2 %collective-permute-start.15 = (f32[8,1024]{1,0:T(8,128)S(1)}, f32[8,1024]{1,0:T(8,128)S(1)}, u32[]{:S(2)}, u32[]{:S(2)}) collective-permute-start(f32[8,1024]{1,0:T(8,128)S(1)} %get-tuple-element.59.refs_3_), channel_id=1, source_target_pairs={{0,8},{8,0},{16,24},{24,16},{1,9},{9,1},{17,25},{25,17},{2,10},{10... | collective-permute-start | bytes 98312 | tf_op jit(solution)/shard_map/ppermute | solution.py:77
  42.6 8.7 %collective-permute-start.16 = (f32[8,1024]{1,0:T(8,128)S(1)}, f32[8,1024]{1,0:T(8,128)S(1)}, u32[]{:S(2)}, u32[]{:S(2)}) collective-permute-start(f32[8,1024]{1,0:T(8,128)S(1)} %get-tuple-element.63.refs_0_), channel_id=1, source_target_pairs={{0,6},{2,4},{4,2},{6,0},{1,7},{3,5},{5,3},{7,1},{8,14},{10,12},{12... | collective-permute-start | bytes 98312 | tf_op jit(solution)/shard_map/ppermute | solution.py:77
  44.4 7.0 %collective-permute-start.17 = (f32[8,1024]{1,0:T(8,128)S(1)}, f32[8,1024]{1,0:T(8,128)S(1)}, u32[]{:S(2)}, u32[]{:S(2)}) collective-permute-start(f32[8,1024]{1,0:T(8,128)S(1)} %get-tuple-element.64.refs_1_), channel_id=1, source_target_pairs={{0,2},{2,0},{4,6},{6,4},{1,3},{3,1},{5,7},{7,5},{8,10},{10,8},{12,... | collective-permute-start | bytes 98312 | tf_op jit(solution)/shard_map/ppermute | solution.py:77
  44.8 6.6 %collective-permute-start.18 = (f32[8,1024]{1,0:T(8,128)S(1)}, f32[8,1024]{1,0:T(8,128)S(1)}, u32[]{:S(2)}, u32[]{:S(2)}) collective-permute-start(f32[8,1024]{1,0:T(8,128)S(1)} %get-tuple-element.65.refs_2_), channel_id=1, source_target_pairs={{0,24},{8,16},{16,8},{24,0},{1,25},{9,17},{17,9},{25,1},{2,26},{10... | collective-permute-start | bytes 98312 | tf_op jit(solution)/shard_map/ppermute | solution.py:77
  45.5 5.9 %collective-permute-start.19 = (f32[8,1024]{1,0:T(8,128)S(1)}, f32[8,1024]{1,0:T(8,128)S(1)}, u32[]{:S(2)}, u32[]{:S(2)}) collective-permute-start(f32[8,1024]{1,0:T(8,128)S(1)} %get-tuple-element.66.refs_3_), channel_id=1, source_target_pairs={{0,8},{8,0},{16,24},{24,16},{1,9},{9,1},{17,25},{25,17},{2,10},{10... | collective-permute-start | bytes 98312 | tf_op jit(solution)/shard_map/ppermute | solution.py:77

commit v10 on v8

--- a/solution.py
+++ b/solution.py
@@ -210,15 +210,17 @@
     pair = jnp.concatenate([high, low], 0)
     stack = jnp.concatenate([pair, pair], 1)
     both = dot(stack, jnp.concatenate([w_high, w_low], 0), NN)
-    sums[...] = jnp.zeros_like(sums)
-    sums[:, :features] = both[:width] + both[width:]
+    product = both[:width] + both[width:]
+    for block in range(features // 128):
+        sums[block * width : (block + 1) * width] = product[:, block * 128 : (block + 1) * 128]
+    sums[features // 128 * width :] = jnp.zeros((rank, 128), f32)
     gram = dot(pair, pair, NT)
     total = (gram[:width, :width] + gram[width:, width:]) + (
         gram[:width, width:] + gram[width:, :width]
     )
     for edge in range(edges):
         here = slice(edge * rank, (edge + 1) * rank)
-        sums[here, features : features + rank] = total[here, here]
+        sums[features // 128 * width :, here] = total[here, here]
 
 
 def back(held, own, near, mat, extra):
@@ -232,7 +234,7 @@
         name=f"back{mat}",
         out_shape=[
             jax.ShapeDtypeStruct((edges * rank, rows), f32),
-            jax.ShapeDtypeStruct((edges * rank, features + 128), f32),
+            jax.ShapeDtypeStruct((features // 128 * edges * rank + rank, 128), f32),
             jax.ShapeDtypeStruct(held.shape, f32),
         ],
         in_specs=[in_vmem] * (1 + len(ends)),
@@ -247,8 +249,10 @@
     *outs, held = refs
     rank, features = outs[0].shape
     for slot, out in enumerate(outs):
-        here = slice(slot * rank, (slot + 1) * rank)
-        out[...] = mine[here, :features] + other[here, :features]
+        for block in range(features // 128):
+            start = block * edges * rank + slot * rank
+            here = slice(start, start + rank)
+            out[:, block * 128 : (block + 1) * 128] = mine[here] + other[here]
 
 
 def add(held, pair, rank, mat):
@@ -270,7 +274,8 @@
     row = lax.broadcasted_iota(jnp.int32, shape, 1)
     lane = lax.broadcasted_iota(jnp.int32, shape, 2)
     slot = lax.broadcasted_iota(jnp.int32, shape, 0)
-    value = gram.reshape(shape)
+    turned = [gram] + [pltpu.roll(gram, 128 - edge * rank, 1) for edge in range(1, edges)]
+    value = jnp.concatenate(turned, 0).reshape(shape)
     value = jnp.where(lane < rank, value, (lane == width + slot * rank + row).astype(f32))
     pivots = jnp.ones((edges, rank, 1), f32)
     for j in range(rank):
@@ -278,11 +283,11 @@
         pivots = jnp.where(row[:, :, :1] == j, pivot, pivots)
         factor = jnp.where(row > j, value[:, :, j : j + 1] / pivot, 0.0)
         value = value - factor * value[:, j : j + 1, :]
-    return (value / jnp.sqrt(pivots)).reshape(width, 128)
+    return (value / jnp.sqrt(pivots)).reshape(width, 128)[:, width : 2 * width]
 
 
 def inverse_kernel(rank, same, mine, other, inverse, held):
-    inverse[...] = inverse_of(mine[:, -128:] + other[:, -128:], rank)
+    inverse[...] = inverse_of(mine[-rank:, :] + other[-rank:, :], rank)
 
 
 def inverse_factor(held, pair, rank):
@@ -290,7 +295,7 @@
         functools.partial(inverse_kernel, rank),
         name="inverse",
         out_shape=[
-            jax.ShapeDtypeStruct((edges * rank, 128), f32),
+            jax.ShapeDtypeStruct((edges * rank, edges * rank), f32),
             jax.ShapeDtypeStruct(held.shape, f32),
         ],
         in_specs=[in_vmem] * 3,
@@ -319,10 +324,9 @@
     for other in left:
         other.start()
     if mat:
-        factor = inverse_of(factors[0][:, -128:] + factors[1][:, -128:], rank)
+        factor = inverse_of(factors[0][-rank:, :] + factors[1][-rank:, :], rank)
     else:
         factor = factors[0][...]
-    factor = factor[:, width : 2 * width]
     total = jnp.concatenate([b[...] + n[...] for b, n in zip(sums, near)], 0)
     updated = lax.dot_general(
         factor, total, NN, precision=lax.Precision.HIGHEST, preferred_element_type=f32
@@ -339,10 +343,12 @@
         lhs = jnp.concatenate([high, low, high, low], 0)
         held[mat, here, :] -= dot(lhs, terms, TN)
 
-    halves = [copy(mat, 0, chunk // 2, 0), copy(mat, chunk // 2, chunk // 2, steps + 1)]
-    for half in range(2):
-        correct(half * (chunk // 2), chunk // 2)
-        halves[half].start()
+    cut = chunk // 2
+    halves = [copy(mat, 0, cut, 0), copy(mat, cut, chunk - cut, steps + 1)]
+    correct(0, cut)
+    halves[0].start()
+    correct(cut, chunk - cut)
+    halves[1].start()
 
     def place(step):
         return pl.multiple_of(step * chunk, chunk)
@@ -387,7 +393,7 @@
     args += [hbm(array) for array in previous]
     shapes = (*shapes, held.shape)
     return pl.pallas_call(
-        functools.partial(mix_kernel, mat, chunk, 3 * steps // 8),
+        functools.partial(mix_kernel, mat, chunk, steps // 4),
         name=f"mix{mat}",
         out_shape=[jax.ShapeDtypeStruct(shape, f32) for shape in shapes],
         in_specs=specs,

time: 59.6 us -> 59.6 us (level)
  transfers between devices with their start and end apart: 20 -> 20, of which waited for: 4 -> 4; matrix products, arithmetic and copies ran while one was open for 0% -> 0% of each run, Pallas kernels for 36% -> 37%
where the time goes in v10:
time: 59.6 us; the launch traced here: 59.5 us
  Pallas kernels  36.1 us (61%)
  starting transfers between devices  20.4 us (34%)
  waiting for transfers between devices  2.17 us (4%)
  between operations  0.75 us (1%)
    ppermute x16, starting transfers between devices, exchange(): swapped.append(lax.ppermute(value, axis, pairs))  14 us
    pallas_call x2, Pallas kernels, mix(): pl.pallas_call(functools.partial(mix_kernel, mat, chunk, steps // 4), nam...  12.7 us
    pallas_call x2, Pallas kernels, project(): pl.pallas_call(functools.partial(project_kernel, phase, extra, size, firs...  11.6 us
    pallas_call x2, Pallas kernels, back(): pl.pallas_call(functools.partial(back_kernel, mat, extra), name=f'back{ma...  7.56 us
    pallas_call x1, Pallas kernels, load(): pl.pallas_call(functools.partial(load_kernel, size, until), name='load',...  3.5 us
    ppermute x2, starting transfers between devices, from_partner(): return lax.ppermute(value, axis, [(i, i ^ distance) for i in range(count)])  3.35 us
    ppermute x2, starting transfers between devices, shifted(): return lax.ppermute(value, axis, pairs)  3.14 us
  transfers between devices with their start and end apart: 20, of which 4 were waited for; matrix products, arithmetic and copies ran while one was open for 0% of the time, Pallas kernels for 37%

profile of v10, /device:TPU:0, one launch (start us, length us, event | category | flops | bytes accessed | tf_op | source)
XLA Modules:
  0.0 59.5 jit_solution(4366681203133712067)
XLA Ops:
  0.7 0.5 collective-permute-start.1
  1.2 2.6 %collective-permute-start = (f32[1,1,2,8,1024]{4,3,2,1,0:T(8,128)}, f32[1,1,2,8,1024]{4,3,2,1,0:T(8,128)S(1)}, u32[]{:S(2)}, u32[]{:S(2)}) collective-permute-start(f32[1,1,2,8,1024]{4,3,2,1,0:T(8,128)} %f0.3), channel_id=1, source_target_pairs={{0,2},{2,4},{4,6},{6,0},{1,3},{3,5},{5,7},{7,1},{8,10},{10,12},{12... | collective-permute-start | bytes 196616 | tf_op jit(solution)/shard_map/ppermute | solution.py:63
  3.8 3.5 %load.1.same = f32[2,4096,1024]{2,1,0:T(8,128)S(1)} custom-call(f32[1,1,2,4096,1024]{4,3,2,1,0:T(8,128)} %weights.5), custom_call_target="tpu_custom_call" | custom-call | tf_op jit(solution)/shard_map/load/pallas_call | solution.py:108
  7.3 0.0 collective-permute-done.1.f3
  7.3 1.0 %collective-permute-done.f1 = f32[1,1,2,8,1024]{4,3,2,1,0:T(8,128)S(1)} collective-permute-done((f32[1,1,2,8,1024]{4,3,2,1,0:T(8,128)}, f32[1,1,2,8,1024]{4,3,2,1,0:T(8,128)S(1)}, u32[]{:S(2)}, u32[]{:S(2)}) %collective-permute-start) | collective-permute-done | bytes 65568 | tf_op jit(solution)/shard_map/ppermute | solution.py:63
  8.3 6.5 %project0.1 = (f32[8,4608]{1,0:T(8,128)S(1)}, f32[8,4608]{1,0:T(8,128)S(1)}, f32[8,4608]{1,0:T(8,128)S(1)}, f32[8,4608]{1,0:T(8,128)S(1)}, f32[2,4096,1024]{2,1,0:T(8,128)S(1)}) custom-call(f32[2,4096,1024]{2,1,0:T(8,128)S(1)} %load.1.same, f32[1,1,2,8,1024]{4,3,2,1,0:T(8,128)S(1)} %copy-done, ...), custom_call_target="tpu_custom_call", output_to_operand_aliasing={{4}: (0, {})} | custom-call | flops 4294967296 | bytes 33554432 | tf_op jit(solution)/shard_map/project0/pallas_call | solution.py:179
  14.8 2.3 %collective-permute-start.2 = (f32[8,4608]{1,0:T(8,128)S(1)}, f32[8,4608]{1,0:T(8,128)S(1)}, u32[]{:S(2)}, u32[]{:S(2)}) collective-permute-start(f32[8,4608]{1,0:T(8,128)S(1)} %get-tuple-element.40.refs_0_), channel_id=1, source_target_pairs={{0,6},{2,4},{4,2},{6,0},{1,7},{3,5},{5,3},{7,1},{8,14},{10,12},{12... | collective-permute-start | bytes 442376 | tf_op jit(solution)/shard_map/ppermute | solution.py:77
  17.1 0.0 collective-permute-start.3
  17.1 0.8 %collective-permute-start.4 = (f32[8,4608]{1,0:T(8,128)S(1)}, f32[8,4608]{1,0:T(8,128)S(1)}, u32[]{:S(2)}, u32[]{:S(2)}) collective-permute-start(f32[8,4608]{1,0:T(8,128)S(1)} %get-tuple-element.42.refs_2_), channel_id=1, source_target_pairs={{0,24},{8,16},{16,8},{24,0},{1,25},{9,17},{17,9},{25,1},{2,26},{10... | collective-permute-start | bytes 442376 | tf_op jit(solution)/shard_map/ppermute | solution.py:77
  17.9 0.9 %collective-permute-start.5 = (f32[8,4608]{1,0:T(8,128)S(1)}, f32[8,4608]{1,0:T(8,128)S(1)}, u32[]{:S(2)}, u32[]{:S(2)}) collective-permute-start(f32[8,4608]{1,0:T(8,128)S(1)} %get-tuple-element.43.refs_3_), channel_id=1, source_target_pairs={{0,8},{8,0},{16,24},{24,16},{1,9},{9,1},{17,25},{25,17},{2,10},{10... | collective-permute-start | bytes 442376 | tf_op jit(solution)/shard_map/ppermute | solution.py:77
  18.8 5.1 %project1.1 = (f32[8,3584]{1,0:T(8,128)S(1)}, f32[8,3584]{1,0:T(8,128)S(1)}, f32[8,3584]{1,0:T(8,128)S(1)}, f32[8,3584]{1,0:T(8,128)S(1)}, f32[2,4096,1024]{2,1,0:T(8,128)S(1)}) custom-call(f32[2,4096,1024]{2,1,0:T(8,128)S(1)} %get-tuple-element.38.same, f32[1,1,2,8,1024]{4,3,2,1,0:T(8,128)S(1)} %copy-done, ...), custom_call_target="tpu_custom_call", output_to_operand_aliasing={{4}: (0, {})} | custom-call | flops 4294967296 | bytes 33554432 | tf_op jit(solution)/shard_map/project1/pallas_call | solution.py:179
  23.9 2.1 %collective-permute-start.6 = (f32[8,3584]{1,0:T(8,128)S(1)}, f32[8,3584]{1,0:T(8,128)S(1)}, u32[]{:S(2)}, u32[]{:S(2)}) collective-permute-start(f32[8,3584]{1,0:T(8,128)S(1)} %get-tuple-element.45.refs_4_), channel_id=1, source_target_pairs={{0,6},{2,4},{4,2},{6,0},{1,7},{3,5},{5,3},{7,1},{8,14},{10,12},{12... | collective-permute-start | bytes 344072 | tf_op jit(solution)/shard_map/ppermute | solution.py:77
  26.0 0.0 collective-permute-done.2.refs_4_.refs_8_
  26.0 1.1 %collective-permute-start.7 = (f32[8,3584]{1,0:T(8,128)S(1)}, f32[8,3584]{1,0:T(8,128)S(1)}, u32[]{:S(2)}, u32[]{:S(2)}) collective-permute-start(f32[8,3584]{1,0:T(8,128)S(1)} %get-tuple-element.46.refs_5_), channel_id=1, source_target_pairs={{0,2},{2,0},{4,6},{6,4},{1,3},{3,1},{5,7},{7,5},{8,10},{10,8},{12,... | collective-permute-start | bytes 344072 | tf_op jit(solution)/shard_map/ppermute | solution.py:77
  27.1 0.0 collective-permute-done.3.refs_5_.refs_9_
  27.2 0.0 collective-permute-start.8
  27.2 0.0 collective-permute-done.4.refs_6_.refs_10_
  27.2 0.1 collective-permute-start.9
  27.3 0.0 collective-permute-done.5.refs_7_.refs_11_
  27.3 3.8 %back0.1 = (f32[32,4096]{1,0:T(8,128)S(1)}, f32[264,128]{1,0:T(8,128)S(1)}, f32[2,4096,1024]{2,1,0:T(8,128)S(1)}) custom-call(f32[2,4096,1024]{2,1,0:T(8,128)S(1)} %get-tuple-element.39.same, f32[8,4608]{1,0:T(8,128)S(1)} %get-tuple-element.40.refs_0_, f32[8,4608]{1,0:T(8,128)S(1)} %get-tuple-element.41.refs_1_, ...), custom_call_target="tpu_custom_call", output_to_operand_aliasing={{2}: (0, {})} | custom-call | flops 4294967296 | bytes 33554432 | tf_op jit(solution)/shard_map/back0/pallas_call | solution.py:232
  31.1 1.8 %collective-permute-start.10 = (f32[264,128]{1,0:T(8,128)S(1)}, f32[264,128]{1,0:T(8,128)S(1)}, u32[]{:S(2)}, u32[]{:S(2)}) collective-permute-start(f32[264,128]{1,0:T(8,128)S(1)} %get-tuple-element.50.mine), channel_id=1, source_target_pairs={{0,1},{1,0},{2,3},{3,2},{4,5},{5,4},{6,7},{7,6},{8,9},{9,8},{10,11... | collective-permute-start | bytes 405512 | tf_op jit(solution)/shard_map/ppermute | solution.py:68
  32.9 0.0 collective-permute-done.6.refs_12_
  32.9 0.4 collective-permute-done.7.refs_13_
  33.2 0.0 collective-permute-done.8.refs_14_
  33.3 0.0 collective-permute-done.9.refs_15_
  33.3 3.8 %back1.1 = (f32[32,4096]{1,0:T(8,128)S(1)}, f32[264,128]{1,0:T(8,128)S(1)}, f32[2,4096,1024]{2,1,0:T(8,128)S(1)}) custom-call(f32[2,4096,1024]{2,1,0:T(8,128)S(1)} %get-tuple-element.44.same, f32[8,4608]{1,0:T(8,128)S(1)} %get-tuple-element.40.refs_0_, f32[8,4608]{1,0:T(8,128)S(1)} %get-tuple-element.41.refs_1_, ...), custom_call_target="tpu_custom_call", output_to_operand_aliasing={{2}: (0, {})} | custom-call | flops 4294967296 | bytes 33554432 | tf_op jit(solution)/shard_map/back1/pallas_call | solution.py:232
  37.0 1.5 %collective-permute-start.11 = (f32[264,128]{1,0:T(8,128)S(1)}, f32[264,128]{1,0:T(8,128)S(1)}, u32[]{:S(2)}, u32[]{:S(2)}) collective-permute-start(f32[264,128]{1,0:T(8,128)S(1)} %get-tuple-element.53.mine.refs_8_), channel_id=1, source_target_pairs={{0,1},{1,0},{2,3},{3,2},{4,5},{5,4},{6,7},{7,6},{8,9},{9,8},{10,11... | collective-permute-start | bytes 405512 | tf_op jit(solution)/shard_map/ppermute | solution.py:68
  38.6 0.0 collective-permute-done.10.other
  38.6 1.8 %collective-permute-start.12 = (f32[8,1024]{1,0:T(8,128)S(1)}, f32[8,1024]{1,0:T(8,128)S(1)}, u32[]{:S(2)}, u32[]{:S(2)}) collective-permute-start(f32[8,1024]{1,0:T(8,128)S(1)} %get-tuple-element.56.refs_0_), channel_id=1, source_target_pairs={{0,6},{2,4},{4,2},{6,0},{1,7},{3,5},{5,3},{7,1},{8,14},{10,12},{12... | collective-permute-start | bytes 98312 | tf_op jit(solution)/shard_map/ppermute | solution.py:77
  40.4 0.0 collective-permute-start.13
  40.4 0.0 collective-permute-start.14
  40.4 1.0 %collective-permute-start.15 = (f32[8,1024]{1,0:T(8,128)S(1)}, f32[8,1024]{1,0:T(8,128)S(1)}, u32[]{:S(2)}, u32[]{:S(2)}) collective-permute-start(f32[8,1024]{1,0:T(8,128)S(1)} %get-tuple-element.59.refs_3_), channel_id=1, source_target_pairs={{0,8},{8,0},{16,24},{24,16},{1,9},{9,1},{17,25},{25,17},{2,10},{10... | collective-permute-start | bytes 98312 | tf_op jit(solution)/shard_map/ppermute | solution.py:77
  41.4 0.8 %inverse.1 = (f32[32,32]{1,0:T(8,128)S(1)}, f32[2,4096,1024]{2,1,0:T(8,128)S(1)}) custom-call(f32[2,4096,1024]{2,1,0:T(8,128)S(1)} %get-tuple-element.51.same, f32[264,128]{1,0:T(8,128)S(1)} %get-tuple-element.50.mine, f32[264,128]{1,0:T(8,128)S(1)} %collective-permute-done.10.other), custom_call_target="tpu_custom_call", output_to_operand_aliasing={{1}: (0, {})} | custom-call | tf_op jit(solution)/shard_map/inverse/pallas_call | solution.py:294
  42.2 0.3 collective-permute-done.11.other.refs_9_
  42.5 1.5 %collective-permute-start.16 = (f32[8,1024]{1,0:T(8,128)S(1)}, f32[8,1024]{1,0:T(8,128)S(1)}, u32[]{:S(2)}, u32[]{:S(2)}) collective-permute-start(f32[8,1024]{1,0:T(8,128)S(1)} %get-tuple-element.63.refs_0_), channel_id=1, source_target_pairs={{0,6},{2,4},{4,2},{6,0},{1,7},{3,5},{5,3},{7,1},{8,14},{10,12},{12... | collective-permute-start | bytes 98312 | tf_op jit(solution)/shard_map/ppermute | solution.py:77
  44.0 0.5 collective-permute-done.12.refs_4_
  44.5 0.6 collective-permute-start.17
  45.0 0.0 collective-permute-done.13.refs_5_
  45.0 0.6 %collective-permute-start.18 = (f32[8,1024]{1,0:T(8,128)S(1)}, f32[8,1024]{1,0:T(8,128)S(1)}, u32[]{:S(2)}, u32[]{:S(2)}) collective-permute-start(f32[8,1024]{1,0:T(8,128)S(1)} %get-tuple-element.65.refs_2_), channel_id=1, source_target_pairs={{0,24},{8,16},{16,8},{24,0},{1,25},{9,17},{17,9},{25,1},{2,26},{10... | collective-permute-start | bytes 98312 | tf_op jit(solution)/shard_map/ppermute | solution.py:77
  45.7 0.0 collective-permute-done.14.refs_6_
  45.7 1.1 %collective-permute-start.19 = (f32[8,1024]{1,0:T(8,128)S(1)}, f32[8,1024]{1,0:T(8,128)S(1)}, u32[]{:S(2)}, u32[]{:S(2)}) collective-permute-start(f32[8,1024]{1,0:T(8,128)S(1)} %get-tuple-element.66.refs_3_), channel_id=1, source_target_pairs={{0,8},{8,0},{16,24},{24,16},{1,9},{9,1},{17,25},{25,17},{2,10},{10... | collective-permute-start | bytes 98312 | tf_op jit(solution)/shard_map/ppermute | solution.py:77
  46.8 0.0 collective-permute-done.15.refs_7_
  46.8 5.4 %mix0.1 = (f32[1,1,2,4096,1024]{4,3,2,1,0:T(8,128)}, f32[1,1,2,8,1024]{4,3,2,1,0:T(8,128)}, f32[1,1,2,8,1024]{4,3,2,1,0:T(8,128)}, f32[2,4096,1024]{2,1,0:T(8,128)S(1)}) custom-call(f32[2,4096,1024]{2,1,0:T(8,128)S(1)} %get-tuple-element.54.same, f32[32,4096]{1,0:T(8,128)S(1)} %get-tuple-element.55.differ, ...), custom_call_target="tpu_custom_call", output_to_operand_aliasing={{3}: (0, {})} | custom-call | flops 4294967296 | bytes 33554432 | tf_op jit(solution)/shard_map/mix0/pallas_call | solution.py:395
  52.1 0.0 collective-permute-done.16.refs_4_
  52.2 0.0 collective-permute-done.17.refs_5_
  52.2 0.0 collective-permute-done.18.refs_6_
  52.2 0.0 collective-permute-done.19.refs_7_
  52.2 7.3 %mix1.1 = (f32[1,1,2,4096,1024]{4,3,2,1,0:T(8,128)}, f32[1,1,2,8,1024]{4,3,2,1,0:T(8,128)}, f32[1,1,2,8,1024]{4,3,2,1,0:T(8,128)}, f32[2,4096,1024]{2,1,0:T(8,128)S(1)}) custom-call(f32[2,4096,1024]{2,1,0:T(8,128)S(1)} %get-tuple-element.61.same, ...), custom_call_target="tpu_custom_call", output_to_operand_aliasing={{3}: (0, {}), {0}: (12, {}), {1}: (13, {}), {2}: (14, {})} | custom-call | flops 4294967296 | bytes 33554432 | tf_op jit(solution)/shard_map/mix1/pallas_call | solution.py:395
  (6 shorter events, 0.0 us)
Async XLA Ops:
  0.6 7.6 %copy-start.1 = (f32[1,1,2,8,1024]{4,3,2,1,0:T(8,128)S(1)}, f32[1,1,2,8,1024]{4,3,2,1,0:T(8,128)}, u32[]{:S(2)}) copy-start(f32[1,1,2,8,1024]{4,3,2,1,0:T(8,128)} %f2.3) | copy-start | bytes 196612
  0.6 7.6 %copy-start = (f32[1,1,2,8,1024]{4,3,2,1,0:T(8,128)S(1)}, f32[1,1,2,8,1024]{4,3,2,1,0:T(8,128)}, u32[]{:S(2)}) copy-start(f32[1,1,2,8,1024]{4,3,2,1,0:T(8,128)} %f0.3) | copy-start | bytes 196612
  0.7 6.7 %collective-permute-start.1 = (f32[1,1,2,8,1024]{4,3,2,1,0:T(8,128)}, f32[1,1,2,8,1024]{4,3,2,1,0:T(8,128)S(1)}, u32[]{:S(2)}, u32[]{:S(2)}) collective-permute-start(f32[1,1,2,8,1024]{4,3,2,1,0:T(8,128)} %f2.3), channel_id=1, source_target_pairs={{0,8},{8,16},{16,24},{24,0},{1,9},{9,17},{17,25},{25,1},{2,10},{10... | collective-permute-start | bytes 196616 | tf_op jit(solution)/shard_map/ppermute | solution.py:63
  1.2 7.1 %collective-permute-start = (f32[1,1,2,8,1024]{4,3,2,1,0:T(8,128)}, f32[1,1,2,8,1024]{4,3,2,1,0:T(8,128)S(1)}, u32[]{:S(2)}, u32[]{:S(2)}) collective-permute-start(f32[1,1,2,8,1024]{4,3,2,1,0:T(8,128)} %f0.3), channel_id=1, source_target_pairs={{0,2},{2,4},{4,6},{6,0},{1,3},{3,5},{5,7},{7,1},{8,10},{10,12},{12... | collective-permute-start | bytes 196616 | tf_op jit(solution)/shard_map/ppermute | solution.py:63
  14.8 11.2 %collective-permute-start.2 = (f32[8,4608]{1,0:T(8,128)S(1)}, f32[8,4608]{1,0:T(8,128)S(1)}, u32[]{:S(2)}, u32[]{:S(2)}) collective-permute-start(f32[8,4608]{1,0:T(8,128)S(1)} %get-tuple-element.40.refs_0_), channel_id=1, source_target_pairs={{0,6},{2,4},{4,2},{6,0},{1,7},{3,5},{5,3},{7,1},{8,14},{10,12},{12... | collective-permute-start | bytes 442376 | tf_op jit(solution)/shard_map/ppermute | solution.py:77
  17.1 10.1 %collective-permute-start.3 = (f32[8,4608]{1,0:T(8,128)S(1)}, f32[8,4608]{1,0:T(8,128)S(1)}, u32[]{:S(2)}, u32[]{:S(2)}) collective-permute-start(f32[8,4608]{1,0:T(8,128)S(1)} %get-tuple-element.41.refs_1_), channel_id=1, source_target_pairs={{0,2},{2,0},{4,6},{6,4},{1,3},{3,1},{5,7},{7,5},{8,10},{10,8},{12,... | collective-permute-start | bytes 442376 | tf_op jit(solution)/shard_map/ppermute | solution.py:77
  17.1 10.1 %collective-permute-start.4 = (f32[8,4608]{1,0:T(8,128)S(1)}, f32[8,4608]{1,0:T(8,128)S(1)}, u32[]{:S(2)}, u32[]{:S(2)}) collective-permute-start(f32[8,4608]{1,0:T(8,128)S(1)} %get-tuple-element.42.refs_2_), channel_id=1, source_target_pairs={{0,24},{8,16},{16,8},{24,0},{1,25},{9,17},{17,9},{25,1},{2,26},{10... | collective-permute-start | bytes 442376 | tf_op jit(solution)/shard_map/ppermute | solution.py:77
  17.9 9.3 %collective-permute-start.5 = (f32[8,4608]{1,0:T(8,128)S(1)}, f32[8,4608]{1,0:T(8,128)S(1)}, u32[]{:S(2)}, u32[]{:S(2)}) collective-permute-start(f32[8,4608]{1,0:T(8,128)S(1)} %get-tuple-element.43.refs_3_), channel_id=1, source_target_pairs={{0,8},{8,0},{16,24},{24,16},{1,9},{9,1},{17,25},{25,17},{2,10},{10... | collective-permute-start | bytes 442376 | tf_op jit(solution)/shard_map/ppermute | solution.py:77
  23.9 9.0 %collective-permute-start.6 = (f32[8,3584]{1,0:T(8,128)S(1)}, f32[8,3584]{1,0:T(8,128)S(1)}, u32[]{:S(2)}, u32[]{:S(2)}) collective-permute-start(f32[8,3584]{1,0:T(8,128)S(1)} %get-tuple-element.45.refs_4_), channel_id=1, source_target_pairs={{0,6},{2,4},{4,2},{6,0},{1,7},{3,5},{5,3},{7,1},{8,14},{10,12},{12... | collective-permute-start | bytes 344072 | tf_op jit(solution)/shard_map/ppermute | solution.py:77
  26.0 7.2 %collective-permute-start.7 = (f32[8,3584]{1,0:T(8,128)S(1)}, f32[8,3584]{1,0:T(8,128)S(1)}, u32[]{:S(2)}, u32[]{:S(2)}) collective-permute-start(f32[8,3584]{1,0:T(8,128)S(1)} %get-tuple-element.46.refs_5_), channel_id=1, source_target_pairs={{0,2},{2,0},{4,6},{6,4},{1,3},{3,1},{5,7},{7,5},{8,10},{10,8},{12,... | collective-permute-start | bytes 344072 | tf_op jit(solution)/shard_map/ppermute | solution.py:77
  27.2 6.1 %collective-permute-start.8 = (f32[8,3584]{1,0:T(8,128)S(1)}, f32[8,3584]{1,0:T(8,128)S(1)}, u32[]{:S(2)}, u32[]{:S(2)}) collective-permute-start(f32[8,3584]{1,0:T(8,128)S(1)} %get-tuple-element.47.refs_6_), channel_id=1, source_target_pairs={{0,24},{8,16},{16,8},{24,0},{1,25},{9,17},{17,9},{25,1},{2,26},{10... | collective-permute-start | bytes 344072 | tf_op jit(solution)/shard_map/ppermute | solution.py:77
  27.2 6.1 %collective-permute-start.9 = (f32[8,3584]{1,0:T(8,128)S(1)}, f32[8,3584]{1,0:T(8,128)S(1)}, u32[]{:S(2)}, u32[]{:S(2)}) collective-permute-start(f32[8,3584]{1,0:T(8,128)S(1)} %get-tuple-element.48.refs_7_), channel_id=1, source_target_pairs={{0,8},{8,0},{16,24},{24,16},{1,9},{9,1},{17,25},{25,17},{2,10},{10... | collective-permute-start | bytes 344072 | tf_op jit(solution)/shard_map/ppermute | solution.py:77
  31.1 7.5 %collective-permute-start.10 = (f32[264,128]{1,0:T(8,128)S(1)}, f32[264,128]{1,0:T(8,128)S(1)}, u32[]{:S(2)}, u32[]{:S(2)}) collective-permute-start(f32[264,128]{1,0:T(8,128)S(1)} %get-tuple-element.50.mine), channel_id=1, source_target_pairs={{0,1},{1,0},{2,3},{3,2},{4,5},{5,4},{6,7},{7,6},{8,9},{9,8},{10,11... | collective-permute-start | bytes 405512 | tf_op jit(solution)/shard_map/ppermute | solution.py:68
  37.0 5.4 %collective-permute-start.11 = (f32[264,128]{1,0:T(8,128)S(1)}, f32[264,128]{1,0:T(8,128)S(1)}, u32[]{:S(2)}, u32[]{:S(2)}) collective-permute-start(f32[264,128]{1,0:T(8,128)S(1)} %get-tuple-element.53.mine.refs_8_), channel_id=1, source_target_pairs={{0,1},{1,0},{2,3},{3,2},{4,5},{5,4},{6,7},{7,6},{8,9},{9,8},{10,11... | collective-permute-start | bytes 405512 | tf_op jit(solution)/shard_map/ppermute | solution.py:68
  38.6 5.9 %collective-permute-start.12 = (f32[8,1024]{1,0:T(8,128)S(1)}, f32[8,1024]{1,0:T(8,128)S(1)}, u32[]{:S(2)}, u32[]{:S(2)}) collective-permute-start(f32[8,1024]{1,0:T(8,128)S(1)} %get-tuple-element.56.refs_0_), channel_id=1, source_target_pairs={{0,6},{2,4},{4,2},{6,0},{1,7},{3,5},{5,3},{7,1},{8,14},{10,12},{12... | collective-permute-start | bytes 98312 | tf_op jit(solution)/shard_map/ppermute | solution.py:77
  40.4 4.7 %collective-permute-start.13 = (f32[8,1024]{1,0:T(8,128)S(1)}, f32[8,1024]{1,0:T(8,128)S(1)}, u32[]{:S(2)}, u32[]{:S(2)}) collective-permute-start(f32[8,1024]{1,0:T(8,128)S(1)} %get-tuple-element.57.refs_1_), channel_id=1, source_target_pairs={{0,2},{2,0},{4,6},{6,4},{1,3},{3,1},{5,7},{7,5},{8,10},{10,8},{12,... | collective-permute-start | bytes 98312 | tf_op jit(solution)/shard_map/ppermute | solution.py:77
  40.4 5.3 %collective-permute-start.14 = (f32[8,1024]{1,0:T(8,128)S(1)}, f32[8,1024]{1,0:T(8,128)S(1)}, u32[]{:S(2)}, u32[]{:S(2)}) collective-permute-start(f32[8,1024]{1,0:T(8,128)S(1)} %get-tuple-element.58.refs_2_), channel_id=1, source_target_pairs={{0,24},{8,16},{16,8},{24,0},{1,25},{9,17},{17,9},{25,1},{2,26},{10... | collective-permute-start | bytes 98312 | tf_op jit(solution)/shard_map/ppermute | solution.py:77
  40.4 6.4 %collective-permute-start.15 = (f32[8,1024]{1,0:T(8,128)S(1)}, f32[8,1024]{1,0:T(8,128)S(1)}, u32[]{:S(2)}, u32[]{:S(2)}) collective-permute-start(f32[8,1024]{1,0:T(8,128)S(1)} %get-tuple-element.59.refs_3_), channel_id=1, source_target_pairs={{0,8},{8,0},{16,24},{24,16},{1,9},{9,1},{17,25},{25,17},{2,10},{10... | collective-permute-start | bytes 98312 | tf_op jit(solution)/shard_map/ppermute | solution.py:77
  42.5 9.7 %collective-permute-start.16 = (f32[8,1024]{1,0:T(8,128)S(1)}, f32[8,1024]{1,0:T(8,128)S(1)}, u32[]{:S(2)}, u32[]{:S(2)}) collective-permute-start(f32[8,1024]{1,0:T(8,128)S(1)} %get-tuple-element.63.refs_0_), channel_id=1, source_target_pairs={{0,6},{2,4},{4,2},{6,0},{1,7},{3,5},{5,3},{7,1},{8,14},{10,12},{12... | collective-permute-start | bytes 98312 | tf_op jit(solution)/shard_map/ppermute | solution.py:77
  44.5 7.7 %collective-permute-start.17 = (f32[8,1024]{1,0:T(8,128)S(1)}, f32[8,1024]{1,0:T(8,128)S(1)}, u32[]{:S(2)}, u32[]{:S(2)}) collective-permute-start(f32[8,1024]{1,0:T(8,128)S(1)} %get-tuple-element.64.refs_1_), channel_id=1, source_target_pairs={{0,2},{2,0},{4,6},{6,4},{1,3},{3,1},{5,7},{7,5},{8,10},{10,8},{12,... | collective-permute-start | bytes 98312 | tf_op jit(solution)/shard_map/ppermute | solution.py:77
  45.0 7.1 %collective-permute-start.18 = (f32[8,1024]{1,0:T(8,128)S(1)}, f32[8,1024]{1,0:T(8,128)S(1)}, u32[]{:S(2)}, u32[]{:S(2)}) collective-permute-start(f32[8,1024]{1,0:T(8,128)S(1)} %get-tuple-element.65.refs_2_), channel_id=1, source_target_pairs={{0,24},{8,16},{16,8},{24,0},{1,25},{9,17},{17,9},{25,1},{2,26},{10... | collective-permute-start | bytes 98312 | tf_op jit(solution)/shard_map/ppermute | solution.py:77
  45.7 6.5 %collective-permute-start.19 = (f32[8,1024]{1,0:T(8,128)S(1)}, f32[8,1024]{1,0:T(8,128)S(1)}, u32[]{:S(2)}, u32[]{:S(2)}) collective-permute-start(f32[8,1024]{1,0:T(8,128)S(1)} %get-tuple-element.66.refs_3_), channel_id=1, source_target_pairs={{0,8},{8,0},{16,24},{24,16},{1,9},{9,1},{17,25},{25,17},{2,10},{10... | collective-permute-start | bytes 98312 | tf_op jit(solution)/shard_map/ppermute | solution.py:77
